TPU v7x, 128 devices: a whole 4x4x4 slice. The times are simulated.
128 devices in a mesh: fsdp: 16 (over y_hi, x, core), tp: 8 (over y_lo, z).
Axes of the slice: x: 4, y: 4 (y_hi: 2, y_lo: 2; y = y_hi * 2 + y_lo), z: 4, core: 2. Of those that a mesh axis runs over, the one named last changes fastest.
Arguments:
- tokens: bfloat16 [12288, 3584], P('fsdp', 'tp'), may hold values from -6 to 6
- gate_master: float32 [3584, 9216], P('fsdp', 'tp'), may hold values from -0.09375 to 0.09375
- up_master: float32 [3584, 9216], P('fsdp', 'tp'), may hold values from -0.09375 to 0.09375
- down_master: float32 [9216, 3584], P('fsdp', 'tp'), may hold values from -0.0625 to 0.0625
Outputs:
- mixed: bfloat16 [12288, 3584], P('fsdp', 'tp')
- log_amax: float32 [3, 28, 72], replicated
All inputs are finite; a program needn't handle non-finite values.
Results may differ from a plain program's by a relative error of at most 0.0071.
Values may be sent and summed in bfloat16 or wider, within the bound.
No kernel may reach another device: no remote copies, remote signals or barrier semaphores. Data moves between devices by JAX's collectives and lax.ppermute only.
A program may use at most 192 MiB of HBM per device.

v0:
```python
import functools

import jax
import jax.numpy as jnp
from jax import lax
from jax.experimental import pallas as pl
from jax.experimental.pallas import tpu as pltpu
from jax.sharding import PartitionSpec as P

D = 3584
FF = 9216
BLOCK = 128

FP8_MAX = 448.0
EPS = 1e-06
SMALLEST_NORMAL = 2.0 ** (-6)
AXES = ("fsdp", "tp")
VMEM_LIMIT = 48 * 1024 * 1024
TILE = 256
WIDE = 512


def snapped(value):
    magnitude = jnp.abs(value)
    exponent = jnp.floor(jnp.log2(jnp.maximum(magnitude, SMALLEST_NORMAL)))
    step_size = jnp.exp2(exponent - 3.0)
    return jnp.sign(value) * step_size * jnp.floor(magnitude / step_size + 0.5)


def place(y, x, core, z):
    y, x, z = y % 4, x % 4, z % 4
    return (((y // 2) * 4 + x) * 2 + core) * 8 + (y % 2) * 4 + z


def send(array, target):
    pairs = [
        (place(y, x, core, z), place(*target(y, x, core, z)))
        for y in range(4)
        for x in range(4)
        for core in range(2)
        for z in range(4)
    ]
    return lax.ppermute(array, AXES, pairs)


def x_up(y, x, core, z):
    return y, x + 1, core, z


def x_down(y, x, core, z):
    return y, x - 1, core, z


def z_up(y, x, core, z):
    return y, x, core, z + 1


def z_down(y, x, core, z):
    return y, x, core, z - 1


def y_near(y, x, core, z):
    return y ^ 1, x, core, z


def y_far(y, x, core, z):
    return y + 2, x, core, z


def other_core(y, x, core, z):
    return y, x, 1 - core, z


def to_ff_group(y, x, core, z):
    y_hi, y_lo = y // 2, y % 2
    return (y_lo ^ y_hi) * 2 + y_hi, z - x, core, x


def to_chunk(dy, dx):
    def target(y, x, core, z):
        y_hi, y_lo = y // 2, y % 2
        return y_hi * 2 + (y_lo ^ y_hi ^ dy), x, core, z + x + dx

    return target


def block_maxima(local, row_start, column_start, rows, columns):
    height, breadth = local.shape
    span_rows = (height - 1) // BLOCK + 2
    span_columns = (breadth - 1) // BLOCK + 2
    magnitude = jnp.abs(local)
    which_row = (row_start % BLOCK + jnp.arange(height, dtype=jnp.int32)) // BLOCK
    by_row = jnp.stack(
        [
            jnp.max(jnp.where((which_row == k)[:, None], magnitude, 0.0), axis=0)
            for k in range(span_rows)
        ]
    )
    which_column = (column_start % BLOCK + jnp.arange(breadth, dtype=jnp.int32)) // BLOCK
    pick = which_column[None, :] == jnp.arange(span_columns, dtype=jnp.int32)[:, None]
    part = jnp.max(jnp.where(pick[None], by_row[:, None, :], 0.0), axis=2)
    table = jnp.zeros((rows // BLOCK + span_rows, columns // BLOCK + span_columns), jnp.float32)
    return lax.dynamic_update_slice(table, part, (row_start // BLOCK, column_start // BLOCK))


def spread(scales, row_start, height, column_start, breadth):
    span_rows = (height - 1) // BLOCK + 2
    span_columns = (breadth - 1) // BLOCK + 2
    near = lax.dynamic_slice(
        scales, (row_start // BLOCK, column_start // BLOCK), (span_rows, span_columns)
    )
    which_row = (row_start % BLOCK + jnp.arange(height, dtype=jnp.int32)) // BLOCK
    which_column = (column_start % BLOCK + jnp.arange(breadth, dtype=jnp.int32)) // BLOCK
    wide = jnp.zeros((span_rows, breadth), jnp.float32)
    for k in range(span_columns):
        wide = jnp.where((which_column == k)[None, :], near[:, k : k + 1], wide)
    full = jnp.zeros((height, breadth), jnp.float32)
    for k in range(span_rows):
        full = jnp.where((which_row == k)[:, None], wide[k : k + 1, :], full)
    return full


def rollout(master, table, row_start, column_start):
    height, breadth = master.shape
    scale = spread((table + EPS) / FP8_MAX, row_start, height, column_start, breadth)
    return (snapped(master / scale) * scale).astype(jnp.bfloat16)


ORDER = ((0, 0), (1, 0), (0, -1), (0, 1), (1, -1), (1, 1), (0, 2), (1, 2))


def after(array, *others):
    return lax.optimization_barrier((array, *others))[0]


def ring(own, across, up, down, others=(), between=lambda n, blocks: ()):
    far = send(own, across)
    own_l, own_r = send(own, up), send(own, down)
    far = after(far, own_l, own_r, *others)
    far_l, far_r = send(far, up), send(far, down)
    others = between(0, [own, far, own_l, own_r])
    own_l, far_r = after(own_l, far_l, *others), after(far_r, far_l, *others)
    own_ll, far_rr = send(own_l, up), send(far_r, down)
    between(1, [far_l, far_r])
    return [own, far, own_l, own_r, far_l, far_r, own_ll, far_rr]


TOKEN_ORDER = ((0, 0), (1, 0), (0, -1), (1, -1), (0, 1), (1, 1), (0, 2), (1, 2))


def token_ring(own):
    pair = jnp.stack([own, send(own, y_near)])
    left, right = send(pair, z_up), send(pair, z_down)
    own_ll, near_rr = send(left[0], z_up), send(right[1], z_down)
    return jnp.concatenate([pair, left, right, own_ll[None], near_rr[None]])


def token_kernel(count, has_before, last, info, *refs):
    tokens, refs = refs[:count], list(refs[count:])
    before = refs.pop(0) if has_before else None
    blocks, (out, scratch, sems) = refs[: 2 * count], refs[2 * count :]
    half = blocks[0].shape[0]

    @pl.when(pl.program_id(0) == 0)
    def _():
        copies = []
        for n in range(count):
            for side in range(2):
                place = info[8] if side == 0 else 1 - info[8]
                rows = pl.ds(pl.multiple_of(n * WIDE + place * half, 16), half)
                copies.append(
                    pltpu.make_async_copy(
                        blocks[2 * n + side], scratch.at[rows, :], sems.at[2 * n + side]
                    )
                )
        for copy in copies:
            copy.start()
        for n in range(count):
            pad = WIDE - 2 * half
            scratch[n * WIDE + 2 * half : (n + 1) * WIDE, :] = jnp.zeros(
                (pad, scratch.shape[1]), scratch.dtype
            )
        for copy in copies:
            copy.wait()

    rows = jnp.concatenate([token[...] for token in tokens], axis=1)
    total = jnp.dot(rows, scratch[...], preferred_element_type=jnp.float32)
    if has_before:
        total += before[...]
    if last:
        middle = total.shape[1] // 2
        gate = total[:, :middle]
        total = gate / (1.0 + jnp.exp(-gate)) * total[:, middle:]
    out[...] = total.astype(out.dtype)


def token_sum(info, tokens, first, blocks, before=None, last=False):
    rows, columns = tokens.shape[1], blocks[0].shape[1]
    count = len(blocks) // 2
    width = columns // 2 if last else columns

    def token_block(n):
        return pl.BlockSpec((None, TILE, WIDE), lambda m, info: (info[first + n], m, 0))

    def tile(width):
        return pl.BlockSpec((TILE, width), lambda m, info: (m, 0))

    return pl.pallas_call(
        functools.partial(token_kernel, count, before is not None, last),
        out_shape=jax.ShapeDtypeStruct((rows, width), jnp.bfloat16 if last else jnp.float32),
        grid_spec=pltpu.PrefetchScalarGridSpec(
            num_scalar_prefetch=1,
            grid=(rows // TILE,),
            in_specs=[token_block(n) for n in range(count)]
            + ([] if before is None else [tile(columns)])
            + [pl.BlockSpec(memory_space=pl.ANY)] * (2 * count),
            out_specs=tile(width),
            scratch_shapes=[
                pltpu.VMEM((count * WIDE, columns), jnp.bfloat16),
                pltpu.SemaphoreType.DMA((2 * count,)),
            ],
        ),
        compiler_params=pltpu.CompilerParams(vmem_limit_bytes=VMEM_LIMIT),
        cost_estimate=pl.CostEstimate(
            flops=2 * rows * columns * count * WIDE,
            bytes_accessed=rows * columns * 8,
            transcendentals=0,
        ),
    )(info, *([tokens] * count), *([] if before is None else [before]), *blocks)


def vmem(n):
    return [pl.BlockSpec(memory_space=pltpu.VMEM)] * n


def down_kernel(info, hidden, *refs):
    blocks, outs = refs[: 2 * len(refs) // 3], refs[2 * len(refs) // 3 :]
    for n, out in enumerate(outs):
        mine, theirs = blocks[2 * n][...], blocks[2 * n + 1][...]
        low = jnp.where(info[8] == 0, mine, theirs)
        high = jnp.where(info[8] == 0, theirs, mine)
        out[...] = lax.dot_general(
            jnp.concatenate([low, high], axis=1),
            hidden[...],
            (((1,), (1,)), ((), ())),
            preferred_element_type=jnp.float32,
        ).astype(out.dtype)


def down_terms(info, hidden, blocks):
    rows, depth = hidden.shape
    columns = blocks[0].shape[0]
    count = len(blocks) // 2
    return pl.pallas_call(
        down_kernel,
        out_shape=[jax.ShapeDtypeStruct((columns, rows), jnp.bfloat16)] * count,
        in_specs=[pl.BlockSpec(memory_space=pltpu.SMEM)] + vmem(1 + len(blocks)),
        out_specs=vmem(count),
        compiler_params=pltpu.CompilerParams(vmem_limit_bytes=VMEM_LIMIT),
        cost_estimate=pl.CostEstimate(
            flops=2 * count * rows * columns * depth,
            bytes_accessed=rows * columns * 4,
            transcendentals=0,
        ),
    )(info, hidden, *blocks)


def on_device(tokens, gate_master, up_master, down_master):
    fsdp_place = lax.axis_index("fsdp")
    tp_place = lax.axis_index("tp")
    core = fsdp_place % 2
    y_hi, x = fsdp_place // 8, (fsdp_place // 2) % 4
    y_lo, z = tp_place // 4, tp_place % 4
    chips = [(y_hi ^ dy, (x + dx + 4) % 4) for dy, dx in ORDER]
    gate_height, gate_breadth = gate_master.shape
    down_height, down_breadth = down_master.shape
    gate_at = (fsdp_place * gate_height, tp_place * gate_breadth)
    down_at = (fsdp_place * down_height, tp_place * down_breadth)

    tables = [
        block_maxima(gate_master, *gate_at, D, FF),
        block_maxima(up_master, *gate_at, D, FF),
        block_maxima(down_master, *down_at, FF, D),
    ]
    rows = D // BLOCK + 12
    columns = FF // BLOCK + 56
    pad = lambda a: jnp.pad(a, ((0, rows - a.shape[0]), (0, columns - a.shape[1])))
    table = jnp.concatenate([pad(tables[0]), pad(tables[1]), pad(tables[2].T)])

    def step(table, target):
        return jnp.maximum(table, send(table, target))

    padded = jnp.pad(after(tokens, table), ((0, 0), (0, WIDE - tokens.shape[1])))
    table = step(table, other_core)
    table, padded = lax.optimization_barrier((table, padded))
    relative = token_ring(padded)
    down_table = step(table, lambda y, x, core, z: (y, x, core, z ^ 1))
    table = step(table, lambda y, x, core, z: (y, x ^ 1, core, z))
    gate_up = jnp.concatenate(
        [
            rollout(gate_master, table[:rows], *gate_at),
            rollout(up_master, table[rows : 2 * rows], *gate_at),
        ],
        axis=1,
    )
    gate_up, down_table = lax.optimization_barrier((gate_up, down_table))
    pairs = []

    def swap(n, blocks):
        others = [send(block, other_core) for block in blocks]
        for block, other in zip(blocks, others):
            pairs.extend((block, other))
        return others

    blocks = ring(gate_up, y_far, x_up, x_down, (), swap)
    swap(2, blocks[6:])
    down_table = after(down_table, *blocks[:4])
    down_weight = rollout(down_master, down_table[2 * rows :].T, *down_at)
    down_block = send(after(down_weight.T, blocks[4]), to_ff_group)

    table = jnp.maximum(table, down_table)
    every = jnp.max(lax.all_gather(table, "fsdp"), axis=0)
    every = jnp.max(lax.all_gather(every, "tp"), axis=0)
    log_amax = jnp.log(
        jnp.stack([every[k * rows : k * rows + D // BLOCK, : FF // BLOCK] for k in range(3)]) + EPS
    )

    order = [TOKEN_ORDER.index((dy, dx)) for dy in range(2) for dx in (0, 1, 2, -1)]
    by_offset = jnp.array(order, jnp.int32)
    info = jnp.stack(
        [by_offset[(chip_y ^ y_lo) * 4 + (chip_x - z + 4) % 4] for chip_y, chip_x in chips] + [core]
    )

    early = token_sum(info, relative, 0, pairs[:12])
    down_block, early = lax.optimization_barrier((down_block, early))
    down_block = after(down_block, blocks[6], blocks[7])
    hidden = token_sum(info, relative, 6, pairs[12:], early, last=True)
    down_blocks = ring(down_block, y_far, x_up, x_down, (hidden,))

    def both(blocks):
        return [b for block in blocks for b in (block, send(block, other_core))]

    total = 0.0
    for n in range(0, 8, 2):
        terms = down_terms(info, hidden, both(down_blocks[n : n + 2]))
        for k in range(2):
            total += send(terms[k], to_chunk(*ORDER[n + k])).astype(jnp.float32)
    return total.astype(jnp.bfloat16).T, log_amax


def solution(mesh):
    return jax.shard_map(
        on_device,
        mesh=mesh,
        in_specs=(P("fsdp", "tp"), P("fsdp", "tp"), P("fsdp", "tp"), P("fsdp", "tp")),
        out_specs=(P("fsdp", "tp"), P()),
        check_vma=False,
    )
```

profile of v0, /device:TPU:6, one launch (start us, length us, event | category | flops | bytes accessed | tf_op | source)
XLA Modules:
  0.0 331.6 jit_solution(12512816440047368091)
XLA Ops:
  17.9 3.2 collective-permute-start.8
  23.7 21.4 %collective-permute-done.8.refs_8_ = bf16[224,2304]{1,0:T(8,128)(2,1)S(1)} collective-permute-done((bf16[224,2304]{1,0:T(8,128)(2,1)S(1)}, bf16[224,2304]{1,0:T(8,128)(2,1)S(1)}, u32[]{:S(2)}, u32[]{:S(2)}) %collective-permute-start.8) | collective-permute-done | bytes 1032224 | tf_op jit(solution)/shard_map/ppermute | solution.py:43
  46.1 13.9 %collective-permute-done.1 = bf16[768,512]{1,0:T(8,128)(2,1)S(1)} collective-permute-done((bf16[768,512]{1,0:T(8,128)(2,1)S(1)}, bf16[768,512]{1,0:T(8,128)(2,1)S(1)}, u32[]{:S(2)}, u32[]{:S(2)}) %collective-permute-start.1) | collective-permute-done | bytes 786464 | tf_op jit(solution)/shard_map/ppermute | solution.py:43
  63.2 4.5 %collective-permute-done.11.refs_14_ = bf16[224,2304]{1,0:T(8,128)(2,1)S(1)} collective-permute-done((bf16[224,2304]{1,0:T(8,128)(2,1)S(1)}, bf16[224,2304]{1,0:T(8,128)(2,1)S(1)}, u32[]{:S(2)}, u32[]{:S(2)}) %collective-permute-start.11) | collective-permute-done | bytes 1032224 | tf_op jit(solution)/shard_map/ppermute | solution.py:43
  69.7 5.0 %stack.73.info = s32[9]{0:T(128)S(1)} concatenate(s32[1]{0:T(128)} %get-tuple-element.119, s32[1]{0:T(128)} %get-tuple-element.118, s32[1]{0:T(128)} %get-tuple-element.117, s32[1]{0:T(128)} %get-tuple-element.116, s32[1]{0:T(128)} %get-tuple-element.115, s32[1]{0:T(128)} %get-tuple-element.114, s32[1]{0:T(128)} %get-tuple-element.120, s32[1]{0:T(128)} %get-tuple-element.113, s32[1]{0:T(128)} %bitcast), dimensions={0} | concatenate | bytes 72 | tf_op jit(solution)/shard_map/stack | solution.py:330
  74.8 2.6 collective-permute-start.3
  78.7 12.4 %collective-permute-done.18.refs_16_ = bf16[224,2304]{1,0:T(8,128)(2,1)} collective-permute-done((bf16[224,2304]{1,0:T(8,128)(2,1)S(1)}, bf16[224,2304]{1,0:T(8,128)(2,1)}, u32[]{:S(2)}, u32[]{:S(2)}) %collective-permute-start.18) | collective-permute-done | bytes 1032224 | tf_op jit(solution)/shard_map/ppermute | solution.py:43
  91.1 3.2 collective-permute-start.20
  94.4 2.6 collective-permute-done.2
  98.4 10.3 %collective-permute-done.3 = bf16[2,768,512]{2,1,0:T(8,128)(2,1)S(1)} collective-permute-done((bf16[2,768,512]{2,1,0:T(8,128)(2,1)}, bf16[2,768,512]{2,1,0:T(8,128)(2,1)S(1)}, u32[]{:S(2)}, u32[]{:S(2)}) %collective-permute-start.3) | collective-permute-done | bytes 1572896 | tf_op jit(solution)/shard_map/ppermute | solution.py:43
  108.7 7.7 %collective-permute-done.4 = bf16[768,512]{1,0:T(8,128)(2,1)S(1)} collective-permute-done((bf16[768,512]{1,0:T(8,128)(2,1)S(1)}, bf16[768,512]{1,0:T(8,128)(2,1)S(1)}, u32[]{:S(2)}, u32[]{:S(2)}) %collective-permute-start.4) | collective-permute-done | bytes 786464 | tf_op jit(solution)/shard_map/ppermute | solution.py:43
  117.7 2.7 fusion.1
  122.1 12.0 %collective-permute-done.5 = bf16[768,512]{1,0:T(8,128)(2,1)S(1)} collective-permute-done((bf16[768,512]{1,0:T(8,128)(2,1)S(1)}, bf16[768,512]{1,0:T(8,128)(2,1)S(1)}, u32[]{:S(2)}, u32[]{:S(2)}) %collective-permute-start.5) | collective-permute-done | bytes 786464 | tf_op jit(solution)/shard_map/ppermute | solution.py:43
  134.1 2.7 collective-permute-start.16
  137.0 2.5 copy-done.2
  141.6 19.9 %shard_map.68.refs_2_ = f32[768,2304]{1,0:T(8,128)} custom-call(s32[9]{0:T(128)S(1)} %stack.73.info, bf16[8,768,512]{2,1,0:T(8,128)(2,1)} %copy-done.2, bf16[8,768,512]{2,1,0:T(8,128)(2,1)} %copy-done.2, bf16[8,768,512]{2,1,0:T(8,128)(2,1)} %copy-done.2, bf16[8,768,512]{2,1,0:T(8,128)(2,1)} %copy-done.2, bf16[8,768,512]{2,1,0:T(8,128)(2,1)} %copy-done.2, ...), custom_call_target="tpu_custom_call" | custom-call | flops 10871635968 | bytes 14155776 | tf_op jit(solution)/shard_map/pallas_call | solution.py:208
  164.7 8.9 %shard_map.69.hidden = bf16[768,1152]{1,0:T(8,128)(2,1)S(1)} custom-call(s32[9]{0:T(128)S(1)} %stack.73.info, bf16[8,768,512]{2,1,0:T(8,128)(2,1)} %copy-done.2, bf16[8,768,512]{2,1,0:T(8,128)(2,1)} %copy-done.2, f32[768,2304]{1,0:T(8,128)} %shard_map.68.refs_2_, bf16[224,2304]{1,0:T(8,128)(2,1)S(1)} %collective-permute-done.20.refs_3_, ...), custom_call_target="tpu_custom_call" | custom-call | flops 3623878656 | bytes 14155776 | tf_op jit(solution)/shard_map/pallas_call | solution.py:208
  173.7 3.3 %collective-permute-done.26.refs_0_ = bf16[448,576]{1,0:T(8,128)(2,1)S(1)} collective-permute-done((bf16[448,576]{1,0:T(8,128)(2,1)S(1)}, bf16[448,576]{1,0:T(8,128)(2,1)S(1)}, u32[]{:S(2)}, u32[]{:S(2)}) %collective-permute-start.26) | collective-permute-done | bytes 516128 | tf_op jit(solution)/shard_map/ppermute | solution.py:43
  183.2 11.4 %collective-permute-done.31.refs_0_ = bf16[448,576]{1,0:T(8,128)(2,1)S(1)} collective-permute-done((bf16[448,576]{1,0:T(8,128)(2,1)S(1)}, bf16[448,576]{1,0:T(8,128)(2,1)S(1)}, u32[]{:S(2)}, u32[]{:S(2)}) %collective-permute-start.31) | collective-permute-done | bytes 516128 | tf_op jit(solution)/shard_map/ppermute | solution.py:43
  194.6 3.3 collective-permute-done.37.refs_2_
  203.0 5.7 %collective-permute-start.30 = (bf16[448,768]{1,0:T(8,128)(2,1)S(1)}, bf16[448,768]{1,0:T(8,128)(2,1)S(1)}, u32[]{:S(2)}, u32[]{:S(2)}) collective-permute-start(bf16[448,768]{1,0:T(8,128)(2,1)S(1)} %get-tuple-element.41), channel_id=1, source_target_pairs={{0,4},{1,5},{2,6},{3,7},{8,12},{9,13},{10,14},{11,15},{16,21},{17,... | collective-permute-start | bytes 2064392 | tf_op jit(solution)/shard_map/ppermute | solution.py:43
  208.7 2.6 shard_map.72
  213.3 4.1 %collective-permute-start.40 = (bf16[448,768]{1,0:T(8,128)(2,1)S(1)}, bf16[448,768]{1,0:T(8,128)(2,1)}, u32[]{:S(2)}, u32[]{:S(2)}) collective-permute-start(bf16[448,768]{1,0:T(8,128)(2,1)S(1)} %get-tuple-element.47), channel_id=1, source_target_pairs={{0,5},{1,6},{2,7},{3,4},{8,13},{9,14},{10,15},{11,12},{16,22},{17,... | collective-permute-start | bytes 2064392 | tf_op jit(solution)/shard_map/ppermute | solution.py:43
  218.0 2.5 shard_map.71
  220.6 3.0 collective-permute-start.39
  225.1 3.4 %shard_map.73 = (bf16[448,768]{1,0:T(8,128)(2,1)}, bf16[448,768]{1,0:T(8,128)(2,1)}) custom-call(s32[9]{0:T(128)S(1)} %stack.73.info, bf16[768,1152]{1,0:T(8,128)(2,1)S(1)} %shard_map.69.hidden, bf16[448,576]{1,0:T(8,128)(2,1)S(1)} %collective-permute-done.41.refs_0_, bf16[448,576]{1,0:T(8,128)(2,1)S(1)} %collective-permute-done.42.refs_1_, ...), custom_call_target="tpu_custom_call" | custom-call | flops 1585446912 | bytes 1376256 | tf_op jit(solution)/shard_map/pallas_call | solution.py:254
  228.5 3.7 %collective-permute-start.34 = (bf16[448,768]{1,0:T(8,128)(2,1)S(1)}, bf16[448,768]{1,0:T(8,128)(2,1)}, u32[]{:S(2)}, u32[]{:S(2)}) collective-permute-start(bf16[448,768]{1,0:T(8,128)(2,1)S(1)} %get-tuple-element.43), channel_id=1, source_target_pairs={{0,3},{1,0},{2,1},{3,2},{8,11},{9,8},{10,9},{11,10},{16,16},{17,17... | collective-permute-start | bytes 2064392 | tf_op jit(solution)/shard_map/ppermute | solution.py:43
  232.3 6.6 %collective-permute-done.29 = bf16[448,768]{1,0:T(8,128)(2,1)} collective-permute-done((bf16[448,768]{1,0:T(8,128)(2,1)S(1)}, bf16[448,768]{1,0:T(8,128)(2,1)}, u32[]{:S(2)}, u32[]{:S(2)}) %collective-permute-start.29) | collective-permute-done | bytes 688160 | tf_op jit(solution)/shard_map/ppermute | solution.py:43
  238.9 2.7 collective-permute-start.46
  244.2 47.7 %all-gather = f32[1920,128]{1,0:T(8,128)} all-gather(f32[120,128]{1,0:T(8,128)S(1)} %max.31), channel_id=2, replica_groups=mesh['fsdp'=16,'tp'=8] {'fsdp'}, dimensions={0}, use_global_device_ids=true | all-gather | bytes 1044480 | tf_op jit(solution)/shard_map/all_gather | solution.py:322
  293.2 33.7 %all-gather.1 = f32[960,128]{1,0:T(8,128)S(1)} all-gather(f32[120,128]{1,0:T(8,128)S(1)} %reduce_max.168), channel_id=3, replica_groups=mesh['fsdp'=16,'tp'=8] {'tp'}, dimensions={0}, use_global_device_ids=true | all-gather | bytes 552960 | tf_op jit(solution)/shard_map/all_gather | solution.py:323
  327.7 3.9 %fusion = bf16[768,448]{0,1:T(8,128)(2,1)} fusion(bf16[448,768]{1,0:T(8,128)(2,1)} %collective-permute-done.46, bf16[448,768]{1,0:T(8,128)(2,1)} %collective-permute-done.45, bf16[448,768]{1,0:T(8,128)(2,1)} %collective-permute-done.40, bf16[448,768]{1,0:T(8,128)(2,1)} %collective-permute-done.39, bf16[448,768]{1,0:T(8,128)(2,1)} %collective-permute-done.35, ...), kind=kLoop, calls=%fused_computation.22 | loop fusion | flops 5505024 | bytes 6193152 | tf_op jit(solution)/shard_map/transpose | solution.py:348
  (183 shorter events, 56.5 us)
Async XLA Ops:
  17.9 27.3 %collective-permute-start.8 = (bf16[224,2304]{1,0:T(8,128)(2,1)S(1)}, bf16[224,2304]{1,0:T(8,128)(2,1)S(1)}, u32[]{:S(2)}, u32[]{:S(2)}) collective-permute-start(bf16[224,2304]{1,0:T(8,128)(2,1)S(1)} %pad_maximum_fusion.1.refs_6_), channel_id=1, source_target_pairs={{0,64},{1,65},{2,66},{3,67},{8,72},{9,73},{10,74},{11,75},{16,80},... | collective-permute-start | bytes 3096584 | tf_op jit(solution)/shard_map/ppermute | solution.py:43
  21.0 24.1 %collective-permute-start.9 = (bf16[224,2304]{1,0:T(8,128)(2,1)S(1)}, bf16[224,2304]{1,0:T(8,128)(2,1)S(1)}, u32[]{:S(2)}, u32[]{:S(2)}) collective-permute-start(bf16[224,2304]{1,0:T(8,128)(2,1)S(1)} %pad_maximum_fusion.1.refs_6_), channel_id=1, source_target_pairs={{0,16},{1,17},{2,18},{3,19},{8,24},{9,25},{10,26},{11,27},{16,32},... | collective-permute-start | bytes 3096584 | tf_op jit(solution)/shard_map/ppermute | solution.py:43
  21.6 24.2 %collective-permute-start.10 = (bf16[224,2304]{1,0:T(8,128)(2,1)S(1)}, bf16[224,2304]{1,0:T(8,128)(2,1)}, u32[]{:S(2)}, u32[]{:S(2)}) collective-permute-start(bf16[224,2304]{1,0:T(8,128)(2,1)S(1)} %pad_maximum_fusion.1.refs_6_), channel_id=1, source_target_pairs={{0,48},{1,49},{2,50},{3,51},{8,56},{9,57},{10,58},{11,59},{16,0},{... | collective-permute-start | bytes 3096584 | tf_op jit(solution)/shard_map/ppermute | solution.py:43
  23.1 36.9 %collective-permute-start.1 = (bf16[768,512]{1,0:T(8,128)(2,1)S(1)}, bf16[768,512]{1,0:T(8,128)(2,1)S(1)}, u32[]{:S(2)}, u32[]{:S(2)}) collective-permute-start(bf16[768,512]{1,0:T(8,128)(2,1)S(1)} %pad.18), channel_id=1, source_target_pairs={{0,4},{1,5},{2,6},{3,7},{8,12},{9,13},{10,14},{11,15},{16,20},{17,... | collective-permute-start | bytes 2359304 | tf_op jit(solution)/shard_map/ppermute | solution.py:43
  23.7 38.0 %collective-permute-start.12 = (bf16[224,2304]{1,0:T(8,128)(2,1)S(1)}, bf16[224,2304]{1,0:T(8,128)(2,1)S(1)}, u32[]{:S(2)}, u32[]{:S(2)}) collective-permute-start(bf16[224,2304]{1,0:T(8,128)(2,1)S(1)} %pad_maximum_fusion.1.refs_6_), channel_id=1, source_target_pairs={{0,8},{1,9},{2,10},{3,11},{8,0},{9,1},{10,2},{11,3},{16,24},{17,25... | collective-permute-start | bytes 3096584 | tf_op jit(solution)/shard_map/ppermute | solution.py:43
  45.8 22.0 %collective-permute-start.11 = (bf16[224,2304]{1,0:T(8,128)(2,1)S(1)}, bf16[224,2304]{1,0:T(8,128)(2,1)S(1)}, u32[]{:S(2)}, u32[]{:S(2)}) collective-permute-start(bf16[224,2304]{1,0:T(8,128)(2,1)S(1)} %collective-permute-done.8.refs_8_), channel_id=1, source_target_pairs={{0,16},{1,17},{2,18},{3,19},{8,24},{9,25},{10,26},{11,27},{16,32},... | collective-permute-start | bytes 3096584 | tf_op jit(solution)/shard_map/ppermute | solution.py:43
  46.1 28.7 %collective-permute-start.13 = (bf16[224,2304]{1,0:T(8,128)(2,1)S(1)}, bf16[224,2304]{1,0:T(8,128)(2,1)}, u32[]{:S(2)}, u32[]{:S(2)}) collective-permute-start(bf16[224,2304]{1,0:T(8,128)(2,1)S(1)} %collective-permute-done.8.refs_8_), channel_id=1, source_target_pairs={{0,8},{1,9},{2,10},{3,11},{8,0},{9,1},{10,2},{11,3},{16,24},{17,25... | collective-permute-start | bytes 3096584 | tf_op jit(solution)/shard_map/ppermute | solution.py:43
  61.4 35.6 %collective-permute-start.2 = (bf16[2,768,512]{2,1,0:T(8,128)(2,1)}, bf16[2,768,512]{2,1,0:T(8,128)(2,1)}, u32[]{:S(2)}, u32[]{:S(2)}) collective-permute-start(bf16[2,768,512]{2,1,0:T(8,128)(2,1)} %pad_maximum_fusion), channel_id=1, source_target_pairs={{0,1},{1,2},{2,3},{3,0},{8,9},{9,10},{10,11},{11,8},{16,17},{17,18... | collective-permute-start | bytes 4718600 | tf_op jit(solution)/shard_map/ppermute | solution.py:43
  61.8 16.9 %collective-permute-start.14 = (bf16[224,2304]{1,0:T(8,128)(2,1)S(1)}, bf16[224,2304]{1,0:T(8,128)(2,1)}, u32[]{:S(2)}, u32[]{:S(2)}) collective-permute-start(bf16[224,2304]{1,0:T(8,128)(2,1)S(1)} %collective-permute-done.9.refs_10_), channel_id=1, source_target_pairs={{0,8},{1,9},{2,10},{3,11},{8,0},{9,1},{10,2},{11,3},{16,24},{17,25... | collective-permute-start | bytes 3096584 | tf_op jit(solution)/shard_map/ppermute | solution.py:43
  68.8 22.4 %collective-permute-start.18 = (bf16[224,2304]{1,0:T(8,128)(2,1)S(1)}, bf16[224,2304]{1,0:T(8,128)(2,1)}, u32[]{:S(2)}, u32[]{:S(2)}) collective-permute-start(bf16[224,2304]{1,0:T(8,128)(2,1)S(1)} %collective-permute-done.8.refs_8_), channel_id=1, source_target_pairs={{0,48},{1,49},{2,50},{3,51},{8,56},{9,57},{10,58},{11,59},{16,0},{... | collective-permute-start | bytes 3096584 | tf_op jit(solution)/shard_map/ppermute | solution.py:43
  74.8 33.9 %collective-permute-start.3 = (bf16[2,768,512]{2,1,0:T(8,128)(2,1)}, bf16[2,768,512]{2,1,0:T(8,128)(2,1)S(1)}, u32[]{:S(2)}, u32[]{:S(2)}) collective-permute-start(bf16[2,768,512]{2,1,0:T(8,128)(2,1)} %pad_maximum_fusion), channel_id=1, source_target_pairs={{0,3},{1,0},{2,1},{3,2},{8,11},{9,8},{10,9},{11,10},{16,19},{17,16... | collective-permute-start | bytes 4718600 | tf_op jit(solution)/shard_map/ppermute | solution.py:43
  91.1 49.5 %collective-permute-start.19 = (bf16[224,2304]{1,0:T(8,128)(2,1)}, bf16[224,2304]{1,0:T(8,128)(2,1)S(1)}, u32[]{:S(2)}, u32[]{:S(2)}) collective-permute-start(bf16[224,2304]{1,0:T(8,128)(2,1)} %collective-permute-done.18.refs_16_), channel_id=1, source_target_pairs={{0,8},{1,9},{2,10},{3,11},{8,0},{9,1},{10,2},{11,3},{16,24},{17,25... | collective-permute-start | bytes 3096584 | tf_op jit(solution)/shard_map/ppermute | solution.py:43
  91.1 45.9 %collective-permute-start.22 = (bf16[224,2304]{1,0:T(8,128)(2,1)}, bf16[224,2304]{1,0:T(8,128)(2,1)S(1)}, u32[]{:S(2)}, u32[]{:S(2)}) collective-permute-start(bf16[224,2304]{1,0:T(8,128)(2,1)} %collective-permute-done.18.refs_16_), channel_id=1, source_target_pairs={{0,48},{1,49},{2,50},{3,51},{8,56},{9,57},{10,58},{11,59},{16,0},{... | collective-permute-start | bytes 3096584 | tf_op jit(solution)/shard_map/ppermute | solution.py:43
  91.1 45.8 %collective-permute-start.20 = (bf16[224,2304]{1,0:T(8,128)(2,1)S(1)}, bf16[224,2304]{1,0:T(8,128)(2,1)S(1)}, u32[]{:S(2)}, u32[]{:S(2)}) collective-permute-start(bf16[224,2304]{1,0:T(8,128)(2,1)S(1)} %collective-permute-done.9.refs_10_), channel_id=1, source_target_pairs={{0,16},{1,17},{2,18},{3,19},{8,24},{9,25},{10,26},{11,27},{16,32},... | collective-permute-start | bytes 3096584 | tf_op jit(solution)/shard_map/ppermute | solution.py:43
  98.2 18.2 %collective-permute-start.4 = (bf16[768,512]{1,0:T(8,128)(2,1)S(1)}, bf16[768,512]{1,0:T(8,128)(2,1)S(1)}, u32[]{:S(2)}, u32[]{:S(2)}) collective-permute-start(bf16[768,512]{1,0:T(8,128)(2,1)S(1)} %slice_bitcast_fusion.1), channel_id=1, source_target_pairs={{0,1},{1,2},{2,3},{3,0},{8,9},{9,10},{10,11},{11,8},{16,17},{17,18... | collective-permute-start | bytes 2359304 | tf_op jit(solution)/shard_map/ppermute | solution.py:43
  108.7 30.9 %collective-permute-start.17 = (bf16[224,2304]{1,0:T(8,128)(2,1)S(1)}, bf16[224,2304]{1,0:T(8,128)(2,1)S(1)}, u32[]{:S(2)}, u32[]{:S(2)}) collective-permute-start(bf16[224,2304]{1,0:T(8,128)(2,1)S(1)} %copy-done.11), channel_id=1, source_target_pairs={{0,8},{1,9},{2,10},{3,11},{8,0},{9,1},{10,2},{11,3},{16,24},{17,25... | collective-permute-start | bytes 3096584 | tf_op jit(solution)/shard_map/ppermute | solution.py:43
  116.4 17.7 %collective-permute-start.5 = (bf16[768,512]{1,0:T(8,128)(2,1)S(1)}, bf16[768,512]{1,0:T(8,128)(2,1)S(1)}, u32[]{:S(2)}, u32[]{:S(2)}) collective-permute-start(bf16[768,512]{1,0:T(8,128)(2,1)S(1)} %slice_bitcast_fusion), channel_id=1, source_target_pairs={{0,3},{1,0},{2,1},{3,2},{8,11},{9,8},{10,9},{11,10},{16,19},{17,16... | collective-permute-start | bytes 2359304 | tf_op jit(solution)/shard_map/ppermute | solution.py:43
  134.1 27.4 %collective-permute-start.16 = (bf16[448,576]{1,0:T(8,128)(2,1)}, bf16[448,576]{1,0:T(8,128)(2,1)S(1)}, u32[]{:S(2)}, u32[]{:S(2)}) collective-permute-start(bf16[448,576]{1,0:T(8,128)(2,1)} %fusion.1), channel_id=1, source_target_pairs={{0,0},{1,16},{2,32},{3,48},{8,8},{9,24},{10,40},{11,56},{16,49},{1... | collective-permute-start | bytes 1548296 | tf_op jit(solution)/shard_map/ppermute | solution.py:43
  136.9 27.8 %collective-permute-start.21 = (bf16[224,2304]{1,0:T(8,128)(2,1)S(1)}, bf16[224,2304]{1,0:T(8,128)(2,1)S(1)}, u32[]{:S(2)}, u32[]{:S(2)}) collective-permute-start(bf16[224,2304]{1,0:T(8,128)(2,1)S(1)} %collective-permute-done.20.refs_3_), channel_id=1, source_target_pairs={{0,8},{1,9},{2,10},{3,11},{8,0},{9,1},{10,2},{11,3},{16,24},{17,25... | collective-permute-start | bytes 3096584 | tf_op jit(solution)/shard_map/ppermute | solution.py:43
  139.6 25.1 %collective-permute-start.23 = (bf16[224,2304]{1,0:T(8,128)(2,1)S(1)}, bf16[224,2304]{1,0:T(8,128)(2,1)S(1)}, u32[]{:S(2)}, u32[]{:S(2)}) collective-permute-start(bf16[224,2304]{1,0:T(8,128)(2,1)S(1)} %collective-permute-done.22.refs_5_), channel_id=1, source_target_pairs={{0,8},{1,9},{2,10},{3,11},{8,0},{9,1},{10,2},{11,3},{16,24},{17,25... | collective-permute-start | bytes 3096584 | tf_op jit(solution)/shard_map/ppermute | solution.py:43
  161.6 17.0 %collective-permute-start.25 = (bf16[448,576]{1,0:T(8,128)(2,1)S(1)}, bf16[448,576]{1,0:T(8,128)(2,1)S(1)}, u32[]{:S(2)}, u32[]{:S(2)}) collective-permute-start(bf16[448,576]{1,0:T(8,128)(2,1)S(1)} %collective-permute-done.16.refs_0_), channel_id=1, source_target_pairs={{0,64},{1,65},{2,66},{3,67},{8,72},{9,73},{10,74},{11,75},{16,80},... | collective-permute-start | bytes 1548296 | tf_op jit(solution)/shard_map/ppermute | solution.py:43
  162.9 17.4 %collective-permute-start.27 = (bf16[448,576]{1,0:T(8,128)(2,1)S(1)}, bf16[448,576]{1,0:T(8,128)(2,1)S(1)}, u32[]{:S(2)}, u32[]{:S(2)}) collective-permute-start(bf16[448,576]{1,0:T(8,128)(2,1)S(1)} %collective-permute-done.16.refs_0_), channel_id=1, source_target_pairs={{0,48},{1,49},{2,50},{3,51},{8,56},{9,57},{10,58},{11,59},{16,0},{... | collective-permute-start | bytes 1548296 | tf_op jit(solution)/shard_map/ppermute | solution.py:43
  198.7 18.7 %collective-permute-start.43 = (bf16[448,576]{1,0:T(8,128)(2,1)S(1)}, bf16[448,576]{1,0:T(8,128)(2,1)S(1)}, u32[]{:S(2)}, u32[]{:S(2)}) collective-permute-start(bf16[448,576]{1,0:T(8,128)(2,1)S(1)} %collective-permute-done.37.refs_2_), channel_id=1, source_target_pairs={{0,48},{1,49},{2,50},{3,51},{8,56},{9,57},{10,58},{11,59},{16,0},{... | collective-permute-start | bytes 1548296 | tf_op jit(solution)/shard_map/ppermute | solution.py:43
  200.4 17.1 %collective-permute-start.32 = (bf16[448,576]{1,0:T(8,128)(2,1)S(1)}, bf16[448,576]{1,0:T(8,128)(2,1)S(1)}, u32[]{:S(2)}, u32[]{:S(2)}) collective-permute-start(bf16[448,576]{1,0:T(8,128)(2,1)S(1)} %collective-permute-done.26.refs_0_), channel_id=1, source_target_pairs={{0,8},{1,9},{2,10},{3,11},{8,0},{9,1},{10,2},{11,3},{16,24},{17,25... | collective-permute-start | bytes 1548296 | tf_op jit(solution)/shard_map/ppermute | solution.py:43
  203.0 25.6 %collective-permute-start.30 = (bf16[448,768]{1,0:T(8,128)(2,1)S(1)}, bf16[448,768]{1,0:T(8,128)(2,1)S(1)}, u32[]{:S(2)}, u32[]{:S(2)}) collective-permute-start(bf16[448,768]{1,0:T(8,128)(2,1)S(1)} %get-tuple-element.41), channel_id=1, source_target_pairs={{0,4},{1,5},{2,6},{3,7},{8,12},{9,13},{10,14},{11,15},{16,21},{17,... | collective-permute-start | bytes 2064392 | tf_op jit(solution)/shard_map/ppermute | solution.py:43
  211.3 27.7 %collective-permute-start.29 = (bf16[448,768]{1,0:T(8,128)(2,1)S(1)}, bf16[448,768]{1,0:T(8,128)(2,1)}, u32[]{:S(2)}, u32[]{:S(2)}) collective-permute-start(bf16[448,768]{1,0:T(8,128)(2,1)S(1)} %get-tuple-element.40), channel_id=1, source_target_pairs={{0,0},{1,1},{2,2},{3,3},{8,8},{9,9},{10,10},{11,11},{16,17},{17,18... | collective-permute-start | bytes 2064392 | tf_op jit(solution)/shard_map/ppermute | solution.py:43
  213.3 28.4 %collective-permute-start.40 = (bf16[448,768]{1,0:T(8,128)(2,1)S(1)}, bf16[448,768]{1,0:T(8,128)(2,1)}, u32[]{:S(2)}, u32[]{:S(2)}) collective-permute-start(bf16[448,768]{1,0:T(8,128)(2,1)S(1)} %get-tuple-element.47), channel_id=1, source_target_pairs={{0,5},{1,6},{2,7},{3,4},{8,13},{9,14},{10,15},{11,12},{16,22},{17,... | collective-permute-start | bytes 2064392 | tf_op jit(solution)/shard_map/ppermute | solution.py:43
  220.6 107.1 %collective-permute-start.39 = (bf16[448,768]{1,0:T(8,128)(2,1)S(1)}, bf16[448,768]{1,0:T(8,128)(2,1)}, u32[]{:S(2)}, u32[]{:S(2)}) collective-permute-start(bf16[448,768]{1,0:T(8,128)(2,1)S(1)} %get-tuple-element.46), channel_id=1, source_target_pairs={{0,7},{1,4},{2,5},{3,6},{8,15},{9,12},{10,13},{11,14},{16,20},{17,... | collective-permute-start | bytes 2064392 | tf_op jit(solution)/shard_map/ppermute | solution.py:43
  223.6 104.1 %collective-permute-start.35 = (bf16[448,768]{1,0:T(8,128)(2,1)S(1)}, bf16[448,768]{1,0:T(8,128)(2,1)}, u32[]{:S(2)}, u32[]{:S(2)}) collective-permute-start(bf16[448,768]{1,0:T(8,128)(2,1)S(1)} %get-tuple-element.44), channel_id=1, source_target_pairs={{0,1},{1,2},{2,3},{3,0},{8,9},{9,10},{10,11},{11,8},{16,18},{17,19... | collective-permute-start | bytes 2064392 | tf_op jit(solution)/shard_map/ppermute | solution.py:43
  228.5 99.1 %collective-permute-start.34 = (bf16[448,768]{1,0:T(8,128)(2,1)S(1)}, bf16[448,768]{1,0:T(8,128)(2,1)}, u32[]{:S(2)}, u32[]{:S(2)}) collective-permute-start(bf16[448,768]{1,0:T(8,128)(2,1)S(1)} %get-tuple-element.43), channel_id=1, source_target_pairs={{0,3},{1,0},{2,1},{3,2},{8,11},{9,8},{10,9},{11,10},{16,16},{17,17... | collective-permute-start | bytes 2064392 | tf_op jit(solution)/shard_map/ppermute | solution.py:43
  238.9 88.7 %collective-permute-start.46 = (bf16[448,768]{1,0:T(8,128)(2,1)}, bf16[448,768]{1,0:T(8,128)(2,1)}, u32[]{:S(2)}, u32[]{:S(2)}) collective-permute-start(bf16[448,768]{1,0:T(8,128)(2,1)} %get-tuple-element.49), channel_id=1, source_target_pairs={{0,6},{1,7},{2,4},{3,5},{8,14},{9,15},{10,12},{11,13},{16,23},{17,... | collective-permute-start | bytes 2064392 | tf_op jit(solution)/shard_map/ppermute | solution.py:43
  241.7 86.0 %collective-permute-start.45 = (bf16[448,768]{1,0:T(8,128)(2,1)}, bf16[448,768]{1,0:T(8,128)(2,1)}, u32[]{:S(2)}, u32[]{:S(2)}) collective-permute-start(bf16[448,768]{1,0:T(8,128)(2,1)} %get-tuple-element.48), channel_id=1, source_target_pairs={{0,2},{1,3},{2,0},{3,1},{8,10},{9,11},{10,8},{11,9},{16,19},{17,16... | collective-permute-start | bytes 2064392 | tf_op jit(solution)/shard_map/ppermute | solution.py:43
  (33 other events, 372.2 us)
where the time goes:
time: 337 us; the launch traced here: 332 us
  waiting for transfers between devices  118 us (35%)
  blocking collectives  81.5 us (24%)
  starting transfers between devices  55 us (16%)
  Pallas kernels  39.9 us (12%)
  local copies, waits for them, and re-layouts  19.1 us (6%)
  other arithmetic  16.8 us (5%)
    ppermute x47, waiting for transfers between devices, send(): return lax.ppermute(array, AXES, pairs)  118 us
    ppermute x47, starting transfers between devices, send(): return lax.ppermute(array, AXES, pairs)  55 us
    all_gather x1, blocking collectives, on_device(): every = jnp.max(lax.all_gather(table, 'fsdp'), axis=0)  47.7 us
    all_gather x1, blocking collectives, on_device(): every = jnp.max(lax.all_gather(every, 'tp'), axis=0)  33.7 us
    pallas_call x2, Pallas kernels, token_sum(): pl.pallas_call(functools.partial(token_kernel, count, before is not None,...  28.9 us
    pallas_call x4, Pallas kernels, down_terms(): pl.pallas_call(down_kernel, out_shape=[jax.ShapeDtypeStruct((columns, row...  11 us
    unnamed x41, local copies, waits for them, and re-layouts  9.42 us
  transfers between devices with their start and end apart: 47, of which 19 were waited for; matrix products, arithmetic and copies ran while one was open for 5% of the time, Pallas kernels for 12%

commit v1 on v0

--- a/solution.py
+++ b/solution.py
@@ -17,7 +17,7 @@
 AXES = ("fsdp", "tp")
 VMEM_LIMIT = 48 * 1024 * 1024
 TILE = 256
-WIDE = 512
+HALF = 256
 
 
 def snapped(value):
@@ -133,23 +133,21 @@
     return lax.optimization_barrier((array, *others))[0]
 
 
-def ring(own, across, up, down, others=(), between=lambda n, blocks: ()):
-    far = send(own, across)
+def ring(own, far, up, down, others=(), between=lambda blocks: ()):
     own_l, own_r = send(own, up), send(own, down)
     far = after(far, own_l, own_r, *others)
     far_l, far_r = send(far, up), send(far, down)
-    others = between(0, [own, far, own_l, own_r])
+    others = between([own, far, own_l, own_r])
     own_l, far_r = after(own_l, far_l, *others), after(far_r, far_l, *others)
     own_ll, far_rr = send(own_l, up), send(far_r, down)
-    between(1, [far_l, far_r])
     return [own, far, own_l, own_r, far_l, far_r, own_ll, far_rr]
 
 
 TOKEN_ORDER = ((0, 0), (1, 0), (0, -1), (1, -1), (0, 1), (1, 1), (0, 2), (1, 2))
 
 
-def token_ring(own):
-    pair = jnp.stack([own, send(own, y_near)])
+def token_ring(own, near):
+    pair = jnp.stack([own, near])
     left, right = send(pair, z_up), send(pair, z_down)
     own_ll, near_rr = send(left[0], z_up), send(right[1], z_down)
     return jnp.concatenate([pair, left, right, own_ll[None], near_rr[None]])
@@ -158,27 +156,22 @@
 def token_kernel(count, has_before, last, info, *refs):
     tokens, refs = refs[:count], list(refs[count:])
     before = refs.pop(0) if has_before else None
-    blocks, (out, scratch, sems) = refs[: 2 * count], refs[2 * count :]
-    half = blocks[0].shape[0]
+    blocks, (out, scratch, sems) = refs[:count], refs[count:]
+    height = blocks[0].shape[0]
 
     @pl.when(pl.program_id(0) == 0)
     def _():
-        copies = []
-        for n in range(count):
-            for side in range(2):
-                place = info[8] if side == 0 else 1 - info[8]
-                rows = pl.ds(pl.multiple_of(n * WIDE + place * half, 16), half)
-                copies.append(
-                    pltpu.make_async_copy(
-                        blocks[2 * n + side], scratch.at[rows, :], sems.at[2 * n + side]
-                    )
-                )
+        copies = [
+            pltpu.make_async_copy(
+                block, scratch.at[pl.ds(n * HALF, height), :], sems.at[n]
+            )
+            for n, block in enumerate(blocks)
+        ]
         for copy in copies:
             copy.start()
         for n in range(count):
-            pad = WIDE - 2 * half
-            scratch[n * WIDE + 2 * half : (n + 1) * WIDE, :] = jnp.zeros(
-                (pad, scratch.shape[1]), scratch.dtype
+            scratch[n * HALF + height : (n + 1) * HALF, :] = jnp.zeros(
+                (HALF - height, scratch.shape[1]), scratch.dtype
             )
         for copy in copies:
             copy.wait()
@@ -196,11 +189,15 @@
 
 def token_sum(info, tokens, first, blocks, before=None, last=False):
     rows, columns = tokens.shape[1], blocks[0].shape[1]
-    count = len(blocks) // 2
+    count = len(blocks)
     width = columns // 2 if last else columns
 
     def token_block(n):
-        return pl.BlockSpec((None, TILE, WIDE), lambda m, info: (info[first + n], m, 0))
+        side = n % 2
+        return pl.BlockSpec(
+            (None, TILE, HALF),
+            lambda m, info: (info[first + n // 2], m, 1 - info[8] if side else info[8]),
+        )
 
     def tile(width):
         return pl.BlockSpec((TILE, width), lambda m, info: (m, 0))
@@ -213,16 +210,16 @@
             grid=(rows // TILE,),
             in_specs=[token_block(n) for n in range(count)]
             + ([] if before is None else [tile(columns)])
-            + [pl.BlockSpec(memory_space=pl.ANY)] * (2 * count),
+            + [pl.BlockSpec(memory_space=pl.ANY)] * count,
             out_specs=tile(width),
             scratch_shapes=[
-                pltpu.VMEM((count * WIDE, columns), jnp.bfloat16),
-                pltpu.SemaphoreType.DMA((2 * count,)),
+                pltpu.VMEM((count * HALF, columns), jnp.bfloat16),
+                pltpu.SemaphoreType.DMA((count,)),
             ],
         ),
         compiler_params=pltpu.CompilerParams(vmem_limit_bytes=VMEM_LIMIT),
         cost_estimate=pl.CostEstimate(
-            flops=2 * rows * columns * count * WIDE,
+            flops=2 * rows * columns * count * HALF,
             bytes_accessed=rows * columns * 8,
             transcendentals=0,
         ),
@@ -277,6 +274,16 @@
     gate_at = (fsdp_place * gate_height, tp_place * gate_breadth)
     down_at = (fsdp_place * down_height, tp_place * down_breadth)
 
+    half = tokens.shape[1] // 2
+    padded = jnp.concatenate(
+        [jnp.pad(tokens[:, k * half : (k + 1) * half], ((0, 0), (0, HALF - half))) for k in range(2)],
+        axis=1,
+    )
+    near = send(padded, y_near)
+    gate_master, up_master, down_master, padded = lax.optimization_barrier(
+        (gate_master, up_master, down_master, padded)
+    )
+
     tables = [
         block_maxima(gate_master, *gate_at, D, FF),
         block_maxima(up_master, *gate_at, D, FF),
@@ -285,15 +292,13 @@
     rows = D // BLOCK + 12
     columns = FF // BLOCK + 56
     pad = lambda a: jnp.pad(a, ((0, rows - a.shape[0]), (0, columns - a.shape[1])))
-    table = jnp.concatenate([pad(tables[0]), pad(tables[1]), pad(tables[2].T)])
+    spare = jnp.zeros((8, columns), jnp.float32)
+    table = jnp.concatenate([pad(tables[0]), pad(tables[1]), pad(tables[2].T), spare])
 
     def step(table, target):
         return jnp.maximum(table, send(table, target))
 
-    padded = jnp.pad(after(tokens, table), ((0, 0), (0, WIDE - tokens.shape[1])))
     table = step(table, other_core)
-    table, padded = lax.optimization_barrier((table, padded))
-    relative = token_ring(padded)
     down_table = step(table, lambda y, x, core, z: (y, x, core, z ^ 1))
     table = step(table, lambda y, x, core, z: (y, x ^ 1, core, z))
     gate_up = jnp.concatenate(
@@ -303,46 +308,58 @@
         ],
         axis=1,
     )
-    gate_up, down_table = lax.optimization_barrier((gate_up, down_table))
+    gate_up, down_table, near, padded = lax.optimization_barrier(
+        (gate_up, down_table, near, padded)
+    )
+    relative = token_ring(padded, near)
     pairs = []
 
-    def swap(n, blocks):
+    def swap(blocks):
         others = [send(block, other_core) for block in blocks]
         for block, other in zip(blocks, others):
             pairs.extend((block, other))
         return others
 
-    blocks = ring(gate_up, y_far, x_up, x_down, (), swap)
-    swap(2, blocks[6:])
-    down_table = after(down_table, *blocks[:4])
-    down_weight = rollout(down_master, down_table[2 * rows :].T, *down_at)
-    down_block = send(after(down_weight.T, blocks[4]), to_ff_group)
+    blocks = ring(gate_up, send(gate_up, y_far), x_up, x_down, (), swap)
+    swap(blocks[4:6])
 
     table = jnp.maximum(table, down_table)
     every = jnp.max(lax.all_gather(table, "fsdp"), axis=0)
-    every = jnp.max(lax.all_gather(every, "tp"), axis=0)
-    log_amax = jnp.log(
-        jnp.stack([every[k * rows : k * rows + D // BLOCK, : FF // BLOCK] for k in range(3)]) + EPS
-    )
-
     order = [TOKEN_ORDER.index((dy, dx)) for dy in range(2) for dx in (0, 1, 2, -1)]
     by_offset = jnp.array(order, jnp.int32)
     info = jnp.stack(
         [by_offset[(chip_y ^ y_lo) * 4 + (chip_x - z + 4) % 4] for chip_y, chip_x in chips] + [core]
     )
 
-    early = token_sum(info, relative, 0, pairs[:12])
-    down_block, early = lax.optimization_barrier((down_block, early))
-    down_block = after(down_block, blocks[6], blocks[7])
-    hidden = token_sum(info, relative, 6, pairs[12:], early, last=True)
-    down_blocks = ring(down_block, y_far, x_up, x_down, (hidden,))
+    relative, every = lax.optimization_barrier((relative, every))
+    early = token_sum(info, relative, 0, pairs)
 
     def both(blocks):
         return [b for block in blocks for b in (block, send(block, other_core))]
 
+    down_table = after(down_table, *blocks[:4])
+    down_weight = rollout(down_master, down_table[2 * rows : 3 * rows].T, *down_at)
+    down_block = send(after(down_weight.T, blocks[4], blocks[5]), to_ff_group)
+    down_far = send(down_block, y_far)
+    down_pairs = [both([down_block, down_far])]
+    down_block, early, own_ll, far_rr = lax.optimization_barrier(
+        (down_block, early, blocks[6], blocks[7])
+    )
+    pairs = both([own_ll, far_rr])
+    early = after(early, *down_pairs[0])
+    hidden = token_sum(info, relative, 6, pairs, early, last=True)
+    down_blocks = ring(down_block, down_far, x_up, x_down, (hidden,))
+    down_pairs += [both(down_blocks[n : n + 2]) for n in (2, 4, 6)]
+
+    every = jnp.pad(every, ((0, every.shape[0]), (0, 0)))
+    every = jnp.max(lax.all_gather(every, "tp"), axis=0)
+    log_amax = jnp.log(
+        jnp.stack([every[k * rows : k * rows + D // BLOCK, : FF // BLOCK] for k in range(3)]) + EPS
+    )
+
     total = 0.0
     for n in range(0, 8, 2):
-        terms = down_terms(info, hidden, both(down_blocks[n : n + 2]))
+        terms = down_terms(info, hidden, down_pairs[n // 2])
         for k in range(2):
             total += send(terms[k], to_chunk(*ORDER[n + k])).astype(jnp.float32)
     return total.astype(jnp.bfloat16).T, log_amax

time: 337 us -> 330 us (0.979)
  the two profiles are of different devices: /device:TPU:6 before, /device:TPU:19 now
where the time goes in v1:
time: 330 us; the launch traced here: 329 us
  waiting for transfers between devices  148 us (45%)
  starting transfers between devices  72.3 us (22%)
  Pallas kernels  42.8 us (13%)
  local copies, waits for them, and re-layouts  30.7 us (9%)
  other arithmetic  19.7 us (6%)
  between operations  15.1 us (5%)
    ppermute x47, waiting for transfers between devices, send(): return lax.ppermute(array, AXES, pairs)  130 us
    ppermute x47, starting transfers between devices, send(): return lax.ppermute(array, AXES, pairs)  72.2 us
    pallas_call x2, Pallas kernels, token_sum(): pl.pallas_call(functools.partial(token_kernel, count, before is not None,...  29.1 us
    all_gather x1, waiting for transfers between devices, on_device(): every = jnp.max(lax.all_gather(table, 'fsdp'), axis=0)  18 us
    unnamed x45, local copies, waits for them, and re-layouts  16 us
    pallas_call x4, Pallas kernels, down_terms(): pl.pallas_call(down_kernel, out_shape=[jax.ShapeDtypeStruct((columns, row...  13.7 us
  transfers between devices with their start and end apart: 49, of which 17 were waited for; matrix products, arithmetic and copies ran while one was open for 12% of the time, Pallas kernels for 13%

profile of v1, /device:TPU:19, one launch (start us, length us, event | category | flops | bytes accessed | tf_op | source)
XLA Modules:
  0.0 328.9 jit_solution(5769994676690568380)
XLA Ops:
  22.6 2.5 multiply_convert_fusion.2
  27.6 2.4 pad_maximum_fusion
  35.0 15.1 %collective-permute-done.10.refs_18_ = bf16[224,2304]{1,0:T(8,128)(2,1)} collective-permute-done((bf16[224,2304]{1,0:T(8,128)(2,1)S(1)}, bf16[224,2304]{1,0:T(8,128)(2,1)}, u32[]{:S(2)}, u32[]{:S(2)}) %collective-permute-start.10) | collective-permute-done | bytes 1032224 | tf_op jit(solution)/shard_map/ppermute | solution.py:43
  50.2 2.5 collective-permute-start.12
  54.3 5.0 %stack.73.info = s32[9]{0:T(128)S(1)} concatenate(s32[1]{0:T(128)} %get-tuple-element.133, s32[1]{0:T(128)} %get-tuple-element.132, s32[1]{0:T(128)} %get-tuple-element.131, s32[1]{0:T(128)} %get-tuple-element.130, s32[1]{0:T(128)} %get-tuple-element.129, s32[1]{0:T(128)} %get-tuple-element.128, s32[1]{0:T(128)} %get-tuple-element.134, s32[1]{0:T(128)} %get-tuple-element.127, s32[1]{0:T(128)} %bitcast), dimensions={0} | concatenate | bytes 72 | tf_op jit(solution)/shard_map/stack | solution.py:330
  63.1 3.8 %collective-permute-done.4 = bf16[2,768,512]{2,1,0:T(8,128)(2,1)} collective-permute-done((bf16[2,768,512]{2,1,0:T(8,128)(2,1)}, bf16[2,768,512]{2,1,0:T(8,128)(2,1)}, u32[]{:S(2)}, u32[]{:S(2)}) %collective-permute-start.4) | collective-permute-done | bytes 1572896 | tf_op jit(solution)/shard_map/ppermute | solution.py:43
  66.9 2.5 collective-permute-start.14
  71.5 2.7 constant_dynamic-update-slice_fusion.1
  74.3 2.7 constant_dynamic-update-slice_fusion
  81.1 18.0 %all-gather.5.cloned.1.call-done = f32[2048,128]{1,0:T(8,128)} async-done(((f32[128,128]{1,0:T(8,128)}), f32[2048,128]{1,0:T(8,128)}) %all-gather.5.cloned.1.call-update) | async-done | bytes 1048592 | tf_op jit(solution)/shard_map/all_gather | solution.py:327
  105.5 3.1 fusion.3
  108.7 12.3 %collective-permute-done.6 = bf16[768,512]{1,0:T(8,128)(2,1)S(1)} collective-permute-done((bf16[768,512]{1,0:T(8,128)(2,1)}, bf16[768,512]{1,0:T(8,128)(2,1)S(1)}, u32[]{:S(2)}, u32[]{:S(2)}) %collective-permute-start.6) | collective-permute-done | bytes 786464 | tf_op jit(solution)/shard_map/ppermute | solution.py:43
  120.9 5.0 %collective-permute-start.17 = (bf16[448,576]{1,0:T(8,128)(2,1)S(1)}, bf16[448,576]{1,0:T(8,128)(2,1)S(1)}, u32[]{:S(2)}, u32[]{:S(2)}) collective-permute-start(bf16[448,576]{1,0:T(8,128)(2,1)S(1)} %fusion.3), channel_id=1, source_target_pairs={{0,0},{1,16},{2,32},{3,48},{8,8},{9,24},{10,40},{11,56},{16,49},{1... | collective-permute-start | bytes 1548296 | tf_op jit(solution)/shard_map/ppermute | solution.py:43
  127.9 11.8 %collective-permute-done.17.refs_0_ = bf16[448,576]{1,0:T(8,128)(2,1)S(1)} collective-permute-done((bf16[448,576]{1,0:T(8,128)(2,1)S(1)}, bf16[448,576]{1,0:T(8,128)(2,1)S(1)}, u32[]{:S(2)}, u32[]{:S(2)}) %collective-permute-start.17) | collective-permute-done | bytes 516128 | tf_op jit(solution)/shard_map/ppermute | solution.py:43
  139.6 2.6 collective-permute-start.23
  144.3 19.9 %shard_map.68.refs_4_ = f32[768,2304]{1,0:T(8,128)} custom-call(s32[9]{0:T(128)S(1)} %stack.73.info, bf16[8,768,512]{2,1,0:T(8,128)(2,1)} %bitcast_dynamic-update-slice_fusion.refs_0_.refs_1_.refs_2_.refs_3_.refs_4_.refs_5_.refs_6_.refs_7_.refs_8_.refs_9_.refs_10_.refs_11_, ...), custom_call_target="tpu_custom_call" | custom-call | flops 10871635968 | bytes 14155776 | tf_op jit(solution)/shard_map/pallas_call | solution.py:205
  166.5 2.9 collective-permute-start.29
  171.3 9.2 %shard_map.69.hidden = bf16[768,1152]{1,0:T(8,128)(2,1)S(1)} custom-call(s32[9]{0:T(128)S(1)} %stack.73.info, bf16[8,768,512]{2,1,0:T(8,128)(2,1)} %bitcast_dynamic-update-slice_fusion.refs_0_.refs_1_.refs_2_.refs_3_.refs_4_.refs_5_.refs_6_.refs_7_.refs_8_.refs_9_.refs_10_.refs_11_, ...), custom_call_target="tpu_custom_call" | custom-call | flops 3623878656 | bytes 14155776 | tf_op jit(solution)/shard_map/pallas_call | solution.py:205
  181.3 6.0 %collective-permute-done.30.refs_2_ = bf16[448,576]{1,0:T(8,128)(2,1)} collective-permute-done((bf16[448,576]{1,0:T(8,128)(2,1)S(1)}, bf16[448,576]{1,0:T(8,128)(2,1)}, u32[]{:S(2)}, u32[]{:S(2)}) %collective-permute-start.30) | collective-permute-done | bytes 516128 | tf_op jit(solution)/shard_map/ppermute | solution.py:43
  187.3 3.8 %collective-permute-start.31 = (bf16[448,576]{1,0:T(8,128)(2,1)}, bf16[448,576]{1,0:T(8,128)(2,1)}, u32[]{:S(2)}, u32[]{:S(2)}) collective-permute-start(bf16[448,576]{1,0:T(8,128)(2,1)} %collective-permute-done.23.refs_2_), channel_id=1, source_target_pairs={{0,16},{1,17},{2,18},{3,19},{8,24},{9,25},{10,26},{11,27},{16,32},... | collective-permute-start | bytes 1548296 | tf_op jit(solution)/shard_map/ppermute | solution.py:43
  192.9 10.0 %collective-permute-done.31.refs_0_ = bf16[448,576]{1,0:T(8,128)(2,1)} collective-permute-done((bf16[448,576]{1,0:T(8,128)(2,1)}, bf16[448,576]{1,0:T(8,128)(2,1)}, u32[]{:S(2)}, u32[]{:S(2)}) %collective-permute-start.31) | collective-permute-done | bytes 516128 | tf_op jit(solution)/shard_map/ppermute | solution.py:43
  211.3 3.0 shard_map.70
  216.3 3.2 shard_map.71
  221.5 2.7 collective-permute-start.34
  225.7 4.1 %shard_map.72 = (bf16[448,768]{1,0:T(8,128)(2,1)}, bf16[448,768]{1,0:T(8,128)(2,1)}) custom-call(s32[9]{0:T(128)S(1)} %stack.73.info, bf16[768,1152]{1,0:T(8,128)(2,1)S(1)} %shard_map.69.hidden, bf16[448,576]{1,0:T(8,128)(2,1)} %collective-permute-done.31.refs_0_, bf16[448,576]{1,0:T(8,128)(2,1)S(1)} %collective-permute-done.36.refs_1_, ...), custom_call_target="tpu_custom_call" | custom-call | flops 1585446912 | bytes 1376256 | tf_op jit(solution)/shard_map/pallas_call | solution.py:251
  229.8 7.2 %collective-permute-start.35 = (bf16[448,768]{1,0:T(8,128)(2,1)S(1)}, bf16[448,768]{1,0:T(8,128)(2,1)}, u32[]{:S(2)}, u32[]{:S(2)}) collective-permute-start(bf16[448,768]{1,0:T(8,128)(2,1)S(1)} %get-tuple-element.57), channel_id=1, source_target_pairs={{0,1},{1,2},{2,3},{3,0},{8,9},{9,10},{10,11},{11,8},{16,18},{17,19... | collective-permute-start | bytes 2064392 | tf_op jit(solution)/shard_map/ppermute | solution.py:43
  237.0 6.7 %collective-permute-start.39 = (bf16[448,768]{1,0:T(8,128)(2,1)}, bf16[448,768]{1,0:T(8,128)(2,1)}, u32[]{:S(2)}, u32[]{:S(2)}) collective-permute-start(bf16[448,768]{1,0:T(8,128)(2,1)} %get-tuple-element.59), channel_id=1, source_target_pairs={{0,7},{1,4},{2,5},{3,6},{8,15},{9,12},{10,13},{11,14},{16,20},{17,... | collective-permute-start | bytes 2064392 | tf_op jit(solution)/shard_map/ppermute | solution.py:43
  243.8 3.4 %shard_map.73 = (bf16[448,768]{1,0:T(8,128)(2,1)}, bf16[448,768]{1,0:T(8,128)(2,1)}) custom-call(s32[9]{0:T(128)S(1)} %stack.73.info, bf16[768,1152]{1,0:T(8,128)(2,1)S(1)} %shard_map.69.hidden, bf16[448,576]{1,0:T(8,128)(2,1)S(1)} %collective-permute-done.41.refs_0_, bf16[448,576]{1,0:T(8,128)(2,1)S(1)} %collective-permute-done.42.refs_1_, ...), custom_call_target="tpu_custom_call" | custom-call | flops 1585446912 | bytes 1376256 | tf_op jit(solution)/shard_map/pallas_call | solution.py:251
  249.1 34.3 %collective-permute-done.28 = bf16[448,768]{1,0:T(8,128)(2,1)S(1)} collective-permute-done((bf16[448,768]{1,0:T(8,128)(2,1)S(1)}, bf16[448,768]{1,0:T(8,128)(2,1)S(1)}, u32[]{:S(2)}, u32[]{:S(2)}) %collective-permute-start.28) | collective-permute-done | bytes 688160 | tf_op jit(solution)/shard_map/ppermute | solution.py:43
  290.2 12.7 %collective-permute-done.45 = bf16[448,768]{1,0:T(8,128)(2,1)} collective-permute-done((bf16[448,768]{1,0:T(8,128)(2,1)}, bf16[448,768]{1,0:T(8,128)(2,1)}, u32[]{:S(2)}, u32[]{:S(2)}) %collective-permute-start.45) | collective-permute-done | bytes 688160 | tf_op jit(solution)/shard_map/ppermute | solution.py:43
  303.0 15.6 %collective-permute-done.46 = bf16[448,768]{1,0:T(8,128)(2,1)} collective-permute-done((bf16[448,768]{1,0:T(8,128)(2,1)}, bf16[448,768]{1,0:T(8,128)(2,1)}, u32[]{:S(2)}, u32[]{:S(2)}) %collective-permute-start.46) | collective-permute-done | bytes 688160 | tf_op jit(solution)/shard_map/ppermute | solution.py:43
  318.6 3.5 %fusion.2 = bf16[768,448]{0,1:T(8,128)(2,1)} fusion(bf16[448,768]{1,0:T(8,128)(2,1)} %collective-permute-done.46, bf16[448,768]{1,0:T(8,128)(2,1)} %collective-permute-done.45, bf16[448,768]{1,0:T(8,128)(2,1)S(1)} %collective-permute-done.40, bf16[448,768]{1,0:T(8,128)(2,1)} %collective-permute-done.39, bf16[448,768]{1,0:T(8,128)(2,1)} %collective-permute-done.35, ...), kind=kLoop, calls=%fused_computation.25 | loop fusion | flops 5505024 | bytes 6193152 | tf_op jit(solution)/shard_map/transpose | solution.py:365
  (198 shorter events, 73.6 us)
Async XLA Ops:
  7.2 91.9 %all-gather.5.cloned.1.call-start = ((), (), s32[]{:S(2)}) async-start(), calls=%async_computation | async-start | bytes 1114112 | tf_op jit(solution)/shard_map/all_gather | solution.py:327
  8.7 18.6 %collective-permute-start.3 = (bf16[768,512]{1,0:T(8,128)(2,1)S(1)}, bf16[768,512]{1,0:T(8,128)(2,1)}, u32[]{:S(2)}, u32[]{:S(2)}) collective-permute-start(bf16[768,512]{1,0:T(8,128)(2,1)S(1)} %fusion.1), channel_id=1, source_target_pairs={{0,4},{1,5},{2,6},{3,7},{8,12},{9,13},{10,14},{11,15},{16,20},{17,... | collective-permute-start | bytes 2359304 | tf_op jit(solution)/shard_map/ppermute | solution.py:43
  27.3 22.9 %collective-permute-start.10 = (bf16[224,2304]{1,0:T(8,128)(2,1)S(1)}, bf16[224,2304]{1,0:T(8,128)(2,1)}, u32[]{:S(2)}, u32[]{:S(2)}) collective-permute-start(bf16[224,2304]{1,0:T(8,128)(2,1)S(1)} %pad_maximum_fusion.1.refs_12_), channel_id=1, source_target_pairs={{0,48},{1,49},{2,50},{3,51},{8,56},{9,57},{10,58},{11,59},{16,0},{... | collective-permute-start | bytes 3096584 | tf_op jit(solution)/shard_map/ppermute | solution.py:43
  30.0 37.0 %collective-permute-start.4 = (bf16[2,768,512]{2,1,0:T(8,128)(2,1)}, bf16[2,768,512]{2,1,0:T(8,128)(2,1)}, u32[]{:S(2)}, u32[]{:S(2)}) collective-permute-start(bf16[2,768,512]{2,1,0:T(8,128)(2,1)} %pad_maximum_fusion), channel_id=1, source_target_pairs={{0,1},{1,2},{2,3},{3,0},{8,9},{9,10},{10,11},{11,8},{16,17},{17,18... | collective-permute-start | bytes 4718600 | tf_op jit(solution)/shard_map/ppermute | solution.py:43
  31.6 37.8 %collective-permute-start.5 = (bf16[2,768,512]{2,1,0:T(8,128)(2,1)}, bf16[2,768,512]{2,1,0:T(8,128)(2,1)}, u32[]{:S(2)}, u32[]{:S(2)}) collective-permute-start(bf16[2,768,512]{2,1,0:T(8,128)(2,1)} %pad_maximum_fusion), channel_id=1, source_target_pairs={{0,3},{1,0},{2,1},{3,2},{8,11},{9,8},{10,9},{11,10},{16,19},{17,16... | collective-permute-start | bytes 4718600 | tf_op jit(solution)/shard_map/ppermute | solution.py:43
  33.8 27.6 %collective-permute-start.8 = (bf16[224,2304]{1,0:T(8,128)(2,1)S(1)}, bf16[224,2304]{1,0:T(8,128)(2,1)S(1)}, u32[]{:S(2)}, u32[]{:S(2)}) collective-permute-start(bf16[224,2304]{1,0:T(8,128)(2,1)S(1)} %pad_maximum_fusion.1.refs_12_), channel_id=1, source_target_pairs={{0,64},{1,65},{2,66},{3,67},{8,72},{9,73},{10,74},{11,75},{16,80},... | collective-permute-start | bytes 3096584 | tf_op jit(solution)/shard_map/ppermute | solution.py:43
  33.8 27.6 %collective-permute-start.9 = (bf16[224,2304]{1,0:T(8,128)(2,1)S(1)}, bf16[224,2304]{1,0:T(8,128)(2,1)S(1)}, u32[]{:S(2)}, u32[]{:S(2)}) collective-permute-start(bf16[224,2304]{1,0:T(8,128)(2,1)S(1)} %pad_maximum_fusion.1.refs_12_), channel_id=1, source_target_pairs={{0,16},{1,17},{2,18},{3,19},{8,24},{9,25},{10,26},{11,27},{16,32},... | collective-permute-start | bytes 3096584 | tf_op jit(solution)/shard_map/ppermute | solution.py:43
  53.3 234.9 %all-gather.7.cloned.1.call-start = ((), (), s32[]{:S(2)}) async-start(), calls=%async_computation.1 | async-start | bytes 1179648 | tf_op jit(solution)/shard_map/all_gather | solution.py:355
  61.4 39.0 %collective-permute-start.11 = (bf16[224,2304]{1,0:T(8,128)(2,1)S(1)}, bf16[224,2304]{1,0:T(8,128)(2,1)}, u32[]{:S(2)}, u32[]{:S(2)}) collective-permute-start(bf16[224,2304]{1,0:T(8,128)(2,1)S(1)} %collective-permute-done.8.refs_14_), channel_id=1, source_target_pairs={{0,16},{1,17},{2,18},{3,19},{8,24},{9,25},{10,26},{11,27},{16,32},... | collective-permute-start | bytes 3096584 | tf_op jit(solution)/shard_map/ppermute | solution.py:43
  62.6 39.3 %collective-permute-start.13 = (bf16[224,2304]{1,0:T(8,128)(2,1)S(1)}, bf16[224,2304]{1,0:T(8,128)(2,1)}, u32[]{:S(2)}, u32[]{:S(2)}) collective-permute-start(bf16[224,2304]{1,0:T(8,128)(2,1)S(1)} %collective-permute-done.8.refs_14_), channel_id=1, source_target_pairs={{0,8},{1,9},{2,10},{3,11},{8,0},{9,1},{10,2},{11,3},{16,24},{17,25... | collective-permute-start | bytes 3096584 | tf_op jit(solution)/shard_map/ppermute | solution.py:43
  62.9 40.5 %collective-permute-start.16 = (bf16[224,2304]{1,0:T(8,128)(2,1)S(1)}, bf16[224,2304]{1,0:T(8,128)(2,1)}, u32[]{:S(2)}, u32[]{:S(2)}) collective-permute-start(bf16[224,2304]{1,0:T(8,128)(2,1)S(1)} %collective-permute-done.8.refs_14_), channel_id=1, source_target_pairs={{0,48},{1,49},{2,50},{3,51},{8,56},{9,57},{10,58},{11,59},{16,0},{... | collective-permute-start | bytes 3096584 | tf_op jit(solution)/shard_map/ppermute | solution.py:43
  66.9 36.5 %collective-permute-start.14 = (bf16[224,2304]{1,0:T(8,128)(2,1)S(1)}, bf16[224,2304]{1,0:T(8,128)(2,1)}, u32[]{:S(2)}, u32[]{:S(2)}) collective-permute-start(bf16[224,2304]{1,0:T(8,128)(2,1)S(1)} %collective-permute-done.9.refs_16_), channel_id=1, source_target_pairs={{0,8},{1,9},{2,10},{3,11},{8,0},{9,1},{10,2},{11,3},{16,24},{17,25... | collective-permute-start | bytes 3096584 | tf_op jit(solution)/shard_map/ppermute | solution.py:43
  69.4 34.0 %collective-permute-start.15 = (bf16[224,2304]{1,0:T(8,128)(2,1)}, bf16[224,2304]{1,0:T(8,128)(2,1)}, u32[]{:S(2)}, u32[]{:S(2)}) collective-permute-start(bf16[224,2304]{1,0:T(8,128)(2,1)} %collective-permute-done.10.refs_18_), channel_id=1, source_target_pairs={{0,8},{1,9},{2,10},{3,11},{8,0},{9,1},{10,2},{11,3},{16,24},{17,25... | collective-permute-start | bytes 3096584 | tf_op jit(solution)/shard_map/ppermute | solution.py:43
  100.4 20.6 %collective-permute-start.6 = (bf16[768,512]{1,0:T(8,128)(2,1)}, bf16[768,512]{1,0:T(8,128)(2,1)S(1)}, u32[]{:S(2)}, u32[]{:S(2)}) collective-permute-start(bf16[768,512]{1,0:T(8,128)(2,1)} %slice_bitcast_fusion.1), channel_id=1, source_target_pairs={{0,1},{1,2},{2,3},{3,0},{8,9},{9,10},{10,11},{11,8},{16,17},{17,18... | collective-permute-start | bytes 2359304 | tf_op jit(solution)/shard_map/ppermute | solution.py:43
  101.9 25.0 %collective-permute-start.7 = (bf16[768,512]{1,0:T(8,128)(2,1)}, bf16[768,512]{1,0:T(8,128)(2,1)S(1)}, u32[]{:S(2)}, u32[]{:S(2)}) collective-permute-start(bf16[768,512]{1,0:T(8,128)(2,1)} %slice_bitcast_fusion), channel_id=1, source_target_pairs={{0,3},{1,0},{2,1},{3,2},{8,11},{9,8},{10,9},{11,10},{16,19},{17,16... | collective-permute-start | bytes 2359304 | tf_op jit(solution)/shard_map/ppermute | solution.py:43
  103.4 38.8 %collective-permute-start.19 = (bf16[224,2304]{1,0:T(8,128)(2,1)}, bf16[224,2304]{1,0:T(8,128)(2,1)S(1)}, u32[]{:S(2)}, u32[]{:S(2)}) collective-permute-start(bf16[224,2304]{1,0:T(8,128)(2,1)} %collective-permute-done.16.refs_22_), channel_id=1, source_target_pairs={{0,8},{1,9},{2,10},{3,11},{8,0},{9,1},{10,2},{11,3},{16,24},{17,25... | collective-permute-start | bytes 3096584 | tf_op jit(solution)/shard_map/ppermute | solution.py:43
  104.2 60.0 %collective-permute-start.21 = (bf16[224,2304]{1,0:T(8,128)(2,1)}, bf16[224,2304]{1,0:T(8,128)(2,1)S(1)}, u32[]{:S(2)}, u32[]{:S(2)}) collective-permute-start(bf16[224,2304]{1,0:T(8,128)(2,1)} %collective-permute-done.16.refs_22_), channel_id=1, source_target_pairs={{0,48},{1,49},{2,50},{3,51},{8,56},{9,57},{10,58},{11,59},{16,0},{... | collective-permute-start | bytes 3096584 | tf_op jit(solution)/shard_map/ppermute | solution.py:43
  105.1 37.1 %collective-permute-start.18 = (bf16[224,2304]{1,0:T(8,128)(2,1)}, bf16[224,2304]{1,0:T(8,128)(2,1)S(1)}, u32[]{:S(2)}, u32[]{:S(2)}) collective-permute-start(bf16[224,2304]{1,0:T(8,128)(2,1)} %collective-permute-done.11.refs_20_), channel_id=1, source_target_pairs={{0,8},{1,9},{2,10},{3,11},{8,0},{9,1},{10,2},{11,3},{16,24},{17,25... | collective-permute-start | bytes 3096584 | tf_op jit(solution)/shard_map/ppermute | solution.py:43
  120.9 18.7 %collective-permute-start.17 = (bf16[448,576]{1,0:T(8,128)(2,1)S(1)}, bf16[448,576]{1,0:T(8,128)(2,1)S(1)}, u32[]{:S(2)}, u32[]{:S(2)}) collective-permute-start(bf16[448,576]{1,0:T(8,128)(2,1)S(1)} %fusion.3), channel_id=1, source_target_pairs={{0,0},{1,16},{2,32},{3,48},{8,8},{9,24},{10,40},{11,56},{16,49},{1... | collective-permute-start | bytes 1548296 | tf_op jit(solution)/shard_map/ppermute | solution.py:43
  126.9 37.3 %collective-permute-start.20 = (bf16[224,2304]{1,0:T(8,128)(2,1)S(1)}, bf16[224,2304]{1,0:T(8,128)(2,1)S(1)}, u32[]{:S(2)}, u32[]{:S(2)}) collective-permute-start(bf16[224,2304]{1,0:T(8,128)(2,1)S(1)} %collective-permute-done.9.refs_16_), channel_id=1, source_target_pairs={{0,16},{1,17},{2,18},{3,19},{8,24},{9,25},{10,26},{11,27},{16,32},... | collective-permute-start | bytes 3096584 | tf_op jit(solution)/shard_map/ppermute | solution.py:43
  139.6 26.7 %collective-permute-start.23 = (bf16[448,576]{1,0:T(8,128)(2,1)S(1)}, bf16[448,576]{1,0:T(8,128)(2,1)}, u32[]{:S(2)}, u32[]{:S(2)}) collective-permute-start(bf16[448,576]{1,0:T(8,128)(2,1)S(1)} %collective-permute-done.17.refs_0_), channel_id=1, source_target_pairs={{0,64},{1,65},{2,66},{3,67},{8,72},{9,73},{10,74},{11,75},{16,80},... | collective-permute-start | bytes 1548296 | tf_op jit(solution)/shard_map/ppermute | solution.py:43
  191.1 17.7 %collective-permute-start.33 = (bf16[448,576]{1,0:T(8,128)(2,1)}, bf16[448,576]{1,0:T(8,128)(2,1)}, u32[]{:S(2)}, u32[]{:S(2)}) collective-permute-start(bf16[448,576]{1,0:T(8,128)(2,1)} %collective-permute-done.30.refs_2_), channel_id=1, source_target_pairs={{0,8},{1,9},{2,10},{3,11},{8,0},{9,1},{10,2},{11,3},{16,24},{17,25... | collective-permute-start | bytes 1548296 | tf_op jit(solution)/shard_map/ppermute | solution.py:43
  207.7 16.5 %collective-permute-start.43 = (bf16[448,576]{1,0:T(8,128)(2,1)}, bf16[448,576]{1,0:T(8,128)(2,1)S(1)}, u32[]{:S(2)}, u32[]{:S(2)}) collective-permute-start(bf16[448,576]{1,0:T(8,128)(2,1)} %collective-permute-done.37.refs_2_), channel_id=1, source_target_pairs={{0,48},{1,49},{2,50},{3,51},{8,56},{9,57},{10,58},{11,59},{16,0},{... | collective-permute-start | bytes 1548296 | tf_op jit(solution)/shard_map/ppermute | solution.py:43
  208.8 16.8 %collective-permute-start.41 = (bf16[448,576]{1,0:T(8,128)(2,1)S(1)}, bf16[448,576]{1,0:T(8,128)(2,1)S(1)}, u32[]{:S(2)}, u32[]{:S(2)}) collective-permute-start(bf16[448,576]{1,0:T(8,128)(2,1)S(1)} %collective-permute-done.29.refs_0_), channel_id=1, source_target_pairs={{0,16},{1,17},{2,18},{3,19},{8,24},{9,25},{10,26},{11,27},{16,32},... | collective-permute-start | bytes 1548296 | tf_op jit(solution)/shard_map/ppermute | solution.py:43
  214.4 32.7 %collective-permute-start.27 = (bf16[448,768]{1,0:T(8,128)(2,1)S(1)}, bf16[448,768]{1,0:T(8,128)(2,1)S(1)}, u32[]{:S(2)}, u32[]{:S(2)}) collective-permute-start(bf16[448,768]{1,0:T(8,128)(2,1)S(1)} %get-tuple-element.51), channel_id=1, source_target_pairs={{0,0},{1,1},{2,2},{3,3},{8,8},{9,9},{10,10},{11,11},{16,17},{17,18... | collective-permute-start | bytes 2064392 | tf_op jit(solution)/shard_map/ppermute | solution.py:43
  219.6 63.8 %collective-permute-start.28 = (bf16[448,768]{1,0:T(8,128)(2,1)S(1)}, bf16[448,768]{1,0:T(8,128)(2,1)S(1)}, u32[]{:S(2)}, u32[]{:S(2)}) collective-permute-start(bf16[448,768]{1,0:T(8,128)(2,1)S(1)} %get-tuple-element.52), channel_id=1, source_target_pairs={{0,4},{1,5},{2,6},{3,7},{8,12},{9,13},{10,14},{11,15},{16,21},{17,... | collective-permute-start | bytes 2064392 | tf_op jit(solution)/shard_map/ppermute | solution.py:43
  221.5 63.7 %collective-permute-start.34 = (bf16[448,768]{1,0:T(8,128)(2,1)S(1)}, bf16[448,768]{1,0:T(8,128)(2,1)S(1)}, u32[]{:S(2)}, u32[]{:S(2)}) collective-permute-start(bf16[448,768]{1,0:T(8,128)(2,1)S(1)} %get-tuple-element.56), channel_id=1, source_target_pairs={{0,3},{1,0},{2,1},{3,2},{8,11},{9,8},{10,9},{11,10},{16,16},{17,17... | collective-permute-start | bytes 2064392 | tf_op jit(solution)/shard_map/ppermute | solution.py:43
  229.8 60.4 %collective-permute-start.35 = (bf16[448,768]{1,0:T(8,128)(2,1)S(1)}, bf16[448,768]{1,0:T(8,128)(2,1)}, u32[]{:S(2)}, u32[]{:S(2)}) collective-permute-start(bf16[448,768]{1,0:T(8,128)(2,1)S(1)} %get-tuple-element.57), channel_id=1, source_target_pairs={{0,1},{1,2},{2,3},{3,0},{8,9},{9,10},{10,11},{11,8},{16,18},{17,19... | collective-permute-start | bytes 2064392 | tf_op jit(solution)/shard_map/ppermute | solution.py:43
  237.0 53.2 %collective-permute-start.39 = (bf16[448,768]{1,0:T(8,128)(2,1)}, bf16[448,768]{1,0:T(8,128)(2,1)}, u32[]{:S(2)}, u32[]{:S(2)}) collective-permute-start(bf16[448,768]{1,0:T(8,128)(2,1)} %get-tuple-element.59), channel_id=1, source_target_pairs={{0,7},{1,4},{2,5},{3,6},{8,15},{9,12},{10,13},{11,14},{16,20},{17,... | collective-permute-start | bytes 2064392 | tf_op jit(solution)/shard_map/ppermute | solution.py:43
  247.1 43.1 %collective-permute-start.40 = (bf16[448,768]{1,0:T(8,128)(2,1)}, bf16[448,768]{1,0:T(8,128)(2,1)S(1)}, u32[]{:S(2)}, u32[]{:S(2)}) collective-permute-start(bf16[448,768]{1,0:T(8,128)(2,1)} %get-tuple-element.60), channel_id=1, source_target_pairs={{0,5},{1,6},{2,7},{3,4},{8,13},{9,14},{10,15},{11,12},{16,22},{17,... | collective-permute-start | bytes 2064392 | tf_op jit(solution)/shard_map/ppermute | solution.py:43
  283.3 19.7 %collective-permute-start.45 = (bf16[448,768]{1,0:T(8,128)(2,1)}, bf16[448,768]{1,0:T(8,128)(2,1)}, u32[]{:S(2)}, u32[]{:S(2)}) collective-permute-start(bf16[448,768]{1,0:T(8,128)(2,1)} %get-tuple-element.61), channel_id=1, source_target_pairs={{0,2},{1,3},{2,0},{3,1},{8,10},{9,11},{10,8},{11,9},{16,19},{17,16... | collective-permute-start | bytes 2064392 | tf_op jit(solution)/shard_map/ppermute | solution.py:43
  286.1 32.4 %collective-permute-start.46 = (bf16[448,768]{1,0:T(8,128)(2,1)}, bf16[448,768]{1,0:T(8,128)(2,1)}, u32[]{:S(2)}, u32[]{:S(2)}) collective-permute-start(bf16[448,768]{1,0:T(8,128)(2,1)} %get-tuple-element.62), channel_id=1, source_target_pairs={{0,6},{1,7},{2,4},{3,5},{8,14},{9,15},{10,12},{11,13},{16,23},{17,... | collective-permute-start | bytes 2064392 | tf_op jit(solution)/shard_map/ppermute | solution.py:43
  (38 other events, 420.9 us)
Sparse Core Ops, SparseCore 0:
  53.4 45.6 all-gather.4
  193.0 49.1 all-gather.6

commit v2 on v1

--- a/solution.py
+++ b/solution.py
@@ -73,13 +73,15 @@
 
 def to_ff_group(y, x, core, z):
     y_hi, y_lo = y // 2, y % 2
-    return (y_lo ^ y_hi) * 2 + y_hi, z - x, core, x
+    across = y_lo ^ y_hi
+    return across * 2 + y_hi, z - x - 2 * across, core, x
 
 
 def to_chunk(dy, dx):
     def target(y, x, core, z):
         y_hi, y_lo = y // 2, y % 2
-        return y_hi * 2 + (y_lo ^ y_hi ^ dy), x, core, z + x + dx
+        across = y_hi ^ dy
+        return y_hi * 2 + (y_lo ^ across), x, core, z + x + dx + 2 * across
 
     return target
 
@@ -133,9 +135,9 @@
     return lax.optimization_barrier((array, *others))[0]
 
 
-def ring(own, far, up, down, others=(), between=lambda blocks: ()):
+def ring(own, far, up, down, between):
     own_l, own_r = send(own, up), send(own, down)
-    far = after(far, own_l, own_r, *others)
+    far = after(far, own_l, own_r)
     far_l, far_r = send(far, up), send(far, down)
     others = between([own, far, own_l, own_r])
     own_l, far_r = after(own_l, far_l, *others), after(far_r, far_l, *others)
@@ -146,74 +148,90 @@
 TOKEN_ORDER = ((0, 0), (1, 0), (0, -1), (1, -1), (0, 1), (1, 1), (0, 2), (1, 2))
 
 
-def token_ring(own, near):
-    pair = jnp.stack([own, near])
+def token_ring(pair):
     left, right = send(pair, z_up), send(pair, z_down)
-    own_ll, near_rr = send(left[0], z_up), send(right[1], z_down)
-    return jnp.concatenate([pair, left, right, own_ll[None], near_rr[None]])
+    return [pair, left, right, send(left[0], z_up)[None], send(right[1], z_down)[None]]
 
 
 def token_kernel(count, has_before, last, info, *refs):
-    tokens, refs = refs[:count], list(refs[count:])
+    tokens, refs = refs[:5], list(refs[5:])
     before = refs.pop(0) if has_before else None
-    blocks, (out, scratch, sems) = refs[:count], refs[count:]
+    blocks, (out, wide, scratch, wide_sems, sems) = refs[:count], refs[count:]
     height = blocks[0].shape[0]
-
-    @pl.when(pl.program_id(0) == 0)
+    pieces = [ref.at[k] for ref in tokens for k in range(ref.shape[0])]
+
+    def block_copy(n):
+        rows = pl.ds(n * HALF, height)
+        return pltpu.make_async_copy(blocks[n], scratch.at[rows, :], sems.at[n])
+
+    def token_copy(n, piece=0):
+        return pltpu.make_async_copy(pieces[piece], wide.at[n], wide_sems.at[n])
+
+    def rows_of(m, n):
+        start = pl.multiple_of(m * TILE, TILE)
+        low, high = wide[n, pl.ds(start, TILE), :HALF], wide[n, pl.ds(start, TILE), HALF:]
+        swapped = info[8] == 1
+        return jnp.where(swapped, high, low), jnp.where(swapped, low, high)
+
+    def finish(total):
+        if has_before:
+            total += before[...]
+        if last:
+            middle = total.shape[1] // 2
+            gate = total[:, :middle]
+            total = gate / (1.0 + jnp.exp(-gate)) * total[:, middle:]
+        out[...] = total.astype(out.dtype)
+
+    m = pl.program_id(0)
+
+    @pl.when(m == 0)
     def _():
-        copies = [
-            pltpu.make_async_copy(
-                block, scratch.at[pl.ds(n * HALF, height), :], sems.at[n]
-            )
-            for n, block in enumerate(blocks)
-        ]
-        for copy in copies:
-            copy.start()
+        for n in range(count // 2):
+            for piece in range(len(pieces)):
+
+                @pl.when(info[n] == piece)
+                def _():
+                    token_copy(n, piece).start()
+
+            block_copy(2 * n).start()
+            block_copy(2 * n + 1).start()
         for n in range(count):
             scratch[n * HALF + height : (n + 1) * HALF, :] = jnp.zeros(
                 (HALF - height, scratch.shape[1]), scratch.dtype
             )
-        for copy in copies:
-            copy.wait()
-
-    rows = jnp.concatenate([token[...] for token in tokens], axis=1)
-    total = jnp.dot(rows, scratch[...], preferred_element_type=jnp.float32)
-    if has_before:
-        total += before[...]
-    if last:
-        middle = total.shape[1] // 2
-        gate = total[:, :middle]
-        total = gate / (1.0 + jnp.exp(-gate)) * total[:, middle:]
-    out[...] = total.astype(out.dtype)
+        for n in range(count // 2):
+            token_copy(n).wait()
+            block_copy(2 * n).wait()
+            block_copy(2 * n + 1).wait()
+
+    rows = jnp.concatenate([part for n in range(count // 2) for part in rows_of(m, n)], axis=1)
+    finish(jnp.dot(rows, scratch[...], preferred_element_type=jnp.float32))
 
 
 def token_sum(info, tokens, first, blocks, before=None, last=False):
-    rows, columns = tokens.shape[1], blocks[0].shape[1]
+    rows, columns = tokens[0].shape[1], blocks[0].shape[1]
     count = len(blocks)
     width = columns // 2 if last else columns
 
-    def token_block(n):
-        side = n % 2
-        return pl.BlockSpec(
-            (None, TILE, HALF),
-            lambda m, info: (info[first + n // 2], m, 1 - info[8] if side else info[8]),
-        )
-
     def tile(width):
         return pl.BlockSpec((TILE, width), lambda m, info: (m, 0))
 
+    if first:
+        info = jnp.concatenate([info[first:8], info[:first], info[8:]])
     return pl.pallas_call(
         functools.partial(token_kernel, count, before is not None, last),
         out_shape=jax.ShapeDtypeStruct((rows, width), jnp.bfloat16 if last else jnp.float32),
         grid_spec=pltpu.PrefetchScalarGridSpec(
             num_scalar_prefetch=1,
             grid=(rows // TILE,),
-            in_specs=[token_block(n) for n in range(count)]
+            in_specs=[pl.BlockSpec(memory_space=pl.ANY)] * 5
             + ([] if before is None else [tile(columns)])
             + [pl.BlockSpec(memory_space=pl.ANY)] * count,
             out_specs=tile(width),
             scratch_shapes=[
+                pltpu.VMEM((count // 2, rows, 2 * HALF), jnp.bfloat16),
                 pltpu.VMEM((count * HALF, columns), jnp.bfloat16),
+                pltpu.SemaphoreType.DMA((count // 2,)),
                 pltpu.SemaphoreType.DMA((count,)),
             ],
         ),
@@ -223,7 +241,7 @@
             bytes_accessed=rows * columns * 8,
             transcendentals=0,
         ),
-    )(info, *([tokens] * count), *([] if before is None else [before]), *blocks)
+    )(info, *tokens, *([] if before is None else [before]), *blocks)
 
 
 def vmem(n):
@@ -292,14 +310,12 @@
     rows = D // BLOCK + 12
     columns = FF // BLOCK + 56
     pad = lambda a: jnp.pad(a, ((0, rows - a.shape[0]), (0, columns - a.shape[1])))
-    spare = jnp.zeros((8, columns), jnp.float32)
-    table = jnp.concatenate([pad(tables[0]), pad(tables[1]), pad(tables[2].T), spare])
+    table = jnp.concatenate([pad(tables[0]), pad(tables[1]), pad(tables[2].T)])
 
     def step(table, target):
         return jnp.maximum(table, send(table, target))
 
     table = step(table, other_core)
-    down_table = step(table, lambda y, x, core, z: (y, x, core, z ^ 1))
     table = step(table, lambda y, x, core, z: (y, x ^ 1, core, z))
     gate_up = jnp.concatenate(
         [
@@ -308,31 +324,34 @@
         ],
         axis=1,
     )
-    gate_up, down_table, near, padded = lax.optimization_barrier(
-        (gate_up, down_table, near, padded)
-    )
-    relative = token_ring(padded, near)
+    every = step(table, lambda y, x, core, z: (y, x, core, z ^ 1))
+    pair = jnp.stack([padded, near])
+    gate_up, pair, every = lax.optimization_barrier((gate_up, pair, every))
+    down_table = every
+    relative = token_ring(pair)
     pairs = []
 
     def swap(blocks):
+        nonlocal every
+        if len(blocks) == 4:
+            every = step(after(every, *blocks), y_near)
         others = [send(block, other_core) for block in blocks]
         for block, other in zip(blocks, others):
             pairs.extend((block, other))
-        return others
-
-    blocks = ring(gate_up, send(gate_up, y_far), x_up, x_down, (), swap)
+        return others + [every]
+
+    blocks = ring(gate_up, send(gate_up, y_far), x_up, x_down, swap)
     swap(blocks[4:6])
 
-    table = jnp.maximum(table, down_table)
-    every = jnp.max(lax.all_gather(table, "fsdp"), axis=0)
     order = [TOKEN_ORDER.index((dy, dx)) for dy in range(2) for dx in (0, 1, 2, -1)]
     by_offset = jnp.array(order, jnp.int32)
     info = jnp.stack(
         [by_offset[(chip_y ^ y_lo) * 4 + (chip_x - z + 4) % 4] for chip_y, chip_x in chips] + [core]
     )
 
-    relative, every = lax.optimization_barrier((relative, every))
+    ready = after(every, relative[3], relative[4], blocks[4], blocks[5])
     early = token_sum(info, relative, 0, pairs)
+    every = step(ready, lambda y, x, core, z: (y, x, core, z ^ 2))
 
     def both(blocks):
         return [b for block in blocks for b in (block, send(block, other_core))]
@@ -342,26 +361,32 @@
     down_block = send(after(down_weight.T, blocks[4], blocks[5]), to_ff_group)
     down_far = send(down_block, y_far)
     down_pairs = [both([down_block, down_far])]
-    down_block, early, own_ll, far_rr = lax.optimization_barrier(
-        (down_block, early, blocks[6], blocks[7])
+    down_block, early, own_ll, far_rr, every = lax.optimization_barrier(
+        (down_block, early, blocks[6], blocks[7], every)
     )
     pairs = both([own_ll, far_rr])
+    every = step(after(every, *down_pairs[0]), y_far)
     early = after(early, *down_pairs[0])
     hidden = token_sum(info, relative, 6, pairs, early, last=True)
-    down_blocks = ring(down_block, down_far, x_up, x_down, (hidden,))
-    down_pairs += [both(down_blocks[n : n + 2]) for n in (2, 4, 6)]
-
-    every = jnp.pad(every, ((0, every.shape[0]), (0, 0)))
-    every = jnp.max(lax.all_gather(every, "tp"), axis=0)
+    def sums(n, pair):
+        terms = down_terms(info, hidden, pair)
+        return terms, [send(term, to_chunk(*ORDER[n + k])) for k, term in enumerate(terms)]
+
+    own_l, own_r = send(down_block, x_up), send(down_block, x_down)
+    own_l, own_r, down_far, hidden = lax.optimization_barrier((own_l, own_r, down_far, hidden))
+    _, parts = sums(0, down_pairs[0])
+    far_l, far_r = send(down_far, x_up), send(down_far, x_down)
+    terms, more = sums(2, both([own_l, own_r]))
+    own_l, far_r, *_ = lax.optimization_barrier((own_l, far_r, far_l, *terms, *parts))
+    own_ll, far_rr = send(own_l, x_up), send(far_r, x_down)
+    parts += more
+    parts += sums(4, both([far_l, far_r]))[1]
+    parts += sums(6, both([own_ll, far_rr]))[1]
+    every = step(after(every, own_ll, far_rr), lambda y, x, core, z: (y, x ^ 2, core, z))
     log_amax = jnp.log(
         jnp.stack([every[k * rows : k * rows + D // BLOCK, : FF // BLOCK] for k in range(3)]) + EPS
     )
-
-    total = 0.0
-    for n in range(0, 8, 2):
-        terms = down_terms(info, hidden, down_pairs[n // 2])
-        for k in range(2):
-            total += send(terms[k], to_chunk(*ORDER[n + k])).astype(jnp.float32)
+    total = sum(part.astype(jnp.float32) for part in parts)
     return total.astype(jnp.bfloat16).T, log_amax
 
 

time: 330 us -> 283 us (0.86)
  the two profiles are of different devices: /device:TPU:19 before, /device:TPU:6 now
where the time goes in v2:
time: 283 us; the launch traced here: 280 us
  waiting for transfers between devices  132 us (47%)
  starting transfers between devices  63.9 us (23%)
  Pallas kernels  40.9 us (14%)
  local copies, waits for them, and re-layouts  29.8 us (11%)
  other arithmetic  12.7 us (4%)
    ppermute x51, waiting for transfers between devices, send(): return lax.ppermute(array, AXES, pairs)  132 us
    ppermute x51, starting transfers between devices, send(): return lax.ppermute(array, AXES, pairs)  63.9 us
    pallas_call x2, Pallas kernels, token_sum(): pl.pallas_call(functools.partial(token_kernel, count, before is not None,...  29.3 us
    unnamed x48, local copies, waits for them, and re-layouts  14 us
    pallas_call x4, Pallas kernels, down_terms(): pl.pallas_call(down_kernel, out_shape=[jax.ShapeDtypeStruct((columns, row...  11.6 us
  transfers between devices with their start and end apart: 51, of which 23 were waited for; matrix products, arithmetic and copies ran while one was open for 8% of the time, Pallas kernels for 15%

profile of v2, /device:TPU:6, one launch (start us, length us, event | category | flops | bytes accessed | tf_op | source)
XLA Modules:
  0.0 280.4 jit_solution(10382144327743990866)
XLA Ops:
  10.8 3.4 %collective-permute-done.1 = f32[120,128]{1,0:T(8,128)S(1)} collective-permute-done((f32[120,128]{1,0:T(8,128)S(1)}, f32[120,128]{1,0:T(8,128)S(1)}, u32[]{:S(2)}, u32[]{:S(2)}) %collective-permute-start.1) | collective-permute-done | bytes 61472 | tf_op jit(solution)/shard_map/ppermute | solution.py:43
  17.7 2.5 multiply_convert_fusion.2
  24.1 3.3 %collective-permute-start.4 = (bf16[224,2304]{1,0:T(8,128)(2,1)S(1)}, bf16[224,2304]{1,0:T(8,128)(2,1)S(1)}, u32[]{:S(2)}, u32[]{:S(2)}) collective-permute-start(bf16[224,2304]{1,0:T(8,128)(2,1)S(1)} %pad_maximum_fusion.1.refs_5_), channel_id=1, source_target_pairs={{0,64},{1,65},{2,66},{3,67},{8,72},{9,73},{10,74},{11,75},{16,80},... | collective-permute-start | bytes 3096584 | tf_op jit(solution)/shard_map/ppermute | solution.py:43
  33.5 15.9 %collective-permute-done.4.refs_7_ = bf16[224,2304]{1,0:T(8,128)(2,1)S(1)} collective-permute-done((bf16[224,2304]{1,0:T(8,128)(2,1)S(1)}, bf16[224,2304]{1,0:T(8,128)(2,1)S(1)}, u32[]{:S(2)}, u32[]{:S(2)}) %collective-permute-start.4) | collective-permute-done | bytes 1032224 | tf_op jit(solution)/shard_map/ppermute | solution.py:43
  49.4 5.3 %collective-permute-done.5.refs_9_ = bf16[224,2304]{1,0:T(8,128)(2,1)} collective-permute-done((bf16[224,2304]{1,0:T(8,128)(2,1)S(1)}, bf16[224,2304]{1,0:T(8,128)(2,1)}, u32[]{:S(2)}, u32[]{:S(2)}) %collective-permute-start.5) | collective-permute-done | bytes 1032224 | tf_op jit(solution)/shard_map/ppermute | solution.py:43
  57.1 2.9 %collective-permute-start.7 = (bf16[224,2304]{1,0:T(8,128)(2,1)S(1)}, bf16[224,2304]{1,0:T(8,128)(2,1)}, u32[]{:S(2)}, u32[]{:S(2)}) collective-permute-start(bf16[224,2304]{1,0:T(8,128)(2,1)S(1)} %collective-permute-done.4.refs_7_), channel_id=1, source_target_pairs={{0,16},{1,17},{2,18},{3,19},{8,24},{9,25},{10,26},{11,27},{16,32},... | collective-permute-start | bytes 3096584 | tf_op jit(solution)/shard_map/ppermute | solution.py:43
  60.3 4.4 %collective-permute-done.15.refs_1_ = bf16[2,768,512]{2,1,0:T(8,128)(2,1)S(1)} collective-permute-done((bf16[2,768,512]{2,1,0:T(8,128)(2,1)S(1)}, bf16[2,768,512]{2,1,0:T(8,128)(2,1)S(1)}, u32[]{:S(2)}, u32[]{:S(2)}) %collective-permute-start.15) | collective-permute-done | bytes 1572896 | tf_op jit(solution)/shard_map/ppermute | solution.py:43
  68.7 11.0 %collective-permute-done.13.refs_15_ = bf16[224,2304]{1,0:T(8,128)(2,1)} collective-permute-done((bf16[224,2304]{1,0:T(8,128)(2,1)S(1)}, bf16[224,2304]{1,0:T(8,128)(2,1)}, u32[]{:S(2)}, u32[]{:S(2)}) %collective-permute-start.13) | collective-permute-done | bytes 1032224 | tf_op jit(solution)/shard_map/ppermute | solution.py:43
  79.7 3.2 %collective-permute-start.18 = (bf16[768,512]{1,0:T(8,128)(2,1)S(1)}, bf16[768,512]{1,0:T(8,128)(2,1)S(1)}, u32[]{:S(2)}, u32[]{:S(2)}) collective-permute-start(bf16[768,512]{1,0:T(8,128)(2,1)S(1)} %slice_bitcast_fusion), channel_id=1, source_target_pairs={{0,3},{1,0},{2,1},{3,2},{8,11},{9,8},{10,9},{11,10},{16,19},{17,16... | collective-permute-start | bytes 2359304 | tf_op jit(solution)/shard_map/ppermute | solution.py:43
  84.0 2.7 fusion.3
  88.6 20.7 %collective-permute-done.17 = bf16[768,512]{1,0:T(8,128)(2,1)S(1)} collective-permute-done((bf16[768,512]{1,0:T(8,128)(2,1)S(1)}, bf16[768,512]{1,0:T(8,128)(2,1)S(1)}, u32[]{:S(2)}, u32[]{:S(2)}) %collective-permute-start.17) | collective-permute-done | bytes 786464 | tf_op jit(solution)/shard_map/ppermute | solution.py:43
  111.4 5.5 %collective-permute-done.23 = f32[120,128]{1,0:T(8,128)S(1)} collective-permute-done((f32[120,128]{1,0:T(8,128)S(1)}, f32[120,128]{1,0:T(8,128)S(1)}, u32[]{:S(2)}, u32[]{:S(2)}) %collective-permute-start.23) | collective-permute-done | bytes 61472 | tf_op jit(solution)/shard_map/ppermute | solution.py:43
  117.6 5.2 %stack.73.info = s32[9]{0:T(128)S(1)} concatenate(s32[1]{0:T(128)} %get-tuple-element.141, s32[1]{0:T(128)} %get-tuple-element.140, s32[1]{0:T(128)} %get-tuple-element.139, s32[1]{0:T(128)} %get-tuple-element.138, s32[1]{0:T(128)} %get-tuple-element.137, s32[1]{0:T(128)} %get-tuple-element.136, s32[1]{0:T(128)} %get-tuple-element.142, s32[1]{0:T(128)} %get-tuple-element.135, s32[1]{0:T(128)} %bitcast), dimensions={0} | concatenate | bytes 72 | tf_op jit(solution)/shard_map/stack | solution.py:348
  122.8 3.5 %collective-permute-start.26 = (bf16[448,576]{1,0:T(8,128)(2,1)}, bf16[448,576]{1,0:T(8,128)(2,1)}, u32[]{:S(2)}, u32[]{:S(2)}) collective-permute-start(bf16[448,576]{1,0:T(8,128)(2,1)} %collective-permute-done.14.refs_0_), channel_id=1, source_target_pairs={{0,64},{1,65},{2,66},{3,67},{8,72},{9,73},{10,74},{11,75},{16,80},... | collective-permute-start | bytes 1548296 | tf_op jit(solution)/shard_map/ppermute | solution.py:43
  131.0 19.0 %shard_map.68.refs_5_ = f32[768,2304]{1,0:T(8,128)} custom-call(s32[9]{0:T(128)S(1)} %stack.73.info, bf16[2,768,512]{2,1,0:T(8,128)(2,1)} %copy-done.13, bf16[2,768,512]{2,1,0:T(8,128)(2,1)} %copy-done.18, bf16[2,768,512]{2,1,0:T(8,128)(2,1)} %copy-done.19, bf16[1,768,512]{2,1,0:T(8,128)(2,1)S(1)} %bitcast.44, bf16[1,768,512]{2,1,0:T(8,128)(2,1)S(1)} %bitcast.46, ...), custom_call_target="tpu_custom_call" | custom-call | flops 10871635968 | bytes 14155776 | tf_op jit(solution)/shard_map/pallas_call | solution.py:221
  151.6 4.4 %collective-permute-done.27.refs_1_ = bf16[448,576]{1,0:T(8,128)(2,1)S(1)} collective-permute-done((bf16[448,576]{1,0:T(8,128)(2,1)}, bf16[448,576]{1,0:T(8,128)(2,1)S(1)}, u32[]{:S(2)}, u32[]{:S(2)}) %collective-permute-start.27) | collective-permute-done | bytes 516128 | tf_op jit(solution)/shard_map/ppermute | solution.py:43
  157.0 5.2 %concatenate.18.info = s32[9]{0:T(128)S(1)} concatenate(s32[1]{0:T(128)} %get-tuple-element.142, s32[1]{0:T(128)} %get-tuple-element.135, s32[1]{0:T(128)} %get-tuple-element.141, s32[1]{0:T(128)} %get-tuple-element.140, s32[1]{0:T(128)} %get-tuple-element.139, s32[1]{0:T(128)} %get-tuple-element.138, s32[1]{0:T(128)} %get-tuple-element.137, s32[1]{0:T(128)} %get-tuple-element.136, ...), dimensions={0} | concatenate | bytes 72 | tf_op jit(solution)/shard_map/concatenate | solution.py:220
  164.5 10.3 %shard_map.69.hidden = bf16[768,1152]{1,0:T(8,128)(2,1)} custom-call(s32[9]{0:T(128)S(1)} %concatenate.18.info, bf16[2,768,512]{2,1,0:T(8,128)(2,1)} %copy-done.13, bf16[2,768,512]{2,1,0:T(8,128)(2,1)} %copy-done.18, bf16[2,768,512]{2,1,0:T(8,128)(2,1)} %copy-done.19, bf16[1,768,512]{2,1,0:T(8,128)(2,1)S(1)} %bitcast.45, bf16[1,768,512]{2,1,0:T(8,128)(2,1)S(1)} %bitcast.47, ...), custom_call_target="tpu_custom_call" | custom-call | flops 3623878656 | bytes 14155776 | tf_op jit(solution)/shard_map/pallas_call | solution.py:221
  176.4 3.4 %shard_map.70 = (bf16[448,768]{1,0:T(8,128)(2,1)S(1)}, bf16[448,768]{1,0:T(8,128)(2,1)S(1)}) custom-call(s32[9]{0:T(128)S(1)} %stack.73.info, bf16[768,1152]{1,0:T(8,128)(2,1)S(1)} %copy-done, bf16[448,576]{1,0:T(8,128)(2,1)} %collective-permute-done.14.refs_0_, bf16[448,576]{1,0:T(8,128)(2,1)S(1)} %copy-done.12, ...), custom_call_target="tpu_custom_call" | custom-call | flops 1585446912 | bytes 1376256 | tf_op jit(solution)/shard_map/pallas_call | solution.py:269
  179.7 6.0 %collective-permute-start.31 = (bf16[448,768]{1,0:T(8,128)(2,1)S(1)}, bf16[448,768]{1,0:T(8,128)(2,1)S(1)}, u32[]{:S(2)}, u32[]{:S(2)}) collective-permute-start(bf16[448,768]{1,0:T(8,128)(2,1)S(1)} %get-tuple-element.58), channel_id=1, source_target_pairs={{0,0},{1,1},{2,2},{3,3},{8,8},{9,9},{10,10},{11,11},{16,17},{17,18... | collective-permute-start | bytes 2064392 | tf_op jit(solution)/shard_map/ppermute | solution.py:43
  190.2 3.2 %shard_map.71 = (bf16[448,768]{1,0:T(8,128)(2,1)S(1)}, bf16[448,768]{1,0:T(8,128)(2,1)S(1)}) custom-call(s32[9]{0:T(128)S(1)} %stack.73.info, bf16[768,1152]{1,0:T(8,128)(2,1)S(1)} %copy-done, bf16[448,576]{1,0:T(8,128)(2,1)} %collective-permute-done.24.refs_0_, bf16[448,576]{1,0:T(8,128)(2,1)S(1)} %collective-permute-done.33.refs_1_, ...), custom_call_target="tpu_custom_call" | custom-call | flops 1585446912 | bytes 1376256 | tf_op jit(solution)/shard_map/pallas_call | solution.py:269
  193.4 10.2 %collective-permute-done.37.refs_0_ = bf16[448,576]{1,0:T(8,128)(2,1)S(1)} collective-permute-done((bf16[448,576]{1,0:T(8,128)(2,1)}, bf16[448,576]{1,0:T(8,128)(2,1)S(1)}, u32[]{:S(2)}, u32[]{:S(2)}) %collective-permute-start.37) | collective-permute-done | bytes 516128 | tf_op jit(solution)/shard_map/ppermute | solution.py:43
  209.8 5.7 %collective-permute-done.49 = f32[120,128]{1,0:T(8,128)S(1)} collective-permute-done((f32[120,128]{1,0:T(8,128)S(1)}, f32[120,128]{1,0:T(8,128)S(1)}, u32[]{:S(2)}, u32[]{:S(2)}) %collective-permute-start.49) | collective-permute-done | bytes 61472 | tf_op jit(solution)/shard_map/ppermute | solution.py:43
  217.4 4.2 %collective-permute-done.43.refs_0_ = bf16[448,576]{1,0:T(8,128)(2,1)S(1)} collective-permute-done((bf16[448,576]{1,0:T(8,128)(2,1)}, bf16[448,576]{1,0:T(8,128)(2,1)S(1)}, u32[]{:S(2)}, u32[]{:S(2)}) %collective-permute-start.43) | collective-permute-done | bytes 516128 | tf_op jit(solution)/shard_map/ppermute | solution.py:43
  225.5 2.5 shard_map.72
  228.1 3.2 %collective-permute-start.41 = (bf16[448,768]{1,0:T(8,128)(2,1)S(1)}, bf16[448,768]{1,0:T(8,128)(2,1)S(1)}, u32[]{:S(2)}, u32[]{:S(2)}) collective-permute-start(bf16[448,768]{1,0:T(8,128)(2,1)S(1)} %get-tuple-element.66), channel_id=1, source_target_pairs={{0,5},{1,6},{2,7},{3,4},{8,13},{9,14},{10,15},{11,12},{16,22},{17,... | collective-permute-start | bytes 2064392 | tf_op jit(solution)/shard_map/ppermute | solution.py:43
  231.3 5.5 %collective-permute-start.42 = (bf16[448,768]{1,0:T(8,128)(2,1)S(1)}, bf16[448,768]{1,0:T(8,128)(2,1)S(1)}, u32[]{:S(2)}, u32[]{:S(2)}) collective-permute-start(bf16[448,768]{1,0:T(8,128)(2,1)S(1)} %get-tuple-element.67), channel_id=1, source_target_pairs={{0,7},{1,4},{2,5},{3,6},{8,15},{9,12},{10,13},{11,14},{16,20},{17,... | collective-permute-start | bytes 2064392 | tf_op jit(solution)/shard_map/ppermute | solution.py:43
  236.8 2.5 shard_map.73
  241.3 5.9 %collective-permute-start.48 = (bf16[448,768]{1,0:T(8,128)(2,1)S(1)}, bf16[448,768]{1,0:T(8,128)(2,1)S(1)}, u32[]{:S(2)}, u32[]{:S(2)}) collective-permute-start(bf16[448,768]{1,0:T(8,128)(2,1)S(1)} %get-tuple-element.70), channel_id=1, source_target_pairs={{0,4},{1,5},{2,6},{3,7},{8,12},{9,13},{10,14},{11,15},{16,21},{17,... | collective-permute-start | bytes 2064392 | tf_op jit(solution)/shard_map/ppermute | solution.py:43
  248.2 17.7 %collective-permute-done.42 = bf16[448,768]{1,0:T(8,128)(2,1)S(1)} collective-permute-done((bf16[448,768]{1,0:T(8,128)(2,1)S(1)}, bf16[448,768]{1,0:T(8,128)(2,1)S(1)}, u32[]{:S(2)}, u32[]{:S(2)}) %collective-permute-start.42) | collective-permute-done | bytes 688160 | tf_op jit(solution)/shard_map/ppermute | solution.py:43
  266.0 8.0 %collective-permute-done.47 = bf16[448,768]{1,0:T(8,128)(2,1)S(1)} collective-permute-done((bf16[448,768]{1,0:T(8,128)(2,1)S(1)}, bf16[448,768]{1,0:T(8,128)(2,1)S(1)}, u32[]{:S(2)}, u32[]{:S(2)}) %collective-permute-start.47) | collective-permute-done | bytes 688160 | tf_op jit(solution)/shard_map/ppermute | solution.py:43
  273.9 4.9 %collective-permute-done.48 = bf16[448,768]{1,0:T(8,128)(2,1)S(1)} collective-permute-done((bf16[448,768]{1,0:T(8,128)(2,1)S(1)}, bf16[448,768]{1,0:T(8,128)(2,1)S(1)}, u32[]{:S(2)}, u32[]{:S(2)}) %collective-permute-start.48) | collective-permute-done | bytes 688160 | tf_op jit(solution)/shard_map/ppermute | solution.py:43
  (202 shorter events, 67.4 us)
Async XLA Ops:
  3.0 19.6 %collective-permute-start.2 = (bf16[768,512]{1,0:T(8,128)(2,1)}, bf16[768,512]{1,0:T(8,128)(2,1)}, u32[]{:S(2)}, u32[]{:S(2)}) collective-permute-start(bf16[768,512]{1,0:T(8,128)(2,1)} %fusion.1), channel_id=1, source_target_pairs={{0,4},{1,5},{2,6},{3,7},{8,12},{9,13},{10,14},{11,15},{16,20},{17,... | collective-permute-start | bytes 2359304 | tf_op jit(solution)/shard_map/ppermute | solution.py:43
  24.1 25.3 %collective-permute-start.4 = (bf16[224,2304]{1,0:T(8,128)(2,1)S(1)}, bf16[224,2304]{1,0:T(8,128)(2,1)S(1)}, u32[]{:S(2)}, u32[]{:S(2)}) collective-permute-start(bf16[224,2304]{1,0:T(8,128)(2,1)S(1)} %pad_maximum_fusion.1.refs_5_), channel_id=1, source_target_pairs={{0,64},{1,65},{2,66},{3,67},{8,72},{9,73},{10,74},{11,75},{16,80},... | collective-permute-start | bytes 3096584 | tf_op jit(solution)/shard_map/ppermute | solution.py:43
  27.4 37.3 %collective-permute-start.15 = (bf16[2,768,512]{2,1,0:T(8,128)(2,1)S(1)}, bf16[2,768,512]{2,1,0:T(8,128)(2,1)S(1)}, u32[]{:S(2)}, u32[]{:S(2)}) collective-permute-start(bf16[2,768,512]{2,1,0:T(8,128)(2,1)S(1)} %pad_maximum_fusion.refs_0_), channel_id=1, source_target_pairs={{0,1},{1,2},{2,3},{3,0},{8,9},{9,10},{10,11},{11,8},{16,17},{17,18... | collective-permute-start | bytes 4718600 | tf_op jit(solution)/shard_map/ppermute | solution.py:43
  29.3 35.4 %collective-permute-start.16 = (bf16[2,768,512]{2,1,0:T(8,128)(2,1)S(1)}, bf16[2,768,512]{2,1,0:T(8,128)(2,1)S(1)}, u32[]{:S(2)}, u32[]{:S(2)}) collective-permute-start(bf16[2,768,512]{2,1,0:T(8,128)(2,1)S(1)} %pad_maximum_fusion.refs_0_), channel_id=1, source_target_pairs={{0,3},{1,0},{2,1},{3,2},{8,11},{9,8},{10,9},{11,10},{16,19},{17,16... | collective-permute-start | bytes 4718600 | tf_op jit(solution)/shard_map/ppermute | solution.py:43
  31.5 23.2 %collective-permute-start.5 = (bf16[224,2304]{1,0:T(8,128)(2,1)S(1)}, bf16[224,2304]{1,0:T(8,128)(2,1)}, u32[]{:S(2)}, u32[]{:S(2)}) collective-permute-start(bf16[224,2304]{1,0:T(8,128)(2,1)S(1)} %pad_maximum_fusion.1.refs_5_), channel_id=1, source_target_pairs={{0,16},{1,17},{2,18},{3,19},{8,24},{9,25},{10,26},{11,27},{16,32},... | collective-permute-start | bytes 3096584 | tf_op jit(solution)/shard_map/ppermute | solution.py:43
  31.9 24.2 %collective-permute-start.6 = (bf16[224,2304]{1,0:T(8,128)(2,1)S(1)}, bf16[224,2304]{1,0:T(8,128)(2,1)}, u32[]{:S(2)}, u32[]{:S(2)}) collective-permute-start(bf16[224,2304]{1,0:T(8,128)(2,1)S(1)} %pad_maximum_fusion.1.refs_5_), channel_id=1, source_target_pairs={{0,48},{1,49},{2,50},{3,51},{8,56},{9,57},{10,58},{11,59},{16,0},{... | collective-permute-start | bytes 3096584 | tf_op jit(solution)/shard_map/ppermute | solution.py:43
  56.8 23.0 %collective-permute-start.13 = (bf16[224,2304]{1,0:T(8,128)(2,1)S(1)}, bf16[224,2304]{1,0:T(8,128)(2,1)}, u32[]{:S(2)}, u32[]{:S(2)}) collective-permute-start(bf16[224,2304]{1,0:T(8,128)(2,1)S(1)} %collective-permute-done.4.refs_7_), channel_id=1, source_target_pairs={{0,48},{1,49},{2,50},{3,51},{8,56},{9,57},{10,58},{11,59},{16,0},{... | collective-permute-start | bytes 3096584 | tf_op jit(solution)/shard_map/ppermute | solution.py:43
  57.1 22.6 %collective-permute-start.7 = (bf16[224,2304]{1,0:T(8,128)(2,1)S(1)}, bf16[224,2304]{1,0:T(8,128)(2,1)}, u32[]{:S(2)}, u32[]{:S(2)}) collective-permute-start(bf16[224,2304]{1,0:T(8,128)(2,1)S(1)} %collective-permute-done.4.refs_7_), channel_id=1, source_target_pairs={{0,16},{1,17},{2,18},{3,19},{8,24},{9,25},{10,26},{11,27},{16,32},... | collective-permute-start | bytes 3096584 | tf_op jit(solution)/shard_map/ppermute | solution.py:43
  60.3 22.7 %collective-permute-start.9 = (bf16[224,2304]{1,0:T(8,128)(2,1)S(1)}, bf16[224,2304]{1,0:T(8,128)(2,1)}, u32[]{:S(2)}, u32[]{:S(2)}) collective-permute-start(bf16[224,2304]{1,0:T(8,128)(2,1)S(1)} %collective-permute-done.4.refs_7_), channel_id=1, source_target_pairs={{0,8},{1,9},{2,10},{3,11},{8,0},{9,1},{10,2},{11,3},{16,24},{17,25... | collective-permute-start | bytes 3096584 | tf_op jit(solution)/shard_map/ppermute | solution.py:43
  64.7 18.3 %collective-permute-start.10 = (bf16[224,2304]{1,0:T(8,128)(2,1)}, bf16[224,2304]{1,0:T(8,128)(2,1)}, u32[]{:S(2)}, u32[]{:S(2)}) collective-permute-start(bf16[224,2304]{1,0:T(8,128)(2,1)} %collective-permute-done.5.refs_9_), channel_id=1, source_target_pairs={{0,8},{1,9},{2,10},{3,11},{8,0},{9,1},{10,2},{11,3},{16,24},{17,25... | collective-permute-start | bytes 3096584 | tf_op jit(solution)/shard_map/ppermute | solution.py:43
  67.0 16.0 %collective-permute-start.11 = (bf16[224,2304]{1,0:T(8,128)(2,1)}, bf16[224,2304]{1,0:T(8,128)(2,1)}, u32[]{:S(2)}, u32[]{:S(2)}) collective-permute-start(bf16[224,2304]{1,0:T(8,128)(2,1)} %collective-permute-done.6.refs_11_), channel_id=1, source_target_pairs={{0,8},{1,9},{2,10},{3,11},{8,0},{9,1},{10,2},{11,3},{16,24},{17,25... | collective-permute-start | bytes 3096584 | tf_op jit(solution)/shard_map/ppermute | solution.py:43
  79.7 29.6 %collective-permute-start.17 = (bf16[768,512]{1,0:T(8,128)(2,1)S(1)}, bf16[768,512]{1,0:T(8,128)(2,1)S(1)}, u32[]{:S(2)}, u32[]{:S(2)}) collective-permute-start(bf16[768,512]{1,0:T(8,128)(2,1)S(1)} %slice_bitcast_fusion.1), channel_id=1, source_target_pairs={{0,1},{1,2},{2,3},{3,0},{8,9},{9,10},{10,11},{11,8},{16,17},{17,18... | collective-permute-start | bytes 2359304 | tf_op jit(solution)/shard_map/ppermute | solution.py:43
  79.7 30.5 %collective-permute-start.18 = (bf16[768,512]{1,0:T(8,128)(2,1)S(1)}, bf16[768,512]{1,0:T(8,128)(2,1)S(1)}, u32[]{:S(2)}, u32[]{:S(2)}) collective-permute-start(bf16[768,512]{1,0:T(8,128)(2,1)S(1)} %slice_bitcast_fusion), channel_id=1, source_target_pairs={{0,3},{1,0},{2,1},{3,2},{8,11},{9,8},{10,9},{11,10},{16,19},{17,16... | collective-permute-start | bytes 2359304 | tf_op jit(solution)/shard_map/ppermute | solution.py:43
  83.0 43.4 %collective-permute-start.20 = (bf16[224,2304]{1,0:T(8,128)(2,1)}, bf16[224,2304]{1,0:T(8,128)(2,1)}, u32[]{:S(2)}, u32[]{:S(2)}) collective-permute-start(bf16[224,2304]{1,0:T(8,128)(2,1)} %collective-permute-done.13.refs_15_), channel_id=1, source_target_pairs={{0,8},{1,9},{2,10},{3,11},{8,0},{9,1},{10,2},{11,3},{16,24},{17,25... | collective-permute-start | bytes 3096584 | tf_op jit(solution)/shard_map/ppermute | solution.py:43
  83.4 42.9 %collective-permute-start.19 = (bf16[224,2304]{1,0:T(8,128)(2,1)}, bf16[224,2304]{1,0:T(8,128)(2,1)}, u32[]{:S(2)}, u32[]{:S(2)}) collective-permute-start(bf16[224,2304]{1,0:T(8,128)(2,1)} %collective-permute-done.7.refs_13_), channel_id=1, source_target_pairs={{0,8},{1,9},{2,10},{3,11},{8,0},{9,1},{10,2},{11,3},{16,24},{17,25... | collective-permute-start | bytes 3096584 | tf_op jit(solution)/shard_map/ppermute | solution.py:43
  86.7 36.1 %collective-permute-start.14 = (bf16[448,576]{1,0:T(8,128)(2,1)}, bf16[448,576]{1,0:T(8,128)(2,1)}, u32[]{:S(2)}, u32[]{:S(2)}) collective-permute-start(bf16[448,576]{1,0:T(8,128)(2,1)} %fusion.3), channel_id=1, source_target_pairs={{0,0},{1,16},{2,32},{3,48},{8,8},{9,24},{10,40},{11,56},{16,49},{1... | collective-permute-start | bytes 1548296 | tf_op jit(solution)/shard_map/ppermute | solution.py:43
  111.2 38.9 %collective-permute-start.22 = (bf16[224,2304]{1,0:T(8,128)(2,1)}, bf16[224,2304]{1,0:T(8,128)(2,1)S(1)}, u32[]{:S(2)}, u32[]{:S(2)}) collective-permute-start(bf16[224,2304]{1,0:T(8,128)(2,1)} %collective-permute-done.13.refs_15_), channel_id=1, source_target_pairs={{0,48},{1,49},{2,50},{3,51},{8,56},{9,57},{10,58},{11,59},{16,0},{... | collective-permute-start | bytes 3096584 | tf_op jit(solution)/shard_map/ppermute | solution.py:43
  116.9 33.2 %collective-permute-start.21 = (bf16[224,2304]{1,0:T(8,128)(2,1)}, bf16[224,2304]{1,0:T(8,128)(2,1)S(1)}, u32[]{:S(2)}, u32[]{:S(2)}) collective-permute-start(bf16[224,2304]{1,0:T(8,128)(2,1)} %collective-permute-done.5.refs_9_), channel_id=1, source_target_pairs={{0,16},{1,17},{2,18},{3,19},{8,24},{9,25},{10,26},{11,27},{16,32},... | collective-permute-start | bytes 3096584 | tf_op jit(solution)/shard_map/ppermute | solution.py:43
  122.8 28.0 %collective-permute-start.26 = (bf16[448,576]{1,0:T(8,128)(2,1)}, bf16[448,576]{1,0:T(8,128)(2,1)}, u32[]{:S(2)}, u32[]{:S(2)}) collective-permute-start(bf16[448,576]{1,0:T(8,128)(2,1)} %collective-permute-done.14.refs_0_), channel_id=1, source_target_pairs={{0,64},{1,65},{2,66},{3,67},{8,72},{9,73},{10,74},{11,75},{16,80},... | collective-permute-start | bytes 1548296 | tf_op jit(solution)/shard_map/ppermute | solution.py:43
  151.2 23.6 %collective-permute-start.24 = (bf16[448,576]{1,0:T(8,128)(2,1)}, bf16[448,576]{1,0:T(8,128)(2,1)}, u32[]{:S(2)}, u32[]{:S(2)}) collective-permute-start(bf16[448,576]{1,0:T(8,128)(2,1)} %collective-permute-done.14.refs_0_), channel_id=1, source_target_pairs={{0,16},{1,17},{2,18},{3,19},{8,24},{9,25},{10,26},{11,27},{16,32},... | collective-permute-start | bytes 1548296 | tf_op jit(solution)/shard_map/ppermute | solution.py:43
  156.8 17.9 %collective-permute-start.25 = (bf16[448,576]{1,0:T(8,128)(2,1)}, bf16[448,576]{1,0:T(8,128)(2,1)}, u32[]{:S(2)}, u32[]{:S(2)}) collective-permute-start(bf16[448,576]{1,0:T(8,128)(2,1)} %collective-permute-done.14.refs_0_), channel_id=1, source_target_pairs={{0,48},{1,49},{2,50},{3,51},{8,56},{9,57},{10,58},{11,59},{16,0},{... | collective-permute-start | bytes 1548296 | tf_op jit(solution)/shard_map/ppermute | solution.py:43
  179.7 25.1 %collective-permute-start.31 = (bf16[448,768]{1,0:T(8,128)(2,1)S(1)}, bf16[448,768]{1,0:T(8,128)(2,1)S(1)}, u32[]{:S(2)}, u32[]{:S(2)}) collective-permute-start(bf16[448,768]{1,0:T(8,128)(2,1)S(1)} %get-tuple-element.58), channel_id=1, source_target_pairs={{0,0},{1,1},{2,2},{3,3},{8,8},{9,9},{10,10},{11,11},{16,17},{17,18... | collective-permute-start | bytes 2064392 | tf_op jit(solution)/shard_map/ppermute | solution.py:43
  185.8 21.4 %collective-permute-start.32 = (bf16[448,768]{1,0:T(8,128)(2,1)S(1)}, bf16[448,768]{1,0:T(8,128)(2,1)S(1)}, u32[]{:S(2)}, u32[]{:S(2)}) collective-permute-start(bf16[448,768]{1,0:T(8,128)(2,1)S(1)} %get-tuple-element.59), channel_id=1, source_target_pairs={{0,6},{1,7},{2,4},{3,5},{8,14},{9,15},{10,12},{11,13},{16,23},{17,... | collective-permute-start | bytes 2064392 | tf_op jit(solution)/shard_map/ppermute | solution.py:43
  188.1 15.5 %collective-permute-start.37 = (bf16[448,576]{1,0:T(8,128)(2,1)}, bf16[448,576]{1,0:T(8,128)(2,1)S(1)}, u32[]{:S(2)}, u32[]{:S(2)}) collective-permute-start(bf16[448,576]{1,0:T(8,128)(2,1)} %collective-permute-done.26.refs_2_), channel_id=1, source_target_pairs={{0,16},{1,17},{2,18},{3,19},{8,24},{9,25},{10,26},{11,27},{16,32},... | collective-permute-start | bytes 1548296 | tf_op jit(solution)/shard_map/ppermute | solution.py:43
  188.1 16.7 %collective-permute-start.39 = (bf16[448,576]{1,0:T(8,128)(2,1)}, bf16[448,576]{1,0:T(8,128)(2,1)S(1)}, u32[]{:S(2)}, u32[]{:S(2)}) collective-permute-start(bf16[448,576]{1,0:T(8,128)(2,1)} %collective-permute-done.26.refs_2_), channel_id=1, source_target_pairs={{0,48},{1,49},{2,50},{3,51},{8,56},{9,57},{10,58},{11,59},{16,0},{... | collective-permute-start | bytes 1548296 | tf_op jit(solution)/shard_map/ppermute | solution.py:43
  215.5 23.9 %collective-permute-start.35 = (bf16[448,768]{1,0:T(8,128)(2,1)S(1)}, bf16[448,768]{1,0:T(8,128)(2,1)S(1)}, u32[]{:S(2)}, u32[]{:S(2)}) collective-permute-start(bf16[448,768]{1,0:T(8,128)(2,1)S(1)} %get-tuple-element.62), channel_id=1, source_target_pairs={{0,3},{1,0},{2,1},{3,2},{8,11},{9,8},{10,9},{11,10},{16,16},{17,17... | collective-permute-start | bytes 2064392 | tf_op jit(solution)/shard_map/ppermute | solution.py:43
  222.6 25.3 %collective-permute-start.36 = (bf16[448,768]{1,0:T(8,128)(2,1)S(1)}, bf16[448,768]{1,0:T(8,128)(2,1)S(1)}, u32[]{:S(2)}, u32[]{:S(2)}) collective-permute-start(bf16[448,768]{1,0:T(8,128)(2,1)S(1)} %get-tuple-element.63), channel_id=1, source_target_pairs={{0,1},{1,2},{2,3},{3,0},{8,9},{9,10},{10,11},{11,8},{16,18},{17,19... | collective-permute-start | bytes 2064392 | tf_op jit(solution)/shard_map/ppermute | solution.py:43
  223.3 18.0 %collective-permute-start.50 = (f32[120,128]{1,0:T(8,128)S(1)}, f32[120,128]{1,0:T(8,128)S(1)}, u32[]{:S(2)}, u32[]{:S(2)}) collective-permute-start(f32[120,128]{1,0:T(8,128)S(1)} %max.42), channel_id=1, source_target_pairs={{0,32},{1,33},{2,34},{3,35},{8,40},{9,41},{10,42},{11,43},{16,48},... | collective-permute-start | bytes 184328 | tf_op jit(solution)/shard_map/ppermute | solution.py:43
  228.1 20.2 %collective-permute-start.41 = (bf16[448,768]{1,0:T(8,128)(2,1)S(1)}, bf16[448,768]{1,0:T(8,128)(2,1)S(1)}, u32[]{:S(2)}, u32[]{:S(2)}) collective-permute-start(bf16[448,768]{1,0:T(8,128)(2,1)S(1)} %get-tuple-element.66), channel_id=1, source_target_pairs={{0,5},{1,6},{2,7},{3,4},{8,13},{9,14},{10,15},{11,12},{16,22},{17,... | collective-permute-start | bytes 2064392 | tf_op jit(solution)/shard_map/ppermute | solution.py:43
  231.3 34.7 %collective-permute-start.42 = (bf16[448,768]{1,0:T(8,128)(2,1)S(1)}, bf16[448,768]{1,0:T(8,128)(2,1)S(1)}, u32[]{:S(2)}, u32[]{:S(2)}) collective-permute-start(bf16[448,768]{1,0:T(8,128)(2,1)S(1)} %get-tuple-element.67), channel_id=1, source_target_pairs={{0,7},{1,4},{2,5},{3,6},{8,15},{9,12},{10,13},{11,14},{16,20},{17,... | collective-permute-start | bytes 2064392 | tf_op jit(solution)/shard_map/ppermute | solution.py:43
  239.4 34.6 %collective-permute-start.47 = (bf16[448,768]{1,0:T(8,128)(2,1)S(1)}, bf16[448,768]{1,0:T(8,128)(2,1)S(1)}, u32[]{:S(2)}, u32[]{:S(2)}) collective-permute-start(bf16[448,768]{1,0:T(8,128)(2,1)S(1)} %get-tuple-element.69), channel_id=1, source_target_pairs={{0,2},{1,3},{2,0},{3,1},{8,10},{9,11},{10,8},{11,9},{16,19},{17,16... | collective-permute-start | bytes 2064392 | tf_op jit(solution)/shard_map/ppermute | solution.py:43
  241.3 37.6 %collective-permute-start.48 = (bf16[448,768]{1,0:T(8,128)(2,1)S(1)}, bf16[448,768]{1,0:T(8,128)(2,1)S(1)}, u32[]{:S(2)}, u32[]{:S(2)}) collective-permute-start(bf16[448,768]{1,0:T(8,128)(2,1)S(1)} %get-tuple-element.70), channel_id=1, source_target_pairs={{0,4},{1,5},{2,6},{3,7},{8,12},{9,13},{10,14},{11,15},{16,21},{17,... | collective-permute-start | bytes 2064392 | tf_op jit(solution)/shard_map/ppermute | solution.py:43
  (44 other events, 330.8 us)

commit v3 on v2

--- a/solution.py
+++ b/solution.py
@@ -15,9 +15,10 @@
 EPS = 1e-06
 SMALLEST_NORMAL = 2.0 ** (-6)
 AXES = ("fsdp", "tp")
-VMEM_LIMIT = 48 * 1024 * 1024
+VMEM_LIMIT = 60 * 1024 * 1024
 TILE = 256
 HALF = 256
+FREE = pl.CostEstimate(flops=0, bytes_accessed=0, transcendentals=0)
 
 
 def snapped(value):
@@ -135,9 +136,9 @@
     return lax.optimization_barrier((array, *others))[0]
 
 
-def ring(own, far, up, down, between):
+def ring(own, far, up, down, others, between):
     own_l, own_r = send(own, up), send(own, down)
-    far = after(far, own_l, own_r)
+    far = after(far, own_l, own_r, *others)
     far_l, far_r = send(far, up), send(far, down)
     others = between([own, far, own_l, own_r])
     own_l, far_r = after(own_l, far_l, *others), after(far_r, far_l, *others)
@@ -145,20 +146,13 @@
     return [own, far, own_l, own_r, far_l, far_r, own_ll, far_rr]
 
 
-TOKEN_ORDER = ((0, 0), (1, 0), (0, -1), (1, -1), (0, 1), (1, 1), (0, 2), (1, 2))
-
-
-def token_ring(pair):
-    left, right = send(pair, z_up), send(pair, z_down)
-    return [pair, left, right, send(left[0], z_up)[None], send(right[1], z_down)[None]]
-
-
-def token_kernel(count, has_before, last, info, *refs):
-    tokens, refs = refs[:5], list(refs[5:])
+def token_kernel(count, first, has_before, last, info, *refs):
+    pieces, refs = refs[:8], list(refs[8:])
     before = refs.pop(0) if has_before else None
     blocks, (out, wide, scratch, wide_sems, sems) = refs[:count], refs[count:]
+    blocks = [blocks[n // 4 * 2 + n % 2].at[n // 2 % 2] for n in range(2 * count)]
+    count = len(blocks)
     height = blocks[0].shape[0]
-    pieces = [ref.at[k] for ref in tokens for k in range(ref.shape[0])]
 
     def block_copy(n):
         rows = pl.ds(n * HALF, height)
@@ -189,7 +183,7 @@
         for n in range(count // 2):
             for piece in range(len(pieces)):
 
-                @pl.when(info[n] == piece)
+                @pl.when(info[first + n] == piece)
                 def _():
                     token_copy(n, piece).start()
 
@@ -209,24 +203,22 @@
 
 
 def token_sum(info, tokens, first, blocks, before=None, last=False):
-    rows, columns = tokens[0].shape[1], blocks[0].shape[1]
-    count = len(blocks)
+    rows, columns = tokens[0].shape[0], blocks[0].shape[2]
+    count = 2 * len(blocks)
     width = columns // 2 if last else columns
 
     def tile(width):
         return pl.BlockSpec((TILE, width), lambda m, info: (m, 0))
 
-    if first:
-        info = jnp.concatenate([info[first:8], info[:first], info[8:]])
     return pl.pallas_call(
-        functools.partial(token_kernel, count, before is not None, last),
+        functools.partial(token_kernel, len(blocks), first, before is not None, last),
         out_shape=jax.ShapeDtypeStruct((rows, width), jnp.bfloat16 if last else jnp.float32),
         grid_spec=pltpu.PrefetchScalarGridSpec(
             num_scalar_prefetch=1,
             grid=(rows // TILE,),
-            in_specs=[pl.BlockSpec(memory_space=pl.ANY)] * 5
+            in_specs=[pl.BlockSpec(memory_space=pl.ANY)] * 8
             + ([] if before is None else [tile(columns)])
-            + [pl.BlockSpec(memory_space=pl.ANY)] * count,
+            + [pl.BlockSpec(memory_space=pl.ANY)] * len(blocks),
             out_specs=tile(width),
             scratch_shapes=[
                 pltpu.VMEM((count // 2, rows, 2 * HALF), jnp.bfloat16),
@@ -236,11 +228,7 @@
             ],
         ),
         compiler_params=pltpu.CompilerParams(vmem_limit_bytes=VMEM_LIMIT),
-        cost_estimate=pl.CostEstimate(
-            flops=2 * rows * columns * count * HALF,
-            bytes_accessed=rows * columns * 8,
-            transcendentals=0,
-        ),
+        cost_estimate=FREE,
     )(info, *tokens, *([] if before is None else [before]), *blocks)
 
 
@@ -248,12 +236,13 @@
     return [pl.BlockSpec(memory_space=pltpu.VMEM)] * n
 
 
-def down_kernel(info, hidden, *refs):
-    blocks, outs = refs[: 2 * len(refs) // 3], refs[2 * len(refs) // 3 :]
+DOWN_ORDER = ((0, 0), (1, 0), (0, -1), (1, -1), (0, 1), (1, 1), (0, 2), (1, 2))
+
+
+def down_kernel(info, hidden, mine, theirs, *outs):
     for n, out in enumerate(outs):
-        mine, theirs = blocks[2 * n][...], blocks[2 * n + 1][...]
-        low = jnp.where(info[8] == 0, mine, theirs)
-        high = jnp.where(info[8] == 0, theirs, mine)
+        low = jnp.where(info[8] == 0, mine[n], theirs[n])
+        high = jnp.where(info[8] == 0, theirs[n], mine[n])
         out[...] = lax.dot_general(
             jnp.concatenate([low, high], axis=1),
             hidden[...],
@@ -262,22 +251,17 @@
         ).astype(out.dtype)
 
 
-def down_terms(info, hidden, blocks):
+def down_terms(info, hidden, mine, theirs):
     rows, depth = hidden.shape
-    columns = blocks[0].shape[0]
-    count = len(blocks) // 2
+    count, columns, _ = mine.shape
     return pl.pallas_call(
         down_kernel,
         out_shape=[jax.ShapeDtypeStruct((columns, rows), jnp.bfloat16)] * count,
-        in_specs=[pl.BlockSpec(memory_space=pltpu.SMEM)] + vmem(1 + len(blocks)),
+        in_specs=[pl.BlockSpec(memory_space=pltpu.SMEM)] + vmem(3),
         out_specs=vmem(count),
         compiler_params=pltpu.CompilerParams(vmem_limit_bytes=VMEM_LIMIT),
-        cost_estimate=pl.CostEstimate(
-            flops=2 * count * rows * columns * depth,
-            bytes_accessed=rows * columns * 4,
-            transcendentals=0,
-        ),
-    )(info, hidden, *blocks)
+        cost_estimate=FREE,
+    )(info, hidden, mine, theirs)
 
 
 def on_device(tokens, gate_master, up_master, down_master):
@@ -286,7 +270,6 @@
     core = fsdp_place % 2
     y_hi, x = fsdp_place // 8, (fsdp_place // 2) % 4
     y_lo, z = tp_place // 4, tp_place % 4
-    chips = [(y_hi ^ dy, (x + dx + 4) % 4) for dy, dx in ORDER]
     gate_height, gate_breadth = gate_master.shape
     down_height, down_breadth = down_master.shape
     gate_at = (fsdp_place * gate_height, tp_place * gate_breadth)
@@ -298,6 +281,7 @@
         axis=1,
     )
     near = send(padded, y_near)
+    tokens_l, tokens_r = send(padded, z_up), send(padded, z_down)
     gate_master, up_master, down_master, padded = lax.optimization_barrier(
         (gate_master, up_master, down_master, padded)
     )
@@ -325,64 +309,72 @@
         axis=1,
     )
     every = step(table, lambda y, x, core, z: (y, x, core, z ^ 1))
-    pair = jnp.stack([padded, near])
-    gate_up, pair, every = lax.optimization_barrier((gate_up, pair, every))
+    gate_up, near, tokens_l, tokens_r, every = lax.optimization_barrier(
+        (gate_up, near, tokens_l, tokens_r, every)
+    )
     down_table = every
-    relative = token_ring(pair)
+    near_l, near_r = send(near, z_up), send(near, z_down)
+    tokens_l, near_r = after(tokens_l, near_l), after(near_r, near_l)
+    tokens_ll, near_rr = send(tokens_l, z_up), send(near_r, z_down)
+    pieces = [padded, near, tokens_l, tokens_r, near_l, near_r, tokens_ll, near_rr]
+    down_weight = rollout(down_master, down_table[2 * rows : 3 * rows].T, *down_at)
     pairs = []
 
     def swap(blocks):
-        nonlocal every
-        if len(blocks) == 4:
-            every = step(after(every, *blocks), y_near)
-        others = [send(block, other_core) for block in blocks]
-        for block, other in zip(blocks, others):
-            pairs.extend((block, other))
-        return others + [every]
-
-    blocks = ring(gate_up, send(gate_up, y_far), x_up, x_down, swap)
+        for n in range(0, len(blocks), 2):
+            pair = jnp.stack(blocks[n : n + 2])
+            pairs.extend((pair, send(pair, other_core)))
+
+    down_block = send(after(down_weight.T, near_l, near_r), to_ff_group)
+    down_far = send(down_block, y_far)
+
+    def between(blocks):
+        swap(blocks)
+        return [pairs[1], pairs[3], down_far]
+
+    blocks = ring(
+        gate_up, send(gate_up, y_far), x_up, x_down, (tokens_ll, near_rr, down_block), between
+    )
+    every = step(after(every, *blocks[:4]), y_near)
     swap(blocks[4:6])
 
-    order = [TOKEN_ORDER.index((dy, dx)) for dy in range(2) for dx in (0, 1, 2, -1)]
-    by_offset = jnp.array(order, jnp.int32)
-    info = jnp.stack(
-        [by_offset[(chip_y ^ y_lo) * 4 + (chip_x - z + 4) % 4] for chip_y, chip_x in chips] + [core]
-    )
-
-    ready = after(every, relative[3], relative[4], blocks[4], blocks[5])
-    early = token_sum(info, relative, 0, pairs)
-    every = step(ready, lambda y, x, core, z: (y, x, core, z ^ 2))
-
-    def both(blocks):
-        return [b for block in blocks for b in (block, send(block, other_core))]
-
-    down_table = after(down_table, *blocks[:4])
-    down_weight = rollout(down_master, down_table[2 * rows : 3 * rows].T, *down_at)
-    down_block = send(after(down_weight.T, blocks[4], blocks[5]), to_ff_group)
-    down_far = send(down_block, y_far)
-    down_pairs = [both([down_block, down_far])]
-    down_block, early, own_ll, far_rr, every = lax.optimization_barrier(
-        (down_block, early, blocks[6], blocks[7], every)
-    )
-    pairs = both([own_ll, far_rr])
-    every = step(after(every, *down_pairs[0]), y_far)
-    early = after(early, *down_pairs[0])
-    hidden = token_sum(info, relative, 6, pairs, early, last=True)
-    def sums(n, pair):
-        terms = down_terms(info, hidden, pair)
-        return terms, [send(term, to_chunk(*ORDER[n + k])) for k, term in enumerate(terms)]
-
-    own_l, own_r = send(down_block, x_up), send(down_block, x_down)
-    own_l, own_r, down_far, hidden = lax.optimization_barrier((own_l, own_r, down_far, hidden))
-    _, parts = sums(0, down_pairs[0])
-    far_l, far_r = send(down_far, x_up), send(down_far, x_down)
-    terms, more = sums(2, both([own_l, own_r]))
-    own_l, far_r, *_ = lax.optimization_barrier((own_l, far_r, far_l, *terms, *parts))
-    own_ll, far_rr = send(own_l, x_up), send(far_r, x_down)
+    steps = jnp.array([dy + 4 * (dx % 4) for dy, dx in ORDER] + [0] * 8, jnp.int32)
+    chip_y, chip_x = (steps % 4) ^ (y_hi ^ y_lo), (steps // 4 + x - z + 4) % 4
+    info = jnp.where(
+        chip_x == 0,
+        chip_y,
+        jnp.where(chip_x == 2, 6 + chip_y, 2 + 2 * chip_y + jnp.where(chip_x == 1, 1, 0)),
+    )
+    info = jnp.where(jnp.arange(16) == 8, core, info)
+
+    down_pair = jnp.stack([down_block, down_far])
+    down_theirs = send(after(down_pair, blocks[4], blocks[5]), other_core)
+
+    early = token_sum(info, pieces, 0, [after(pairs[0], down_theirs)] + pairs[1:])
+    early, own_ll, far_rr = lax.optimization_barrier((early, blocks[6], blocks[7]))
+    every = step(after(every, early), lambda y, x, core, z: (y, x, core, z ^ 2))
+    down_pair = after(down_pair, own_ll)
+    left, right = send(down_pair, x_up), send(down_pair, x_down)
+    last = jnp.stack([own_ll, far_rr])
+    last = [last, send(last, other_core)]
+    hidden = token_sum(info, pieces, 6, last, early, last=True)
+
+    def sums(n, mine, theirs, *before):
+        terms = down_terms(info, hidden, mine, theirs)
+        return [
+            send(after(term, *before), to_chunk(*DOWN_ORDER[n + k])) for k, term in enumerate(terms)
+        ], terms
+
+    parts, terms = sums(0, down_pair, down_theirs)
+    left, right = after(left, *terms), after(right, *terms)
+    rest = jnp.stack([send(left[0], x_up), send(right[1], x_down)])
+    parts += sums(2, left, send(left, other_core))[0]
+    rest = after(rest, *parts[:2])
+    parts += sums(4, right, send(right, other_core), *parts[:2])[0]
+    more, terms = sums(6, rest, send(rest, other_core), *parts[2:4])
     parts += more
-    parts += sums(4, both([far_l, far_r]))[1]
-    parts += sums(6, both([own_ll, far_rr]))[1]
-    every = step(after(every, own_ll, far_rr), lambda y, x, core, z: (y, x ^ 2, core, z))
+    every = step(after(every, *terms), y_far)
+    every = step(every, lambda y, x, core, z: (y, x ^ 2, core, z))
     log_amax = jnp.log(
         jnp.stack([every[k * rows : k * rows + D // BLOCK, : FF // BLOCK] for k in range(3)]) + EPS
     )

time: 283 us -> 286 us (1.011)
  local copies, waits for them, and re-layouts: 29.8 us -> 12.4 us
  Pallas kernels: 40.9 us -> 50.7 us
  other arithmetic: 12.7 us -> 20.2 us
  starting transfers between devices: 63.9 us -> 70.1 us
    pallas_call x4, Pallas kernels: 11.6 us -> 20.3 us  [down_terms(): pl.pallas_call(down_kernel, out_shape=[jax.ShapeDtypeStruct((columns, row...]
    unnamed x48 -> x46, local copies, waits for them, and re-layouts: 14 us -> 6.89 us
    ppermute x51 -> x43, starting transfers between devices: 63.9 us -> 70.1 us  [send(): return lax.ppermute(array, AXES, pairs)]
    another operation x3 -> x2, local copies, waits for them, and re-layouts: 5.23 us -> 0.01 us  [the longest x1 5.22 us: on_device(): jnp.stack([by_offset[(chip_y ^ y_lo) * 4 + (chip_x - z + 4) % 4] for chip...]
    concatenate x1 -> x0, local copies, waits for them, and re-layouts: 5.22 us -> none  [token_sum(): info = jnp.concatenate([info[first:8], info[:first], info[8:]])]
    another operation x1 -> x6, other arithmetic: 1.52 us -> 5.07 us  [the longest x3 3.01 us: swap(): pair = jnp.stack(blocks[n:n + 2])]
    ppermute x51 -> x43, waiting for transfers between devices: 132 us -> 130 us  [send(): return lax.ppermute(array, AXES, pairs)]
  transfers between devices with their start and end apart: 51 -> 43, of which waited for: 23 -> 21; matrix products, arithmetic and copies ran while one was open for 8% -> 6% of each run, Pallas kernels for 15% -> 18%
where the time goes in v3:
time: 286 us; the launch traced here: 285 us
  waiting for transfers between devices  130 us (45%)
  starting transfers between devices  70.1 us (25%)
  Pallas kernels  50.7 us (18%)
  other arithmetic  20.2 us (7%)
  local copies, waits for them, and re-layouts  12.4 us (4%)
    ppermute x43, waiting for transfers between devices, send(): return lax.ppermute(array, AXES, pairs)  130 us
    ppermute x43, starting transfers between devices, send(): return lax.ppermute(array, AXES, pairs)  70.1 us
    pallas_call x2, Pallas kernels, token_sum(): pl.pallas_call(functools.partial(token_kernel, len(blocks), first, before...  30.4 us
    pallas_call x4, Pallas kernels, down_terms(): pl.pallas_call(down_kernel, out_shape=[jax.ShapeDtypeStruct((columns, row...  20.3 us
    unnamed x46, local copies, waits for them, and re-layouts  6.89 us
  transfers between devices with their start and end apart: 43, of which 21 were waited for; matrix products, arithmetic and copies ran while one was open for 6% of the time, Pallas kernels for 18%

profile of v3, /device:TPU:6, one launch (start us, length us, event | category | flops | bytes accessed | tf_op | source)
XLA Modules:
  0.0 285.3 jit_solution(13417172815654904428)
XLA Ops:
  2.1 4.1 %collective-permute-start.4 = (bf16[768,512]{1,0:T(8,128)(2,1)S(1)}, bf16[768,512]{1,0:T(8,128)(2,1)}, u32[]{:S(2)}, u32[]{:S(2)}) collective-permute-start(bf16[768,512]{1,0:T(8,128)(2,1)S(1)} %fusion.1.refs_0_), channel_id=1, source_target_pairs={{0,3},{1,0},{2,1},{3,2},{8,11},{9,8},{10,9},{11,10},{16,19},{17,16... | collective-permute-start | bytes 2359304 | tf_op jit(solution)/shard_map/ppermute | solution.py:44
  15.3 3.4 %collective-permute-done.1 = f32[120,128]{1,0:T(8,128)S(1)} collective-permute-done((f32[120,128]{1,0:T(8,128)S(1)}, f32[120,128]{1,0:T(8,128)S(1)}, u32[]{:S(2)}, u32[]{:S(2)}) %collective-permute-start.1) | collective-permute-done | bytes 61472 | tf_op jit(solution)/shard_map/ppermute | solution.py:44
  20.1 3.5 %multiply_convert_fusion.2 = (bf16[224,1152]{1,0:T(8,128)(2,1)S(1)}, bf16[224,1152]{1,0:T(8,128)(2,1)S(1)}) fusion(f32[224,1152]{1,0:T(8,128)S(1)} %copy-done.8, f32[1152]{0:T(1024)S(1)} %get-tuple-element.93, f32[1152]{0:T(1024)S(1)} %get-tuple-element.94, f32[1152]{0:T(1024)S(1)} %get-tuple-element.92, pred[224]{0:T(512)(128)(4,1)S(1)} %broadcast_compare_fusion.23, ...), kind=kLoop, calls=%fused_computation.18 | loop fusion | flops 9289728 | bytes 3124896 | tf_op jit(solution)/shard_map/convert_element_type | solution.py:129
  31.8 3.2 %collective-permute-start.10 = (bf16[224,2304]{1,0:T(8,128)(2,1)S(1)}, bf16[224,2304]{1,0:T(8,128)(2,1)S(1)}, u32[]{:S(2)}, u32[]{:S(2)}) collective-permute-start(bf16[224,2304]{1,0:T(8,128)(2,1)S(1)} %pad_maximum_fusion.6), channel_id=1, source_target_pairs={{0,64},{1,65},{2,66},{3,67},{8,72},{9,73},{10,74},{11,75},{16,80},... | collective-permute-start | bytes 3096584 | tf_op jit(solution)/shard_map/ppermute | solution.py:44
  35.2 9.7 %collective-permute-done.7.refs_5_ = bf16[768,512]{1,0:T(8,128)(2,1)S(1)} collective-permute-done((bf16[768,512]{1,0:T(8,128)(2,1)}, bf16[768,512]{1,0:T(8,128)(2,1)S(1)}, u32[]{:S(2)}, u32[]{:S(2)}) %collective-permute-start.7) | collective-permute-done | bytes 786464 | tf_op jit(solution)/shard_map/ppermute | solution.py:44
  48.2 3.2 %collective-permute-start.9 = (bf16[768,512]{1,0:T(8,128)(2,1)S(1)}, bf16[768,512]{1,0:T(8,128)(2,1)S(1)}, u32[]{:S(2)}, u32[]{:S(2)}) collective-permute-start(bf16[768,512]{1,0:T(8,128)(2,1)S(1)} %collective-permute-done.7.refs_5_), channel_id=1, source_target_pairs={{0,3},{1,0},{2,1},{3,2},{8,11},{9,8},{10,9},{11,10},{16,19},{17,16... | collective-permute-start | bytes 2359304 | tf_op jit(solution)/shard_map/ppermute | solution.py:44
  53.5 3.3 %collective-permute-start.13 = (bf16[448,576]{1,0:T(8,128)(2,1)S(1)}, bf16[448,576]{1,0:T(8,128)(2,1)S(1)}, u32[]{:S(2)}, u32[]{:S(2)}) collective-permute-start(bf16[448,576]{1,0:T(8,128)(2,1)S(1)} %fusion.3), channel_id=1, source_target_pairs={{0,0},{1,16},{2,32},{3,48},{8,8},{9,24},{10,40},{11,56},{16,49},{1... | collective-permute-start | bytes 1548296 | tf_op jit(solution)/shard_map/ppermute | solution.py:44
  58.5 11.8 %collective-permute-done.13 = bf16[448,576]{1,0:T(8,128)(2,1)S(1)} collective-permute-done((bf16[448,576]{1,0:T(8,128)(2,1)S(1)}, bf16[448,576]{1,0:T(8,128)(2,1)S(1)}, u32[]{:S(2)}, u32[]{:S(2)}) %collective-permute-start.13) | collective-permute-done | bytes 516128 | tf_op jit(solution)/shard_map/ppermute | solution.py:44
  70.3 8.1 %collective-permute-done.8.refs_6_ = bf16[768,512]{1,0:T(8,128)(2,1)S(1)} collective-permute-done((bf16[768,512]{1,0:T(8,128)(2,1)}, bf16[768,512]{1,0:T(8,128)(2,1)S(1)}, u32[]{:S(2)}, u32[]{:S(2)}) %collective-permute-start.8) | collective-permute-done | bytes 786464 | tf_op jit(solution)/shard_map/ppermute | solution.py:44
  85.2 14.3 %collective-permute-done.14 = bf16[448,576]{1,0:T(8,128)(2,1)S(1)} collective-permute-done((bf16[448,576]{1,0:T(8,128)(2,1)S(1)}, bf16[448,576]{1,0:T(8,128)(2,1)S(1)}, u32[]{:S(2)}, u32[]{:S(2)}) %collective-permute-start.14) | collective-permute-done | bytes 516128 | tf_op jit(solution)/shard_map/ppermute | solution.py:44
  99.5 7.0 %collective-permute-done.16 = bf16[224,2304]{1,0:T(8,128)(2,1)} collective-permute-done((bf16[224,2304]{1,0:T(8,128)(2,1)S(1)}, bf16[224,2304]{1,0:T(8,128)(2,1)}, u32[]{:S(2)}, u32[]{:S(2)}) %collective-permute-start.16) | collective-permute-done | bytes 1032224 | tf_op jit(solution)/shard_map/ppermute | solution.py:44
  110.6 3.2 %collective-permute-start.21 = (bf16[224,2304]{1,0:T(8,128)(2,1)}, bf16[224,2304]{1,0:T(8,128)(2,1)}, u32[]{:S(2)}, u32[]{:S(2)}) collective-permute-start(bf16[224,2304]{1,0:T(8,128)(2,1)} %collective-permute-done.11), channel_id=1, source_target_pairs={{0,16},{1,17},{2,18},{3,19},{8,24},{9,25},{10,26},{11,27},{16,32},... | collective-permute-start | bytes 3096584 | tf_op jit(solution)/shard_map/ppermute | solution.py:44
  115.3 19.6 %shard_map.68.refs_8_ = f32[768,2304]{1,0:T(8,128)} custom-call(s32[16]{0:T(128)} %compare_select_fusion.5.info, bf16[768,512]{1,0:T(8,128)(2,1)} %copy-done.4, bf16[768,512]{1,0:T(8,128)(2,1)} %collective-permute-done.2.refs_1_, bf16[768,512]{1,0:T(8,128)(2,1)} %collective-permute-done.3.refs_2_, bf16[768,512]{1,0:T(8,128)(2,1)} %collective-permute-done.4.refs_3_, ...), custom_call_target="tpu_custom_call" | custom-call | tf_op jit(solution)/shard_map/pallas_call | solution.py:213
  143.4 10.7 %shard_map.69.hidden = bf16[768,1152]{1,0:T(8,128)(2,1)} custom-call(s32[16]{0:T(128)} %compare_select_fusion.5.info, bf16[768,512]{1,0:T(8,128)(2,1)} %copy-done.4, bf16[768,512]{1,0:T(8,128)(2,1)} %collective-permute-done.2.refs_1_, bf16[768,512]{1,0:T(8,128)(2,1)} %collective-permute-done.3.refs_2_, bf16[768,512]{1,0:T(8,128)(2,1)} %collective-permute-done.4.refs_3_, ...), custom_call_target="tpu_custom_call" | custom-call | tf_op jit(solution)/shard_map/pallas_call | solution.py:213
  154.1 5.0 %shard_map.70 = (bf16[448,768]{1,0:T(8,128)(2,1)}, bf16[448,768]{1,0:T(8,128)(2,1)}) custom-call(s32[16]{0:T(128)} %compare_select_fusion.5.info, bf16[768,1152]{1,0:T(8,128)(2,1)} %shard_map.69.hidden, bf16[2,448,576]{2,1,0:T(8,128)(2,1)} %copy-done.6, bf16[2,448,576]{2,1,0:T(8,128)(2,1)} %collective-permute-done.19.theirs), custom_call_target="tpu_custom_call" | custom-call | tf_op jit(solution)/shard_map/pallas_call | solution.py:257
  159.1 9.1 %collective-permute-done.30.mine = bf16[2,448,576]{2,1,0:T(8,128)(2,1)} collective-permute-done((bf16[2,448,576]{2,1,0:T(8,128)(2,1)S(1)}, bf16[2,448,576]{2,1,0:T(8,128)(2,1)}, u32[]{:S(2)}, u32[]{:S(2)}) %collective-permute-start.30) | collective-permute-done | bytes 1032224 | tf_op jit(solution)/shard_map/ppermute | solution.py:44
  172.6 6.1 %collective-permute-start.24 = (bf16[448,768]{1,0:T(8,128)(2,1)S(1)}, bf16[448,768]{1,0:T(8,128)(2,1)}, u32[]{:S(2)}, u32[]{:S(2)}) collective-permute-start(bf16[448,768]{1,0:T(8,128)(2,1)S(1)} %copy-done.21), channel_id=1, source_target_pairs={{0,0},{1,1},{2,2},{3,3},{8,8},{9,9},{10,10},{11,11},{16,17},{17,18... | collective-permute-start | bytes 2064392 | tf_op jit(solution)/shard_map/ppermute | solution.py:44
  180.0 5.1 %collective-permute-done.35 = bf16[448,576]{1,0:T(8,128)(2,1)S(1)} collective-permute-done((bf16[448,576]{1,0:T(8,128)(2,1)S(1)}, bf16[448,576]{1,0:T(8,128)(2,1)S(1)}, u32[]{:S(2)}, u32[]{:S(2)}) %collective-permute-start.35) | collective-permute-done | bytes 516128 | tf_op jit(solution)/shard_map/ppermute | solution.py:44
  185.1 10.2 %collective-permute-done.34 = bf16[448,576]{1,0:T(8,128)(2,1)S(1)} collective-permute-done((bf16[448,576]{1,0:T(8,128)(2,1)S(1)}, bf16[448,576]{1,0:T(8,128)(2,1)S(1)}, u32[]{:S(2)}, u32[]{:S(2)}) %collective-permute-start.34) | collective-permute-done | bytes 516128 | tf_op jit(solution)/shard_map/ppermute | solution.py:44
  195.6 5.3 %shard_map.71 = (bf16[448,768]{1,0:T(8,128)(2,1)}, bf16[448,768]{1,0:T(8,128)(2,1)}) custom-call(s32[16]{0:T(128)} %compare_select_fusion.5.info, bf16[768,1152]{1,0:T(8,128)(2,1)} %shard_map.69.hidden, bf16[2,448,576]{2,1,0:T(8,128)(2,1)} %collective-permute-done.26.mine, bf16[2,448,576]{2,1,0:T(8,128)(2,1)} %collective-permute-done.27.theirs), custom_call_target="tpu_custom_call" | custom-call | tf_op jit(solution)/shard_map/pallas_call | solution.py:257
  203.3 2.6 collective-permute-start.28
  207.0 5.0 %shard_map.72 = (bf16[448,768]{1,0:T(8,128)(2,1)}, bf16[448,768]{1,0:T(8,128)(2,1)}) custom-call(s32[16]{0:T(128)} %compare_select_fusion.5.info, bf16[768,1152]{1,0:T(8,128)(2,1)} %shard_map.69.hidden, bf16[2,448,576]{2,1,0:T(8,128)(2,1)} %collective-permute-done.30.mine, bf16[2,448,576]{2,1,0:T(8,128)(2,1)} %copy-done.15), custom_call_target="tpu_custom_call" | custom-call | tf_op jit(solution)/shard_map/pallas_call | solution.py:257
  212.0 5.7 %collective-permute-start.33 = (bf16[448,768]{1,0:T(8,128)(2,1)}, bf16[448,768]{1,0:T(8,128)(2,1)S(1)}, u32[]{:S(2)}, u32[]{:S(2)}) collective-permute-start(bf16[448,768]{1,0:T(8,128)(2,1)} %get-tuple-element.71), channel_id=1, source_target_pairs={{0,7},{1,4},{2,5},{3,6},{8,15},{9,12},{10,13},{11,14},{16,20},{17,... | collective-permute-start | bytes 2064392 | tf_op jit(solution)/shard_map/ppermute | solution.py:44
  217.7 6.8 %collective-permute-start.32 = (bf16[448,768]{1,0:T(8,128)(2,1)}, bf16[448,768]{1,0:T(8,128)(2,1)}, u32[]{:S(2)}, u32[]{:S(2)}) collective-permute-start(bf16[448,768]{1,0:T(8,128)(2,1)} %get-tuple-element.69), channel_id=1, source_target_pairs={{0,1},{1,2},{2,3},{3,0},{8,9},{9,10},{10,11},{11,8},{16,18},{17,19... | collective-permute-start | bytes 2064392 | tf_op jit(solution)/shard_map/ppermute | solution.py:44
  225.5 5.0 %shard_map.73 = (bf16[448,768]{1,0:T(8,128)(2,1)}, bf16[448,768]{1,0:T(8,128)(2,1)}) custom-call(s32[16]{0:T(128)} %compare_select_fusion.5.info, bf16[768,1152]{1,0:T(8,128)(2,1)} %shard_map.69.hidden, bf16[2,448,576]{2,1,0:T(8,128)(2,1)} %copy-done.7, bf16[2,448,576]{2,1,0:T(8,128)(2,1)} %copy-done.16), custom_call_target="tpu_custom_call" | custom-call | tf_op jit(solution)/shard_map/pallas_call | solution.py:257
  230.5 8.5 %collective-permute-done.28 = bf16[448,768]{1,0:T(8,128)(2,1)} collective-permute-done((bf16[448,768]{1,0:T(8,128)(2,1)}, bf16[448,768]{1,0:T(8,128)(2,1)}, u32[]{:S(2)}, u32[]{:S(2)}) %collective-permute-start.28) | collective-permute-done | bytes 688160 | tf_op jit(solution)/shard_map/ppermute | solution.py:44
  240.9 6.1 %collective-permute-start.38 = (bf16[448,768]{1,0:T(8,128)(2,1)}, bf16[448,768]{1,0:T(8,128)(2,1)S(1)}, u32[]{:S(2)}, u32[]{:S(2)}) collective-permute-start(bf16[448,768]{1,0:T(8,128)(2,1)} %get-tuple-element.76), channel_id=1, source_target_pairs={{0,4},{1,5},{2,6},{3,7},{8,12},{9,13},{10,14},{11,15},{16,21},{17,... | collective-permute-start | bytes 2064392 | tf_op jit(solution)/shard_map/ppermute | solution.py:44
  247.6 15.5 %collective-permute-done.39 = f32[120,128]{1,0:T(8,128)S(1)} collective-permute-done((f32[120,128]{1,0:T(8,128)}, f32[120,128]{1,0:T(8,128)S(1)}, u32[]{:S(2)}, u32[]{:S(2)}) %collective-permute-start.39) | collective-permute-done | bytes 61472 | tf_op jit(solution)/shard_map/ppermute | solution.py:44
  264.0 5.7 %collective-permute-done.40 = f32[120,128]{1,0:T(8,128)S(1)} collective-permute-done((f32[120,128]{1,0:T(8,128)S(1)}, f32[120,128]{1,0:T(8,128)S(1)}, u32[]{:S(2)}, u32[]{:S(2)}) %collective-permute-start.40) | collective-permute-done | bytes 61472 | tf_op jit(solution)/shard_map/ppermute | solution.py:44
  269.8 5.7 %collective-permute-done.41 = f32[120,128]{1,0:T(8,128)S(1)} collective-permute-done((f32[120,128]{1,0:T(8,128)S(1)}, f32[120,128]{1,0:T(8,128)S(1)}, u32[]{:S(2)}, u32[]{:S(2)}) %collective-permute-start.41) | collective-permute-done | bytes 61472 | tf_op jit(solution)/shard_map/ppermute | solution.py:44
  275.6 5.7 %collective-permute-done.42 = f32[120,128]{1,0:T(8,128)S(1)} collective-permute-done((f32[120,128]{1,0:T(8,128)S(1)}, f32[120,128]{1,0:T(8,128)S(1)}, u32[]{:S(2)}, u32[]{:S(2)}) %collective-permute-start.42) | collective-permute-done | bytes 61472 | tf_op jit(solution)/shard_map/ppermute | solution.py:44
  282.0 3.3 %fusion.2 = bf16[768,448]{0,1:T(8,128)(2,1)} fusion(bf16[448,768]{1,0:T(8,128)(2,1)S(1)} %collective-permute-done.38, bf16[448,768]{1,0:T(8,128)(2,1)S(1)} %collective-permute-done.37, bf16[448,768]{1,0:T(8,128)(2,1)S(1)} %collective-permute-done.33, bf16[448,768]{1,0:T(8,128)(2,1)} %collective-permute-done.32, bf16[448,768]{1,0:T(8,128)(2,1)} %collective-permute-done.29, ...), kind=kLoop, calls=%fused_computation.26 | loop fusion | flops 5505024 | bytes 6193152 | tf_op jit(solution)/shard_map/transpose | solution.py:382
  (187 shorter events, 62.1 us)
Async XLA Ops:
  2.1 22.2 %collective-permute-start.4 = (bf16[768,512]{1,0:T(8,128)(2,1)S(1)}, bf16[768,512]{1,0:T(8,128)(2,1)}, u32[]{:S(2)}, u32[]{:S(2)}) collective-permute-start(bf16[768,512]{1,0:T(8,128)(2,1)S(1)} %fusion.1.refs_0_), channel_id=1, source_target_pairs={{0,3},{1,0},{2,1},{3,2},{8,11},{9,8},{10,9},{11,10},{16,19},{17,16... | collective-permute-start | bytes 2359304 | tf_op jit(solution)/shard_map/ppermute | solution.py:44
  6.2 20.3 %collective-permute-start.3 = (bf16[768,512]{1,0:T(8,128)(2,1)S(1)}, bf16[768,512]{1,0:T(8,128)(2,1)}, u32[]{:S(2)}, u32[]{:S(2)}) collective-permute-start(bf16[768,512]{1,0:T(8,128)(2,1)S(1)} %fusion.1.refs_0_), channel_id=1, source_target_pairs={{0,1},{1,2},{2,3},{3,0},{8,9},{9,10},{10,11},{11,8},{16,17},{17,18... | collective-permute-start | bytes 2359304 | tf_op jit(solution)/shard_map/ppermute | solution.py:44
  6.2 20.3 %collective-permute-start.2 = (bf16[768,512]{1,0:T(8,128)(2,1)S(1)}, bf16[768,512]{1,0:T(8,128)(2,1)}, u32[]{:S(2)}, u32[]{:S(2)}) collective-permute-start(bf16[768,512]{1,0:T(8,128)(2,1)S(1)} %fusion.1.refs_0_), channel_id=1, source_target_pairs={{0,4},{1,5},{2,6},{3,7},{8,12},{9,13},{10,14},{11,15},{16,20},{17,... | collective-permute-start | bytes 2359304 | tf_op jit(solution)/shard_map/ppermute | solution.py:44
  26.6 18.3 %collective-permute-start.7 = (bf16[768,512]{1,0:T(8,128)(2,1)}, bf16[768,512]{1,0:T(8,128)(2,1)S(1)}, u32[]{:S(2)}, u32[]{:S(2)}) collective-permute-start(bf16[768,512]{1,0:T(8,128)(2,1)} %collective-permute-done.2.refs_1_), channel_id=1, source_target_pairs={{0,3},{1,0},{2,1},{3,2},{8,11},{9,8},{10,9},{11,10},{16,19},{17,16... | collective-permute-start | bytes 2359304 | tf_op jit(solution)/shard_map/ppermute | solution.py:44
  28.3 19.0 %collective-permute-start.6 = (bf16[768,512]{1,0:T(8,128)(2,1)}, bf16[768,512]{1,0:T(8,128)(2,1)S(1)}, u32[]{:S(2)}, u32[]{:S(2)}) collective-permute-start(bf16[768,512]{1,0:T(8,128)(2,1)} %collective-permute-done.2.refs_1_), channel_id=1, source_target_pairs={{0,1},{1,2},{2,3},{3,0},{8,9},{9,10},{10,11},{11,8},{16,17},{17,18... | collective-permute-start | bytes 2359304 | tf_op jit(solution)/shard_map/ppermute | solution.py:44
  28.6 24.9 %collective-permute-start.12 = (bf16[224,2304]{1,0:T(8,128)(2,1)S(1)}, bf16[224,2304]{1,0:T(8,128)(2,1)S(1)}, u32[]{:S(2)}, u32[]{:S(2)}) collective-permute-start(bf16[224,2304]{1,0:T(8,128)(2,1)S(1)} %pad_maximum_fusion.6), channel_id=1, source_target_pairs={{0,48},{1,49},{2,50},{3,51},{8,56},{9,57},{10,58},{11,59},{16,0},{... | collective-permute-start | bytes 3096584 | tf_op jit(solution)/shard_map/ppermute | solution.py:44
  29.4 27.4 %collective-permute-start.11 = (bf16[224,2304]{1,0:T(8,128)(2,1)S(1)}, bf16[224,2304]{1,0:T(8,128)(2,1)}, u32[]{:S(2)}, u32[]{:S(2)}) collective-permute-start(bf16[224,2304]{1,0:T(8,128)(2,1)S(1)} %pad_maximum_fusion.6), channel_id=1, source_target_pairs={{0,16},{1,17},{2,18},{3,19},{8,24},{9,25},{10,26},{11,27},{16,32},... | collective-permute-start | bytes 3096584 | tf_op jit(solution)/shard_map/ppermute | solution.py:44
  31.8 26.7 %collective-permute-start.10 = (bf16[224,2304]{1,0:T(8,128)(2,1)S(1)}, bf16[224,2304]{1,0:T(8,128)(2,1)S(1)}, u32[]{:S(2)}, u32[]{:S(2)}) collective-permute-start(bf16[224,2304]{1,0:T(8,128)(2,1)S(1)} %pad_maximum_fusion.6), channel_id=1, source_target_pairs={{0,64},{1,65},{2,66},{3,67},{8,72},{9,73},{10,74},{11,75},{16,80},... | collective-permute-start | bytes 3096584 | tf_op jit(solution)/shard_map/ppermute | solution.py:44
  48.2 30.3 %collective-permute-start.8 = (bf16[768,512]{1,0:T(8,128)(2,1)}, bf16[768,512]{1,0:T(8,128)(2,1)S(1)}, u32[]{:S(2)}, u32[]{:S(2)}) collective-permute-start(bf16[768,512]{1,0:T(8,128)(2,1)} %collective-permute-done.3.refs_2_), channel_id=1, source_target_pairs={{0,1},{1,2},{2,3},{3,0},{8,9},{9,10},{10,11},{11,8},{16,17},{17,18... | collective-permute-start | bytes 2359304 | tf_op jit(solution)/shard_map/ppermute | solution.py:44
  48.2 30.3 %collective-permute-start.9 = (bf16[768,512]{1,0:T(8,128)(2,1)S(1)}, bf16[768,512]{1,0:T(8,128)(2,1)S(1)}, u32[]{:S(2)}, u32[]{:S(2)}) collective-permute-start(bf16[768,512]{1,0:T(8,128)(2,1)S(1)} %collective-permute-done.7.refs_5_), channel_id=1, source_target_pairs={{0,3},{1,0},{2,1},{3,2},{8,11},{9,8},{10,9},{11,10},{16,19},{17,16... | collective-permute-start | bytes 2359304 | tf_op jit(solution)/shard_map/ppermute | solution.py:44
  53.5 16.8 %collective-permute-start.13 = (bf16[448,576]{1,0:T(8,128)(2,1)S(1)}, bf16[448,576]{1,0:T(8,128)(2,1)S(1)}, u32[]{:S(2)}, u32[]{:S(2)}) collective-permute-start(bf16[448,576]{1,0:T(8,128)(2,1)S(1)} %fusion.3), channel_id=1, source_target_pairs={{0,0},{1,16},{2,32},{3,48},{8,8},{9,24},{10,40},{11,56},{16,49},{1... | collective-permute-start | bytes 1548296 | tf_op jit(solution)/shard_map/ppermute | solution.py:44
  58.3 48.2 %collective-permute-start.18 = (bf16[2,224,2304]{2,1,0:T(8,128)(2,1)S(1)}, bf16[2,224,2304]{2,1,0:T(8,128)(2,1)S(1)}, u32[]{:S(2)}, u32[]{:S(2)}) collective-permute-start(bf16[2,224,2304]{2,1,0:T(8,128)(2,1)S(1)} %pad_maximum_fusion.1.refs_10_), channel_id=1, source_target_pairs={{0,8},{1,9},{2,10},{3,11},{8,0},{9,1},{10,2},{11,3},{16,24},{17,25... | collective-permute-start | bytes 6193160 | tf_op jit(solution)/shard_map/ppermute | solution.py:44
  79.8 26.6 %collective-permute-start.17 = (bf16[2,224,2304]{2,1,0:T(8,128)(2,1)S(1)}, bf16[2,224,2304]{2,1,0:T(8,128)(2,1)S(1)}, u32[]{:S(2)}, u32[]{:S(2)}) collective-permute-start(bf16[2,224,2304]{2,1,0:T(8,128)(2,1)S(1)} %pad_maximum_fusion.refs_8_), channel_id=1, source_target_pairs={{0,8},{1,9},{2,10},{3,11},{8,0},{9,1},{10,2},{11,3},{16,24},{17,25... | collective-permute-start | bytes 6193160 | tf_op jit(solution)/shard_map/ppermute | solution.py:44
  79.9 26.5 %collective-permute-start.16 = (bf16[224,2304]{1,0:T(8,128)(2,1)S(1)}, bf16[224,2304]{1,0:T(8,128)(2,1)}, u32[]{:S(2)}, u32[]{:S(2)}) collective-permute-start(bf16[224,2304]{1,0:T(8,128)(2,1)S(1)} %collective-permute-done.10), channel_id=1, source_target_pairs={{0,48},{1,49},{2,50},{3,51},{8,56},{9,57},{10,58},{11,59},{16,0},{... | collective-permute-start | bytes 3096584 | tf_op jit(solution)/shard_map/ppermute | solution.py:44
  80.8 25.6 %collective-permute-start.15 = (bf16[224,2304]{1,0:T(8,128)(2,1)S(1)}, bf16[224,2304]{1,0:T(8,128)(2,1)S(1)}, u32[]{:S(2)}, u32[]{:S(2)}) collective-permute-start(bf16[224,2304]{1,0:T(8,128)(2,1)S(1)} %collective-permute-done.10), channel_id=1, source_target_pairs={{0,16},{1,17},{2,18},{3,19},{8,24},{9,25},{10,26},{11,27},{16,32},... | collective-permute-start | bytes 3096584 | tf_op jit(solution)/shard_map/ppermute | solution.py:44
  83.2 16.3 %collective-permute-start.14 = (bf16[448,576]{1,0:T(8,128)(2,1)S(1)}, bf16[448,576]{1,0:T(8,128)(2,1)S(1)}, u32[]{:S(2)}, u32[]{:S(2)}) collective-permute-start(bf16[448,576]{1,0:T(8,128)(2,1)S(1)} %collective-permute-done.13), channel_id=1, source_target_pairs={{0,64},{1,65},{2,66},{3,67},{8,72},{9,73},{10,74},{11,75},{16,80},... | collective-permute-start | bytes 1548296 | tf_op jit(solution)/shard_map/ppermute | solution.py:44
  110.6 26.7 %collective-permute-start.22 = (bf16[224,2304]{1,0:T(8,128)(2,1)}, bf16[224,2304]{1,0:T(8,128)(2,1)}, u32[]{:S(2)}, u32[]{:S(2)}) collective-permute-start(bf16[224,2304]{1,0:T(8,128)(2,1)} %collective-permute-done.16), channel_id=1, source_target_pairs={{0,48},{1,49},{2,50},{3,51},{8,56},{9,57},{10,58},{11,59},{16,0},{... | collective-permute-start | bytes 3096584 | tf_op jit(solution)/shard_map/ppermute | solution.py:44
  110.6 26.7 %collective-permute-start.21 = (bf16[224,2304]{1,0:T(8,128)(2,1)}, bf16[224,2304]{1,0:T(8,128)(2,1)}, u32[]{:S(2)}, u32[]{:S(2)}) collective-permute-start(bf16[224,2304]{1,0:T(8,128)(2,1)} %collective-permute-done.11), channel_id=1, source_target_pairs={{0,16},{1,17},{2,18},{3,19},{8,24},{9,25},{10,26},{11,27},{16,32},... | collective-permute-start | bytes 3096584 | tf_op jit(solution)/shard_map/ppermute | solution.py:44
  139.2 29.0 %collective-permute-start.30 = (bf16[2,448,576]{2,1,0:T(8,128)(2,1)S(1)}, bf16[2,448,576]{2,1,0:T(8,128)(2,1)}, u32[]{:S(2)}, u32[]{:S(2)}) collective-permute-start(bf16[2,448,576]{2,1,0:T(8,128)(2,1)S(1)} %pad_maximum_fusion.4.mine), channel_id=1, source_target_pairs={{0,48},{1,49},{2,50},{3,51},{8,56},{9,57},{10,58},{11,59},{16,0},{... | collective-permute-start | bytes 3096584 | tf_op jit(solution)/shard_map/ppermute | solution.py:44
  140.3 27.9 %collective-permute-start.26 = (bf16[2,448,576]{2,1,0:T(8,128)(2,1)S(1)}, bf16[2,448,576]{2,1,0:T(8,128)(2,1)}, u32[]{:S(2)}, u32[]{:S(2)}) collective-permute-start(bf16[2,448,576]{2,1,0:T(8,128)(2,1)S(1)} %pad_maximum_fusion.4.mine), channel_id=1, source_target_pairs={{0,16},{1,17},{2,18},{3,19},{8,24},{9,25},{10,26},{11,27},{16,32},... | collective-permute-start | bytes 3096584 | tf_op jit(solution)/shard_map/ppermute | solution.py:44
  170.6 24.9 %collective-permute-start.25 = (bf16[448,768]{1,0:T(8,128)(2,1)}, bf16[448,768]{1,0:T(8,128)(2,1)S(1)}, u32[]{:S(2)}, u32[]{:S(2)}) collective-permute-start(bf16[448,768]{1,0:T(8,128)(2,1)} %get-tuple-element.63), channel_id=1, source_target_pairs={{0,6},{1,7},{2,4},{3,5},{8,14},{9,15},{10,12},{11,13},{16,23},{17,... | collective-permute-start | bytes 2064392 | tf_op jit(solution)/shard_map/ppermute | solution.py:44
  172.6 22.9 %collective-permute-start.24 = (bf16[448,768]{1,0:T(8,128)(2,1)S(1)}, bf16[448,768]{1,0:T(8,128)(2,1)}, u32[]{:S(2)}, u32[]{:S(2)}) collective-permute-start(bf16[448,768]{1,0:T(8,128)(2,1)S(1)} %copy-done.21), channel_id=1, source_target_pairs={{0,0},{1,1},{2,2},{3,3},{8,8},{9,9},{10,10},{11,11},{16,17},{17,18... | collective-permute-start | bytes 2064392 | tf_op jit(solution)/shard_map/ppermute | solution.py:44
  178.7 17.0 %collective-permute-start.27 = (bf16[2,448,576]{2,1,0:T(8,128)(2,1)}, bf16[2,448,576]{2,1,0:T(8,128)(2,1)}, u32[]{:S(2)}, u32[]{:S(2)}) collective-permute-start(bf16[2,448,576]{2,1,0:T(8,128)(2,1)} %collective-permute-done.26.mine), channel_id=1, source_target_pairs={{0,8},{1,9},{2,10},{3,11},{8,0},{9,1},{10,2},{11,3},{16,24},{17,25... | collective-permute-start | bytes 3096584 | tf_op jit(solution)/shard_map/ppermute | solution.py:44
  185.1 20.8 %collective-permute-start.31 = (bf16[2,448,576]{2,1,0:T(8,128)(2,1)}, bf16[2,448,576]{2,1,0:T(8,128)(2,1)S(1)}, u32[]{:S(2)}, u32[]{:S(2)}) collective-permute-start(bf16[2,448,576]{2,1,0:T(8,128)(2,1)} %collective-permute-done.30.mine), channel_id=1, source_target_pairs={{0,8},{1,9},{2,10},{3,11},{8,0},{9,1},{10,2},{11,3},{16,24},{17,25... | collective-permute-start | bytes 3096584 | tf_op jit(solution)/shard_map/ppermute | solution.py:44
  195.5 28.9 %collective-permute-start.36 = (bf16[2,448,576]{2,1,0:T(8,128)(2,1)S(1)}, bf16[2,448,576]{2,1,0:T(8,128)(2,1)S(1)}, u32[]{:S(2)}, u32[]{:S(2)}) collective-permute-start(bf16[2,448,576]{2,1,0:T(8,128)(2,1)S(1)} %pad_maximum_fusion.5.mine), channel_id=1, source_target_pairs={{0,8},{1,9},{2,10},{3,11},{8,0},{9,1},{10,2},{11,3},{16,24},{17,25... | collective-permute-start | bytes 3096584 | tf_op jit(solution)/shard_map/ppermute | solution.py:44
  200.9 29.6 %collective-permute-start.29 = (bf16[448,768]{1,0:T(8,128)(2,1)}, bf16[448,768]{1,0:T(8,128)(2,1)}, u32[]{:S(2)}, u32[]{:S(2)}) collective-permute-start(bf16[448,768]{1,0:T(8,128)(2,1)} %get-tuple-element.66), channel_id=1, source_target_pairs={{0,5},{1,6},{2,7},{3,4},{8,13},{9,14},{10,15},{11,12},{16,22},{17,... | collective-permute-start | bytes 2064392 | tf_op jit(solution)/shard_map/ppermute | solution.py:44
  203.3 35.7 %collective-permute-start.28 = (bf16[448,768]{1,0:T(8,128)(2,1)}, bf16[448,768]{1,0:T(8,128)(2,1)}, u32[]{:S(2)}, u32[]{:S(2)}) collective-permute-start(bf16[448,768]{1,0:T(8,128)(2,1)} %get-tuple-element.65), channel_id=1, source_target_pairs={{0,3},{1,0},{2,1},{3,2},{8,11},{9,8},{10,9},{11,10},{16,16},{17,17... | collective-permute-start | bytes 2064392 | tf_op jit(solution)/shard_map/ppermute | solution.py:44
  212.0 70.0 %collective-permute-start.33 = (bf16[448,768]{1,0:T(8,128)(2,1)}, bf16[448,768]{1,0:T(8,128)(2,1)S(1)}, u32[]{:S(2)}, u32[]{:S(2)}) collective-permute-start(bf16[448,768]{1,0:T(8,128)(2,1)} %get-tuple-element.71), channel_id=1, source_target_pairs={{0,7},{1,4},{2,5},{3,6},{8,15},{9,12},{10,13},{11,14},{16,20},{17,... | collective-permute-start | bytes 2064392 | tf_op jit(solution)/shard_map/ppermute | solution.py:44
  217.7 64.3 %collective-permute-start.32 = (bf16[448,768]{1,0:T(8,128)(2,1)}, bf16[448,768]{1,0:T(8,128)(2,1)}, u32[]{:S(2)}, u32[]{:S(2)}) collective-permute-start(bf16[448,768]{1,0:T(8,128)(2,1)} %get-tuple-element.69), channel_id=1, source_target_pairs={{0,1},{1,2},{2,3},{3,0},{8,9},{9,10},{10,11},{11,8},{16,18},{17,19... | collective-permute-start | bytes 2064392 | tf_op jit(solution)/shard_map/ppermute | solution.py:44
  239.0 43.0 %collective-permute-start.37 = (bf16[448,768]{1,0:T(8,128)(2,1)}, bf16[448,768]{1,0:T(8,128)(2,1)S(1)}, u32[]{:S(2)}, u32[]{:S(2)}) collective-permute-start(bf16[448,768]{1,0:T(8,128)(2,1)} %get-tuple-element.74), channel_id=1, source_target_pairs={{0,2},{1,3},{2,0},{3,1},{8,10},{9,11},{10,8},{11,9},{16,19},{17,16... | collective-permute-start | bytes 2064392 | tf_op jit(solution)/shard_map/ppermute | solution.py:44
  240.9 41.1 %collective-permute-start.38 = (bf16[448,768]{1,0:T(8,128)(2,1)}, bf16[448,768]{1,0:T(8,128)(2,1)S(1)}, u32[]{:S(2)}, u32[]{:S(2)}) collective-permute-start(bf16[448,768]{1,0:T(8,128)(2,1)} %get-tuple-element.76), channel_id=1, source_target_pairs={{0,4},{1,5},{2,6},{3,7},{8,12},{9,13},{10,14},{11,15},{16,21},{17,... | collective-permute-start | bytes 2064392 | tf_op jit(solution)/shard_map/ppermute | solution.py:44
  247.1 16.1 %collective-permute-start.39 = (f32[120,128]{1,0:T(8,128)}, f32[120,128]{1,0:T(8,128)S(1)}, u32[]{:S(2)}, u32[]{:S(2)}) collective-permute-start(f32[120,128]{1,0:T(8,128)} %copy-done.17), channel_id=1, source_target_pairs={{0,4},{1,5},{2,6},{3,7},{8,12},{9,13},{10,14},{11,15},{16,20},{17,... | collective-permute-start | bytes 184328 | tf_op jit(solution)/shard_map/ppermute | solution.py:44
  (35 other events, 264.3 us)

commit v4 on v3

--- a/solution.py
+++ b/solution.py
@@ -236,9 +236,6 @@
     return [pl.BlockSpec(memory_space=pltpu.VMEM)] * n
 
 
-DOWN_ORDER = ((0, 0), (1, 0), (0, -1), (1, -1), (0, 1), (1, 1), (0, 2), (1, 2))
-
-
 def down_kernel(info, hidden, mine, theirs, *outs):
     for n, out in enumerate(outs):
         low = jnp.where(info[8] == 0, mine[n], theirs[n])
@@ -259,7 +256,7 @@
         out_shape=[jax.ShapeDtypeStruct((columns, rows), jnp.bfloat16)] * count,
         in_specs=[pl.BlockSpec(memory_space=pltpu.SMEM)] + vmem(3),
         out_specs=vmem(count),
-        compiler_params=pltpu.CompilerParams(vmem_limit_bytes=VMEM_LIMIT),
+        compiler_params=pltpu.CompilerParams(vmem_limit_bytes=VMEM_LIMIT // 3),
         cost_estimate=FREE,
     )(info, hidden, mine, theirs)
 
@@ -320,23 +317,25 @@
     down_weight = rollout(down_master, down_table[2 * rows : 3 * rows].T, *down_at)
     pairs = []
 
-    def swap(blocks):
+    def swap(blocks, *before):
+        blocks = [after(block, *before) for block in blocks]
         for n in range(0, len(blocks), 2):
             pair = jnp.stack(blocks[n : n + 2])
             pairs.extend((pair, send(pair, other_core)))
 
     down_block = send(after(down_weight.T, near_l, near_r), to_ff_group)
     down_far = send(down_block, y_far)
+    every = step(after(every, near_l, near_r), y_near)
 
     def between(blocks):
-        swap(blocks)
-        return [pairs[1], pairs[3], down_far]
-
-    blocks = ring(
-        gate_up, send(gate_up, y_far), x_up, x_down, (tokens_ll, near_rr, down_block), between
-    )
-    every = step(after(every, *blocks[:4]), y_near)
+        swap(blocks[:2], tokens_ll, near_rr)
+        return [pairs[1], down_far]
+
+    far = send(gate_up, y_far)
+    blocks = ring(gate_up, far, x_up, x_down, (near_l, near_r, down_block, every), between)
+    swap(blocks[2:4], blocks[4], blocks[5])
     swap(blocks[4:6])
+    every = step(after(every, *blocks[4:6]), lambda y, x, core, z: (y, x, core, z ^ 2))
 
     steps = jnp.array([dy + 4 * (dx % 4) for dy, dx in ORDER] + [0] * 8, jnp.int32)
     chip_y, chip_x = (steps % 4) ^ (y_hi ^ y_lo), (steps // 4 + x - z + 4) % 4
@@ -347,34 +346,36 @@
     )
     info = jnp.where(jnp.arange(16) == 8, core, info)
 
-    down_pair = jnp.stack([down_block, down_far])
-    down_theirs = send(after(down_pair, blocks[4], blocks[5]), other_core)
-
-    early = token_sum(info, pieces, 0, [after(pairs[0], down_theirs)] + pairs[1:])
+    pairs[0], every = lax.optimization_barrier((pairs[0], every))
+    early = token_sum(info, pieces, 0, pairs)
     early, own_ll, far_rr = lax.optimization_barrier((early, blocks[6], blocks[7]))
-    every = step(after(every, early), lambda y, x, core, z: (y, x, core, z ^ 2))
-    down_pair = after(down_pair, own_ll)
-    left, right = send(down_pair, x_up), send(down_pair, x_down)
+    every = step(after(every, early), y_far)
     last = jnp.stack([own_ll, far_rr])
     last = [last, send(last, other_core)]
-    hidden = token_sum(info, pieces, 6, last, early, last=True)
-
-    def sums(n, mine, theirs, *before):
+    down_block = after(down_block, own_ll)
+    own_l, own_r = send(down_block, x_up), send(down_block, x_down)
+    down_pair = jnp.stack([down_block, down_far])
+    down_theirs = send(down_pair, other_core)
+    hidden = token_sum(info, pieces, 6, last, after(early, down_theirs, every), last=True)
+
+    parts = []
+
+    def sums(mine):
+        mine = jnp.stack(mine)
+        theirs = send(mine, other_core) if parts else down_theirs
         terms = down_terms(info, hidden, mine, theirs)
-        return [
-            send(after(term, *before), to_chunk(*DOWN_ORDER[n + k])) for k, term in enumerate(terms)
-        ], terms
-
-    parts, terms = sums(0, down_pair, down_theirs)
-    left, right = after(left, *terms), after(right, *terms)
-    rest = jnp.stack([send(left[0], x_up), send(right[1], x_down)])
-    parts += sums(2, left, send(left, other_core))[0]
-    rest = after(rest, *parts[:2])
-    parts += sums(4, right, send(right, other_core), *parts[:2])[0]
-    more, terms = sums(6, rest, send(rest, other_core), *parts[2:4])
-    parts += more
-    every = step(after(every, *terms), y_far)
-    every = step(every, lambda y, x, core, z: (y, x ^ 2, core, z))
+        for term in terms:
+            parts.append(send(term, to_chunk(*ORDER[len(parts)])))
+        return terms
+
+    terms = sums([down_block, down_far])
+    far = after(down_far, own_l, own_r)
+    far_l, far_r = send(far, x_up), send(far, x_down)
+    terms = sums([after(own_l, *terms), own_r])
+    terms = sums([far_l, after(far_r, *terms)])
+    own_l, far_r = after(own_l, far_l, *parts[:2]), after(far_r, far_l, *parts[:2])
+    terms = sums([after(send(own_l, x_up), *parts[2:4]), send(far_r, x_down)])
+    every = step(after(every, *terms), lambda y, x, core, z: (y, x ^ 2, core, z))
     log_amax = jnp.log(
         jnp.stack([every[k * rows : k * rows + D // BLOCK, : FF // BLOCK] for k in range(3)]) + EPS
     )

time: 286 us -> 273 us (0.955)
  Pallas kernels: 50.7 us -> 40.5 us
  starting transfers between devices: 70.1 us -> 65 us
  waiting for transfers between devices: 130 us -> 135 us
  local copies, waits for them, and re-layouts: 12.4 us -> 8.88 us
    pallas_call x4, Pallas kernels: 20.3 us -> 10.1 us  [down_terms(): pl.pallas_call(down_kernel, out_shape=[jax.ShapeDtypeStruct((columns, row...]
    ppermute x43 -> x45, starting transfers between devices: 70.1 us -> 65 us  [send(): return lax.ppermute(array, AXES, pairs)]
    ppermute x43 -> x45, waiting for transfers between devices: 130 us -> 135 us  [send(): return lax.ppermute(array, AXES, pairs)]
    unnamed x46 -> x42, local copies, waits for them, and re-layouts: 6.89 us -> 5.58 us
  transfers between devices with their start and end apart: 43 -> 45, of which waited for: 21 -> 21; matrix products, arithmetic and copies ran while one was open for 6% -> 6% of each run, Pallas kernels for 18% -> 15%
where the time goes in v4:
time: 273 us; the launch traced here: 271 us
  waiting for transfers between devices  135 us (49%)
  starting transfers between devices  65 us (24%)
  Pallas kernels  40.5 us (15%)
  other arithmetic  20.1 us (7%)
  local copies, waits for them, and re-layouts  8.88 us (3%)
    ppermute x45, waiting for transfers between devices, send(): return lax.ppermute(array, AXES, pairs)  135 us
    ppermute x45, starting transfers between devices, send(): return lax.ppermute(array, AXES, pairs)  65 us
    pallas_call x2, Pallas kernels, token_sum(): pl.pallas_call(functools.partial(token_kernel, len(blocks), first, before...  30.4 us
    pallas_call x4, Pallas kernels, down_terms(): pl.pallas_call(down_kernel, out_shape=[jax.ShapeDtypeStruct((columns, row...  10.1 us
    unnamed x42, local copies, waits for them, and re-layouts  5.58 us
  transfers between devices with their start and end apart: 45, of which 21 were waited for; matrix products, arithmetic and copies ran while one was open for 6% of the time, Pallas kernels for 15%

profile of v4, /device:TPU:6, one launch (start us, length us, event | category | flops | bytes accessed | tf_op | source)
XLA Modules:
  0.0 270.9 jit_solution(6770370120511246159)
XLA Ops:
  2.1 4.1 %collective-permute-start.4 = (bf16[768,512]{1,0:T(8,128)(2,1)S(1)}, bf16[768,512]{1,0:T(8,128)(2,1)}, u32[]{:S(2)}, u32[]{:S(2)}) collective-permute-start(bf16[768,512]{1,0:T(8,128)(2,1)S(1)} %fusion.1.refs_0_), channel_id=1, source_target_pairs={{0,3},{1,0},{2,1},{3,2},{8,11},{9,8},{10,9},{11,10},{16,19},{17,16... | collective-permute-start | bytes 2359304 | tf_op jit(solution)/shard_map/ppermute | solution.py:44
  15.3 3.4 %collective-permute-done.1 = f32[120,128]{1,0:T(8,128)S(1)} collective-permute-done((f32[120,128]{1,0:T(8,128)S(1)}, f32[120,128]{1,0:T(8,128)S(1)}, u32[]{:S(2)}, u32[]{:S(2)}) %collective-permute-start.1) | collective-permute-done | bytes 61472 | tf_op jit(solution)/shard_map/ppermute | solution.py:44
  20.1 3.5 %multiply_convert_fusion.2 = (bf16[224,1152]{1,0:T(8,128)(2,1)S(1)}, bf16[224,1152]{1,0:T(8,128)(2,1)S(1)}) fusion(f32[224,1152]{1,0:T(8,128)S(1)} %copy-done.7, f32[1152]{0:T(1024)S(1)} %get-tuple-element.103, f32[1152]{0:T(1024)S(1)} %get-tuple-element.104, f32[1152]{0:T(1024)S(1)} %get-tuple-element.102, pred[224]{0:T(512)(128)(4,1)S(1)} %broadcast_compare_fusion.23, ...), kind=kLoop, calls=%fused_computation.20 | loop fusion | flops 9289728 | bytes 3124896 | tf_op jit(solution)/shard_map/convert_element_type | solution.py:129
  32.0 3.2 %collective-permute-start.10 = (bf16[224,2304]{1,0:T(8,128)(2,1)S(1)}, bf16[224,2304]{1,0:T(8,128)(2,1)S(1)}, u32[]{:S(2)}, u32[]{:S(2)}) collective-permute-start(bf16[224,2304]{1,0:T(8,128)(2,1)S(1)} %pad_maximum_fusion.8), channel_id=1, source_target_pairs={{0,64},{1,65},{2,66},{3,67},{8,72},{9,73},{10,74},{11,75},{16,80},... | collective-permute-start | bytes 3096584 | tf_op jit(solution)/shard_map/ppermute | solution.py:44
  35.3 9.5 %collective-permute-done.7.refs_5_ = bf16[768,512]{1,0:T(8,128)(2,1)S(1)} collective-permute-done((bf16[768,512]{1,0:T(8,128)(2,1)}, bf16[768,512]{1,0:T(8,128)(2,1)S(1)}, u32[]{:S(2)}, u32[]{:S(2)}) %collective-permute-start.7) | collective-permute-done | bytes 786464 | tf_op jit(solution)/shard_map/ppermute | solution.py:44
  49.2 8.2 %collective-permute-done.14 = f32[120,128]{1,0:T(8,128)S(1)} collective-permute-done((f32[120,128]{1,0:T(8,128)S(1)}, f32[120,128]{1,0:T(8,128)S(1)}, u32[]{:S(2)}, u32[]{:S(2)}) %collective-permute-start.14) | collective-permute-done | bytes 61472 | tf_op jit(solution)/shard_map/ppermute | solution.py:44
  60.3 4.0 %collective-permute-start.13 = (bf16[448,576]{1,0:T(8,128)(2,1)S(1)}, bf16[448,576]{1,0:T(8,128)(2,1)S(1)}, u32[]{:S(2)}, u32[]{:S(2)}) collective-permute-start(bf16[448,576]{1,0:T(8,128)(2,1)S(1)} %fusion.3), channel_id=1, source_target_pairs={{0,0},{1,16},{2,32},{3,48},{8,8},{9,24},{10,40},{11,56},{16,49},{1... | collective-permute-start | bytes 1548296 | tf_op jit(solution)/shard_map/ppermute | solution.py:44
  64.3 12.9 %collective-permute-done.13 = bf16[448,576]{1,0:T(8,128)(2,1)S(1)} collective-permute-done((bf16[448,576]{1,0:T(8,128)(2,1)S(1)}, bf16[448,576]{1,0:T(8,128)(2,1)S(1)}, u32[]{:S(2)}, u32[]{:S(2)}) %collective-permute-start.13) | collective-permute-done | bytes 516128 | tf_op jit(solution)/shard_map/ppermute | solution.py:44
  77.3 9.9 %collective-permute-done.8.refs_6_ = bf16[768,512]{1,0:T(8,128)(2,1)S(1)} collective-permute-done((bf16[768,512]{1,0:T(8,128)(2,1)}, bf16[768,512]{1,0:T(8,128)(2,1)S(1)}, u32[]{:S(2)}, u32[]{:S(2)}) %collective-permute-start.8) | collective-permute-done | bytes 786464 | tf_op jit(solution)/shard_map/ppermute | solution.py:44
  91.3 22.6 %collective-permute-done.15 = bf16[224,2304]{1,0:T(8,128)(2,1)S(1)} collective-permute-done((bf16[224,2304]{1,0:T(8,128)(2,1)S(1)}, bf16[224,2304]{1,0:T(8,128)(2,1)S(1)}, u32[]{:S(2)}, u32[]{:S(2)}) %collective-permute-start.15) | collective-permute-done | bytes 1032224 | tf_op jit(solution)/shard_map/ppermute | solution.py:44
  119.3 3.0 %collective-permute-start.22 = (bf16[224,2304]{1,0:T(8,128)(2,1)}, bf16[224,2304]{1,0:T(8,128)(2,1)}, u32[]{:S(2)}, u32[]{:S(2)}) collective-permute-start(bf16[224,2304]{1,0:T(8,128)(2,1)} %collective-permute-done.11), channel_id=1, source_target_pairs={{0,16},{1,17},{2,18},{3,19},{8,24},{9,25},{10,26},{11,27},{16,32},... | collective-permute-start | bytes 3096584 | tf_op jit(solution)/shard_map/ppermute | solution.py:44
  123.7 4.2 %collective-permute-done.19 = f32[120,128]{1,0:T(8,128)S(1)} collective-permute-done((f32[120,128]{1,0:T(8,128)S(1)}, f32[120,128]{1,0:T(8,128)S(1)}, u32[]{:S(2)}, u32[]{:S(2)}) %collective-permute-start.19) | collective-permute-done | bytes 61472 | tf_op jit(solution)/shard_map/ppermute | solution.py:44
  128.0 19.7 %shard_map.68.refs_8_ = f32[768,2304]{1,0:T(8,128)} custom-call(s32[16]{0:T(128)} %compare_select_fusion.5.info, bf16[768,512]{1,0:T(8,128)(2,1)} %copy-done.5, bf16[768,512]{1,0:T(8,128)(2,1)} %collective-permute-done.2.refs_1_, bf16[768,512]{1,0:T(8,128)(2,1)} %collective-permute-done.3.refs_2_, bf16[768,512]{1,0:T(8,128)(2,1)} %collective-permute-done.4.refs_3_, ...), custom_call_target="tpu_custom_call" | custom-call | tf_op jit(solution)/shard_map/pallas_call | solution.py:213
  154.9 3.8 %collective-permute-done.25 = f32[120,128]{1,0:T(8,128)S(1)} collective-permute-done((f32[120,128]{1,0:T(8,128)S(1)}, f32[120,128]{1,0:T(8,128)S(1)}, u32[]{:S(2)}, u32[]{:S(2)}) %collective-permute-start.25) | collective-permute-done | bytes 61472 | tf_op jit(solution)/shard_map/ppermute | solution.py:44
  159.6 10.8 %shard_map.69.hidden = bf16[768,1152]{1,0:T(8,128)(2,1)} custom-call(s32[16]{0:T(128)} %compare_select_fusion.5.info, bf16[768,512]{1,0:T(8,128)(2,1)} %copy-done.5, bf16[768,512]{1,0:T(8,128)(2,1)} %collective-permute-done.2.refs_1_, bf16[768,512]{1,0:T(8,128)(2,1)} %collective-permute-done.3.refs_2_, bf16[768,512]{1,0:T(8,128)(2,1)} %collective-permute-done.4.refs_3_, ...), custom_call_target="tpu_custom_call" | custom-call | tf_op jit(solution)/shard_map/pallas_call | solution.py:213
  171.8 2.5 shard_map.70
  175.7 3.1 %collective-permute-start.27 = (bf16[448,768]{1,0:T(8,128)(2,1)S(1)}, bf16[448,768]{1,0:T(8,128)(2,1)S(1)}, u32[]{:S(2)}, u32[]{:S(2)}) collective-permute-start(bf16[448,768]{1,0:T(8,128)(2,1)S(1)} %get-tuple-element.75), channel_id=1, source_target_pairs={{0,0},{1,1},{2,2},{3,3},{8,8},{9,9},{10,10},{11,11},{16,17},{17,18... | collective-permute-start | bytes 2064392 | tf_op jit(solution)/shard_map/ppermute | solution.py:44
  178.8 3.6 %collective-permute-start.28 = (bf16[448,768]{1,0:T(8,128)(2,1)S(1)}, bf16[448,768]{1,0:T(8,128)(2,1)S(1)}, u32[]{:S(2)}, u32[]{:S(2)}) collective-permute-start(bf16[448,768]{1,0:T(8,128)(2,1)S(1)} %get-tuple-element.76), channel_id=1, source_target_pairs={{0,6},{1,7},{2,4},{3,5},{8,14},{9,15},{10,12},{11,13},{16,23},{17,... | collective-permute-start | bytes 2064392 | tf_op jit(solution)/shard_map/ppermute | solution.py:44
  184.7 2.5 shard_map.71
  187.2 3.4 %collective-permute-start.32 = (bf16[448,768]{1,0:T(8,128)(2,1)S(1)}, bf16[448,768]{1,0:T(8,128)(2,1)S(1)}, u32[]{:S(2)}, u32[]{:S(2)}) collective-permute-start(bf16[448,768]{1,0:T(8,128)(2,1)S(1)} %get-tuple-element.78), channel_id=1, source_target_pairs={{0,3},{1,0},{2,1},{3,2},{8,11},{9,8},{10,9},{11,10},{16,16},{17,17... | collective-permute-start | bytes 2064392 | tf_op jit(solution)/shard_map/ppermute | solution.py:44
  190.6 6.8 %collective-permute-done.34 = bf16[448,576]{1,0:T(8,128)(2,1)S(1)} collective-permute-done((bf16[448,576]{1,0:T(8,128)(2,1)S(1)}, bf16[448,576]{1,0:T(8,128)(2,1)S(1)}, u32[]{:S(2)}, u32[]{:S(2)}) %collective-permute-start.34) | collective-permute-done | bytes 516128 | tf_op jit(solution)/shard_map/ppermute | solution.py:44
  198.2 3.6 %collective-permute-done.28 = bf16[448,768]{1,0:T(8,128)(2,1)S(1)} collective-permute-done((bf16[448,768]{1,0:T(8,128)(2,1)S(1)}, bf16[448,768]{1,0:T(8,128)(2,1)S(1)}, u32[]{:S(2)}, u32[]{:S(2)}) %collective-permute-start.28) | collective-permute-done | bytes 688160 | tf_op jit(solution)/shard_map/ppermute | solution.py:44
  204.1 10.9 %collective-permute-done.39 = bf16[448,576]{1,0:T(8,128)(2,1)S(1)} collective-permute-done((bf16[448,576]{1,0:T(8,128)(2,1)S(1)}, bf16[448,576]{1,0:T(8,128)(2,1)S(1)}, u32[]{:S(2)}, u32[]{:S(2)}) %collective-permute-start.39) | collective-permute-done | bytes 516128 | tf_op jit(solution)/shard_map/ppermute | solution.py:44
  216.7 2.5 shard_map.72
  219.2 2.7 collective-permute-start.37
  221.9 5.9 %collective-permute-start.38 = (bf16[448,768]{1,0:T(8,128)(2,1)S(1)}, bf16[448,768]{1,0:T(8,128)(2,1)S(1)}, u32[]{:S(2)}, u32[]{:S(2)}) collective-permute-start(bf16[448,768]{1,0:T(8,128)(2,1)S(1)} %get-tuple-element.83), channel_id=1, source_target_pairs={{0,7},{1,4},{2,5},{3,6},{8,15},{9,12},{10,13},{11,14},{16,20},{17,... | collective-permute-start | bytes 2064392 | tf_op jit(solution)/shard_map/ppermute | solution.py:44
  227.8 2.5 shard_map.73
  232.5 5.0 %collective-permute-start.43 = (bf16[448,768]{1,0:T(8,128)(2,1)S(1)}, bf16[448,768]{1,0:T(8,128)(2,1)S(1)}, u32[]{:S(2)}, u32[]{:S(2)}) collective-permute-start(bf16[448,768]{1,0:T(8,128)(2,1)S(1)} %get-tuple-element.88), channel_id=1, source_target_pairs={{0,4},{1,5},{2,6},{3,7},{8,12},{9,13},{10,14},{11,15},{16,21},{17,... | collective-permute-start | bytes 2064392 | tf_op jit(solution)/shard_map/ppermute | solution.py:44
  237.6 5.7 %collective-permute-done.44 = f32[120,128]{1,0:T(8,128)S(1)} collective-permute-done((f32[120,128]{1,0:T(8,128)S(1)}, f32[120,128]{1,0:T(8,128)S(1)}, u32[]{:S(2)}, u32[]{:S(2)}) %collective-permute-start.44) | collective-permute-done | bytes 61472 | tf_op jit(solution)/shard_map/ppermute | solution.py:44
  244.0 12.9 %collective-permute-done.38 = bf16[448,768]{1,0:T(8,128)(2,1)S(1)} collective-permute-done((bf16[448,768]{1,0:T(8,128)(2,1)S(1)}, bf16[448,768]{1,0:T(8,128)(2,1)S(1)}, u32[]{:S(2)}, u32[]{:S(2)}) %collective-permute-start.38) | collective-permute-done | bytes 688160 | tf_op jit(solution)/shard_map/ppermute | solution.py:44
  256.8 8.6 %collective-permute-done.42 = bf16[448,768]{1,0:T(8,128)(2,1)S(1)} collective-permute-done((bf16[448,768]{1,0:T(8,128)(2,1)S(1)}, bf16[448,768]{1,0:T(8,128)(2,1)S(1)}, u32[]{:S(2)}, u32[]{:S(2)}) %collective-permute-start.42) | collective-permute-done | bytes 688160 | tf_op jit(solution)/shard_map/ppermute | solution.py:44
  265.4 3.9 %collective-permute-done.43 = bf16[448,768]{1,0:T(8,128)(2,1)S(1)} collective-permute-done((bf16[448,768]{1,0:T(8,128)(2,1)S(1)}, bf16[448,768]{1,0:T(8,128)(2,1)S(1)}, u32[]{:S(2)}, u32[]{:S(2)}) %collective-permute-start.43) | collective-permute-done | bytes 688160 | tf_op jit(solution)/shard_map/ppermute | solution.py:44
  (187 shorter events, 60.4 us)
Async XLA Ops:
  2.1 22.2 %collective-permute-start.4 = (bf16[768,512]{1,0:T(8,128)(2,1)S(1)}, bf16[768,512]{1,0:T(8,128)(2,1)}, u32[]{:S(2)}, u32[]{:S(2)}) collective-permute-start(bf16[768,512]{1,0:T(8,128)(2,1)S(1)} %fusion.1.refs_0_), channel_id=1, source_target_pairs={{0,3},{1,0},{2,1},{3,2},{8,11},{9,8},{10,9},{11,10},{16,19},{17,16... | collective-permute-start | bytes 2359304 | tf_op jit(solution)/shard_map/ppermute | solution.py:44
  6.2 20.3 %collective-permute-start.3 = (bf16[768,512]{1,0:T(8,128)(2,1)S(1)}, bf16[768,512]{1,0:T(8,128)(2,1)}, u32[]{:S(2)}, u32[]{:S(2)}) collective-permute-start(bf16[768,512]{1,0:T(8,128)(2,1)S(1)} %fusion.1.refs_0_), channel_id=1, source_target_pairs={{0,1},{1,2},{2,3},{3,0},{8,9},{9,10},{10,11},{11,8},{16,17},{17,18... | collective-permute-start | bytes 2359304 | tf_op jit(solution)/shard_map/ppermute | solution.py:44
  6.2 20.3 %collective-permute-start.2 = (bf16[768,512]{1,0:T(8,128)(2,1)S(1)}, bf16[768,512]{1,0:T(8,128)(2,1)}, u32[]{:S(2)}, u32[]{:S(2)}) collective-permute-start(bf16[768,512]{1,0:T(8,128)(2,1)S(1)} %fusion.1.refs_0_), channel_id=1, source_target_pairs={{0,4},{1,5},{2,6},{3,7},{8,12},{9,13},{10,14},{11,15},{16,20},{17,... | collective-permute-start | bytes 2359304 | tf_op jit(solution)/shard_map/ppermute | solution.py:44
  26.6 18.3 %collective-permute-start.7 = (bf16[768,512]{1,0:T(8,128)(2,1)}, bf16[768,512]{1,0:T(8,128)(2,1)S(1)}, u32[]{:S(2)}, u32[]{:S(2)}) collective-permute-start(bf16[768,512]{1,0:T(8,128)(2,1)} %collective-permute-done.2.refs_1_), channel_id=1, source_target_pairs={{0,3},{1,0},{2,1},{3,2},{8,11},{9,8},{10,9},{11,10},{16,19},{17,16... | collective-permute-start | bytes 2359304 | tf_op jit(solution)/shard_map/ppermute | solution.py:44
  28.3 19.0 %collective-permute-start.6 = (bf16[768,512]{1,0:T(8,128)(2,1)}, bf16[768,512]{1,0:T(8,128)(2,1)}, u32[]{:S(2)}, u32[]{:S(2)}) collective-permute-start(bf16[768,512]{1,0:T(8,128)(2,1)} %collective-permute-done.2.refs_1_), channel_id=1, source_target_pairs={{0,1},{1,2},{2,3},{3,0},{8,9},{9,10},{10,11},{11,8},{16,17},{17,18... | collective-permute-start | bytes 2359304 | tf_op jit(solution)/shard_map/ppermute | solution.py:44
  28.7 31.7 %collective-permute-start.12 = (bf16[224,2304]{1,0:T(8,128)(2,1)S(1)}, bf16[224,2304]{1,0:T(8,128)(2,1)S(1)}, u32[]{:S(2)}, u32[]{:S(2)}) collective-permute-start(bf16[224,2304]{1,0:T(8,128)(2,1)S(1)} %pad_maximum_fusion.8), channel_id=1, source_target_pairs={{0,48},{1,49},{2,50},{3,51},{8,56},{9,57},{10,58},{11,59},{16,0},{... | collective-permute-start | bytes 3096584 | tf_op jit(solution)/shard_map/ppermute | solution.py:44
  29.6 34.8 %collective-permute-start.11 = (bf16[224,2304]{1,0:T(8,128)(2,1)S(1)}, bf16[224,2304]{1,0:T(8,128)(2,1)}, u32[]{:S(2)}, u32[]{:S(2)}) collective-permute-start(bf16[224,2304]{1,0:T(8,128)(2,1)S(1)} %pad_maximum_fusion.8), channel_id=1, source_target_pairs={{0,16},{1,17},{2,18},{3,19},{8,24},{9,25},{10,26},{11,27},{16,32},... | collective-permute-start | bytes 3096584 | tf_op jit(solution)/shard_map/ppermute | solution.py:44
  32.0 32.4 %collective-permute-start.10 = (bf16[224,2304]{1,0:T(8,128)(2,1)S(1)}, bf16[224,2304]{1,0:T(8,128)(2,1)S(1)}, u32[]{:S(2)}, u32[]{:S(2)}) collective-permute-start(bf16[224,2304]{1,0:T(8,128)(2,1)S(1)} %pad_maximum_fusion.8), channel_id=1, source_target_pairs={{0,64},{1,65},{2,66},{3,67},{8,72},{9,73},{10,74},{11,75},{16,80},... | collective-permute-start | bytes 3096584 | tf_op jit(solution)/shard_map/ppermute | solution.py:44
  48.9 38.2 %collective-permute-start.9 = (bf16[768,512]{1,0:T(8,128)(2,1)S(1)}, bf16[768,512]{1,0:T(8,128)(2,1)S(1)}, u32[]{:S(2)}, u32[]{:S(2)}) collective-permute-start(bf16[768,512]{1,0:T(8,128)(2,1)S(1)} %collective-permute-done.7.refs_5_), channel_id=1, source_target_pairs={{0,3},{1,0},{2,1},{3,2},{8,11},{9,8},{10,9},{11,10},{16,19},{17,16... | collective-permute-start | bytes 2359304 | tf_op jit(solution)/shard_map/ppermute | solution.py:44
  57.4 29.8 %collective-permute-start.8 = (bf16[768,512]{1,0:T(8,128)(2,1)}, bf16[768,512]{1,0:T(8,128)(2,1)S(1)}, u32[]{:S(2)}, u32[]{:S(2)}) collective-permute-start(bf16[768,512]{1,0:T(8,128)(2,1)} %collective-permute-done.3.refs_2_), channel_id=1, source_target_pairs={{0,1},{1,2},{2,3},{3,0},{8,9},{9,10},{10,11},{11,8},{16,17},{17,18... | collective-permute-start | bytes 2359304 | tf_op jit(solution)/shard_map/ppermute | solution.py:44
  60.3 17.0 %collective-permute-start.13 = (bf16[448,576]{1,0:T(8,128)(2,1)S(1)}, bf16[448,576]{1,0:T(8,128)(2,1)S(1)}, u32[]{:S(2)}, u32[]{:S(2)}) collective-permute-start(bf16[448,576]{1,0:T(8,128)(2,1)S(1)} %fusion.3), channel_id=1, source_target_pairs={{0,0},{1,16},{2,32},{3,48},{8,8},{9,24},{10,40},{11,56},{16,49},{1... | collective-permute-start | bytes 1548296 | tf_op jit(solution)/shard_map/ppermute | solution.py:44
  88.5 25.5 %collective-permute-start.17 = (bf16[2,224,2304]{2,1,0:T(8,128)(2,1)S(1)}, bf16[2,224,2304]{2,1,0:T(8,128)(2,1)S(1)}, u32[]{:S(2)}, u32[]{:S(2)}) collective-permute-start(bf16[2,224,2304]{2,1,0:T(8,128)(2,1)S(1)} %pad_maximum_fusion.refs_8_), channel_id=1, source_target_pairs={{0,8},{1,9},{2,10},{3,11},{8,0},{9,1},{10,2},{11,3},{16,24},{17,25... | collective-permute-start | bytes 6193160 | tf_op jit(solution)/shard_map/ppermute | solution.py:44
  88.8 25.2 %collective-permute-start.15 = (bf16[224,2304]{1,0:T(8,128)(2,1)S(1)}, bf16[224,2304]{1,0:T(8,128)(2,1)S(1)}, u32[]{:S(2)}, u32[]{:S(2)}) collective-permute-start(bf16[224,2304]{1,0:T(8,128)(2,1)S(1)} %collective-permute-done.10), channel_id=1, source_target_pairs={{0,16},{1,17},{2,18},{3,19},{8,24},{9,25},{10,26},{11,27},{16,32},... | collective-permute-start | bytes 3096584 | tf_op jit(solution)/shard_map/ppermute | solution.py:44
  88.8 26.5 %collective-permute-start.16 = (bf16[224,2304]{1,0:T(8,128)(2,1)S(1)}, bf16[224,2304]{1,0:T(8,128)(2,1)S(1)}, u32[]{:S(2)}, u32[]{:S(2)}) collective-permute-start(bf16[224,2304]{1,0:T(8,128)(2,1)S(1)} %collective-permute-done.10), channel_id=1, source_target_pairs={{0,48},{1,49},{2,50},{3,51},{8,56},{9,57},{10,58},{11,59},{16,0},{... | collective-permute-start | bytes 3096584 | tf_op jit(solution)/shard_map/ppermute | solution.py:44
  90.9 23.1 %collective-permute-start.18 = (bf16[448,576]{1,0:T(8,128)(2,1)S(1)}, bf16[448,576]{1,0:T(8,128)(2,1)S(1)}, u32[]{:S(2)}, u32[]{:S(2)}) collective-permute-start(bf16[448,576]{1,0:T(8,128)(2,1)S(1)} %collective-permute-done.13), channel_id=1, source_target_pairs={{0,64},{1,65},{2,66},{3,67},{8,72},{9,73},{10,74},{11,75},{16,80},... | collective-permute-start | bytes 1548296 | tf_op jit(solution)/shard_map/ppermute | solution.py:44
  119.0 28.7 %collective-permute-start.23 = (bf16[224,2304]{1,0:T(8,128)(2,1)S(1)}, bf16[224,2304]{1,0:T(8,128)(2,1)}, u32[]{:S(2)}, u32[]{:S(2)}) collective-permute-start(bf16[224,2304]{1,0:T(8,128)(2,1)S(1)} %collective-permute-done.16), channel_id=1, source_target_pairs={{0,48},{1,49},{2,50},{3,51},{8,56},{9,57},{10,58},{11,59},{16,0},{... | collective-permute-start | bytes 3096584 | tf_op jit(solution)/shard_map/ppermute | solution.py:44
  119.3 28.4 %collective-permute-start.22 = (bf16[224,2304]{1,0:T(8,128)(2,1)}, bf16[224,2304]{1,0:T(8,128)(2,1)}, u32[]{:S(2)}, u32[]{:S(2)}) collective-permute-start(bf16[224,2304]{1,0:T(8,128)(2,1)} %collective-permute-done.11), channel_id=1, source_target_pairs={{0,16},{1,17},{2,18},{3,19},{8,24},{9,25},{10,26},{11,27},{16,32},... | collective-permute-start | bytes 3096584 | tf_op jit(solution)/shard_map/ppermute | solution.py:44
  150.9 23.4 %collective-permute-start.29 = (bf16[448,576]{1,0:T(8,128)(2,1)S(1)}, bf16[448,576]{1,0:T(8,128)(2,1)S(1)}, u32[]{:S(2)}, u32[]{:S(2)}) collective-permute-start(bf16[448,576]{1,0:T(8,128)(2,1)S(1)} %copy-done.15), channel_id=1, source_target_pairs={{0,16},{1,17},{2,18},{3,19},{8,24},{9,25},{10,26},{11,27},{16,32},... | collective-permute-start | bytes 1548296 | tf_op jit(solution)/shard_map/ppermute | solution.py:44
  151.5 22.9 %collective-permute-start.30 = (bf16[448,576]{1,0:T(8,128)(2,1)S(1)}, bf16[448,576]{1,0:T(8,128)(2,1)}, u32[]{:S(2)}, u32[]{:S(2)}) collective-permute-start(bf16[448,576]{1,0:T(8,128)(2,1)S(1)} %copy-done.15), channel_id=1, source_target_pairs={{0,48},{1,49},{2,50},{3,51},{8,56},{9,57},{10,58},{11,59},{16,0},{... | collective-permute-start | bytes 1548296 | tf_op jit(solution)/shard_map/ppermute | solution.py:44
  175.7 22.4 %collective-permute-start.27 = (bf16[448,768]{1,0:T(8,128)(2,1)S(1)}, bf16[448,768]{1,0:T(8,128)(2,1)S(1)}, u32[]{:S(2)}, u32[]{:S(2)}) collective-permute-start(bf16[448,768]{1,0:T(8,128)(2,1)S(1)} %get-tuple-element.75), channel_id=1, source_target_pairs={{0,0},{1,1},{2,2},{3,3},{8,8},{9,9},{10,10},{11,11},{16,17},{17,18... | collective-permute-start | bytes 2064392 | tf_op jit(solution)/shard_map/ppermute | solution.py:44
  178.8 23.0 %collective-permute-start.28 = (bf16[448,768]{1,0:T(8,128)(2,1)S(1)}, bf16[448,768]{1,0:T(8,128)(2,1)S(1)}, u32[]{:S(2)}, u32[]{:S(2)}) collective-permute-start(bf16[448,768]{1,0:T(8,128)(2,1)S(1)} %get-tuple-element.76), channel_id=1, source_target_pairs={{0,6},{1,7},{2,4},{3,5},{8,14},{9,15},{10,12},{11,13},{16,23},{17,... | collective-permute-start | bytes 2064392 | tf_op jit(solution)/shard_map/ppermute | solution.py:44
  182.4 15.1 %collective-permute-start.34 = (bf16[448,576]{1,0:T(8,128)(2,1)S(1)}, bf16[448,576]{1,0:T(8,128)(2,1)S(1)}, u32[]{:S(2)}, u32[]{:S(2)}) collective-permute-start(bf16[448,576]{1,0:T(8,128)(2,1)S(1)} %copy-done.13), channel_id=1, source_target_pairs={{0,16},{1,17},{2,18},{3,19},{8,24},{9,25},{10,26},{11,27},{16,32},... | collective-permute-start | bytes 1548296 | tf_op jit(solution)/shard_map/ppermute | solution.py:44
  182.7 19.1 %collective-permute-start.35 = (bf16[448,576]{1,0:T(8,128)(2,1)S(1)}, bf16[448,576]{1,0:T(8,128)(2,1)S(1)}, u32[]{:S(2)}, u32[]{:S(2)}) collective-permute-start(bf16[448,576]{1,0:T(8,128)(2,1)S(1)} %copy-done.13), channel_id=1, source_target_pairs={{0,48},{1,49},{2,50},{3,51},{8,56},{9,57},{10,58},{11,59},{16,0},{... | collective-permute-start | bytes 1548296 | tf_op jit(solution)/shard_map/ppermute | solution.py:44
  187.2 27.9 %collective-permute-start.32 = (bf16[448,768]{1,0:T(8,128)(2,1)S(1)}, bf16[448,768]{1,0:T(8,128)(2,1)S(1)}, u32[]{:S(2)}, u32[]{:S(2)}) collective-permute-start(bf16[448,768]{1,0:T(8,128)(2,1)S(1)} %get-tuple-element.78), channel_id=1, source_target_pairs={{0,3},{1,0},{2,1},{3,2},{8,11},{9,8},{10,9},{11,10},{16,16},{17,17... | collective-permute-start | bytes 2064392 | tf_op jit(solution)/shard_map/ppermute | solution.py:44
  197.5 17.6 %collective-permute-start.33 = (bf16[448,768]{1,0:T(8,128)(2,1)S(1)}, bf16[448,768]{1,0:T(8,128)(2,1)S(1)}, u32[]{:S(2)}, u32[]{:S(2)}) collective-permute-start(bf16[448,768]{1,0:T(8,128)(2,1)S(1)} %get-tuple-element.79), channel_id=1, source_target_pairs={{0,1},{1,2},{2,3},{3,0},{8,9},{9,10},{10,11},{11,8},{16,18},{17,19... | collective-permute-start | bytes 2064392 | tf_op jit(solution)/shard_map/ppermute | solution.py:44
  201.8 13.2 %collective-permute-start.39 = (bf16[448,576]{1,0:T(8,128)(2,1)S(1)}, bf16[448,576]{1,0:T(8,128)(2,1)S(1)}, u32[]{:S(2)}, u32[]{:S(2)}) collective-permute-start(bf16[448,576]{1,0:T(8,128)(2,1)S(1)} %collective-permute-done.29), channel_id=1, source_target_pairs={{0,16},{1,17},{2,18},{3,19},{8,24},{9,25},{10,26},{11,27},{16,32},... | collective-permute-start | bytes 1548296 | tf_op jit(solution)/shard_map/ppermute | solution.py:44
  201.8 14.6 %collective-permute-start.40 = (bf16[448,576]{1,0:T(8,128)(2,1)S(1)}, bf16[448,576]{1,0:T(8,128)(2,1)S(1)}, u32[]{:S(2)}, u32[]{:S(2)}) collective-permute-start(bf16[448,576]{1,0:T(8,128)(2,1)S(1)} %collective-permute-done.35), channel_id=1, source_target_pairs={{0,48},{1,49},{2,50},{3,51},{8,56},{9,57},{10,58},{11,59},{16,0},{... | collective-permute-start | bytes 1548296 | tf_op jit(solution)/shard_map/ppermute | solution.py:44
  204.0 12.7 %collective-permute-start.36 = (bf16[2,448,576]{2,1,0:T(8,128)(2,1)S(1)}, bf16[2,448,576]{2,1,0:T(8,128)(2,1)S(1)}, u32[]{:S(2)}, u32[]{:S(2)}) collective-permute-start(bf16[2,448,576]{2,1,0:T(8,128)(2,1)S(1)} %pad_maximum_fusion.6.mine), channel_id=1, source_target_pairs={{0,8},{1,9},{2,10},{3,11},{8,0},{9,1},{10,2},{11,3},{16,24},{17,25... | collective-permute-start | bytes 3096584 | tf_op jit(solution)/shard_map/ppermute | solution.py:44
  219.2 24.8 %collective-permute-start.37 = (bf16[448,768]{1,0:T(8,128)(2,1)S(1)}, bf16[448,768]{1,0:T(8,128)(2,1)S(1)}, u32[]{:S(2)}, u32[]{:S(2)}) collective-permute-start(bf16[448,768]{1,0:T(8,128)(2,1)S(1)} %get-tuple-element.82), channel_id=1, source_target_pairs={{0,5},{1,6},{2,7},{3,4},{8,13},{9,14},{10,15},{11,12},{16,22},{17,... | collective-permute-start | bytes 2064392 | tf_op jit(solution)/shard_map/ppermute | solution.py:44
  221.9 34.9 %collective-permute-start.38 = (bf16[448,768]{1,0:T(8,128)(2,1)S(1)}, bf16[448,768]{1,0:T(8,128)(2,1)S(1)}, u32[]{:S(2)}, u32[]{:S(2)}) collective-permute-start(bf16[448,768]{1,0:T(8,128)(2,1)S(1)} %get-tuple-element.83), channel_id=1, source_target_pairs={{0,7},{1,4},{2,5},{3,6},{8,15},{9,12},{10,13},{11,14},{16,20},{17,... | collective-permute-start | bytes 2064392 | tf_op jit(solution)/shard_map/ppermute | solution.py:44
  230.3 35.1 %collective-permute-start.42 = (bf16[448,768]{1,0:T(8,128)(2,1)S(1)}, bf16[448,768]{1,0:T(8,128)(2,1)S(1)}, u32[]{:S(2)}, u32[]{:S(2)}) collective-permute-start(bf16[448,768]{1,0:T(8,128)(2,1)S(1)} %get-tuple-element.87), channel_id=1, source_target_pairs={{0,2},{1,3},{2,0},{3,1},{8,10},{9,11},{10,8},{11,9},{16,19},{17,16... | collective-permute-start | bytes 2064392 | tf_op jit(solution)/shard_map/ppermute | solution.py:44
  232.5 36.8 %collective-permute-start.43 = (bf16[448,768]{1,0:T(8,128)(2,1)S(1)}, bf16[448,768]{1,0:T(8,128)(2,1)S(1)}, u32[]{:S(2)}, u32[]{:S(2)}) collective-permute-start(bf16[448,768]{1,0:T(8,128)(2,1)S(1)} %get-tuple-element.88), channel_id=1, source_target_pairs={{0,4},{1,5},{2,6},{3,7},{8,12},{9,13},{10,14},{11,15},{16,21},{17,... | collective-permute-start | bytes 2064392 | tf_op jit(solution)/shard_map/ppermute | solution.py:44
  (35 other events, 299.6 us)

commit v5 on v4

--- a/solution.py
+++ b/solution.py
@@ -227,7 +227,9 @@
                 pltpu.SemaphoreType.DMA((count,)),
             ],
         ),
-        compiler_params=pltpu.CompilerParams(vmem_limit_bytes=VMEM_LIMIT),
+        compiler_params=pltpu.CompilerParams(
+            vmem_limit_bytes=VMEM_LIMIT // 3 if last else VMEM_LIMIT
+        ),
         cost_estimate=FREE,
     )(info, *tokens, *([] if before is None else [before]), *blocks)
 
@@ -306,9 +308,8 @@
         axis=1,
     )
     every = step(table, lambda y, x, core, z: (y, x, core, z ^ 1))
-    gate_up, near, tokens_l, tokens_r, every = lax.optimization_barrier(
-        (gate_up, near, tokens_l, tokens_r, every)
-    )
+    gate_up, every = lax.optimization_barrier((gate_up, every))
+    near, tokens_l, tokens_r = lax.optimization_barrier((near, tokens_l, tokens_r))
     down_table = every
     near_l, near_r = send(near, z_up), send(near, z_down)
     tokens_l, near_r = after(tokens_l, near_l), after(near_r, near_l)
@@ -324,18 +325,20 @@
             pairs.extend((pair, send(pair, other_core)))
 
     down_block = send(after(down_weight.T, near_l, near_r), to_ff_group)
-    down_far = send(down_block, y_far)
     every = step(after(every, near_l, near_r), y_near)
 
+    down_far = None
+
     def between(blocks):
-        swap(blocks[:2], tokens_ll, near_rr)
-        return [pairs[1], down_far]
+        nonlocal down_far
+        swap(blocks[:2])
+        down_far = send(after(down_block, pairs[1]), y_far)
+        return [pairs[1], tokens_ll, near_rr]
 
     far = send(gate_up, y_far)
     blocks = ring(gate_up, far, x_up, x_down, (near_l, near_r, down_block, every), between)
-    swap(blocks[2:4], blocks[4], blocks[5])
+    swap(blocks[2:4], blocks[4], blocks[5], down_far)
     swap(blocks[4:6])
-    every = step(after(every, *blocks[4:6]), lambda y, x, core, z: (y, x, core, z ^ 2))
 
     steps = jnp.array([dy + 4 * (dx % 4) for dy, dx in ORDER] + [0] * 8, jnp.int32)
     chip_y, chip_x = (steps % 4) ^ (y_hi ^ y_lo), (steps // 4 + x - z + 4) % 4
@@ -346,10 +349,9 @@
     )
     info = jnp.where(jnp.arange(16) == 8, core, info)
 
-    pairs[0], every = lax.optimization_barrier((pairs[0], every))
     early = token_sum(info, pieces, 0, pairs)
     early, own_ll, far_rr = lax.optimization_barrier((early, blocks[6], blocks[7]))
-    every = step(after(every, early), y_far)
+    every = step(after(every, early), lambda y, x, core, z: (y, x, core, z ^ 2))
     last = jnp.stack([own_ll, far_rr])
     last = [last, send(last, other_core)]
     down_block = after(down_block, own_ll)
@@ -372,10 +374,11 @@
     far = after(down_far, own_l, own_r)
     far_l, far_r = send(far, x_up), send(far, x_down)
     terms = sums([after(own_l, *terms), own_r])
-    terms = sums([far_l, after(far_r, *terms)])
-    own_l, far_r = after(own_l, far_l, *parts[:2]), after(far_r, far_l, *parts[:2])
+    sums([far_l, after(far_r, *terms, *parts[:2])])
+    own_l, far_r, *_ = lax.optimization_barrier((own_l, far_r, *parts[:2], *terms))
     terms = sums([after(send(own_l, x_up), *parts[2:4]), send(far_r, x_down)])
-    every = step(after(every, *terms), lambda y, x, core, z: (y, x ^ 2, core, z))
+    every = step(after(every, *terms), y_far)
+    every = step(every, lambda y, x, core, z: (y, x ^ 2, core, z))
     log_amax = jnp.log(
         jnp.stack([every[k * rows : k * rows + D // BLOCK, : FF // BLOCK] for k in range(3)]) + EPS
     )

time: 273 us -> 267 us (0.978)
  starting transfers between devices: 65 us -> 59.7 us
  Pallas kernels: 40.5 us -> 36.9 us
  waiting for transfers between devices: 135 us -> 138 us
    ppermute x45, starting transfers between devices: 65 us -> 59.7 us  [send(): return lax.ppermute(array, AXES, pairs)]
    pallas_call x2, Pallas kernels: 30.4 us -> 26.7 us  [token_sum(): pl.pallas_call(functools.partial(token_kernel, len(blocks), first, before...]
    ppermute x45, waiting for transfers between devices: 135 us -> 138 us  [send(): return lax.ppermute(array, AXES, pairs)]
    unnamed x42 -> x58, local copies, waits for them, and re-layouts: 5.58 us -> 4.41 us
  transfers between devices with their start and end apart: 45 -> 45, of which waited for: 21 -> 18; matrix products, arithmetic and copies ran while one was open for 6% -> 7% of each run, Pallas kernels for 15% -> 14%
where the time goes in v5:
time: 267 us; the launch traced here: 265 us
  waiting for transfers between devices  138 us (52%)
  starting transfers between devices  59.7 us (22%)
  Pallas kernels  36.9 us (14%)
  other arithmetic  21.3 us (8%)
  local copies, waits for them, and re-layouts  7.71 us (3%)
    ppermute x45, waiting for transfers between devices, send(): return lax.ppermute(array, AXES, pairs)  138 us
    ppermute x45, starting transfers between devices, send(): return lax.ppermute(array, AXES, pairs)  59.7 us
    pallas_call x2, Pallas kernels, token_sum(): pl.pallas_call(functools.partial(token_kernel, len(blocks), first, before...  26.7 us
    pallas_call x4, Pallas kernels, down_terms(): pl.pallas_call(down_kernel, out_shape=[jax.ShapeDtypeStruct((columns, row...  10.2 us
  transfers between devices with their start and end apart: 45, of which 18 were waited for; matrix products, arithmetic and copies ran while one was open for 7% of the time, Pallas kernels for 14%

profile of v5, /device:TPU:6, one launch (start us, length us, event | category | flops | bytes accessed | tf_op | source)
XLA Modules:
  0.0 265.0 jit_solution(4041636261342643871)
XLA Ops:
  2.1 4.1 %collective-permute-start.2 = (bf16[768,512]{1,0:T(8,128)(2,1)S(1)}, bf16[768,512]{1,0:T(8,128)(2,1)S(1)}, u32[]{:S(2)}, u32[]{:S(2)}) collective-permute-start(bf16[768,512]{1,0:T(8,128)(2,1)S(1)} %fusion.1.refs_0_), channel_id=1, source_target_pairs={{0,3},{1,0},{2,1},{3,2},{8,11},{9,8},{10,9},{11,10},{16,19},{17,16... | collective-permute-start | bytes 2359304 | tf_op jit(solution)/shard_map/ppermute | solution.py:44
  8.1 2.3 select_reduce_fusion.8
  16.7 3.4 %collective-permute-done.8 = f32[120,128]{1,0:T(8,128)S(1)} collective-permute-done((f32[120,128]{1,0:T(8,128)S(1)}, f32[120,128]{1,0:T(8,128)S(1)}, u32[]{:S(2)}, u32[]{:S(2)}) %collective-permute-start.8) | collective-permute-done | bytes 61472 | tf_op jit(solution)/shard_map/ppermute | solution.py:44
  21.6 3.7 %multiply_convert_fusion.2 = (bf16[224,1152]{1,0:T(8,128)(2,1)S(1)}, bf16[224,1152]{1,0:T(8,128)(2,1)S(1)}) fusion(f32[224,1152]{1,0:T(8,128)} %param.6, f32[1152]{0:T(1024)S(1)} %get-tuple-element.95, f32[1152]{0:T(1024)S(1)} %get-tuple-element.96, f32[1152]{0:T(1024)S(1)} %get-tuple-element.94, pred[224]{0:T(512)(128)(4,1)S(1)} %broadcast_compare_fusion.23, ...), kind=kLoop, calls=%fused_computation.20 | loop fusion | flops 9289728 | bytes 3124896 | tf_op jit(solution)/shard_map/convert_element_type | solution.py:129
  26.3 2.4 collective-permute-start.11
  28.8 2.9 %collective-permute-start.10 = (bf16[224,2304]{1,0:T(8,128)(2,1)S(1)}, bf16[224,2304]{1,0:T(8,128)(2,1)S(1)}, u32[]{:S(2)}, u32[]{:S(2)}) collective-permute-start(bf16[224,2304]{1,0:T(8,128)(2,1)S(1)} %pad_maximum_fusion.8), channel_id=1, source_target_pairs={{0,64},{1,65},{2,66},{3,67},{8,72},{9,73},{10,74},{11,75},{16,80},... | collective-permute-start | bytes 3096584 | tf_op jit(solution)/shard_map/ppermute | solution.py:44
  31.7 3.4 %collective-permute-start.4 = (bf16[768,512]{1,0:T(8,128)(2,1)S(1)}, bf16[768,512]{1,0:T(8,128)(2,1)S(1)}, u32[]{:S(2)}, u32[]{:S(2)}) collective-permute-start(bf16[768,512]{1,0:T(8,128)(2,1)S(1)} %collective-permute-done.refs_1_), channel_id=1, source_target_pairs={{0,3},{1,0},{2,1},{3,2},{8,11},{9,8},{10,9},{11,10},{16,19},{17,16... | collective-permute-start | bytes 2359304 | tf_op jit(solution)/shard_map/ppermute | solution.py:44
  37.4 13.1 %collective-permute-done.4.refs_5_ = bf16[768,512]{1,0:T(8,128)(2,1)S(1)} collective-permute-done((bf16[768,512]{1,0:T(8,128)(2,1)S(1)}, bf16[768,512]{1,0:T(8,128)(2,1)S(1)}, u32[]{:S(2)}, u32[]{:S(2)}) %collective-permute-start.4) | collective-permute-done | bytes 786464 | tf_op jit(solution)/shard_map/ppermute | solution.py:44
  50.6 3.4 %collective-permute-done.3.refs_4_ = bf16[768,512]{1,0:T(8,128)(2,1)S(1)} collective-permute-done((bf16[768,512]{1,0:T(8,128)(2,1)S(1)}, bf16[768,512]{1,0:T(8,128)(2,1)S(1)}, u32[]{:S(2)}, u32[]{:S(2)}) %collective-permute-start.3) | collective-permute-done | bytes 786464 | tf_op jit(solution)/shard_map/ppermute | solution.py:44
  57.6 3.8 %collective-permute-done.14 = f32[120,128]{1,0:T(8,128)S(1)} collective-permute-done((f32[120,128]{1,0:T(8,128)S(1)}, f32[120,128]{1,0:T(8,128)S(1)}, u32[]{:S(2)}, u32[]{:S(2)}) %collective-permute-start.14) | collective-permute-done | bytes 61472 | tf_op jit(solution)/shard_map/ppermute | solution.py:44
  61.5 10.8 %collective-permute-done.13 = bf16[448,576]{1,0:T(8,128)(2,1)S(1)} collective-permute-done((bf16[448,576]{1,0:T(8,128)(2,1)S(1)}, bf16[448,576]{1,0:T(8,128)(2,1)S(1)}, u32[]{:S(2)}, u32[]{:S(2)}) %collective-permute-start.13) | collective-permute-done | bytes 516128 | tf_op jit(solution)/shard_map/ppermute | solution.py:44
  74.7 3.2 %collective-permute-start.6 = (bf16[768,512]{1,0:T(8,128)(2,1)S(1)}, bf16[768,512]{1,0:T(8,128)(2,1)S(1)}, u32[]{:S(2)}, u32[]{:S(2)}) collective-permute-start(bf16[768,512]{1,0:T(8,128)(2,1)S(1)} %collective-permute-done.4.refs_5_), channel_id=1, source_target_pairs={{0,3},{1,0},{2,1},{3,2},{8,11},{9,8},{10,9},{11,10},{16,19},{17,16... | collective-permute-start | bytes 2359304 | tf_op jit(solution)/shard_map/ppermute | solution.py:44
  79.0 18.9 %collective-permute-done.16 = bf16[224,2304]{1,0:T(8,128)(2,1)S(1)} collective-permute-done((bf16[224,2304]{1,0:T(8,128)(2,1)S(1)}, bf16[224,2304]{1,0:T(8,128)(2,1)S(1)}, u32[]{:S(2)}, u32[]{:S(2)}) %collective-permute-start.16) | collective-permute-done | bytes 1032224 | tf_op jit(solution)/shard_map/ppermute | solution.py:44
  105.4 2.4 collective-permute-done.19.refs_11_
  107.8 19.8 %shard_map.68.refs_8_ = f32[768,2304]{1,0:T(8,128)} custom-call(s32[16]{0:T(128)} %compare_select_fusion.5.info, bf16[768,512]{1,0:T(8,128)(2,1)} %copy-done.1, bf16[768,512]{1,0:T(8,128)(2,1)} %copy-done.7, bf16[768,512]{1,0:T(8,128)(2,1)} %copy-done.5, bf16[768,512]{1,0:T(8,128)(2,1)} %copy-done.3, bf16[768,512]{1,0:T(8,128)(2,1)} %copy-done.11, ...), custom_call_target="tpu_custom_call" | custom-call | tf_op jit(solution)/shard_map/pallas_call | solution.py:213
  135.2 5.7 %collective-permute-done.24 = f32[120,128]{1,0:T(8,128)S(1)} collective-permute-done((f32[120,128]{1,0:T(8,128)S(1)}, f32[120,128]{1,0:T(8,128)S(1)}, u32[]{:S(2)}, u32[]{:S(2)}) %collective-permute-start.24) | collective-permute-done | bytes 61472 | tf_op jit(solution)/shard_map/ppermute | solution.py:44
  141.1 3.0 %copy-done = f32[768,2304]{1,0:T(8,128)S(1)} copy-done((f32[768,2304]{1,0:T(8,128)S(1)}, f32[768,2304]{1,0:T(8,128)}, u32[]{:S(2)}) %copy-start) | copy-done | bytes 7077912
  144.1 6.9 %shard_map.69.hidden = bf16[768,1152]{1,0:T(8,128)(2,1)S(1)} custom-call(s32[16]{0:T(128)S(1)} %copy-done.17, bf16[768,512]{1,0:T(8,128)(2,1)S(1)} %copy-done.2, bf16[768,512]{1,0:T(8,128)(2,1)S(1)} %copy-done.8, bf16[768,512]{1,0:T(8,128)(2,1)S(1)} %copy-done.6, bf16[768,512]{1,0:T(8,128)(2,1)S(1)} %copy-done.4, bf16[768,512]{1,0:T(8,128)(2,1)S(1)} %copy-done.12, ...), custom_call_target="tpu_custom_call" | custom-call | tf_op jit(solution)/shard_map/pallas_call | solution.py:213
  151.0 2.5 shard_map.70
  156.0 5.9 %collective-permute-start.27 = (bf16[448,768]{1,0:T(8,128)(2,1)S(1)}, bf16[448,768]{1,0:T(8,128)(2,1)S(1)}, u32[]{:S(2)}, u32[]{:S(2)}) collective-permute-start(bf16[448,768]{1,0:T(8,128)(2,1)S(1)} %get-tuple-element.68), channel_id=1, source_target_pairs={{0,6},{1,7},{2,4},{3,5},{8,14},{9,15},{10,12},{11,13},{16,23},{17,... | collective-permute-start | bytes 2064392 | tf_op jit(solution)/shard_map/ppermute | solution.py:44
  162.0 2.5 shard_map.71
  164.5 4.2 %collective-permute-start.31 = (bf16[448,768]{1,0:T(8,128)(2,1)S(1)}, bf16[448,768]{1,0:T(8,128)(2,1)S(1)}, u32[]{:S(2)}, u32[]{:S(2)}) collective-permute-start(bf16[448,768]{1,0:T(8,128)(2,1)S(1)} %get-tuple-element.70), channel_id=1, source_target_pairs={{0,3},{1,0},{2,1},{3,2},{8,11},{9,8},{10,9},{11,10},{16,16},{17,17... | collective-permute-start | bytes 2064392 | tf_op jit(solution)/shard_map/ppermute | solution.py:44
  169.5 8.5 %collective-permute-done.34 = bf16[448,576]{1,0:T(8,128)(2,1)S(1)} collective-permute-done((bf16[448,576]{1,0:T(8,128)(2,1)S(1)}, bf16[448,576]{1,0:T(8,128)(2,1)S(1)}, u32[]{:S(2)}, u32[]{:S(2)}) %collective-permute-start.34) | collective-permute-done | bytes 516128 | tf_op jit(solution)/shard_map/ppermute | solution.py:44
  181.1 12.8 %collective-permute-done.33 = bf16[448,576]{1,0:T(8,128)(2,1)S(1)} collective-permute-done((bf16[448,576]{1,0:T(8,128)(2,1)S(1)}, bf16[448,576]{1,0:T(8,128)(2,1)S(1)}, u32[]{:S(2)}, u32[]{:S(2)}) %collective-permute-start.33) | collective-permute-done | bytes 516128 | tf_op jit(solution)/shard_map/ppermute | solution.py:44
  194.2 10.1 %collective-permute-done.38 = bf16[448,576]{1,0:T(8,128)(2,1)S(1)} collective-permute-done((bf16[448,576]{1,0:T(8,128)(2,1)S(1)}, bf16[448,576]{1,0:T(8,128)(2,1)S(1)}, u32[]{:S(2)}, u32[]{:S(2)}) %collective-permute-start.38) | collective-permute-done | bytes 516128 | tf_op jit(solution)/shard_map/ppermute | solution.py:44
  204.5 2.5 shard_map.72
  207.1 3.7 %collective-permute-start.36 = (bf16[448,768]{1,0:T(8,128)(2,1)S(1)}, bf16[448,768]{1,0:T(8,128)(2,1)S(1)}, u32[]{:S(2)}, u32[]{:S(2)}) collective-permute-start(bf16[448,768]{1,0:T(8,128)(2,1)S(1)} %get-tuple-element.74), channel_id=1, source_target_pairs={{0,5},{1,6},{2,7},{3,4},{8,13},{9,14},{10,15},{11,12},{16,22},{17,... | collective-permute-start | bytes 2064392 | tf_op jit(solution)/shard_map/ppermute | solution.py:44
  212.8 2.5 shard_map.73
  215.3 4.0 %collective-permute-start.41 = (bf16[448,768]{1,0:T(8,128)(2,1)S(1)}, bf16[448,768]{1,0:T(8,128)(2,1)S(1)}, u32[]{:S(2)}, u32[]{:S(2)}) collective-permute-start(bf16[448,768]{1,0:T(8,128)(2,1)S(1)} %get-tuple-element.79), channel_id=1, source_target_pairs={{0,2},{1,3},{2,0},{3,1},{8,10},{9,11},{10,8},{11,9},{16,19},{17,16... | collective-permute-start | bytes 2064392 | tf_op jit(solution)/shard_map/ppermute | solution.py:44
  219.3 2.7 %collective-permute-start.42 = (bf16[448,768]{1,0:T(8,128)(2,1)S(1)}, bf16[448,768]{1,0:T(8,128)(2,1)S(1)}, u32[]{:S(2)}, u32[]{:S(2)}) collective-permute-start(bf16[448,768]{1,0:T(8,128)(2,1)S(1)} %get-tuple-element.80), channel_id=1, source_target_pairs={{0,4},{1,5},{2,6},{3,7},{8,12},{9,13},{10,14},{11,15},{16,21},{17,... | collective-permute-start | bytes 2064392 | tf_op jit(solution)/shard_map/ppermute | solution.py:44
  222.9 34.1 %collective-permute-done.43 = f32[120,128]{1,0:T(8,128)S(1)} collective-permute-done((f32[120,128]{1,0:T(8,128)S(1)}, f32[120,128]{1,0:T(8,128)S(1)}, u32[]{:S(2)}, u32[]{:S(2)}) %collective-permute-start.43) | collective-permute-done | bytes 61472 | tf_op jit(solution)/shard_map/ppermute | solution.py:44
  257.1 5.7 %collective-permute-done.44 = f32[120,128]{1,0:T(8,128)S(1)} collective-permute-done((f32[120,128]{1,0:T(8,128)S(1)}, f32[120,128]{1,0:T(8,128)S(1)}, u32[]{:S(2)}, u32[]{:S(2)}) %collective-permute-start.44) | collective-permute-done | bytes 61472 | tf_op jit(solution)/shard_map/ppermute | solution.py:44
  (203 shorter events, 48.0 us)
Async XLA Ops:
  2.1 26.7 %collective-permute-start.2 = (bf16[768,512]{1,0:T(8,128)(2,1)S(1)}, bf16[768,512]{1,0:T(8,128)(2,1)S(1)}, u32[]{:S(2)}, u32[]{:S(2)}) collective-permute-start(bf16[768,512]{1,0:T(8,128)(2,1)S(1)} %fusion.1.refs_0_), channel_id=1, source_target_pairs={{0,3},{1,0},{2,1},{3,2},{8,11},{9,8},{10,9},{11,10},{16,19},{17,16... | collective-permute-start | bytes 2359304 | tf_op jit(solution)/shard_map/ppermute | solution.py:44
  6.2 25.5 %collective-permute-start.1 = (bf16[768,512]{1,0:T(8,128)(2,1)S(1)}, bf16[768,512]{1,0:T(8,128)(2,1)S(1)}, u32[]{:S(2)}, u32[]{:S(2)}) collective-permute-start(bf16[768,512]{1,0:T(8,128)(2,1)S(1)} %fusion.1.refs_0_), channel_id=1, source_target_pairs={{0,1},{1,2},{2,3},{3,0},{8,9},{9,10},{10,11},{11,8},{16,17},{17,18... | collective-permute-start | bytes 2359304 | tf_op jit(solution)/shard_map/ppermute | solution.py:44
  6.2 25.5 %collective-permute-start = (bf16[768,512]{1,0:T(8,128)(2,1)S(1)}, bf16[768,512]{1,0:T(8,128)(2,1)S(1)}, u32[]{:S(2)}, u32[]{:S(2)}) collective-permute-start(bf16[768,512]{1,0:T(8,128)(2,1)S(1)} %fusion.1.refs_0_), channel_id=1, source_target_pairs={{0,4},{1,5},{2,6},{3,7},{8,12},{9,13},{10,14},{11,15},{16,20},{17,... | collective-permute-start | bytes 2359304 | tf_op jit(solution)/shard_map/ppermute | solution.py:44
  25.4 36.0 %collective-permute-start.12 = (bf16[224,2304]{1,0:T(8,128)(2,1)S(1)}, bf16[224,2304]{1,0:T(8,128)(2,1)S(1)}, u32[]{:S(2)}, u32[]{:S(2)}) collective-permute-start(bf16[224,2304]{1,0:T(8,128)(2,1)S(1)} %pad_maximum_fusion.8), channel_id=1, source_target_pairs={{0,48},{1,49},{2,50},{3,51},{8,56},{9,57},{10,58},{11,59},{16,0},{... | collective-permute-start | bytes 3096584 | tf_op jit(solution)/shard_map/ppermute | solution.py:44
  26.3 35.1 %collective-permute-start.11 = (bf16[224,2304]{1,0:T(8,128)(2,1)S(1)}, bf16[224,2304]{1,0:T(8,128)(2,1)}, u32[]{:S(2)}, u32[]{:S(2)}) collective-permute-start(bf16[224,2304]{1,0:T(8,128)(2,1)S(1)} %pad_maximum_fusion.8), channel_id=1, source_target_pairs={{0,16},{1,17},{2,18},{3,19},{8,24},{9,25},{10,26},{11,27},{16,32},... | collective-permute-start | bytes 3096584 | tf_op jit(solution)/shard_map/ppermute | solution.py:44
  28.8 32.6 %collective-permute-start.10 = (bf16[224,2304]{1,0:T(8,128)(2,1)S(1)}, bf16[224,2304]{1,0:T(8,128)(2,1)S(1)}, u32[]{:S(2)}, u32[]{:S(2)}) collective-permute-start(bf16[224,2304]{1,0:T(8,128)(2,1)S(1)} %pad_maximum_fusion.8), channel_id=1, source_target_pairs={{0,64},{1,65},{2,66},{3,67},{8,72},{9,73},{10,74},{11,75},{16,80},... | collective-permute-start | bytes 3096584 | tf_op jit(solution)/shard_map/ppermute | solution.py:44
  31.7 18.8 %collective-permute-start.4 = (bf16[768,512]{1,0:T(8,128)(2,1)S(1)}, bf16[768,512]{1,0:T(8,128)(2,1)S(1)}, u32[]{:S(2)}, u32[]{:S(2)}) collective-permute-start(bf16[768,512]{1,0:T(8,128)(2,1)S(1)} %collective-permute-done.refs_1_), channel_id=1, source_target_pairs={{0,3},{1,0},{2,1},{3,2},{8,11},{9,8},{10,9},{11,10},{16,19},{17,16... | collective-permute-start | bytes 2359304 | tf_op jit(solution)/shard_map/ppermute | solution.py:44
  35.1 18.8 %collective-permute-start.3 = (bf16[768,512]{1,0:T(8,128)(2,1)S(1)}, bf16[768,512]{1,0:T(8,128)(2,1)S(1)}, u32[]{:S(2)}, u32[]{:S(2)}) collective-permute-start(bf16[768,512]{1,0:T(8,128)(2,1)S(1)} %collective-permute-done.refs_1_), channel_id=1, source_target_pairs={{0,1},{1,2},{2,3},{3,0},{8,9},{9,10},{10,11},{11,8},{16,17},{17,18... | collective-permute-start | bytes 2359304 | tf_op jit(solution)/shard_map/ppermute | solution.py:44
  54.9 17.3 %collective-permute-start.13 = (bf16[448,576]{1,0:T(8,128)(2,1)S(1)}, bf16[448,576]{1,0:T(8,128)(2,1)S(1)}, u32[]{:S(2)}, u32[]{:S(2)}) collective-permute-start(bf16[448,576]{1,0:T(8,128)(2,1)S(1)} %fusion.3), channel_id=1, source_target_pairs={{0,0},{1,16},{2,32},{3,48},{8,8},{9,24},{10,40},{11,56},{16,49},{1... | collective-permute-start | bytes 1548296 | tf_op jit(solution)/shard_map/ppermute | solution.py:44
  72.6 25.2 %collective-permute-start.16 = (bf16[224,2304]{1,0:T(8,128)(2,1)S(1)}, bf16[224,2304]{1,0:T(8,128)(2,1)S(1)}, u32[]{:S(2)}, u32[]{:S(2)}) collective-permute-start(bf16[224,2304]{1,0:T(8,128)(2,1)S(1)} %collective-permute-done.10), channel_id=1, source_target_pairs={{0,16},{1,17},{2,18},{3,19},{8,24},{9,25},{10,26},{11,27},{16,32},... | collective-permute-start | bytes 3096584 | tf_op jit(solution)/shard_map/ppermute | solution.py:44
  72.7 26.3 %collective-permute-start.17 = (bf16[224,2304]{1,0:T(8,128)(2,1)S(1)}, bf16[224,2304]{1,0:T(8,128)(2,1)S(1)}, u32[]{:S(2)}, u32[]{:S(2)}) collective-permute-start(bf16[224,2304]{1,0:T(8,128)(2,1)S(1)} %collective-permute-done.10), channel_id=1, source_target_pairs={{0,48},{1,49},{2,50},{3,51},{8,56},{9,57},{10,58},{11,59},{16,0},{... | collective-permute-start | bytes 3096584 | tf_op jit(solution)/shard_map/ppermute | solution.py:44
  74.7 23.1 %collective-permute-start.5 = (bf16[768,512]{1,0:T(8,128)(2,1)S(1)}, bf16[768,512]{1,0:T(8,128)(2,1)S(1)}, u32[]{:S(2)}, u32[]{:S(2)}) collective-permute-start(bf16[768,512]{1,0:T(8,128)(2,1)S(1)} %collective-permute-done.1.refs_2_), channel_id=1, source_target_pairs={{0,1},{1,2},{2,3},{3,0},{8,9},{9,10},{10,11},{11,8},{16,17},{17,18... | collective-permute-start | bytes 2359304 | tf_op jit(solution)/shard_map/ppermute | solution.py:44
  74.7 23.1 %collective-permute-start.6 = (bf16[768,512]{1,0:T(8,128)(2,1)S(1)}, bf16[768,512]{1,0:T(8,128)(2,1)S(1)}, u32[]{:S(2)}, u32[]{:S(2)}) collective-permute-start(bf16[768,512]{1,0:T(8,128)(2,1)S(1)} %collective-permute-done.4.refs_5_), channel_id=1, source_target_pairs={{0,3},{1,0},{2,1},{3,2},{8,11},{9,8},{10,9},{11,10},{16,19},{17,16... | collective-permute-start | bytes 2359304 | tf_op jit(solution)/shard_map/ppermute | solution.py:44
  78.0 22.6 %collective-permute-start.18 = (bf16[448,576]{1,0:T(8,128)(2,1)S(1)}, bf16[448,576]{1,0:T(8,128)(2,1)S(1)}, u32[]{:S(2)}, u32[]{:S(2)}) collective-permute-start(bf16[448,576]{1,0:T(8,128)(2,1)S(1)} %collective-permute-done.13), channel_id=1, source_target_pairs={{0,64},{1,65},{2,66},{3,67},{8,72},{9,73},{10,74},{11,75},{16,80},... | collective-permute-start | bytes 1548296 | tf_op jit(solution)/shard_map/ppermute | solution.py:44
  102.8 25.1 %collective-permute-start.21 = (bf16[224,2304]{1,0:T(8,128)(2,1)}, bf16[224,2304]{1,0:T(8,128)(2,1)}, u32[]{:S(2)}, u32[]{:S(2)}) collective-permute-start(bf16[224,2304]{1,0:T(8,128)(2,1)} %collective-permute-done.11), channel_id=1, source_target_pairs={{0,16},{1,17},{2,18},{3,19},{8,24},{9,25},{10,26},{11,27},{16,32},... | collective-permute-start | bytes 3096584 | tf_op jit(solution)/shard_map/ppermute | solution.py:44
  103.4 25.8 %collective-permute-start.22 = (bf16[224,2304]{1,0:T(8,128)(2,1)S(1)}, bf16[224,2304]{1,0:T(8,128)(2,1)}, u32[]{:S(2)}, u32[]{:S(2)}) collective-permute-start(bf16[224,2304]{1,0:T(8,128)(2,1)S(1)} %collective-permute-done.17), channel_id=1, source_target_pairs={{0,48},{1,49},{2,50},{3,51},{8,56},{9,57},{10,58},{11,59},{16,0},{... | collective-permute-start | bytes 3096584 | tf_op jit(solution)/shard_map/ppermute | solution.py:44
  133.2 20.4 %collective-permute-start.28 = (bf16[448,576]{1,0:T(8,128)(2,1)}, bf16[448,576]{1,0:T(8,128)(2,1)S(1)}, u32[]{:S(2)}, u32[]{:S(2)}) collective-permute-start(bf16[448,576]{1,0:T(8,128)(2,1)} %copy-done.24), channel_id=1, source_target_pairs={{0,16},{1,17},{2,18},{3,19},{8,24},{9,25},{10,26},{11,27},{16,32},... | collective-permute-start | bytes 1548296 | tf_op jit(solution)/shard_map/ppermute | solution.py:44
  133.7 19.9 %collective-permute-start.29 = (bf16[448,576]{1,0:T(8,128)(2,1)}, bf16[448,576]{1,0:T(8,128)(2,1)S(1)}, u32[]{:S(2)}, u32[]{:S(2)}) collective-permute-start(bf16[448,576]{1,0:T(8,128)(2,1)} %copy-done.24), channel_id=1, source_target_pairs={{0,48},{1,49},{2,50},{3,51},{8,56},{9,57},{10,58},{11,59},{16,0},{... | collective-permute-start | bytes 1548296 | tf_op jit(solution)/shard_map/ppermute | solution.py:44
  153.8 24.1 %collective-permute-start.26 = (bf16[448,768]{1,0:T(8,128)(2,1)S(1)}, bf16[448,768]{1,0:T(8,128)(2,1)S(1)}, u32[]{:S(2)}, u32[]{:S(2)}) collective-permute-start(bf16[448,768]{1,0:T(8,128)(2,1)S(1)} %get-tuple-element.67), channel_id=1, source_target_pairs={{0,0},{1,1},{2,2},{3,3},{8,8},{9,9},{10,10},{11,11},{16,17},{17,18... | collective-permute-start | bytes 2064392 | tf_op jit(solution)/shard_map/ppermute | solution.py:44
  156.0 23.1 %collective-permute-start.27 = (bf16[448,768]{1,0:T(8,128)(2,1)S(1)}, bf16[448,768]{1,0:T(8,128)(2,1)S(1)}, u32[]{:S(2)}, u32[]{:S(2)}) collective-permute-start(bf16[448,768]{1,0:T(8,128)(2,1)S(1)} %get-tuple-element.68), channel_id=1, source_target_pairs={{0,6},{1,7},{2,4},{3,5},{8,14},{9,15},{10,12},{11,13},{16,23},{17,... | collective-permute-start | bytes 2064392 | tf_op jit(solution)/shard_map/ppermute | solution.py:44
  161.9 16.1 %collective-permute-start.34 = (bf16[448,576]{1,0:T(8,128)(2,1)S(1)}, bf16[448,576]{1,0:T(8,128)(2,1)S(1)}, u32[]{:S(2)}, u32[]{:S(2)}) collective-permute-start(bf16[448,576]{1,0:T(8,128)(2,1)S(1)} %copy-done.23), channel_id=1, source_target_pairs={{0,48},{1,49},{2,50},{3,51},{8,56},{9,57},{10,58},{11,59},{16,0},{... | collective-permute-start | bytes 1548296 | tf_op jit(solution)/shard_map/ppermute | solution.py:44
  164.5 39.7 %collective-permute-start.31 = (bf16[448,768]{1,0:T(8,128)(2,1)S(1)}, bf16[448,768]{1,0:T(8,128)(2,1)S(1)}, u32[]{:S(2)}, u32[]{:S(2)}) collective-permute-start(bf16[448,768]{1,0:T(8,128)(2,1)S(1)} %get-tuple-element.70), channel_id=1, source_target_pairs={{0,3},{1,0},{2,1},{3,2},{8,11},{9,8},{10,9},{11,10},{16,16},{17,17... | collective-permute-start | bytes 2064392 | tf_op jit(solution)/shard_map/ppermute | solution.py:44
  168.8 35.4 %collective-permute-start.32 = (bf16[448,768]{1,0:T(8,128)(2,1)S(1)}, bf16[448,768]{1,0:T(8,128)(2,1)S(1)}, u32[]{:S(2)}, u32[]{:S(2)}) collective-permute-start(bf16[448,768]{1,0:T(8,128)(2,1)S(1)} %get-tuple-element.71), channel_id=1, source_target_pairs={{0,1},{1,2},{2,3},{3,0},{8,9},{9,10},{10,11},{11,8},{16,18},{17,19... | collective-permute-start | bytes 2064392 | tf_op jit(solution)/shard_map/ppermute | solution.py:44
  178.0 15.9 %collective-permute-start.33 = (bf16[448,576]{1,0:T(8,128)(2,1)S(1)}, bf16[448,576]{1,0:T(8,128)(2,1)S(1)}, u32[]{:S(2)}, u32[]{:S(2)}) collective-permute-start(bf16[448,576]{1,0:T(8,128)(2,1)S(1)} %copy-done.23), channel_id=1, source_target_pairs={{0,16},{1,17},{2,18},{3,19},{8,24},{9,25},{10,26},{11,27},{16,32},... | collective-permute-start | bytes 1548296 | tf_op jit(solution)/shard_map/ppermute | solution.py:44
  179.1 25.1 %collective-permute-start.38 = (bf16[448,576]{1,0:T(8,128)(2,1)S(1)}, bf16[448,576]{1,0:T(8,128)(2,1)S(1)}, u32[]{:S(2)}, u32[]{:S(2)}) collective-permute-start(bf16[448,576]{1,0:T(8,128)(2,1)S(1)} %collective-permute-done.28), channel_id=1, source_target_pairs={{0,16},{1,17},{2,18},{3,19},{8,24},{9,25},{10,26},{11,27},{16,32},... | collective-permute-start | bytes 1548296 | tf_op jit(solution)/shard_map/ppermute | solution.py:44
  179.4 24.8 %collective-permute-start.39 = (bf16[448,576]{1,0:T(8,128)(2,1)S(1)}, bf16[448,576]{1,0:T(8,128)(2,1)S(1)}, u32[]{:S(2)}, u32[]{:S(2)}) collective-permute-start(bf16[448,576]{1,0:T(8,128)(2,1)S(1)} %collective-permute-done.34), channel_id=1, source_target_pairs={{0,48},{1,49},{2,50},{3,51},{8,56},{9,57},{10,58},{11,59},{16,0},{... | collective-permute-start | bytes 1548296 | tf_op jit(solution)/shard_map/ppermute | solution.py:44
  194.1 10.4 %collective-permute-start.35 = (bf16[2,448,576]{2,1,0:T(8,128)(2,1)S(1)}, bf16[2,448,576]{2,1,0:T(8,128)(2,1)S(1)}, u32[]{:S(2)}, u32[]{:S(2)}) collective-permute-start(bf16[2,448,576]{2,1,0:T(8,128)(2,1)S(1)} %pad_maximum_fusion.6.mine), channel_id=1, source_target_pairs={{0,8},{1,9},{2,10},{3,11},{8,0},{9,1},{10,2},{11,3},{16,24},{17,25... | collective-permute-start | bytes 3096584 | tf_op jit(solution)/shard_map/ppermute | solution.py:44
  207.1 56.4 %collective-permute-start.36 = (bf16[448,768]{1,0:T(8,128)(2,1)S(1)}, bf16[448,768]{1,0:T(8,128)(2,1)S(1)}, u32[]{:S(2)}, u32[]{:S(2)}) collective-permute-start(bf16[448,768]{1,0:T(8,128)(2,1)S(1)} %get-tuple-element.74), channel_id=1, source_target_pairs={{0,5},{1,6},{2,7},{3,4},{8,13},{9,14},{10,15},{11,12},{16,22},{17,... | collective-permute-start | bytes 2064392 | tf_op jit(solution)/shard_map/ppermute | solution.py:44
  210.8 52.7 %collective-permute-start.37 = (bf16[448,768]{1,0:T(8,128)(2,1)S(1)}, bf16[448,768]{1,0:T(8,128)(2,1)S(1)}, u32[]{:S(2)}, u32[]{:S(2)}) collective-permute-start(bf16[448,768]{1,0:T(8,128)(2,1)S(1)} %get-tuple-element.75), channel_id=1, source_target_pairs={{0,7},{1,4},{2,5},{3,6},{8,15},{9,12},{10,13},{11,14},{16,20},{17,... | collective-permute-start | bytes 2064392 | tf_op jit(solution)/shard_map/ppermute | solution.py:44
  215.3 48.2 %collective-permute-start.41 = (bf16[448,768]{1,0:T(8,128)(2,1)S(1)}, bf16[448,768]{1,0:T(8,128)(2,1)S(1)}, u32[]{:S(2)}, u32[]{:S(2)}) collective-permute-start(bf16[448,768]{1,0:T(8,128)(2,1)S(1)} %get-tuple-element.79), channel_id=1, source_target_pairs={{0,2},{1,3},{2,0},{3,1},{8,10},{9,11},{10,8},{11,9},{16,19},{17,16... | collective-permute-start | bytes 2064392 | tf_op jit(solution)/shard_map/ppermute | solution.py:44
  219.3 44.2 %collective-permute-start.42 = (bf16[448,768]{1,0:T(8,128)(2,1)S(1)}, bf16[448,768]{1,0:T(8,128)(2,1)S(1)}, u32[]{:S(2)}, u32[]{:S(2)}) collective-permute-start(bf16[448,768]{1,0:T(8,128)(2,1)S(1)} %get-tuple-element.80), channel_id=1, source_target_pairs={{0,4},{1,5},{2,6},{3,7},{8,12},{9,13},{10,14},{11,15},{16,21},{17,... | collective-permute-start | bytes 2064392 | tf_op jit(solution)/shard_map/ppermute | solution.py:44
  222.1 34.9 %collective-permute-start.43 = (f32[120,128]{1,0:T(8,128)S(1)}, f32[120,128]{1,0:T(8,128)S(1)}, u32[]{:S(2)}, u32[]{:S(2)}) collective-permute-start(f32[120,128]{1,0:T(8,128)S(1)} %max.41), channel_id=1, source_target_pairs={{0,64},{1,65},{2,66},{3,67},{8,72},{9,73},{10,74},{11,75},{16,80},... | collective-permute-start | bytes 184328 | tf_op jit(solution)/shard_map/ppermute | solution.py:44
  (43 other events, 450.6 us)

commit v6 on v5

--- a/solution.py
+++ b/solution.py
@@ -259,7 +259,9 @@
         in_specs=[pl.BlockSpec(memory_space=pltpu.SMEM)] + vmem(3),
         out_specs=vmem(count),
         compiler_params=pltpu.CompilerParams(vmem_limit_bytes=VMEM_LIMIT // 3),
-        cost_estimate=FREE,
+        cost_estimate=pl.CostEstimate(
+            flops=4 * rows * columns * depth, bytes_accessed=12 * rows * columns, transcendentals=0
+        ),
     )(info, hidden, mine, theirs)
 
 
@@ -349,36 +351,37 @@
     )
     info = jnp.where(jnp.arange(16) == 8, core, info)
 
+    down_pair = jnp.stack([down_block, down_far])
+    down_theirs = send(down_pair, other_core)
+    pairs[0] = after(pairs[0], down_theirs)
     early = token_sum(info, pieces, 0, pairs)
     early, own_ll, far_rr = lax.optimization_barrier((early, blocks[6], blocks[7]))
     every = step(after(every, early), lambda y, x, core, z: (y, x, core, z ^ 2))
     last = jnp.stack([own_ll, far_rr])
     last = [last, send(last, other_core)]
-    down_block = after(down_block, own_ll)
+    down_block, down_far = after(down_block, own_ll), after(down_far, own_ll)
     own_l, own_r = send(down_block, x_up), send(down_block, x_down)
-    down_pair = jnp.stack([down_block, down_far])
-    down_theirs = send(down_pair, other_core)
-    hidden = token_sum(info, pieces, 6, last, after(early, down_theirs, every), last=True)
+    far_l, far_r = send(down_far, x_up), send(down_far, x_down)
+    hidden = token_sum(info, pieces, 6, last, after(early, every), last=True)
 
     parts = []
 
-    def sums(mine):
-        mine = jnp.stack(mine)
+    def sums(mine, *before):
+        mine = jnp.stack(mine) if parts else down_pair
         theirs = send(mine, other_core) if parts else down_theirs
         terms = down_terms(info, hidden, mine, theirs)
         for term in terms:
-            parts.append(send(term, to_chunk(*ORDER[len(parts)])))
+            parts.append(send(after(term, *before), to_chunk(*ORDER[len(parts)])))
         return terms
 
-    terms = sums([down_block, down_far])
-    far = after(down_far, own_l, own_r)
-    far_l, far_r = send(far, x_up), send(far, x_down)
+    every = step(every, y_far)
+    terms = sums((), every)
     terms = sums([after(own_l, *terms), own_r])
-    sums([far_l, after(far_r, *terms, *parts[:2])])
-    own_l, far_r, *_ = lax.optimization_barrier((own_l, far_r, *parts[:2], *terms))
-    terms = sums([after(send(own_l, x_up), *parts[2:4]), send(far_r, x_down)])
-    every = step(after(every, *terms), y_far)
-    every = step(every, lambda y, x, core, z: (y, x ^ 2, core, z))
+    own_l, far_r, *_ = lax.optimization_barrier((own_l, far_r, far_l, *parts[:2], *terms))
+    own_ll, far_rr = send(own_l, x_up), send(far_r, x_down)
+    terms = sums([far_l, after(far_r, *terms)])
+    terms = sums([own_ll, after(far_rr, *terms, *parts[2:4])])
+    every = step(after(every, *terms), lambda y, x, core, z: (y, x ^ 2, core, z))
     log_amax = jnp.log(
         jnp.stack([every[k * rows : k * rows + D // BLOCK, : FF // BLOCK] for k in range(3)]) + EPS
     )

time: 267 us -> 266 us (level); the launches traced: 265 us -> 261 us
  waiting for transfers between devices: 138 us -> 119 us
  starting transfers between devices: 59.7 us -> 71 us
    ppermute x45, waiting for transfers between devices: 138 us -> 119 us  [send(): return lax.ppermute(array, AXES, pairs)]
    ppermute x45, starting transfers between devices: 59.7 us -> 71 us  [send(): return lax.ppermute(array, AXES, pairs)]
    unnamed x58 -> x64, local copies, waits for them, and re-layouts: 4.41 us -> 5.4 us
  transfers between devices with their start and end apart: 45 -> 45, of which waited for: 18 -> 18; matrix products, arithmetic and copies ran while one was open for 7% -> 8% of each run, Pallas kernels for 14% -> 14%
where the time goes in v6:
time: 266 us; the launch traced here: 261 us
  waiting for transfers between devices  119 us (45%)
  starting transfers between devices  71 us (27%)
  Pallas kernels  36.9 us (14%)
  other arithmetic  23.3 us (9%)
  local copies, waits for them, and re-layouts  8.7 us (3%)
    ppermute x45, waiting for transfers between devices, send(): return lax.ppermute(array, AXES, pairs)  119 us
    ppermute x45, starting transfers between devices, send(): return lax.ppermute(array, AXES, pairs)  71 us
    pallas_call x2, Pallas kernels, token_sum(): pl.pallas_call(functools.partial(token_kernel, len(blocks), first, before...  26.7 us
    pallas_call x4, Pallas kernels, down_terms(): pl.pallas_call(down_kernel, out_shape=[jax.ShapeDtypeStruct((columns, row...  10.2 us
    another operation x3, other arithmetic, swap(): pair = jnp.stack(blocks[n:n + 2])  5.87 us
    unnamed x64, local copies, waits for them, and re-layouts  5.4 us
  transfers between devices with their start and end apart: 45, of which 18 were waited for; matrix products, arithmetic and copies ran while one was open for 8% of the time, Pallas kernels for 14%

profile of v6, /device:TPU:6, one launch (start us, length us, event | category | flops | bytes accessed | tf_op | source)
XLA Modules:
  0.0 261.0 jit_solution(17283935404166764190)
XLA Ops:
  2.1 4.1 %collective-permute-start.2 = (bf16[768,512]{1,0:T(8,128)(2,1)S(1)}, bf16[768,512]{1,0:T(8,128)(2,1)S(1)}, u32[]{:S(2)}, u32[]{:S(2)}) collective-permute-start(bf16[768,512]{1,0:T(8,128)(2,1)S(1)} %fusion.1.refs_0_), channel_id=1, source_target_pairs={{0,3},{1,0},{2,1},{3,2},{8,11},{9,8},{10,9},{11,10},{16,19},{17,16... | collective-permute-start | bytes 2359304 | tf_op jit(solution)/shard_map/ppermute | solution.py:44
  16.7 3.4 %collective-permute-done.8 = f32[120,128]{1,0:T(8,128)S(1)} collective-permute-done((f32[120,128]{1,0:T(8,128)S(1)}, f32[120,128]{1,0:T(8,128)S(1)}, u32[]{:S(2)}, u32[]{:S(2)}) %collective-permute-start.8) | collective-permute-done | bytes 61472 | tf_op jit(solution)/shard_map/ppermute | solution.py:44
  21.6 3.7 %multiply_convert_fusion.2 = (bf16[224,1152]{1,0:T(8,128)(2,1)S(1)}, bf16[224,1152]{1,0:T(8,128)(2,1)S(1)}) fusion(f32[224,1152]{1,0:T(8,128)} %param.6, f32[1152]{0:T(1024)S(1)} %get-tuple-element.101, f32[1152]{0:T(1024)S(1)} %get-tuple-element.102, f32[1152]{0:T(1024)S(1)} %get-tuple-element.100, pred[224]{0:T(512)(128)(4,1)S(1)} %broadcast_compare_fusion.23, ...), kind=kLoop, calls=%fused_computation.20 | loop fusion | flops 9289728 | bytes 3124896 | tf_op jit(solution)/shard_map/convert_element_type | solution.py:129
  28.8 2.9 %collective-permute-start.10 = (bf16[224,2304]{1,0:T(8,128)(2,1)S(1)}, bf16[224,2304]{1,0:T(8,128)(2,1)S(1)}, u32[]{:S(2)}, u32[]{:S(2)}) collective-permute-start(bf16[224,2304]{1,0:T(8,128)(2,1)S(1)} %pad_maximum_fusion.8), channel_id=1, source_target_pairs={{0,64},{1,65},{2,66},{3,67},{8,72},{9,73},{10,74},{11,75},{16,80},... | collective-permute-start | bytes 3096584 | tf_op jit(solution)/shard_map/ppermute | solution.py:44
  31.7 3.4 %collective-permute-start.4 = (bf16[768,512]{1,0:T(8,128)(2,1)S(1)}, bf16[768,512]{1,0:T(8,128)(2,1)S(1)}, u32[]{:S(2)}, u32[]{:S(2)}) collective-permute-start(bf16[768,512]{1,0:T(8,128)(2,1)S(1)} %collective-permute-done.refs_1_), channel_id=1, source_target_pairs={{0,3},{1,0},{2,1},{3,2},{8,11},{9,8},{10,9},{11,10},{16,19},{17,16... | collective-permute-start | bytes 2359304 | tf_op jit(solution)/shard_map/ppermute | solution.py:44
  37.4 13.1 %collective-permute-done.4.refs_5_ = bf16[768,512]{1,0:T(8,128)(2,1)S(1)} collective-permute-done((bf16[768,512]{1,0:T(8,128)(2,1)S(1)}, bf16[768,512]{1,0:T(8,128)(2,1)S(1)}, u32[]{:S(2)}, u32[]{:S(2)}) %collective-permute-start.4) | collective-permute-done | bytes 786464 | tf_op jit(solution)/shard_map/ppermute | solution.py:44
  50.6 3.4 %collective-permute-done.3.refs_4_ = bf16[768,512]{1,0:T(8,128)(2,1)S(1)} collective-permute-done((bf16[768,512]{1,0:T(8,128)(2,1)S(1)}, bf16[768,512]{1,0:T(8,128)(2,1)S(1)}, u32[]{:S(2)}, u32[]{:S(2)}) %collective-permute-start.3) | collective-permute-done | bytes 786464 | tf_op jit(solution)/shard_map/ppermute | solution.py:44
  57.5 3.8 %collective-permute-done.14 = f32[120,128]{1,0:T(8,128)S(1)} collective-permute-done((f32[120,128]{1,0:T(8,128)S(1)}, f32[120,128]{1,0:T(8,128)S(1)}, u32[]{:S(2)}, u32[]{:S(2)}) %collective-permute-start.14) | collective-permute-done | bytes 61472 | tf_op jit(solution)/shard_map/ppermute | solution.py:44
  62.0 10.2 %collective-permute-done.13 = bf16[448,576]{1,0:T(8,128)(2,1)S(1)} collective-permute-done((bf16[448,576]{1,0:T(8,128)(2,1)S(1)}, bf16[448,576]{1,0:T(8,128)(2,1)S(1)}, u32[]{:S(2)}, u32[]{:S(2)}) %collective-permute-start.13) | collective-permute-done | bytes 516128 | tf_op jit(solution)/shard_map/ppermute | solution.py:44
  74.7 3.2 %collective-permute-start.6 = (bf16[768,512]{1,0:T(8,128)(2,1)S(1)}, bf16[768,512]{1,0:T(8,128)(2,1)S(1)}, u32[]{:S(2)}, u32[]{:S(2)}) collective-permute-start(bf16[768,512]{1,0:T(8,128)(2,1)S(1)} %collective-permute-done.4.refs_5_), channel_id=1, source_target_pairs={{0,3},{1,0},{2,1},{3,2},{8,11},{9,8},{10,9},{11,10},{16,19},{17,16... | collective-permute-start | bytes 2359304 | tf_op jit(solution)/shard_map/ppermute | solution.py:44
  79.4 18.3 %collective-permute-done.18 = bf16[224,2304]{1,0:T(8,128)(2,1)S(1)} collective-permute-done((bf16[224,2304]{1,0:T(8,128)(2,1)S(1)}, bf16[224,2304]{1,0:T(8,128)(2,1)S(1)}, u32[]{:S(2)}, u32[]{:S(2)}) %collective-permute-start.18) | collective-permute-done | bytes 1032224 | tf_op jit(solution)/shard_map/ppermute | solution.py:44
  99.1 2.7 %pad_maximum_fusion.2.refs_12_ = bf16[2,224,2304]{2,1,0:T(8,128)(2,1)} fusion(bf16[1,224,2304]{2,1,0:T(8,128)(2,1)} %bitcast.27, bf16[1,224,2304]{2,1,0:T(8,128)(2,1)S(1)} %bitcast.54), kind=kLoop, calls=%fused_computation.2 | loop fusion | flops 1032192 | bytes 4128768 | tf_op jit(solution)/shard_map/stack | solution.py:326
  101.9 3.0 %pad_maximum_fusion.1.refs_10_ = bf16[2,224,2304]{2,1,0:T(8,128)(2,1)} fusion(bf16[1,224,2304]{2,1,0:T(8,128)(2,1)S(1)} %bitcast.52, bf16[1,224,2304]{2,1,0:T(8,128)(2,1)} %bitcast.24), kind=kLoop, calls=%fused_computation.1 | loop fusion | flops 1032192 | bytes 4128768 | tf_op jit(solution)/shard_map/stack | solution.py:326
  111.8 19.8 %shard_map.68.refs_8_ = f32[768,2304]{1,0:T(8,128)} custom-call(s32[16]{0:T(128)} %compare_select_fusion.5.info, bf16[768,512]{1,0:T(8,128)(2,1)} %copy-done.1, bf16[768,512]{1,0:T(8,128)(2,1)} %copy-done.7, bf16[768,512]{1,0:T(8,128)(2,1)} %copy-done.5, bf16[768,512]{1,0:T(8,128)(2,1)} %copy-done.3, bf16[768,512]{1,0:T(8,128)(2,1)} %copy-done.11, ...), custom_call_target="tpu_custom_call" | custom-call | tf_op jit(solution)/shard_map/pallas_call | solution.py:213
  137.0 5.7 %collective-permute-done.24 = f32[120,128]{1,0:T(8,128)S(1)} collective-permute-done((f32[120,128]{1,0:T(8,128)S(1)}, f32[120,128]{1,0:T(8,128)S(1)}, u32[]{:S(2)}, u32[]{:S(2)}) %collective-permute-start.24) | collective-permute-done | bytes 61472 | tf_op jit(solution)/shard_map/ppermute | solution.py:44
  142.9 3.0 %copy-done = f32[768,2304]{1,0:T(8,128)S(1)} copy-done((f32[768,2304]{1,0:T(8,128)S(1)}, f32[768,2304]{1,0:T(8,128)}, u32[]{:S(2)}) %copy-start) | copy-done | bytes 7077912
  145.9 6.9 %shard_map.69.hidden = bf16[768,1152]{1,0:T(8,128)(2,1)S(1)} custom-call(s32[16]{0:T(128)S(1)} %copy-done.17, bf16[768,512]{1,0:T(8,128)(2,1)S(1)} %copy-done.2, bf16[768,512]{1,0:T(8,128)(2,1)S(1)} %copy-done.8, bf16[768,512]{1,0:T(8,128)(2,1)S(1)} %copy-done.6, bf16[768,512]{1,0:T(8,128)(2,1)S(1)} %copy-done.4, bf16[768,512]{1,0:T(8,128)(2,1)S(1)} %copy-done.12, ...), custom_call_target="tpu_custom_call" | custom-call | tf_op jit(solution)/shard_map/pallas_call | solution.py:213
  152.8 2.6 shard_map.70
  157.4 4.2 %collective-permute-done.26 = f32[120,128]{1,0:T(8,128)S(1)} collective-permute-done((f32[120,128]{1,0:T(8,128)S(1)}, f32[120,128]{1,0:T(8,128)S(1)}, u32[]{:S(2)}, u32[]{:S(2)}) %collective-permute-start.26) | collective-permute-done | bytes 61472 | tf_op jit(solution)/shard_map/ppermute | solution.py:44
  164.2 6.5 %collective-permute-start.27 = (bf16[448,768]{1,0:T(8,128)(2,1)S(1)}, bf16[448,768]{1,0:T(8,128)(2,1)S(1)}, u32[]{:S(2)}, u32[]{:S(2)}) collective-permute-start(bf16[448,768]{1,0:T(8,128)(2,1)S(1)} %get-tuple-element.71), channel_id=1, source_target_pairs={{0,0},{1,1},{2,2},{3,3},{8,8},{9,9},{10,10},{11,11},{16,17},{17,18... | collective-permute-start | bytes 2064392 | tf_op jit(solution)/shard_map/ppermute | solution.py:44
  170.8 3.2 %collective-permute-start.34 = (bf16[448,576]{1,0:T(8,128)(2,1)S(1)}, bf16[448,576]{1,0:T(8,128)(2,1)S(1)}, u32[]{:S(2)}, u32[]{:S(2)}) collective-permute-start(bf16[448,576]{1,0:T(8,128)(2,1)S(1)} %copy-done.26), channel_id=1, source_target_pairs={{0,16},{1,17},{2,18},{3,19},{8,24},{9,25},{10,26},{11,27},{16,32},... | collective-permute-start | bytes 1548296 | tf_op jit(solution)/shard_map/ppermute | solution.py:44
  174.0 2.5 shard_map.71
  176.6 8.8 %collective-permute-done.35 = bf16[448,576]{1,0:T(8,128)(2,1)S(1)} collective-permute-done((bf16[448,576]{1,0:T(8,128)(2,1)S(1)}, bf16[448,576]{1,0:T(8,128)(2,1)S(1)}, u32[]{:S(2)}, u32[]{:S(2)}) %collective-permute-start.35) | collective-permute-done | bytes 516128 | tf_op jit(solution)/shard_map/ppermute | solution.py:44
  186.4 3.0 %collective-permute-start.32 = (bf16[448,768]{1,0:T(8,128)(2,1)S(1)}, bf16[448,768]{1,0:T(8,128)(2,1)S(1)}, u32[]{:S(2)}, u32[]{:S(2)}) collective-permute-start(bf16[448,768]{1,0:T(8,128)(2,1)S(1)} %get-tuple-element.76), channel_id=1, source_target_pairs={{0,3},{1,0},{2,1},{3,2},{8,11},{9,8},{10,9},{11,10},{16,16},{17,17... | collective-permute-start | bytes 2064392 | tf_op jit(solution)/shard_map/ppermute | solution.py:44
  191.9 3.9 %collective-permute-start.39 = (bf16[448,576]{1,0:T(8,128)(2,1)S(1)}, bf16[448,576]{1,0:T(8,128)(2,1)S(1)}, u32[]{:S(2)}, u32[]{:S(2)}) collective-permute-start(bf16[448,576]{1,0:T(8,128)(2,1)S(1)} %collective-permute-done.29), channel_id=1, source_target_pairs={{0,16},{1,17},{2,18},{3,19},{8,24},{9,25},{10,26},{11,27},{16,32},... | collective-permute-start | bytes 1548296 | tf_op jit(solution)/shard_map/ppermute | solution.py:44
  198.4 10.4 %collective-permute-done.40 = bf16[448,576]{1,0:T(8,128)(2,1)S(1)} collective-permute-done((bf16[448,576]{1,0:T(8,128)(2,1)S(1)}, bf16[448,576]{1,0:T(8,128)(2,1)S(1)}, u32[]{:S(2)}, u32[]{:S(2)}) %collective-permute-start.40) | collective-permute-done | bytes 516128 | tf_op jit(solution)/shard_map/ppermute | solution.py:44
  211.0 3.3 %collective-permute-start.37 = (bf16[448,768]{1,0:T(8,128)(2,1)S(1)}, bf16[448,768]{1,0:T(8,128)(2,1)S(1)}, u32[]{:S(2)}, u32[]{:S(2)}) collective-permute-start(bf16[448,768]{1,0:T(8,128)(2,1)S(1)} %get-tuple-element.81), channel_id=1, source_target_pairs={{0,5},{1,6},{2,7},{3,4},{8,13},{9,14},{10,15},{11,12},{16,22},{17,... | collective-permute-start | bytes 2064392 | tf_op jit(solution)/shard_map/ppermute | solution.py:44
  216.8 3.4 %collective-permute-start.43 = (bf16[448,768]{1,0:T(8,128)(2,1)S(1)}, bf16[448,768]{1,0:T(8,128)(2,1)S(1)}, u32[]{:S(2)}, u32[]{:S(2)}) collective-permute-start(bf16[448,768]{1,0:T(8,128)(2,1)S(1)} %get-tuple-element.86), channel_id=1, source_target_pairs={{0,4},{1,5},{2,6},{3,7},{8,12},{9,13},{10,14},{11,15},{16,21},{17,... | collective-permute-start | bytes 2064392 | tf_op jit(solution)/shard_map/ppermute | solution.py:44
  220.3 2.7 %collective-permute-start.42 = (bf16[448,768]{1,0:T(8,128)(2,1)S(1)}, bf16[448,768]{1,0:T(8,128)(2,1)S(1)}, u32[]{:S(2)}, u32[]{:S(2)}) collective-permute-start(bf16[448,768]{1,0:T(8,128)(2,1)S(1)} %get-tuple-element.85), channel_id=1, source_target_pairs={{0,2},{1,3},{2,0},{3,1},{8,10},{9,11},{10,8},{11,9},{16,19},{17,16... | collective-permute-start | bytes 2064392 | tf_op jit(solution)/shard_map/ppermute | solution.py:44
  223.0 4.0 %collective-permute-start.44 = (f32[120,128]{1,0:T(8,128)S(1)}, f32[120,128]{1,0:T(8,128)S(1)}, u32[]{:S(2)}, u32[]{:S(2)}) collective-permute-start(f32[120,128]{1,0:T(8,128)S(1)} %max.42), channel_id=1, source_target_pairs={{0,32},{1,33},{2,34},{3,35},{8,40},{9,41},{10,42},{11,43},{16,48},... | collective-permute-start | bytes 184328 | tf_op jit(solution)/shard_map/ppermute | solution.py:44
  231.7 11.7 %collective-permute-done.37 = bf16[448,768]{1,0:T(8,128)(2,1)S(1)} collective-permute-done((bf16[448,768]{1,0:T(8,128)(2,1)S(1)}, bf16[448,768]{1,0:T(8,128)(2,1)S(1)}, u32[]{:S(2)}, u32[]{:S(2)}) %collective-permute-start.37) | collective-permute-done | bytes 688160 | tf_op jit(solution)/shard_map/ppermute | solution.py:44
  243.3 16.1 %collective-permute-done.43 = bf16[448,768]{1,0:T(8,128)(2,1)S(1)} collective-permute-done((bf16[448,768]{1,0:T(8,128)(2,1)S(1)}, bf16[448,768]{1,0:T(8,128)(2,1)S(1)}, u32[]{:S(2)}, u32[]{:S(2)}) %collective-permute-start.43) | collective-permute-done | bytes 688160 | tf_op jit(solution)/shard_map/ppermute | solution.py:44
  (209 shorter events, 62.1 us)
Async XLA Ops:
  2.1 26.7 %collective-permute-start.2 = (bf16[768,512]{1,0:T(8,128)(2,1)S(1)}, bf16[768,512]{1,0:T(8,128)(2,1)S(1)}, u32[]{:S(2)}, u32[]{:S(2)}) collective-permute-start(bf16[768,512]{1,0:T(8,128)(2,1)S(1)} %fusion.1.refs_0_), channel_id=1, source_target_pairs={{0,3},{1,0},{2,1},{3,2},{8,11},{9,8},{10,9},{11,10},{16,19},{17,16... | collective-permute-start | bytes 2359304 | tf_op jit(solution)/shard_map/ppermute | solution.py:44
  6.2 25.5 %collective-permute-start.1 = (bf16[768,512]{1,0:T(8,128)(2,1)S(1)}, bf16[768,512]{1,0:T(8,128)(2,1)S(1)}, u32[]{:S(2)}, u32[]{:S(2)}) collective-permute-start(bf16[768,512]{1,0:T(8,128)(2,1)S(1)} %fusion.1.refs_0_), channel_id=1, source_target_pairs={{0,1},{1,2},{2,3},{3,0},{8,9},{9,10},{10,11},{11,8},{16,17},{17,18... | collective-permute-start | bytes 2359304 | tf_op jit(solution)/shard_map/ppermute | solution.py:44
  6.2 25.5 %collective-permute-start = (bf16[768,512]{1,0:T(8,128)(2,1)S(1)}, bf16[768,512]{1,0:T(8,128)(2,1)S(1)}, u32[]{:S(2)}, u32[]{:S(2)}) collective-permute-start(bf16[768,512]{1,0:T(8,128)(2,1)S(1)} %fusion.1.refs_0_), channel_id=1, source_target_pairs={{0,4},{1,5},{2,6},{3,7},{8,12},{9,13},{10,14},{11,15},{16,20},{17,... | collective-permute-start | bytes 2359304 | tf_op jit(solution)/shard_map/ppermute | solution.py:44
  25.4 36.6 %collective-permute-start.12 = (bf16[224,2304]{1,0:T(8,128)(2,1)S(1)}, bf16[224,2304]{1,0:T(8,128)(2,1)S(1)}, u32[]{:S(2)}, u32[]{:S(2)}) collective-permute-start(bf16[224,2304]{1,0:T(8,128)(2,1)S(1)} %pad_maximum_fusion.8), channel_id=1, source_target_pairs={{0,48},{1,49},{2,50},{3,51},{8,56},{9,57},{10,58},{11,59},{16,0},{... | collective-permute-start | bytes 3096584 | tf_op jit(solution)/shard_map/ppermute | solution.py:44
  26.3 35.7 %collective-permute-start.11 = (bf16[224,2304]{1,0:T(8,128)(2,1)S(1)}, bf16[224,2304]{1,0:T(8,128)(2,1)}, u32[]{:S(2)}, u32[]{:S(2)}) collective-permute-start(bf16[224,2304]{1,0:T(8,128)(2,1)S(1)} %pad_maximum_fusion.8), channel_id=1, source_target_pairs={{0,16},{1,17},{2,18},{3,19},{8,24},{9,25},{10,26},{11,27},{16,32},... | collective-permute-start | bytes 3096584 | tf_op jit(solution)/shard_map/ppermute | solution.py:44
  28.8 33.2 %collective-permute-start.10 = (bf16[224,2304]{1,0:T(8,128)(2,1)S(1)}, bf16[224,2304]{1,0:T(8,128)(2,1)S(1)}, u32[]{:S(2)}, u32[]{:S(2)}) collective-permute-start(bf16[224,2304]{1,0:T(8,128)(2,1)S(1)} %pad_maximum_fusion.8), channel_id=1, source_target_pairs={{0,64},{1,65},{2,66},{3,67},{8,72},{9,73},{10,74},{11,75},{16,80},... | collective-permute-start | bytes 3096584 | tf_op jit(solution)/shard_map/ppermute | solution.py:44
  31.7 18.8 %collective-permute-start.4 = (bf16[768,512]{1,0:T(8,128)(2,1)S(1)}, bf16[768,512]{1,0:T(8,128)(2,1)S(1)}, u32[]{:S(2)}, u32[]{:S(2)}) collective-permute-start(bf16[768,512]{1,0:T(8,128)(2,1)S(1)} %collective-permute-done.refs_1_), channel_id=1, source_target_pairs={{0,3},{1,0},{2,1},{3,2},{8,11},{9,8},{10,9},{11,10},{16,19},{17,16... | collective-permute-start | bytes 2359304 | tf_op jit(solution)/shard_map/ppermute | solution.py:44
  35.1 18.8 %collective-permute-start.3 = (bf16[768,512]{1,0:T(8,128)(2,1)S(1)}, bf16[768,512]{1,0:T(8,128)(2,1)S(1)}, u32[]{:S(2)}, u32[]{:S(2)}) collective-permute-start(bf16[768,512]{1,0:T(8,128)(2,1)S(1)} %collective-permute-done.refs_1_), channel_id=1, source_target_pairs={{0,1},{1,2},{2,3},{3,0},{8,9},{9,10},{10,11},{11,8},{16,17},{17,18... | collective-permute-start | bytes 2359304 | tf_op jit(solution)/shard_map/ppermute | solution.py:44
  54.9 17.3 %collective-permute-start.13 = (bf16[448,576]{1,0:T(8,128)(2,1)S(1)}, bf16[448,576]{1,0:T(8,128)(2,1)S(1)}, u32[]{:S(2)}, u32[]{:S(2)}) collective-permute-start(bf16[448,576]{1,0:T(8,128)(2,1)S(1)} %fusion.3), channel_id=1, source_target_pairs={{0,0},{1,16},{2,32},{3,48},{8,8},{9,24},{10,40},{11,56},{16,49},{1... | collective-permute-start | bytes 1548296 | tf_op jit(solution)/shard_map/ppermute | solution.py:44
  72.6 25.2 %collective-permute-start.18 = (bf16[224,2304]{1,0:T(8,128)(2,1)S(1)}, bf16[224,2304]{1,0:T(8,128)(2,1)S(1)}, u32[]{:S(2)}, u32[]{:S(2)}) collective-permute-start(bf16[224,2304]{1,0:T(8,128)(2,1)S(1)} %collective-permute-done.10), channel_id=1, source_target_pairs={{0,16},{1,17},{2,18},{3,19},{8,24},{9,25},{10,26},{11,27},{16,32},... | collective-permute-start | bytes 3096584 | tf_op jit(solution)/shard_map/ppermute | solution.py:44
  72.6 26.4 %collective-permute-start.19 = (bf16[224,2304]{1,0:T(8,128)(2,1)S(1)}, bf16[224,2304]{1,0:T(8,128)(2,1)}, u32[]{:S(2)}, u32[]{:S(2)}) collective-permute-start(bf16[224,2304]{1,0:T(8,128)(2,1)S(1)} %collective-permute-done.10), channel_id=1, source_target_pairs={{0,48},{1,49},{2,50},{3,51},{8,56},{9,57},{10,58},{11,59},{16,0},{... | collective-permute-start | bytes 3096584 | tf_op jit(solution)/shard_map/ppermute | solution.py:44
  74.7 23.1 %collective-permute-start.5 = (bf16[768,512]{1,0:T(8,128)(2,1)S(1)}, bf16[768,512]{1,0:T(8,128)(2,1)S(1)}, u32[]{:S(2)}, u32[]{:S(2)}) collective-permute-start(bf16[768,512]{1,0:T(8,128)(2,1)S(1)} %collective-permute-done.1.refs_2_), channel_id=1, source_target_pairs={{0,1},{1,2},{2,3},{3,0},{8,9},{9,10},{10,11},{11,8},{16,17},{17,18... | collective-permute-start | bytes 2359304 | tf_op jit(solution)/shard_map/ppermute | solution.py:44
  74.7 23.1 %collective-permute-start.6 = (bf16[768,512]{1,0:T(8,128)(2,1)S(1)}, bf16[768,512]{1,0:T(8,128)(2,1)S(1)}, u32[]{:S(2)}, u32[]{:S(2)}) collective-permute-start(bf16[768,512]{1,0:T(8,128)(2,1)S(1)} %collective-permute-done.4.refs_5_), channel_id=1, source_target_pairs={{0,3},{1,0},{2,1},{3,2},{8,11},{9,8},{10,9},{11,10},{16,19},{17,16... | collective-permute-start | bytes 2359304 | tf_op jit(solution)/shard_map/ppermute | solution.py:44
  77.9 24.0 %collective-permute-start.16 = (bf16[448,576]{1,0:T(8,128)(2,1)S(1)}, bf16[448,576]{1,0:T(8,128)(2,1)S(1)}, u32[]{:S(2)}, u32[]{:S(2)}) collective-permute-start(bf16[448,576]{1,0:T(8,128)(2,1)S(1)} %collective-permute-done.13), channel_id=1, source_target_pairs={{0,64},{1,65},{2,66},{3,67},{8,72},{9,73},{10,74},{11,75},{16,80},... | collective-permute-start | bytes 1548296 | tf_op jit(solution)/shard_map/ppermute | solution.py:44
  105.7 26.0 %collective-permute-start.22 = (bf16[224,2304]{1,0:T(8,128)(2,1)}, bf16[224,2304]{1,0:T(8,128)(2,1)}, u32[]{:S(2)}, u32[]{:S(2)}) collective-permute-start(bf16[224,2304]{1,0:T(8,128)(2,1)} %collective-permute-done.11), channel_id=1, source_target_pairs={{0,16},{1,17},{2,18},{3,19},{8,24},{9,25},{10,26},{11,27},{16,32},... | collective-permute-start | bytes 3096584 | tf_op jit(solution)/shard_map/ppermute | solution.py:44
  106.5 26.4 %collective-permute-start.23 = (bf16[224,2304]{1,0:T(8,128)(2,1)}, bf16[224,2304]{1,0:T(8,128)(2,1)}, u32[]{:S(2)}, u32[]{:S(2)}) collective-permute-start(bf16[224,2304]{1,0:T(8,128)(2,1)} %collective-permute-done.19), channel_id=1, source_target_pairs={{0,48},{1,49},{2,50},{3,51},{8,56},{9,57},{10,58},{11,59},{16,0},{... | collective-permute-start | bytes 3096584 | tf_op jit(solution)/shard_map/ppermute | solution.py:44
  134.9 20.4 %collective-permute-start.29 = (bf16[448,576]{1,0:T(8,128)(2,1)S(1)}, bf16[448,576]{1,0:T(8,128)(2,1)S(1)}, u32[]{:S(2)}, u32[]{:S(2)}) collective-permute-start(bf16[448,576]{1,0:T(8,128)(2,1)S(1)} %copy-done.24), channel_id=1, source_target_pairs={{0,16},{1,17},{2,18},{3,19},{8,24},{9,25},{10,26},{11,27},{16,32},... | collective-permute-start | bytes 1548296 | tf_op jit(solution)/shard_map/ppermute | solution.py:44
  135.3 20.1 %collective-permute-start.30 = (bf16[448,576]{1,0:T(8,128)(2,1)S(1)}, bf16[448,576]{1,0:T(8,128)(2,1)S(1)}, u32[]{:S(2)}, u32[]{:S(2)}) collective-permute-start(bf16[448,576]{1,0:T(8,128)(2,1)S(1)} %copy-done.24), channel_id=1, source_target_pairs={{0,48},{1,49},{2,50},{3,51},{8,56},{9,57},{10,58},{11,59},{16,0},{... | collective-permute-start | bytes 1548296 | tf_op jit(solution)/shard_map/ppermute | solution.py:44
  155.5 18.5 %collective-permute-start.31 = (bf16[2,448,576]{2,1,0:T(8,128)(2,1)S(1)}, bf16[2,448,576]{2,1,0:T(8,128)(2,1)S(1)}, u32[]{:S(2)}, u32[]{:S(2)}) collective-permute-start(bf16[2,448,576]{2,1,0:T(8,128)(2,1)S(1)} %pad_maximum_fusion.5.mine), channel_id=1, source_target_pairs={{0,8},{1,9},{2,10},{3,11},{8,0},{9,1},{10,2},{11,3},{16,24},{17,25... | collective-permute-start | bytes 3096584 | tf_op jit(solution)/shard_map/ppermute | solution.py:44
  161.7 23.7 %collective-permute-start.28 = (bf16[448,768]{1,0:T(8,128)(2,1)S(1)}, bf16[448,768]{1,0:T(8,128)(2,1)S(1)}, u32[]{:S(2)}, u32[]{:S(2)}) collective-permute-start(bf16[448,768]{1,0:T(8,128)(2,1)S(1)} %get-tuple-element.73), channel_id=1, source_target_pairs={{0,6},{1,7},{2,4},{3,5},{8,14},{9,15},{10,12},{11,13},{16,23},{17,... | collective-permute-start | bytes 2064392 | tf_op jit(solution)/shard_map/ppermute | solution.py:44
  164.2 21.2 %collective-permute-start.27 = (bf16[448,768]{1,0:T(8,128)(2,1)S(1)}, bf16[448,768]{1,0:T(8,128)(2,1)S(1)}, u32[]{:S(2)}, u32[]{:S(2)}) collective-permute-start(bf16[448,768]{1,0:T(8,128)(2,1)S(1)} %get-tuple-element.71), channel_id=1, source_target_pairs={{0,0},{1,1},{2,2},{3,3},{8,8},{9,9},{10,10},{11,11},{16,17},{17,18... | collective-permute-start | bytes 2064392 | tf_op jit(solution)/shard_map/ppermute | solution.py:44
  170.7 14.6 %collective-permute-start.35 = (bf16[448,576]{1,0:T(8,128)(2,1)S(1)}, bf16[448,576]{1,0:T(8,128)(2,1)S(1)}, u32[]{:S(2)}, u32[]{:S(2)}) collective-permute-start(bf16[448,576]{1,0:T(8,128)(2,1)S(1)} %copy-done.26), channel_id=1, source_target_pairs={{0,48},{1,49},{2,50},{3,51},{8,56},{9,57},{10,58},{11,59},{16,0},{... | collective-permute-start | bytes 1548296 | tf_op jit(solution)/shard_map/ppermute | solution.py:44
  170.8 14.6 %collective-permute-start.34 = (bf16[448,576]{1,0:T(8,128)(2,1)S(1)}, bf16[448,576]{1,0:T(8,128)(2,1)S(1)}, u32[]{:S(2)}, u32[]{:S(2)}) collective-permute-start(bf16[448,576]{1,0:T(8,128)(2,1)S(1)} %copy-done.26), channel_id=1, source_target_pairs={{0,16},{1,17},{2,18},{3,19},{8,24},{9,25},{10,26},{11,27},{16,32},... | collective-permute-start | bytes 1548296 | tf_op jit(solution)/shard_map/ppermute | solution.py:44
  185.6 10.3 %collective-permute-start.36 = (bf16[2,448,576]{2,1,0:T(8,128)(2,1)S(1)}, bf16[2,448,576]{2,1,0:T(8,128)(2,1)S(1)}, u32[]{:S(2)}, u32[]{:S(2)}) collective-permute-start(bf16[2,448,576]{2,1,0:T(8,128)(2,1)S(1)} %pad_maximum_fusion.6.mine), channel_id=1, source_target_pairs={{0,8},{1,9},{2,10},{3,11},{8,0},{9,1},{10,2},{11,3},{16,24},{17,25... | collective-permute-start | bytes 3096584 | tf_op jit(solution)/shard_map/ppermute | solution.py:44
  185.7 23.2 %collective-permute-start.33 = (bf16[448,768]{1,0:T(8,128)(2,1)S(1)}, bf16[448,768]{1,0:T(8,128)(2,1)S(1)}, u32[]{:S(2)}, u32[]{:S(2)}) collective-permute-start(bf16[448,768]{1,0:T(8,128)(2,1)S(1)} %get-tuple-element.77), channel_id=1, source_target_pairs={{0,1},{1,2},{2,3},{3,0},{8,9},{9,10},{10,11},{11,8},{16,18},{17,19... | collective-permute-start | bytes 2064392 | tf_op jit(solution)/shard_map/ppermute | solution.py:44
  186.4 22.4 %collective-permute-start.32 = (bf16[448,768]{1,0:T(8,128)(2,1)S(1)}, bf16[448,768]{1,0:T(8,128)(2,1)S(1)}, u32[]{:S(2)}, u32[]{:S(2)}) collective-permute-start(bf16[448,768]{1,0:T(8,128)(2,1)S(1)} %get-tuple-element.76), channel_id=1, source_target_pairs={{0,3},{1,0},{2,1},{3,2},{8,11},{9,8},{10,9},{11,10},{16,16},{17,17... | collective-permute-start | bytes 2064392 | tf_op jit(solution)/shard_map/ppermute | solution.py:44
  189.4 19.4 %collective-permute-start.40 = (bf16[448,576]{1,0:T(8,128)(2,1)S(1)}, bf16[448,576]{1,0:T(8,128)(2,1)S(1)}, u32[]{:S(2)}, u32[]{:S(2)}) collective-permute-start(bf16[448,576]{1,0:T(8,128)(2,1)S(1)} %collective-permute-done.35), channel_id=1, source_target_pairs={{0,48},{1,49},{2,50},{3,51},{8,56},{9,57},{10,58},{11,59},{16,0},{... | collective-permute-start | bytes 1548296 | tf_op jit(solution)/shard_map/ppermute | solution.py:44
  191.9 16.9 %collective-permute-start.39 = (bf16[448,576]{1,0:T(8,128)(2,1)S(1)}, bf16[448,576]{1,0:T(8,128)(2,1)S(1)}, u32[]{:S(2)}, u32[]{:S(2)}) collective-permute-start(bf16[448,576]{1,0:T(8,128)(2,1)S(1)} %collective-permute-done.29), channel_id=1, source_target_pairs={{0,16},{1,17},{2,18},{3,19},{8,24},{9,25},{10,26},{11,27},{16,32},... | collective-permute-start | bytes 1548296 | tf_op jit(solution)/shard_map/ppermute | solution.py:44
  209.1 22.6 %collective-permute-start.38 = (bf16[448,768]{1,0:T(8,128)(2,1)S(1)}, bf16[448,768]{1,0:T(8,128)(2,1)S(1)}, u32[]{:S(2)}, u32[]{:S(2)}) collective-permute-start(bf16[448,768]{1,0:T(8,128)(2,1)S(1)} %get-tuple-element.82), channel_id=1, source_target_pairs={{0,7},{1,4},{2,5},{3,6},{8,15},{9,12},{10,13},{11,14},{16,20},{17,... | collective-permute-start | bytes 2064392 | tf_op jit(solution)/shard_map/ppermute | solution.py:44
  211.0 32.3 %collective-permute-start.37 = (bf16[448,768]{1,0:T(8,128)(2,1)S(1)}, bf16[448,768]{1,0:T(8,128)(2,1)S(1)}, u32[]{:S(2)}, u32[]{:S(2)}) collective-permute-start(bf16[448,768]{1,0:T(8,128)(2,1)S(1)} %get-tuple-element.81), channel_id=1, source_target_pairs={{0,5},{1,6},{2,7},{3,4},{8,13},{9,14},{10,15},{11,12},{16,22},{17,... | collective-permute-start | bytes 2064392 | tf_op jit(solution)/shard_map/ppermute | solution.py:44
  216.8 42.6 %collective-permute-start.43 = (bf16[448,768]{1,0:T(8,128)(2,1)S(1)}, bf16[448,768]{1,0:T(8,128)(2,1)S(1)}, u32[]{:S(2)}, u32[]{:S(2)}) collective-permute-start(bf16[448,768]{1,0:T(8,128)(2,1)S(1)} %get-tuple-element.86), channel_id=1, source_target_pairs={{0,4},{1,5},{2,6},{3,7},{8,12},{9,13},{10,14},{11,15},{16,21},{17,... | collective-permute-start | bytes 2064392 | tf_op jit(solution)/shard_map/ppermute | solution.py:44
  220.3 39.1 %collective-permute-start.42 = (bf16[448,768]{1,0:T(8,128)(2,1)S(1)}, bf16[448,768]{1,0:T(8,128)(2,1)S(1)}, u32[]{:S(2)}, u32[]{:S(2)}) collective-permute-start(bf16[448,768]{1,0:T(8,128)(2,1)S(1)} %get-tuple-element.85), channel_id=1, source_target_pairs={{0,2},{1,3},{2,0},{3,1},{8,10},{9,11},{10,8},{11,9},{16,19},{17,16... | collective-permute-start | bytes 2064392 | tf_op jit(solution)/shard_map/ppermute | solution.py:44
  (46 other events, 552.3 us)

commit v7 on v6

--- a/solution.py
+++ b/solution.py
@@ -375,7 +375,7 @@
         return terms
 
     every = step(every, y_far)
-    terms = sums((), every)
+    terms = sums((), far_l, far_r, every)
     terms = sums([after(own_l, *terms), own_r])
     own_l, far_r, *_ = lax.optimization_barrier((own_l, far_r, far_l, *parts[:2], *terms))
     own_ll, far_rr = send(own_l, x_up), send(far_r, x_down)

time: 266 us -> 264 us (level); the launches traced: 261 us -> 263 us
  waiting for transfers between devices: 119 us -> 127 us
  starting transfers between devices: 71 us -> 66.3 us
    ppermute x45, waiting for transfers between devices: 119 us -> 127 us  [send(): return lax.ppermute(array, AXES, pairs)]
    ppermute x45, starting transfers between devices: 71 us -> 66.3 us  [send(): return lax.ppermute(array, AXES, pairs)]
    unnamed x64 -> x62, local copies, waits for them, and re-layouts: 5.4 us -> 5.39 us
  transfers between devices with their start and end apart: 45 -> 45, of which waited for: 18 -> 22; matrix products, arithmetic and copies ran while one was open for 8% -> 8% of each run, Pallas kernels for 14% -> 14%
where the time goes in v7:
time: 264 us; the launch traced here: 263 us
  waiting for transfers between devices  127 us (48%)
  starting transfers between devices  66.3 us (25%)
  Pallas kernels  36.9 us (14%)
  other arithmetic  23.3 us (9%)
  local copies, waits for them, and re-layouts  8.69 us (3%)
    ppermute x45, waiting for transfers between devices, send(): return lax.ppermute(array, AXES, pairs)  127 us
    ppermute x45, starting transfers between devices, send(): return lax.ppermute(array, AXES, pairs)  66.3 us
    pallas_call x2, Pallas kernels, token_sum(): pl.pallas_call(functools.partial(token_kernel, len(blocks), first, before...  26.7 us
    pallas_call x4, Pallas kernels, down_terms(): pl.pallas_call(down_kernel, out_shape=[jax.ShapeDtypeStruct((columns, row...  10.2 us
    another operation x3, other arithmetic, swap(): pair = jnp.stack(blocks[n:n + 2])  5.87 us
    unnamed x62, local copies, waits for them, and re-layouts  5.39 us
  transfers between devices with their start and end apart: 45, of which 22 were waited for; matrix products, arithmetic and copies ran while one was open for 8% of the time, Pallas kernels for 14%

profile of v7, /device:TPU:6, one launch (start us, length us, event | category | flops | bytes accessed | tf_op | source)
XLA Modules:
  0.0 263.4 jit_solution(12045979607908319056)
XLA Ops:
  2.1 4.1 %collective-permute-start.2 = (bf16[768,512]{1,0:T(8,128)(2,1)S(1)}, bf16[768,512]{1,0:T(8,128)(2,1)S(1)}, u32[]{:S(2)}, u32[]{:S(2)}) collective-permute-start(bf16[768,512]{1,0:T(8,128)(2,1)S(1)} %fusion.1.refs_0_), channel_id=1, source_target_pairs={{0,3},{1,0},{2,1},{3,2},{8,11},{9,8},{10,9},{11,10},{16,19},{17,16... | collective-permute-start | bytes 2359304 | tf_op jit(solution)/shard_map/ppermute | solution.py:44
  16.7 3.4 %collective-permute-done.8 = f32[120,128]{1,0:T(8,128)S(1)} collective-permute-done((f32[120,128]{1,0:T(8,128)S(1)}, f32[120,128]{1,0:T(8,128)S(1)}, u32[]{:S(2)}, u32[]{:S(2)}) %collective-permute-start.8) | collective-permute-done | bytes 61472 | tf_op jit(solution)/shard_map/ppermute | solution.py:44
  21.6 3.7 %multiply_convert_fusion.2 = (bf16[224,1152]{1,0:T(8,128)(2,1)S(1)}, bf16[224,1152]{1,0:T(8,128)(2,1)S(1)}) fusion(f32[224,1152]{1,0:T(8,128)} %param.6, f32[1152]{0:T(1024)S(1)} %get-tuple-element.101, f32[1152]{0:T(1024)S(1)} %get-tuple-element.102, f32[1152]{0:T(1024)S(1)} %get-tuple-element.100, pred[224]{0:T(512)(128)(4,1)S(1)} %broadcast_compare_fusion.23, ...), kind=kLoop, calls=%fused_computation.20 | loop fusion | flops 9289728 | bytes 3124896 | tf_op jit(solution)/shard_map/convert_element_type | solution.py:129
  28.8 2.9 %collective-permute-start.10 = (bf16[224,2304]{1,0:T(8,128)(2,1)S(1)}, bf16[224,2304]{1,0:T(8,128)(2,1)S(1)}, u32[]{:S(2)}, u32[]{:S(2)}) collective-permute-start(bf16[224,2304]{1,0:T(8,128)(2,1)S(1)} %pad_maximum_fusion.8), channel_id=1, source_target_pairs={{0,64},{1,65},{2,66},{3,67},{8,72},{9,73},{10,74},{11,75},{16,80},... | collective-permute-start | bytes 3096584 | tf_op jit(solution)/shard_map/ppermute | solution.py:44
  31.7 3.4 %collective-permute-start.4 = (bf16[768,512]{1,0:T(8,128)(2,1)S(1)}, bf16[768,512]{1,0:T(8,128)(2,1)S(1)}, u32[]{:S(2)}, u32[]{:S(2)}) collective-permute-start(bf16[768,512]{1,0:T(8,128)(2,1)S(1)} %collective-permute-done.refs_1_), channel_id=1, source_target_pairs={{0,3},{1,0},{2,1},{3,2},{8,11},{9,8},{10,9},{11,10},{16,19},{17,16... | collective-permute-start | bytes 2359304 | tf_op jit(solution)/shard_map/ppermute | solution.py:44
  37.4 13.1 %collective-permute-done.4.refs_5_ = bf16[768,512]{1,0:T(8,128)(2,1)S(1)} collective-permute-done((bf16[768,512]{1,0:T(8,128)(2,1)S(1)}, bf16[768,512]{1,0:T(8,128)(2,1)S(1)}, u32[]{:S(2)}, u32[]{:S(2)}) %collective-permute-start.4) | collective-permute-done | bytes 786464 | tf_op jit(solution)/shard_map/ppermute | solution.py:44
  50.6 3.4 %collective-permute-done.3.refs_4_ = bf16[768,512]{1,0:T(8,128)(2,1)S(1)} collective-permute-done((bf16[768,512]{1,0:T(8,128)(2,1)S(1)}, bf16[768,512]{1,0:T(8,128)(2,1)S(1)}, u32[]{:S(2)}, u32[]{:S(2)}) %collective-permute-start.3) | collective-permute-done | bytes 786464 | tf_op jit(solution)/shard_map/ppermute | solution.py:44
  57.5 3.8 %collective-permute-done.14 = f32[120,128]{1,0:T(8,128)S(1)} collective-permute-done((f32[120,128]{1,0:T(8,128)S(1)}, f32[120,128]{1,0:T(8,128)S(1)}, u32[]{:S(2)}, u32[]{:S(2)}) %collective-permute-start.14) | collective-permute-done | bytes 61472 | tf_op jit(solution)/shard_map/ppermute | solution.py:44
  62.0 10.2 %collective-permute-done.13 = bf16[448,576]{1,0:T(8,128)(2,1)S(1)} collective-permute-done((bf16[448,576]{1,0:T(8,128)(2,1)S(1)}, bf16[448,576]{1,0:T(8,128)(2,1)S(1)}, u32[]{:S(2)}, u32[]{:S(2)}) %collective-permute-start.13) | collective-permute-done | bytes 516128 | tf_op jit(solution)/shard_map/ppermute | solution.py:44
  74.7 3.2 %collective-permute-start.6 = (bf16[768,512]{1,0:T(8,128)(2,1)S(1)}, bf16[768,512]{1,0:T(8,128)(2,1)S(1)}, u32[]{:S(2)}, u32[]{:S(2)}) collective-permute-start(bf16[768,512]{1,0:T(8,128)(2,1)S(1)} %collective-permute-done.4.refs_5_), channel_id=1, source_target_pairs={{0,3},{1,0},{2,1},{3,2},{8,11},{9,8},{10,9},{11,10},{16,19},{17,16... | collective-permute-start | bytes 2359304 | tf_op jit(solution)/shard_map/ppermute | solution.py:44
  79.4 18.3 %collective-permute-done.18 = bf16[224,2304]{1,0:T(8,128)(2,1)S(1)} collective-permute-done((bf16[224,2304]{1,0:T(8,128)(2,1)S(1)}, bf16[224,2304]{1,0:T(8,128)(2,1)S(1)}, u32[]{:S(2)}, u32[]{:S(2)}) %collective-permute-start.18) | collective-permute-done | bytes 1032224 | tf_op jit(solution)/shard_map/ppermute | solution.py:44
  99.1 2.7 %pad_maximum_fusion.2.refs_12_ = bf16[2,224,2304]{2,1,0:T(8,128)(2,1)} fusion(bf16[1,224,2304]{2,1,0:T(8,128)(2,1)} %bitcast.27, bf16[1,224,2304]{2,1,0:T(8,128)(2,1)S(1)} %bitcast.54), kind=kLoop, calls=%fused_computation.2 | loop fusion | flops 1032192 | bytes 4128768 | tf_op jit(solution)/shard_map/stack | solution.py:326
  101.9 3.0 %pad_maximum_fusion.1.refs_10_ = bf16[2,224,2304]{2,1,0:T(8,128)(2,1)} fusion(bf16[1,224,2304]{2,1,0:T(8,128)(2,1)S(1)} %bitcast.52, bf16[1,224,2304]{2,1,0:T(8,128)(2,1)} %bitcast.24), kind=kLoop, calls=%fused_computation.1 | loop fusion | flops 1032192 | bytes 4128768 | tf_op jit(solution)/shard_map/stack | solution.py:326
  111.8 19.8 %shard_map.68.refs_8_ = f32[768,2304]{1,0:T(8,128)} custom-call(s32[16]{0:T(128)} %compare_select_fusion.5.info, bf16[768,512]{1,0:T(8,128)(2,1)} %copy-done.1, bf16[768,512]{1,0:T(8,128)(2,1)} %copy-done.7, bf16[768,512]{1,0:T(8,128)(2,1)} %copy-done.5, bf16[768,512]{1,0:T(8,128)(2,1)} %copy-done.3, bf16[768,512]{1,0:T(8,128)(2,1)} %copy-done.11, ...), custom_call_target="tpu_custom_call" | custom-call | tf_op jit(solution)/shard_map/pallas_call | solution.py:213
  137.1 5.6 %collective-permute-done.24 = f32[120,128]{1,0:T(8,128)S(1)} collective-permute-done((f32[120,128]{1,0:T(8,128)S(1)}, f32[120,128]{1,0:T(8,128)S(1)}, u32[]{:S(2)}, u32[]{:S(2)}) %collective-permute-start.24) | collective-permute-done | bytes 61472 | tf_op jit(solution)/shard_map/ppermute | solution.py:44
  144.4 3.0 %copy-done = f32[768,2304]{1,0:T(8,128)S(1)} copy-done((f32[768,2304]{1,0:T(8,128)S(1)}, f32[768,2304]{1,0:T(8,128)}, u32[]{:S(2)}) %copy-start) | copy-done | bytes 7077912
  147.4 6.9 %shard_map.69.hidden = bf16[768,1152]{1,0:T(8,128)(2,1)S(1)} custom-call(s32[16]{0:T(128)S(1)} %copy-done.17, bf16[768,512]{1,0:T(8,128)(2,1)S(1)} %copy-done.2, bf16[768,512]{1,0:T(8,128)(2,1)S(1)} %copy-done.8, bf16[768,512]{1,0:T(8,128)(2,1)S(1)} %copy-done.6, bf16[768,512]{1,0:T(8,128)(2,1)S(1)} %copy-done.4, bf16[768,512]{1,0:T(8,128)(2,1)S(1)} %copy-done.12, ...), custom_call_target="tpu_custom_call" | custom-call | tf_op jit(solution)/shard_map/pallas_call | solution.py:213
  154.3 2.6 shard_map.70
  158.7 4.3 %collective-permute-done.28 = f32[120,128]{1,0:T(8,128)S(1)} collective-permute-done((f32[120,128]{1,0:T(8,128)S(1)}, f32[120,128]{1,0:T(8,128)S(1)}, u32[]{:S(2)}, u32[]{:S(2)}) %collective-permute-start.28) | collective-permute-done | bytes 61472 | tf_op jit(solution)/shard_map/ppermute | solution.py:44
  166.3 6.5 %collective-permute-start.29 = (bf16[448,768]{1,0:T(8,128)(2,1)S(1)}, bf16[448,768]{1,0:T(8,128)(2,1)S(1)}, u32[]{:S(2)}, u32[]{:S(2)}) collective-permute-start(bf16[448,768]{1,0:T(8,128)(2,1)S(1)} %get-tuple-element.72), channel_id=1, source_target_pairs={{0,0},{1,1},{2,2},{3,3},{8,8},{9,9},{10,10},{11,11},{16,17},{17,18... | collective-permute-start | bytes 2064392 | tf_op jit(solution)/shard_map/ppermute | solution.py:44
  175.4 9.1 %collective-permute-done.30 = bf16[448,768]{1,0:T(8,128)(2,1)S(1)} collective-permute-done((bf16[448,768]{1,0:T(8,128)(2,1)S(1)}, bf16[448,768]{1,0:T(8,128)(2,1)S(1)}, u32[]{:S(2)}, u32[]{:S(2)}) %collective-permute-start.30) | collective-permute-done | bytes 688160 | tf_op jit(solution)/shard_map/ppermute | solution.py:44
  187.7 4.1 %collective-permute-start.34 = (bf16[448,768]{1,0:T(8,128)(2,1)S(1)}, bf16[448,768]{1,0:T(8,128)(2,1)S(1)}, u32[]{:S(2)}, u32[]{:S(2)}) collective-permute-start(bf16[448,768]{1,0:T(8,128)(2,1)S(1)} %get-tuple-element.77), channel_id=1, source_target_pairs={{0,3},{1,0},{2,1},{3,2},{8,11},{9,8},{10,9},{11,10},{16,16},{17,17... | collective-permute-start | bytes 2064392 | tf_op jit(solution)/shard_map/ppermute | solution.py:44
  191.8 2.9 %collective-permute-start.40 = (bf16[448,576]{1,0:T(8,128)(2,1)S(1)}, bf16[448,576]{1,0:T(8,128)(2,1)S(1)}, u32[]{:S(2)}, u32[]{:S(2)}) collective-permute-start(bf16[448,576]{1,0:T(8,128)(2,1)S(1)} %collective-permute-done.27), channel_id=1, source_target_pairs={{0,48},{1,49},{2,50},{3,51},{8,56},{9,57},{10,58},{11,59},{16,0},{... | collective-permute-start | bytes 1548296 | tf_op jit(solution)/shard_map/ppermute | solution.py:44
  195.1 2.5 shard_map.72
  197.7 10.5 %collective-permute-done.40 = bf16[448,576]{1,0:T(8,128)(2,1)S(1)} collective-permute-done((bf16[448,576]{1,0:T(8,128)(2,1)S(1)}, bf16[448,576]{1,0:T(8,128)(2,1)S(1)}, u32[]{:S(2)}, u32[]{:S(2)}) %collective-permute-start.40) | collective-permute-done | bytes 516128 | tf_op jit(solution)/shard_map/ppermute | solution.py:44
  209.6 2.7 %collective-permute-start.38 = (bf16[448,768]{1,0:T(8,128)(2,1)S(1)}, bf16[448,768]{1,0:T(8,128)(2,1)S(1)}, u32[]{:S(2)}, u32[]{:S(2)}) collective-permute-start(bf16[448,768]{1,0:T(8,128)(2,1)S(1)} %get-tuple-element.82), channel_id=1, source_target_pairs={{0,7},{1,4},{2,5},{3,6},{8,15},{9,12},{10,13},{11,14},{16,20},{17,... | collective-permute-start | bytes 2064392 | tf_op jit(solution)/shard_map/ppermute | solution.py:44
  212.3 4.4 %collective-permute-start.37 = (bf16[448,768]{1,0:T(8,128)(2,1)S(1)}, bf16[448,768]{1,0:T(8,128)(2,1)S(1)}, u32[]{:S(2)}, u32[]{:S(2)}) collective-permute-start(bf16[448,768]{1,0:T(8,128)(2,1)S(1)} %get-tuple-element.81), channel_id=1, source_target_pairs={{0,5},{1,6},{2,7},{3,4},{8,13},{9,14},{10,15},{11,12},{16,22},{17,... | collective-permute-start | bytes 2064392 | tf_op jit(solution)/shard_map/ppermute | solution.py:44
  219.3 3.5 %collective-permute-start.43 = (bf16[448,768]{1,0:T(8,128)(2,1)S(1)}, bf16[448,768]{1,0:T(8,128)(2,1)S(1)}, u32[]{:S(2)}, u32[]{:S(2)}) collective-permute-start(bf16[448,768]{1,0:T(8,128)(2,1)S(1)} %get-tuple-element.86), channel_id=1, source_target_pairs={{0,4},{1,5},{2,6},{3,7},{8,12},{9,13},{10,14},{11,15},{16,21},{17,... | collective-permute-start | bytes 2064392 | tf_op jit(solution)/shard_map/ppermute | solution.py:44
  222.7 2.7 %collective-permute-start.42 = (bf16[448,768]{1,0:T(8,128)(2,1)S(1)}, bf16[448,768]{1,0:T(8,128)(2,1)S(1)}, u32[]{:S(2)}, u32[]{:S(2)}) collective-permute-start(bf16[448,768]{1,0:T(8,128)(2,1)S(1)} %get-tuple-element.85), channel_id=1, source_target_pairs={{0,2},{1,3},{2,0},{3,1},{8,10},{9,11},{10,8},{11,9},{16,19},{17,16... | collective-permute-start | bytes 2064392 | tf_op jit(solution)/shard_map/ppermute | solution.py:44
  226.7 4.5 %collective-permute-done.44 = f32[120,128]{1,0:T(8,128)S(1)} collective-permute-done((f32[120,128]{1,0:T(8,128)S(1)}, f32[120,128]{1,0:T(8,128)S(1)}, u32[]{:S(2)}, u32[]{:S(2)}) %collective-permute-start.44) | collective-permute-done | bytes 61472 | tf_op jit(solution)/shard_map/ppermute | solution.py:44
  232.1 13.6 %collective-permute-done.37 = bf16[448,768]{1,0:T(8,128)(2,1)S(1)} collective-permute-done((bf16[448,768]{1,0:T(8,128)(2,1)S(1)}, bf16[448,768]{1,0:T(8,128)(2,1)S(1)}, u32[]{:S(2)}, u32[]{:S(2)}) %collective-permute-start.37) | collective-permute-done | bytes 688160 | tf_op jit(solution)/shard_map/ppermute | solution.py:44
  245.8 16.1 %collective-permute-done.43 = bf16[448,768]{1,0:T(8,128)(2,1)S(1)} collective-permute-done((bf16[448,768]{1,0:T(8,128)(2,1)S(1)}, bf16[448,768]{1,0:T(8,128)(2,1)S(1)}, u32[]{:S(2)}, u32[]{:S(2)}) %collective-permute-start.43) | collective-permute-done | bytes 688160 | tf_op jit(solution)/shard_map/ppermute | solution.py:44
  (207 shorter events, 60.9 us)
Async XLA Ops:
  2.1 26.7 %collective-permute-start.2 = (bf16[768,512]{1,0:T(8,128)(2,1)S(1)}, bf16[768,512]{1,0:T(8,128)(2,1)S(1)}, u32[]{:S(2)}, u32[]{:S(2)}) collective-permute-start(bf16[768,512]{1,0:T(8,128)(2,1)S(1)} %fusion.1.refs_0_), channel_id=1, source_target_pairs={{0,3},{1,0},{2,1},{3,2},{8,11},{9,8},{10,9},{11,10},{16,19},{17,16... | collective-permute-start | bytes 2359304 | tf_op jit(solution)/shard_map/ppermute | solution.py:44
  6.2 25.5 %collective-permute-start.1 = (bf16[768,512]{1,0:T(8,128)(2,1)S(1)}, bf16[768,512]{1,0:T(8,128)(2,1)S(1)}, u32[]{:S(2)}, u32[]{:S(2)}) collective-permute-start(bf16[768,512]{1,0:T(8,128)(2,1)S(1)} %fusion.1.refs_0_), channel_id=1, source_target_pairs={{0,1},{1,2},{2,3},{3,0},{8,9},{9,10},{10,11},{11,8},{16,17},{17,18... | collective-permute-start | bytes 2359304 | tf_op jit(solution)/shard_map/ppermute | solution.py:44
  6.2 25.5 %collective-permute-start = (bf16[768,512]{1,0:T(8,128)(2,1)S(1)}, bf16[768,512]{1,0:T(8,128)(2,1)S(1)}, u32[]{:S(2)}, u32[]{:S(2)}) collective-permute-start(bf16[768,512]{1,0:T(8,128)(2,1)S(1)} %fusion.1.refs_0_), channel_id=1, source_target_pairs={{0,4},{1,5},{2,6},{3,7},{8,12},{9,13},{10,14},{11,15},{16,20},{17,... | collective-permute-start | bytes 2359304 | tf_op jit(solution)/shard_map/ppermute | solution.py:44
  25.4 36.6 %collective-permute-start.12 = (bf16[224,2304]{1,0:T(8,128)(2,1)S(1)}, bf16[224,2304]{1,0:T(8,128)(2,1)S(1)}, u32[]{:S(2)}, u32[]{:S(2)}) collective-permute-start(bf16[224,2304]{1,0:T(8,128)(2,1)S(1)} %pad_maximum_fusion.8), channel_id=1, source_target_pairs={{0,48},{1,49},{2,50},{3,51},{8,56},{9,57},{10,58},{11,59},{16,0},{... | collective-permute-start | bytes 3096584 | tf_op jit(solution)/shard_map/ppermute | solution.py:44
  26.3 35.7 %collective-permute-start.11 = (bf16[224,2304]{1,0:T(8,128)(2,1)S(1)}, bf16[224,2304]{1,0:T(8,128)(2,1)}, u32[]{:S(2)}, u32[]{:S(2)}) collective-permute-start(bf16[224,2304]{1,0:T(8,128)(2,1)S(1)} %pad_maximum_fusion.8), channel_id=1, source_target_pairs={{0,16},{1,17},{2,18},{3,19},{8,24},{9,25},{10,26},{11,27},{16,32},... | collective-permute-start | bytes 3096584 | tf_op jit(solution)/shard_map/ppermute | solution.py:44
  28.8 33.2 %collective-permute-start.10 = (bf16[224,2304]{1,0:T(8,128)(2,1)S(1)}, bf16[224,2304]{1,0:T(8,128)(2,1)S(1)}, u32[]{:S(2)}, u32[]{:S(2)}) collective-permute-start(bf16[224,2304]{1,0:T(8,128)(2,1)S(1)} %pad_maximum_fusion.8), channel_id=1, source_target_pairs={{0,64},{1,65},{2,66},{3,67},{8,72},{9,73},{10,74},{11,75},{16,80},... | collective-permute-start | bytes 3096584 | tf_op jit(solution)/shard_map/ppermute | solution.py:44
  31.7 18.8 %collective-permute-start.4 = (bf16[768,512]{1,0:T(8,128)(2,1)S(1)}, bf16[768,512]{1,0:T(8,128)(2,1)S(1)}, u32[]{:S(2)}, u32[]{:S(2)}) collective-permute-start(bf16[768,512]{1,0:T(8,128)(2,1)S(1)} %collective-permute-done.refs_1_), channel_id=1, source_target_pairs={{0,3},{1,0},{2,1},{3,2},{8,11},{9,8},{10,9},{11,10},{16,19},{17,16... | collective-permute-start | bytes 2359304 | tf_op jit(solution)/shard_map/ppermute | solution.py:44
  35.1 18.8 %collective-permute-start.3 = (bf16[768,512]{1,0:T(8,128)(2,1)S(1)}, bf16[768,512]{1,0:T(8,128)(2,1)S(1)}, u32[]{:S(2)}, u32[]{:S(2)}) collective-permute-start(bf16[768,512]{1,0:T(8,128)(2,1)S(1)} %collective-permute-done.refs_1_), channel_id=1, source_target_pairs={{0,1},{1,2},{2,3},{3,0},{8,9},{9,10},{10,11},{11,8},{16,17},{17,18... | collective-permute-start | bytes 2359304 | tf_op jit(solution)/shard_map/ppermute | solution.py:44
  54.9 17.3 %collective-permute-start.13 = (bf16[448,576]{1,0:T(8,128)(2,1)S(1)}, bf16[448,576]{1,0:T(8,128)(2,1)S(1)}, u32[]{:S(2)}, u32[]{:S(2)}) collective-permute-start(bf16[448,576]{1,0:T(8,128)(2,1)S(1)} %fusion.3), channel_id=1, source_target_pairs={{0,0},{1,16},{2,32},{3,48},{8,8},{9,24},{10,40},{11,56},{16,49},{1... | collective-permute-start | bytes 1548296 | tf_op jit(solution)/shard_map/ppermute | solution.py:44
  72.6 25.2 %collective-permute-start.18 = (bf16[224,2304]{1,0:T(8,128)(2,1)S(1)}, bf16[224,2304]{1,0:T(8,128)(2,1)S(1)}, u32[]{:S(2)}, u32[]{:S(2)}) collective-permute-start(bf16[224,2304]{1,0:T(8,128)(2,1)S(1)} %collective-permute-done.10), channel_id=1, source_target_pairs={{0,16},{1,17},{2,18},{3,19},{8,24},{9,25},{10,26},{11,27},{16,32},... | collective-permute-start | bytes 3096584 | tf_op jit(solution)/shard_map/ppermute | solution.py:44
  72.6 26.4 %collective-permute-start.19 = (bf16[224,2304]{1,0:T(8,128)(2,1)S(1)}, bf16[224,2304]{1,0:T(8,128)(2,1)}, u32[]{:S(2)}, u32[]{:S(2)}) collective-permute-start(bf16[224,2304]{1,0:T(8,128)(2,1)S(1)} %collective-permute-done.10), channel_id=1, source_target_pairs={{0,48},{1,49},{2,50},{3,51},{8,56},{9,57},{10,58},{11,59},{16,0},{... | collective-permute-start | bytes 3096584 | tf_op jit(solution)/shard_map/ppermute | solution.py:44
  74.7 23.1 %collective-permute-start.5 = (bf16[768,512]{1,0:T(8,128)(2,1)S(1)}, bf16[768,512]{1,0:T(8,128)(2,1)S(1)}, u32[]{:S(2)}, u32[]{:S(2)}) collective-permute-start(bf16[768,512]{1,0:T(8,128)(2,1)S(1)} %collective-permute-done.1.refs_2_), channel_id=1, source_target_pairs={{0,1},{1,2},{2,3},{3,0},{8,9},{9,10},{10,11},{11,8},{16,17},{17,18... | collective-permute-start | bytes 2359304 | tf_op jit(solution)/shard_map/ppermute | solution.py:44
  74.7 23.1 %collective-permute-start.6 = (bf16[768,512]{1,0:T(8,128)(2,1)S(1)}, bf16[768,512]{1,0:T(8,128)(2,1)S(1)}, u32[]{:S(2)}, u32[]{:S(2)}) collective-permute-start(bf16[768,512]{1,0:T(8,128)(2,1)S(1)} %collective-permute-done.4.refs_5_), channel_id=1, source_target_pairs={{0,3},{1,0},{2,1},{3,2},{8,11},{9,8},{10,9},{11,10},{16,19},{17,16... | collective-permute-start | bytes 2359304 | tf_op jit(solution)/shard_map/ppermute | solution.py:44
  77.9 24.0 %collective-permute-start.16 = (bf16[448,576]{1,0:T(8,128)(2,1)S(1)}, bf16[448,576]{1,0:T(8,128)(2,1)S(1)}, u32[]{:S(2)}, u32[]{:S(2)}) collective-permute-start(bf16[448,576]{1,0:T(8,128)(2,1)S(1)} %collective-permute-done.13), channel_id=1, source_target_pairs={{0,64},{1,65},{2,66},{3,67},{8,72},{9,73},{10,74},{11,75},{16,80},... | collective-permute-start | bytes 1548296 | tf_op jit(solution)/shard_map/ppermute | solution.py:44
  101.8 10.0 %collective-permute-start.21 = (bf16[2,224,2304]{2,1,0:T(8,128)(2,1)}, bf16[2,224,2304]{2,1,0:T(8,128)(2,1)}, u32[]{:S(2)}, u32[]{:S(2)}) collective-permute-start(bf16[2,224,2304]{2,1,0:T(8,128)(2,1)} %pad_maximum_fusion.2.refs_12_), channel_id=1, source_target_pairs={{0,8},{1,9},{2,10},{3,11},{8,0},{9,1},{10,2},{11,3},{16,24},{17,25... | collective-permute-start | bytes 6193160 | tf_op jit(solution)/shard_map/ppermute | solution.py:44
  105.7 26.0 %collective-permute-start.22 = (bf16[224,2304]{1,0:T(8,128)(2,1)}, bf16[224,2304]{1,0:T(8,128)(2,1)}, u32[]{:S(2)}, u32[]{:S(2)}) collective-permute-start(bf16[224,2304]{1,0:T(8,128)(2,1)} %collective-permute-done.11), channel_id=1, source_target_pairs={{0,16},{1,17},{2,18},{3,19},{8,24},{9,25},{10,26},{11,27},{16,32},... | collective-permute-start | bytes 3096584 | tf_op jit(solution)/shard_map/ppermute | solution.py:44
  106.5 26.4 %collective-permute-start.23 = (bf16[224,2304]{1,0:T(8,128)(2,1)}, bf16[224,2304]{1,0:T(8,128)(2,1)}, u32[]{:S(2)}, u32[]{:S(2)}) collective-permute-start(bf16[224,2304]{1,0:T(8,128)(2,1)} %collective-permute-done.19), channel_id=1, source_target_pairs={{0,48},{1,49},{2,50},{3,51},{8,56},{9,57},{10,58},{11,59},{16,0},{... | collective-permute-start | bytes 3096584 | tf_op jit(solution)/shard_map/ppermute | solution.py:44
  134.9 21.9 %collective-permute-start.31 = (bf16[448,576]{1,0:T(8,128)(2,1)S(1)}, bf16[448,576]{1,0:T(8,128)(2,1)S(1)}, u32[]{:S(2)}, u32[]{:S(2)}) collective-permute-start(bf16[448,576]{1,0:T(8,128)(2,1)S(1)} %copy-done.24), channel_id=1, source_target_pairs={{0,16},{1,17},{2,18},{3,19},{8,24},{9,25},{10,26},{11,27},{16,32},... | collective-permute-start | bytes 1548296 | tf_op jit(solution)/shard_map/ppermute | solution.py:44
  135.3 21.6 %collective-permute-start.32 = (bf16[448,576]{1,0:T(8,128)(2,1)S(1)}, bf16[448,576]{1,0:T(8,128)(2,1)S(1)}, u32[]{:S(2)}, u32[]{:S(2)}) collective-permute-start(bf16[448,576]{1,0:T(8,128)(2,1)S(1)} %copy-done.24), channel_id=1, source_target_pairs={{0,48},{1,49},{2,50},{3,51},{8,56},{9,57},{10,58},{11,59},{16,0},{... | collective-permute-start | bytes 1548296 | tf_op jit(solution)/shard_map/ppermute | solution.py:44
  137.0 26.8 %collective-permute-start.27 = (bf16[448,576]{1,0:T(8,128)(2,1)}, bf16[448,576]{1,0:T(8,128)(2,1)S(1)}, u32[]{:S(2)}, u32[]{:S(2)}) collective-permute-start(bf16[448,576]{1,0:T(8,128)(2,1)} %copy-done.25), channel_id=1, source_target_pairs={{0,48},{1,49},{2,50},{3,51},{8,56},{9,57},{10,58},{11,59},{16,0},{... | collective-permute-start | bytes 1548296 | tf_op jit(solution)/shard_map/ppermute | solution.py:44
  142.7 21.1 %collective-permute-start.26 = (bf16[448,576]{1,0:T(8,128)(2,1)}, bf16[448,576]{1,0:T(8,128)(2,1)S(1)}, u32[]{:S(2)}, u32[]{:S(2)}) collective-permute-start(bf16[448,576]{1,0:T(8,128)(2,1)} %copy-done.25), channel_id=1, source_target_pairs={{0,16},{1,17},{2,18},{3,19},{8,24},{9,25},{10,26},{11,27},{16,32},... | collective-permute-start | bytes 1548296 | tf_op jit(solution)/shard_map/ppermute | solution.py:44
  157.0 15.8 %collective-permute-start.33 = (bf16[2,448,576]{2,1,0:T(8,128)(2,1)S(1)}, bf16[2,448,576]{2,1,0:T(8,128)(2,1)S(1)}, u32[]{:S(2)}, u32[]{:S(2)}) collective-permute-start(bf16[2,448,576]{2,1,0:T(8,128)(2,1)S(1)} %pad_maximum_fusion.5.mine), channel_id=1, source_target_pairs={{0,8},{1,9},{2,10},{3,11},{8,0},{9,1},{10,2},{11,3},{16,24},{17,25... | collective-permute-start | bytes 3096584 | tf_op jit(solution)/shard_map/ppermute | solution.py:44
  163.8 20.7 %collective-permute-start.30 = (bf16[448,768]{1,0:T(8,128)(2,1)S(1)}, bf16[448,768]{1,0:T(8,128)(2,1)S(1)}, u32[]{:S(2)}, u32[]{:S(2)}) collective-permute-start(bf16[448,768]{1,0:T(8,128)(2,1)S(1)} %get-tuple-element.74), channel_id=1, source_target_pairs={{0,6},{1,7},{2,4},{3,5},{8,14},{9,15},{10,12},{11,13},{16,23},{17,... | collective-permute-start | bytes 2064392 | tf_op jit(solution)/shard_map/ppermute | solution.py:44
  166.3 20.4 %collective-permute-start.29 = (bf16[448,768]{1,0:T(8,128)(2,1)S(1)}, bf16[448,768]{1,0:T(8,128)(2,1)S(1)}, u32[]{:S(2)}, u32[]{:S(2)}) collective-permute-start(bf16[448,768]{1,0:T(8,128)(2,1)S(1)} %get-tuple-element.72), channel_id=1, source_target_pairs={{0,0},{1,1},{2,2},{3,3},{8,8},{9,9},{10,10},{11,11},{16,17},{17,18... | collective-permute-start | bytes 2064392 | tf_op jit(solution)/shard_map/ppermute | solution.py:44
  187.0 21.2 %collective-permute-start.35 = (bf16[448,768]{1,0:T(8,128)(2,1)S(1)}, bf16[448,768]{1,0:T(8,128)(2,1)S(1)}, u32[]{:S(2)}, u32[]{:S(2)}) collective-permute-start(bf16[448,768]{1,0:T(8,128)(2,1)S(1)} %get-tuple-element.78), channel_id=1, source_target_pairs={{0,1},{1,2},{2,3},{3,0},{8,9},{9,10},{10,11},{11,8},{16,18},{17,19... | collective-permute-start | bytes 2064392 | tf_op jit(solution)/shard_map/ppermute | solution.py:44
  187.7 21.2 %collective-permute-start.34 = (bf16[448,768]{1,0:T(8,128)(2,1)S(1)}, bf16[448,768]{1,0:T(8,128)(2,1)S(1)}, u32[]{:S(2)}, u32[]{:S(2)}) collective-permute-start(bf16[448,768]{1,0:T(8,128)(2,1)S(1)} %get-tuple-element.77), channel_id=1, source_target_pairs={{0,3},{1,0},{2,1},{3,2},{8,11},{9,8},{10,9},{11,10},{16,16},{17,17... | collective-permute-start | bytes 2064392 | tf_op jit(solution)/shard_map/ppermute | solution.py:44
  191.8 16.4 %collective-permute-start.40 = (bf16[448,576]{1,0:T(8,128)(2,1)S(1)}, bf16[448,576]{1,0:T(8,128)(2,1)S(1)}, u32[]{:S(2)}, u32[]{:S(2)}) collective-permute-start(bf16[448,576]{1,0:T(8,128)(2,1)S(1)} %collective-permute-done.27), channel_id=1, source_target_pairs={{0,48},{1,49},{2,50},{3,51},{8,56},{9,57},{10,58},{11,59},{16,0},{... | collective-permute-start | bytes 1548296 | tf_op jit(solution)/shard_map/ppermute | solution.py:44
  194.8 14.5 %collective-permute-start.39 = (bf16[448,576]{1,0:T(8,128)(2,1)S(1)}, bf16[448,576]{1,0:T(8,128)(2,1)S(1)}, u32[]{:S(2)}, u32[]{:S(2)}) collective-permute-start(bf16[448,576]{1,0:T(8,128)(2,1)S(1)} %collective-permute-done.31), channel_id=1, source_target_pairs={{0,16},{1,17},{2,18},{3,19},{8,24},{9,25},{10,26},{11,27},{16,32},... | collective-permute-start | bytes 1548296 | tf_op jit(solution)/shard_map/ppermute | solution.py:44
  209.6 22.6 %collective-permute-start.38 = (bf16[448,768]{1,0:T(8,128)(2,1)S(1)}, bf16[448,768]{1,0:T(8,128)(2,1)S(1)}, u32[]{:S(2)}, u32[]{:S(2)}) collective-permute-start(bf16[448,768]{1,0:T(8,128)(2,1)S(1)} %get-tuple-element.82), channel_id=1, source_target_pairs={{0,7},{1,4},{2,5},{3,6},{8,15},{9,12},{10,13},{11,14},{16,20},{17,... | collective-permute-start | bytes 2064392 | tf_op jit(solution)/shard_map/ppermute | solution.py:44
  212.3 33.5 %collective-permute-start.37 = (bf16[448,768]{1,0:T(8,128)(2,1)S(1)}, bf16[448,768]{1,0:T(8,128)(2,1)S(1)}, u32[]{:S(2)}, u32[]{:S(2)}) collective-permute-start(bf16[448,768]{1,0:T(8,128)(2,1)S(1)} %get-tuple-element.81), channel_id=1, source_target_pairs={{0,5},{1,6},{2,7},{3,4},{8,13},{9,14},{10,15},{11,12},{16,22},{17,... | collective-permute-start | bytes 2064392 | tf_op jit(solution)/shard_map/ppermute | solution.py:44
  219.3 42.6 %collective-permute-start.43 = (bf16[448,768]{1,0:T(8,128)(2,1)S(1)}, bf16[448,768]{1,0:T(8,128)(2,1)S(1)}, u32[]{:S(2)}, u32[]{:S(2)}) collective-permute-start(bf16[448,768]{1,0:T(8,128)(2,1)S(1)} %get-tuple-element.86), channel_id=1, source_target_pairs={{0,4},{1,5},{2,6},{3,7},{8,12},{9,13},{10,14},{11,15},{16,21},{17,... | collective-permute-start | bytes 2064392 | tf_op jit(solution)/shard_map/ppermute | solution.py:44
  222.7 39.1 %collective-permute-start.42 = (bf16[448,768]{1,0:T(8,128)(2,1)S(1)}, bf16[448,768]{1,0:T(8,128)(2,1)S(1)}, u32[]{:S(2)}, u32[]{:S(2)}) collective-permute-start(bf16[448,768]{1,0:T(8,128)(2,1)S(1)} %get-tuple-element.85), channel_id=1, source_target_pairs={{0,2},{1,3},{2,0},{3,1},{8,10},{9,11},{10,8},{11,9},{16,19},{17,16... | collective-permute-start | bytes 2064392 | tf_op jit(solution)/shard_map/ppermute | solution.py:44
  (45 other events, 551.7 us)

commit v8 on v7

--- a/solution.py
+++ b/solution.py
@@ -310,14 +310,15 @@
         axis=1,
     )
     every = step(table, lambda y, x, core, z: (y, x, core, z ^ 1))
-    gate_up, every = lax.optimization_barrier((gate_up, every))
+    down_weight = rollout(down_master, every[2 * rows : 3 * rows].T, *down_at)
+    down_block = send(down_weight.T, to_ff_group)
+    every = step(every, y_near)
+    gate_up, every, down_block = lax.optimization_barrier((gate_up, every, down_block))
     near, tokens_l, tokens_r = lax.optimization_barrier((near, tokens_l, tokens_r))
-    down_table = every
     near_l, near_r = send(near, z_up), send(near, z_down)
     tokens_l, near_r = after(tokens_l, near_l), after(near_r, near_l)
     tokens_ll, near_rr = send(tokens_l, z_up), send(near_r, z_down)
     pieces = [padded, near, tokens_l, tokens_r, near_l, near_r, tokens_ll, near_rr]
-    down_weight = rollout(down_master, down_table[2 * rows : 3 * rows].T, *down_at)
     pairs = []
 
     def swap(blocks, *before):
@@ -326,8 +327,6 @@
             pair = jnp.stack(blocks[n : n + 2])
             pairs.extend((pair, send(pair, other_core)))
 
-    down_block = send(after(down_weight.T, near_l, near_r), to_ff_group)
-    every = step(after(every, near_l, near_r), y_near)
 
     down_far = None
 
@@ -338,7 +337,7 @@
         return [pairs[1], tokens_ll, near_rr]
 
     far = send(gate_up, y_far)
-    blocks = ring(gate_up, far, x_up, x_down, (near_l, near_r, down_block, every), between)
+    blocks = ring(gate_up, far, x_up, x_down, (near_l, near_r), between)
     swap(blocks[2:4], blocks[4], blocks[5], down_far)
     swap(blocks[4:6])
 

time: 264 us -> 270 us (1.023)
  starting transfers between devices: 66.3 us -> 75 us
  waiting for transfers between devices: 127 us -> 122 us
    ppermute x45, starting transfers between devices: 66.3 us -> 75 us  [send(): return lax.ppermute(array, AXES, pairs)]
    ppermute x45, waiting for transfers between devices: 127 us -> 122 us  [send(): return lax.ppermute(array, AXES, pairs)]
where the time goes in v8:
time: 270 us; the launch traced here: 267 us
  waiting for transfers between devices  122 us (45%)
  starting transfers between devices  75 us (28%)
  Pallas kernels  36.9 us (14%)
  other arithmetic  23.1 us (9%)
  local copies, waits for them, and re-layouts  8.7 us (3%)
    ppermute x45, waiting for transfers between devices, send(): return lax.ppermute(array, AXES, pairs)  122 us
    ppermute x45, starting transfers between devices, send(): return lax.ppermute(array, AXES, pairs)  75 us
    pallas_call x2, Pallas kernels, token_sum(): pl.pallas_call(functools.partial(token_kernel, len(blocks), first, before...  26.7 us
    pallas_call x4, Pallas kernels, down_terms(): pl.pallas_call(down_kernel, out_shape=[jax.ShapeDtypeStruct((columns, row...  10.2 us
    another operation x3, other arithmetic, swap(): pair = jnp.stack(blocks[n:n + 2])  5.87 us
  transfers between devices with their start and end apart: 45, of which 22 were waited for; matrix products, arithmetic and copies ran while one was open for 8% of the time, Pallas kernels for 14%

profile of v8, /device:TPU:6, one launch (start us, length us, event | category | flops | bytes accessed | tf_op | source)
XLA Modules:
  0.0 267.1 jit_solution(8133009929208430559)
XLA Ops:
  2.1 4.1 %collective-permute-start.2 = (bf16[768,512]{1,0:T(8,128)(2,1)S(1)}, bf16[768,512]{1,0:T(8,128)(2,1)S(1)}, u32[]{:S(2)}, u32[]{:S(2)}) collective-permute-start(bf16[768,512]{1,0:T(8,128)(2,1)S(1)} %fusion.1.refs_0_), channel_id=1, source_target_pairs={{0,3},{1,0},{2,1},{3,2},{8,11},{9,8},{10,9},{11,10},{16,19},{17,16... | collective-permute-start | bytes 2359304 | tf_op jit(solution)/shard_map/ppermute | solution.py:44
  16.7 3.4 %collective-permute-done.8 = f32[120,128]{1,0:T(8,128)S(1)} collective-permute-done((f32[120,128]{1,0:T(8,128)S(1)}, f32[120,128]{1,0:T(8,128)S(1)}, u32[]{:S(2)}, u32[]{:S(2)}) %collective-permute-start.8) | collective-permute-done | bytes 61472 | tf_op jit(solution)/shard_map/ppermute | solution.py:44
  21.6 2.8 %collective-permute-done.9 = f32[120,128]{1,0:T(8,128)S(1)} collective-permute-done((f32[120,128]{1,0:T(8,128)S(1)}, f32[120,128]{1,0:T(8,128)S(1)}, u32[]{:S(2)}, u32[]{:S(2)}) %collective-permute-start.9) | collective-permute-done | bytes 61472 | tf_op jit(solution)/shard_map/ppermute | solution.py:44
  24.6 3.1 %fusion.3 = bf16[448,576]{1,0:T(8,128)(2,1)S(1)} fusion(f32[576,448]{0,1:T(8,128)} %param.8, f32[448]{0:T(512)S(1)} %bitcast.72, f32[448]{0:T(512)S(1)} %bitcast.73, f32[448]{0:T(512)S(1)} %bitcast.74, f32[448]{0:T(512)S(1)} %bitcast.75, f32[448]{0:T(512)S(1)} %bitcast.76, f32[448]{0:T(512)S(1)} %bitcast.71, pred[576]{0:T(1024)(128)(4,1)S(1)} %get-tuple-element.147, ...), kind=kLoop, calls=%fused_computation.29 | loop fusion | flops 5419008 | bytes 1562496 | tf_op jit(solution)/shard_map/transpose | solution.py:314
  27.8 6.3 %collective-permute-start.11 = (bf16[448,576]{1,0:T(8,128)(2,1)S(1)}, bf16[448,576]{1,0:T(8,128)(2,1)S(1)}, u32[]{:S(2)}, u32[]{:S(2)}) collective-permute-start(bf16[448,576]{1,0:T(8,128)(2,1)S(1)} %fusion.3), channel_id=1, source_target_pairs={{0,0},{1,16},{2,32},{3,48},{8,8},{9,24},{10,40},{11,56},{16,49},{1... | collective-permute-start | bytes 1548296 | tf_op jit(solution)/shard_map/ppermute | solution.py:44
  38.2 2.8 %collective-permute-done.10 = f32[120,128]{1,0:T(8,128)S(1)} collective-permute-done((f32[120,128]{1,0:T(8,128)S(1)}, f32[120,128]{1,0:T(8,128)S(1)}, u32[]{:S(2)}, u32[]{:S(2)}) %collective-permute-start.10) | collective-permute-done | bytes 61472 | tf_op jit(solution)/shard_map/ppermute | solution.py:44
  41.6 5.2 %collective-permute-done.11 = bf16[448,576]{1,0:T(8,128)(2,1)S(1)} collective-permute-done((bf16[448,576]{1,0:T(8,128)(2,1)S(1)}, bf16[448,576]{1,0:T(8,128)(2,1)S(1)}, u32[]{:S(2)}, u32[]{:S(2)}) %collective-permute-start.11) | collective-permute-done | bytes 516128 | tf_op jit(solution)/shard_map/ppermute | solution.py:44
  50.0 6.6 %collective-permute-start.12 = (bf16[224,2304]{1,0:T(8,128)(2,1)S(1)}, bf16[224,2304]{1,0:T(8,128)(2,1)S(1)}, u32[]{:S(2)}, u32[]{:S(2)}) collective-permute-start(bf16[224,2304]{1,0:T(8,128)(2,1)S(1)} %pad_maximum_fusion.8), channel_id=1, source_target_pairs={{0,64},{1,65},{2,66},{3,67},{8,72},{9,73},{10,74},{11,75},{16,80},... | collective-permute-start | bytes 3096584 | tf_op jit(solution)/shard_map/ppermute | solution.py:44
  58.7 16.6 %collective-permute-done.4.refs_5_ = bf16[768,512]{1,0:T(8,128)(2,1)S(1)} collective-permute-done((bf16[768,512]{1,0:T(8,128)(2,1)S(1)}, bf16[768,512]{1,0:T(8,128)(2,1)S(1)}, u32[]{:S(2)}, u32[]{:S(2)}) %collective-permute-start.4) | collective-permute-done | bytes 786464 | tf_op jit(solution)/shard_map/ppermute | solution.py:44
  81.5 3.2 %collective-permute-start.6 = (bf16[768,512]{1,0:T(8,128)(2,1)S(1)}, bf16[768,512]{1,0:T(8,128)(2,1)S(1)}, u32[]{:S(2)}, u32[]{:S(2)}) collective-permute-start(bf16[768,512]{1,0:T(8,128)(2,1)S(1)} %collective-permute-done.4.refs_5_), channel_id=1, source_target_pairs={{0,3},{1,0},{2,1},{3,2},{8,11},{9,8},{10,9},{11,10},{16,19},{17,16... | collective-permute-start | bytes 2359304 | tf_op jit(solution)/shard_map/ppermute | solution.py:44
  84.7 3.2 %collective-permute-start.16 = (bf16[448,576]{1,0:T(8,128)(2,1)S(1)}, bf16[448,576]{1,0:T(8,128)(2,1)S(1)}, u32[]{:S(2)}, u32[]{:S(2)}) collective-permute-start(bf16[448,576]{1,0:T(8,128)(2,1)S(1)} %collective-permute-done.11), channel_id=1, source_target_pairs={{0,64},{1,65},{2,66},{3,67},{8,72},{9,73},{10,74},{11,75},{16,80},... | collective-permute-start | bytes 1548296 | tf_op jit(solution)/shard_map/ppermute | solution.py:44
  88.0 16.6 %collective-permute-done.18 = bf16[224,2304]{1,0:T(8,128)(2,1)S(1)} collective-permute-done((bf16[224,2304]{1,0:T(8,128)(2,1)S(1)}, bf16[224,2304]{1,0:T(8,128)(2,1)S(1)}, u32[]{:S(2)}, u32[]{:S(2)}) %collective-permute-start.18) | collective-permute-done | bytes 1032224 | tf_op jit(solution)/shard_map/ppermute | solution.py:44
  106.0 2.7 %pad_maximum_fusion.2.refs_12_ = bf16[2,224,2304]{2,1,0:T(8,128)(2,1)} fusion(bf16[1,224,2304]{2,1,0:T(8,128)(2,1)} %bitcast.27, bf16[1,224,2304]{2,1,0:T(8,128)(2,1)S(1)} %bitcast.54), kind=kLoop, calls=%fused_computation.2 | loop fusion | flops 1032192 | bytes 4128768 | tf_op jit(solution)/shard_map/stack | solution.py:327
  108.8 3.0 %pad_maximum_fusion.1.refs_10_ = bf16[2,224,2304]{2,1,0:T(8,128)(2,1)} fusion(bf16[1,224,2304]{2,1,0:T(8,128)(2,1)S(1)} %bitcast.52, bf16[1,224,2304]{2,1,0:T(8,128)(2,1)} %bitcast.24), kind=kLoop, calls=%fused_computation.1 | loop fusion | flops 1032192 | bytes 4128768 | tf_op jit(solution)/shard_map/stack | solution.py:327
  118.7 19.8 %shard_map.68.refs_8_ = f32[768,2304]{1,0:T(8,128)} custom-call(s32[16]{0:T(128)} %compare_select_fusion.5.info, bf16[768,512]{1,0:T(8,128)(2,1)} %copy-done.1, bf16[768,512]{1,0:T(8,128)(2,1)} %copy-done.7, bf16[768,512]{1,0:T(8,128)(2,1)} %copy-done.5, bf16[768,512]{1,0:T(8,128)(2,1)} %copy-done.3, bf16[768,512]{1,0:T(8,128)(2,1)} %copy-done.11, ...), custom_call_target="tpu_custom_call" | custom-call | tf_op jit(solution)/shard_map/pallas_call | solution.py:213
  144.4 5.3 %collective-permute-done.24 = f32[120,128]{1,0:T(8,128)S(1)} collective-permute-done((f32[120,128]{1,0:T(8,128)S(1)}, f32[120,128]{1,0:T(8,128)S(1)}, u32[]{:S(2)}, u32[]{:S(2)}) %collective-permute-start.24) | collective-permute-done | bytes 61472 | tf_op jit(solution)/shard_map/ppermute | solution.py:44
  151.3 3.0 %copy-done = f32[768,2304]{1,0:T(8,128)S(1)} copy-done((f32[768,2304]{1,0:T(8,128)S(1)}, f32[768,2304]{1,0:T(8,128)}, u32[]{:S(2)}) %copy-start) | copy-done | bytes 7077912
  154.3 6.9 %shard_map.69.hidden = bf16[768,1152]{1,0:T(8,128)(2,1)S(1)} custom-call(s32[16]{0:T(128)S(1)} %copy-done.17, bf16[768,512]{1,0:T(8,128)(2,1)S(1)} %copy-done.2, bf16[768,512]{1,0:T(8,128)(2,1)S(1)} %copy-done.8, bf16[768,512]{1,0:T(8,128)(2,1)S(1)} %copy-done.6, bf16[768,512]{1,0:T(8,128)(2,1)S(1)} %copy-done.4, bf16[768,512]{1,0:T(8,128)(2,1)S(1)} %copy-done.12, ...), custom_call_target="tpu_custom_call" | custom-call | tf_op jit(solution)/shard_map/pallas_call | solution.py:213
  161.2 2.6 shard_map.70
  164.0 3.3 %collective-permute-start.28 = (f32[120,128]{1,0:T(8,128)S(1)}, f32[120,128]{1,0:T(8,128)S(1)}, u32[]{:S(2)}, u32[]{:S(2)}) collective-permute-start(f32[120,128]{1,0:T(8,128)S(1)} %max.41), channel_id=1, source_target_pairs={{0,64},{1,65},{2,66},{3,67},{8,72},{9,73},{10,74},{11,75},{16,80},... | collective-permute-start | bytes 184328 | tf_op jit(solution)/shard_map/ppermute | solution.py:44
  167.4 2.6 collective-permute-done.28
  172.6 3.9 %collective-permute-start.29 = (bf16[448,768]{1,0:T(8,128)(2,1)S(1)}, bf16[448,768]{1,0:T(8,128)(2,1)S(1)}, u32[]{:S(2)}, u32[]{:S(2)}) collective-permute-start(bf16[448,768]{1,0:T(8,128)(2,1)S(1)} %get-tuple-element.70), channel_id=1, source_target_pairs={{0,0},{1,1},{2,2},{3,3},{8,8},{9,9},{10,10},{11,11},{16,17},{17,18... | collective-permute-start | bytes 2064392 | tf_op jit(solution)/shard_map/ppermute | solution.py:44
  179.1 12.3 %collective-permute-done.30 = bf16[448,768]{1,0:T(8,128)(2,1)S(1)} collective-permute-done((bf16[448,768]{1,0:T(8,128)(2,1)S(1)}, bf16[448,768]{1,0:T(8,128)(2,1)S(1)}, u32[]{:S(2)}, u32[]{:S(2)}) %collective-permute-start.30) | collective-permute-done | bytes 688160 | tf_op jit(solution)/shard_map/ppermute | solution.py:44
  192.4 3.2 %collective-permute-start.34 = (bf16[448,768]{1,0:T(8,128)(2,1)S(1)}, bf16[448,768]{1,0:T(8,128)(2,1)S(1)}, u32[]{:S(2)}, u32[]{:S(2)}) collective-permute-start(bf16[448,768]{1,0:T(8,128)(2,1)S(1)} %get-tuple-element.75), channel_id=1, source_target_pairs={{0,3},{1,0},{2,1},{3,2},{8,11},{9,8},{10,9},{11,10},{16,16},{17,17... | collective-permute-start | bytes 2064392 | tf_op jit(solution)/shard_map/ppermute | solution.py:44
  195.6 3.9 %collective-permute-start.40 = (bf16[448,576]{1,0:T(8,128)(2,1)S(1)}, bf16[448,576]{1,0:T(8,128)(2,1)S(1)}, u32[]{:S(2)}, u32[]{:S(2)}) collective-permute-start(bf16[448,576]{1,0:T(8,128)(2,1)S(1)} %collective-permute-done.27), channel_id=1, source_target_pairs={{0,48},{1,49},{2,50},{3,51},{8,56},{9,57},{10,58},{11,59},{16,0},{... | collective-permute-start | bytes 1548296 | tf_op jit(solution)/shard_map/ppermute | solution.py:44
  202.3 10.4 %collective-permute-done.40 = bf16[448,576]{1,0:T(8,128)(2,1)S(1)} collective-permute-done((bf16[448,576]{1,0:T(8,128)(2,1)S(1)}, bf16[448,576]{1,0:T(8,128)(2,1)S(1)}, u32[]{:S(2)}, u32[]{:S(2)}) %collective-permute-start.40) | collective-permute-done | bytes 516128 | tf_op jit(solution)/shard_map/ppermute | solution.py:44
  214.2 4.9 %collective-permute-start.38 = (bf16[448,768]{1,0:T(8,128)(2,1)S(1)}, bf16[448,768]{1,0:T(8,128)(2,1)S(1)}, u32[]{:S(2)}, u32[]{:S(2)}) collective-permute-start(bf16[448,768]{1,0:T(8,128)(2,1)S(1)} %get-tuple-element.80), channel_id=1, source_target_pairs={{0,7},{1,4},{2,5},{3,6},{8,15},{9,12},{10,13},{11,14},{16,20},{17,... | collective-permute-start | bytes 2064392 | tf_op jit(solution)/shard_map/ppermute | solution.py:44
  221.5 2.5 shard_map.73
  224.1 5.0 %collective-permute-start.43 = (bf16[448,768]{1,0:T(8,128)(2,1)S(1)}, bf16[448,768]{1,0:T(8,128)(2,1)S(1)}, u32[]{:S(2)}, u32[]{:S(2)}) collective-permute-start(bf16[448,768]{1,0:T(8,128)(2,1)S(1)} %get-tuple-element.84), channel_id=1, source_target_pairs={{0,4},{1,5},{2,6},{3,7},{8,12},{9,13},{10,14},{11,15},{16,21},{17,... | collective-permute-start | bytes 2064392 | tf_op jit(solution)/shard_map/ppermute | solution.py:44
  232.1 4.7 %collective-permute-done.44 = f32[120,128]{1,0:T(8,128)S(1)} collective-permute-done((f32[120,128]{1,0:T(8,128)S(1)}, f32[120,128]{1,0:T(8,128)S(1)}, u32[]{:S(2)}, u32[]{:S(2)}) %collective-permute-start.44) | collective-permute-done | bytes 61472 | tf_op jit(solution)/shard_map/ppermute | solution.py:44
  237.5 13.0 %collective-permute-done.37 = bf16[448,768]{1,0:T(8,128)(2,1)S(1)} collective-permute-done((bf16[448,768]{1,0:T(8,128)(2,1)S(1)}, bf16[448,768]{1,0:T(8,128)(2,1)S(1)}, u32[]{:S(2)}, u32[]{:S(2)}) %collective-permute-start.37) | collective-permute-done | bytes 688160 | tf_op jit(solution)/shard_map/ppermute | solution.py:44
  250.5 15.0 %collective-permute-done.43 = bf16[448,768]{1,0:T(8,128)(2,1)S(1)} collective-permute-done((bf16[448,768]{1,0:T(8,128)(2,1)S(1)}, bf16[448,768]{1,0:T(8,128)(2,1)S(1)}, u32[]{:S(2)}, u32[]{:S(2)}) %collective-permute-start.43) | collective-permute-done | bytes 688160 | tf_op jit(solution)/shard_map/ppermute | solution.py:44
  (209 shorter events, 63.2 us)
Async XLA Ops:
  2.1 47.9 %collective-permute-start.2 = (bf16[768,512]{1,0:T(8,128)(2,1)S(1)}, bf16[768,512]{1,0:T(8,128)(2,1)S(1)}, u32[]{:S(2)}, u32[]{:S(2)}) collective-permute-start(bf16[768,512]{1,0:T(8,128)(2,1)S(1)} %fusion.1.refs_0_), channel_id=1, source_target_pairs={{0,3},{1,0},{2,1},{3,2},{8,11},{9,8},{10,9},{11,10},{16,19},{17,16... | collective-permute-start | bytes 2359304 | tf_op jit(solution)/shard_map/ppermute | solution.py:44
  6.2 50.4 %collective-permute-start.1 = (bf16[768,512]{1,0:T(8,128)(2,1)S(1)}, bf16[768,512]{1,0:T(8,128)(2,1)S(1)}, u32[]{:S(2)}, u32[]{:S(2)}) collective-permute-start(bf16[768,512]{1,0:T(8,128)(2,1)S(1)} %fusion.1.refs_0_), channel_id=1, source_target_pairs={{0,1},{1,2},{2,3},{3,0},{8,9},{9,10},{10,11},{11,8},{16,17},{17,18... | collective-permute-start | bytes 2359304 | tf_op jit(solution)/shard_map/ppermute | solution.py:44
  6.2 50.4 %collective-permute-start = (bf16[768,512]{1,0:T(8,128)(2,1)S(1)}, bf16[768,512]{1,0:T(8,128)(2,1)S(1)}, u32[]{:S(2)}, u32[]{:S(2)}) collective-permute-start(bf16[768,512]{1,0:T(8,128)(2,1)S(1)} %fusion.1.refs_0_), channel_id=1, source_target_pairs={{0,4},{1,5},{2,6},{3,7},{8,12},{9,13},{10,14},{11,15},{16,20},{17,... | collective-permute-start | bytes 2359304 | tf_op jit(solution)/shard_map/ppermute | solution.py:44
  27.8 19.0 %collective-permute-start.11 = (bf16[448,576]{1,0:T(8,128)(2,1)S(1)}, bf16[448,576]{1,0:T(8,128)(2,1)S(1)}, u32[]{:S(2)}, u32[]{:S(2)}) collective-permute-start(bf16[448,576]{1,0:T(8,128)(2,1)S(1)} %fusion.3), channel_id=1, source_target_pairs={{0,0},{1,16},{2,32},{3,48},{8,8},{9,24},{10,40},{11,56},{16,49},{1... | collective-permute-start | bytes 1548296 | tf_op jit(solution)/shard_map/ppermute | solution.py:44
  46.7 30.9 %collective-permute-start.14 = (bf16[224,2304]{1,0:T(8,128)(2,1)S(1)}, bf16[224,2304]{1,0:T(8,128)(2,1)S(1)}, u32[]{:S(2)}, u32[]{:S(2)}) collective-permute-start(bf16[224,2304]{1,0:T(8,128)(2,1)S(1)} %pad_maximum_fusion.8), channel_id=1, source_target_pairs={{0,48},{1,49},{2,50},{3,51},{8,56},{9,57},{10,58},{11,59},{16,0},{... | collective-permute-start | bytes 3096584 | tf_op jit(solution)/shard_map/ppermute | solution.py:44
  48.2 29.5 %collective-permute-start.13 = (bf16[224,2304]{1,0:T(8,128)(2,1)S(1)}, bf16[224,2304]{1,0:T(8,128)(2,1)}, u32[]{:S(2)}, u32[]{:S(2)}) collective-permute-start(bf16[224,2304]{1,0:T(8,128)(2,1)S(1)} %pad_maximum_fusion.8), channel_id=1, source_target_pairs={{0,16},{1,17},{2,18},{3,19},{8,24},{9,25},{10,26},{11,27},{16,32},... | collective-permute-start | bytes 3096584 | tf_op jit(solution)/shard_map/ppermute | solution.py:44
  50.0 29.1 %collective-permute-start.12 = (bf16[224,2304]{1,0:T(8,128)(2,1)S(1)}, bf16[224,2304]{1,0:T(8,128)(2,1)S(1)}, u32[]{:S(2)}, u32[]{:S(2)}) collective-permute-start(bf16[224,2304]{1,0:T(8,128)(2,1)S(1)} %pad_maximum_fusion.8), channel_id=1, source_target_pairs={{0,64},{1,65},{2,66},{3,67},{8,72},{9,73},{10,74},{11,75},{16,80},... | collective-permute-start | bytes 3096584 | tf_op jit(solution)/shard_map/ppermute | solution.py:44
  56.6 18.7 %collective-permute-start.4 = (bf16[768,512]{1,0:T(8,128)(2,1)S(1)}, bf16[768,512]{1,0:T(8,128)(2,1)S(1)}, u32[]{:S(2)}, u32[]{:S(2)}) collective-permute-start(bf16[768,512]{1,0:T(8,128)(2,1)S(1)} %collective-permute-done.refs_1_), channel_id=1, source_target_pairs={{0,3},{1,0},{2,1},{3,2},{8,11},{9,8},{10,9},{11,10},{16,19},{17,16... | collective-permute-start | bytes 2359304 | tf_op jit(solution)/shard_map/ppermute | solution.py:44
  57.2 19.6 %collective-permute-start.3 = (bf16[768,512]{1,0:T(8,128)(2,1)S(1)}, bf16[768,512]{1,0:T(8,128)(2,1)S(1)}, u32[]{:S(2)}, u32[]{:S(2)}) collective-permute-start(bf16[768,512]{1,0:T(8,128)(2,1)S(1)} %collective-permute-done.refs_1_), channel_id=1, source_target_pairs={{0,1},{1,2},{2,3},{3,0},{8,9},{9,10},{10,11},{11,8},{16,17},{17,18... | collective-permute-start | bytes 2359304 | tf_op jit(solution)/shard_map/ppermute | solution.py:44
  79.4 25.2 %collective-permute-start.18 = (bf16[224,2304]{1,0:T(8,128)(2,1)S(1)}, bf16[224,2304]{1,0:T(8,128)(2,1)S(1)}, u32[]{:S(2)}, u32[]{:S(2)}) collective-permute-start(bf16[224,2304]{1,0:T(8,128)(2,1)S(1)} %collective-permute-done.12), channel_id=1, source_target_pairs={{0,16},{1,17},{2,18},{3,19},{8,24},{9,25},{10,26},{11,27},{16,32},... | collective-permute-start | bytes 3096584 | tf_op jit(solution)/shard_map/ppermute | solution.py:44
  79.8 26.2 %collective-permute-start.19 = (bf16[224,2304]{1,0:T(8,128)(2,1)S(1)}, bf16[224,2304]{1,0:T(8,128)(2,1)}, u32[]{:S(2)}, u32[]{:S(2)}) collective-permute-start(bf16[224,2304]{1,0:T(8,128)(2,1)S(1)} %collective-permute-done.12), channel_id=1, source_target_pairs={{0,48},{1,49},{2,50},{3,51},{8,56},{9,57},{10,58},{11,59},{16,0},{... | collective-permute-start | bytes 3096584 | tf_op jit(solution)/shard_map/ppermute | solution.py:44
  81.5 23.1 %collective-permute-start.5 = (bf16[768,512]{1,0:T(8,128)(2,1)S(1)}, bf16[768,512]{1,0:T(8,128)(2,1)S(1)}, u32[]{:S(2)}, u32[]{:S(2)}) collective-permute-start(bf16[768,512]{1,0:T(8,128)(2,1)S(1)} %collective-permute-done.1.refs_2_), channel_id=1, source_target_pairs={{0,1},{1,2},{2,3},{3,0},{8,9},{9,10},{10,11},{11,8},{16,17},{17,18... | collective-permute-start | bytes 2359304 | tf_op jit(solution)/shard_map/ppermute | solution.py:44
  81.5 23.1 %collective-permute-start.6 = (bf16[768,512]{1,0:T(8,128)(2,1)S(1)}, bf16[768,512]{1,0:T(8,128)(2,1)S(1)}, u32[]{:S(2)}, u32[]{:S(2)}) collective-permute-start(bf16[768,512]{1,0:T(8,128)(2,1)S(1)} %collective-permute-done.4.refs_5_), channel_id=1, source_target_pairs={{0,3},{1,0},{2,1},{3,2},{8,11},{9,8},{10,9},{11,10},{16,19},{17,16... | collective-permute-start | bytes 2359304 | tf_op jit(solution)/shard_map/ppermute | solution.py:44
  84.7 24.1 %collective-permute-start.16 = (bf16[448,576]{1,0:T(8,128)(2,1)S(1)}, bf16[448,576]{1,0:T(8,128)(2,1)S(1)}, u32[]{:S(2)}, u32[]{:S(2)}) collective-permute-start(bf16[448,576]{1,0:T(8,128)(2,1)S(1)} %collective-permute-done.11), channel_id=1, source_target_pairs={{0,64},{1,65},{2,66},{3,67},{8,72},{9,73},{10,74},{11,75},{16,80},... | collective-permute-start | bytes 1548296 | tf_op jit(solution)/shard_map/ppermute | solution.py:44
  108.7 10.0 %collective-permute-start.21 = (bf16[2,224,2304]{2,1,0:T(8,128)(2,1)}, bf16[2,224,2304]{2,1,0:T(8,128)(2,1)}, u32[]{:S(2)}, u32[]{:S(2)}) collective-permute-start(bf16[2,224,2304]{2,1,0:T(8,128)(2,1)} %pad_maximum_fusion.2.refs_12_), channel_id=1, source_target_pairs={{0,8},{1,9},{2,10},{3,11},{8,0},{9,1},{10,2},{11,3},{16,24},{17,25... | collective-permute-start | bytes 6193160 | tf_op jit(solution)/shard_map/ppermute | solution.py:44
  112.6 26.0 %collective-permute-start.22 = (bf16[224,2304]{1,0:T(8,128)(2,1)}, bf16[224,2304]{1,0:T(8,128)(2,1)}, u32[]{:S(2)}, u32[]{:S(2)}) collective-permute-start(bf16[224,2304]{1,0:T(8,128)(2,1)} %collective-permute-done.13), channel_id=1, source_target_pairs={{0,16},{1,17},{2,18},{3,19},{8,24},{9,25},{10,26},{11,27},{16,32},... | collective-permute-start | bytes 3096584 | tf_op jit(solution)/shard_map/ppermute | solution.py:44
  113.4 26.4 %collective-permute-start.23 = (bf16[224,2304]{1,0:T(8,128)(2,1)}, bf16[224,2304]{1,0:T(8,128)(2,1)}, u32[]{:S(2)}, u32[]{:S(2)}) collective-permute-start(bf16[224,2304]{1,0:T(8,128)(2,1)} %collective-permute-done.19), channel_id=1, source_target_pairs={{0,48},{1,49},{2,50},{3,51},{8,56},{9,57},{10,58},{11,59},{16,0},{... | collective-permute-start | bytes 3096584 | tf_op jit(solution)/shard_map/ppermute | solution.py:44
  141.8 21.9 %collective-permute-start.31 = (bf16[448,576]{1,0:T(8,128)(2,1)S(1)}, bf16[448,576]{1,0:T(8,128)(2,1)S(1)}, u32[]{:S(2)}, u32[]{:S(2)}) collective-permute-start(bf16[448,576]{1,0:T(8,128)(2,1)S(1)} %copy-done.25), channel_id=1, source_target_pairs={{0,16},{1,17},{2,18},{3,19},{8,24},{9,25},{10,26},{11,27},{16,32},... | collective-permute-start | bytes 1548296 | tf_op jit(solution)/shard_map/ppermute | solution.py:44
  142.2 21.6 %collective-permute-start.32 = (bf16[448,576]{1,0:T(8,128)(2,1)S(1)}, bf16[448,576]{1,0:T(8,128)(2,1)S(1)}, u32[]{:S(2)}, u32[]{:S(2)}) collective-permute-start(bf16[448,576]{1,0:T(8,128)(2,1)S(1)} %copy-done.25), channel_id=1, source_target_pairs={{0,48},{1,49},{2,50},{3,51},{8,56},{9,57},{10,58},{11,59},{16,0},{... | collective-permute-start | bytes 1548296 | tf_op jit(solution)/shard_map/ppermute | solution.py:44
  144.3 26.4 %collective-permute-start.27 = (bf16[448,576]{1,0:T(8,128)(2,1)}, bf16[448,576]{1,0:T(8,128)(2,1)S(1)}, u32[]{:S(2)}, u32[]{:S(2)}) collective-permute-start(bf16[448,576]{1,0:T(8,128)(2,1)} %copy-done.26), channel_id=1, source_target_pairs={{0,48},{1,49},{2,50},{3,51},{8,56},{9,57},{10,58},{11,59},{16,0},{... | collective-permute-start | bytes 1548296 | tf_op jit(solution)/shard_map/ppermute | solution.py:44
  149.7 21.1 %collective-permute-start.26 = (bf16[448,576]{1,0:T(8,128)(2,1)}, bf16[448,576]{1,0:T(8,128)(2,1)S(1)}, u32[]{:S(2)}, u32[]{:S(2)}) collective-permute-start(bf16[448,576]{1,0:T(8,128)(2,1)} %copy-done.26), channel_id=1, source_target_pairs={{0,16},{1,17},{2,18},{3,19},{8,24},{9,25},{10,26},{11,27},{16,32},... | collective-permute-start | bytes 1548296 | tf_op jit(solution)/shard_map/ppermute | solution.py:44
  164.0 12.6 %collective-permute-start.33 = (bf16[2,448,576]{2,1,0:T(8,128)(2,1)S(1)}, bf16[2,448,576]{2,1,0:T(8,128)(2,1)S(1)}, u32[]{:S(2)}, u32[]{:S(2)}) collective-permute-start(bf16[2,448,576]{2,1,0:T(8,128)(2,1)S(1)} %pad_maximum_fusion.5.mine), channel_id=1, source_target_pairs={{0,8},{1,9},{2,10},{3,11},{8,0},{9,1},{10,2},{11,3},{16,24},{17,25... | collective-permute-start | bytes 3096584 | tf_op jit(solution)/shard_map/ppermute | solution.py:44
  170.7 20.7 %collective-permute-start.30 = (bf16[448,768]{1,0:T(8,128)(2,1)S(1)}, bf16[448,768]{1,0:T(8,128)(2,1)S(1)}, u32[]{:S(2)}, u32[]{:S(2)}) collective-permute-start(bf16[448,768]{1,0:T(8,128)(2,1)S(1)} %get-tuple-element.72), channel_id=1, source_target_pairs={{0,6},{1,7},{2,4},{3,5},{8,14},{9,15},{10,12},{11,13},{16,23},{17,... | collective-permute-start | bytes 2064392 | tf_op jit(solution)/shard_map/ppermute | solution.py:44
  172.6 18.7 %collective-permute-start.29 = (bf16[448,768]{1,0:T(8,128)(2,1)S(1)}, bf16[448,768]{1,0:T(8,128)(2,1)S(1)}, u32[]{:S(2)}, u32[]{:S(2)}) collective-permute-start(bf16[448,768]{1,0:T(8,128)(2,1)S(1)} %get-tuple-element.70), channel_id=1, source_target_pairs={{0,0},{1,1},{2,2},{3,3},{8,8},{9,9},{10,10},{11,11},{16,17},{17,18... | collective-permute-start | bytes 2064392 | tf_op jit(solution)/shard_map/ppermute | solution.py:44
  191.7 21.1 %collective-permute-start.35 = (bf16[448,768]{1,0:T(8,128)(2,1)S(1)}, bf16[448,768]{1,0:T(8,128)(2,1)S(1)}, u32[]{:S(2)}, u32[]{:S(2)}) collective-permute-start(bf16[448,768]{1,0:T(8,128)(2,1)S(1)} %get-tuple-element.76), channel_id=1, source_target_pairs={{0,1},{1,2},{2,3},{3,0},{8,9},{9,10},{10,11},{11,8},{16,18},{17,19... | collective-permute-start | bytes 2064392 | tf_op jit(solution)/shard_map/ppermute | solution.py:44
  192.4 21.2 %collective-permute-start.34 = (bf16[448,768]{1,0:T(8,128)(2,1)S(1)}, bf16[448,768]{1,0:T(8,128)(2,1)S(1)}, u32[]{:S(2)}, u32[]{:S(2)}) collective-permute-start(bf16[448,768]{1,0:T(8,128)(2,1)S(1)} %get-tuple-element.75), channel_id=1, source_target_pairs={{0,3},{1,0},{2,1},{3,2},{8,11},{9,8},{10,9},{11,10},{16,16},{17,17... | collective-permute-start | bytes 2064392 | tf_op jit(solution)/shard_map/ppermute | solution.py:44
  195.6 17.2 %collective-permute-start.40 = (bf16[448,576]{1,0:T(8,128)(2,1)S(1)}, bf16[448,576]{1,0:T(8,128)(2,1)S(1)}, u32[]{:S(2)}, u32[]{:S(2)}) collective-permute-start(bf16[448,576]{1,0:T(8,128)(2,1)S(1)} %collective-permute-done.27), channel_id=1, source_target_pairs={{0,48},{1,49},{2,50},{3,51},{8,56},{9,57},{10,58},{11,59},{16,0},{... | collective-permute-start | bytes 1548296 | tf_op jit(solution)/shard_map/ppermute | solution.py:44
  199.4 14.5 %collective-permute-start.39 = (bf16[448,576]{1,0:T(8,128)(2,1)S(1)}, bf16[448,576]{1,0:T(8,128)(2,1)S(1)}, u32[]{:S(2)}, u32[]{:S(2)}) collective-permute-start(bf16[448,576]{1,0:T(8,128)(2,1)S(1)} %collective-permute-done.31), channel_id=1, source_target_pairs={{0,16},{1,17},{2,18},{3,19},{8,24},{9,25},{10,26},{11,27},{16,32},... | collective-permute-start | bytes 1548296 | tf_op jit(solution)/shard_map/ppermute | solution.py:44
  214.2 23.3 %collective-permute-start.38 = (bf16[448,768]{1,0:T(8,128)(2,1)S(1)}, bf16[448,768]{1,0:T(8,128)(2,1)S(1)}, u32[]{:S(2)}, u32[]{:S(2)}) collective-permute-start(bf16[448,768]{1,0:T(8,128)(2,1)S(1)} %get-tuple-element.80), channel_id=1, source_target_pairs={{0,7},{1,4},{2,5},{3,6},{8,15},{9,12},{10,13},{11,14},{16,20},{17,... | collective-permute-start | bytes 2064392 | tf_op jit(solution)/shard_map/ppermute | solution.py:44
  219.2 31.4 %collective-permute-start.37 = (bf16[448,768]{1,0:T(8,128)(2,1)S(1)}, bf16[448,768]{1,0:T(8,128)(2,1)S(1)}, u32[]{:S(2)}, u32[]{:S(2)}) collective-permute-start(bf16[448,768]{1,0:T(8,128)(2,1)S(1)} %get-tuple-element.79), channel_id=1, source_target_pairs={{0,5},{1,6},{2,7},{3,4},{8,13},{9,14},{10,15},{11,12},{16,22},{17,... | collective-permute-start | bytes 2064392 | tf_op jit(solution)/shard_map/ppermute | solution.py:44
  224.1 41.5 %collective-permute-start.43 = (bf16[448,768]{1,0:T(8,128)(2,1)S(1)}, bf16[448,768]{1,0:T(8,128)(2,1)S(1)}, u32[]{:S(2)}, u32[]{:S(2)}) collective-permute-start(bf16[448,768]{1,0:T(8,128)(2,1)S(1)} %get-tuple-element.84), channel_id=1, source_target_pairs={{0,4},{1,5},{2,6},{3,7},{8,12},{9,13},{10,14},{11,15},{16,21},{17,... | collective-permute-start | bytes 2064392 | tf_op jit(solution)/shard_map/ppermute | solution.py:44
  229.1 36.5 %collective-permute-start.42 = (bf16[448,768]{1,0:T(8,128)(2,1)S(1)}, bf16[448,768]{1,0:T(8,128)(2,1)S(1)}, u32[]{:S(2)}, u32[]{:S(2)}) collective-permute-start(bf16[448,768]{1,0:T(8,128)(2,1)S(1)} %get-tuple-element.83), channel_id=1, source_target_pairs={{0,2},{1,3},{2,0},{3,1},{8,10},{9,11},{10,8},{11,9},{16,19},{17,16... | collective-permute-start | bytes 2064392 | tf_op jit(solution)/shard_map/ppermute | solution.py:44
  (46 other events, 530.7 us)

commit v9 on v7

--- a/solution.py
+++ b/solution.py
@@ -338,8 +338,8 @@
         return [pairs[1], tokens_ll, near_rr]
 
     far = send(gate_up, y_far)
-    blocks = ring(gate_up, far, x_up, x_down, (near_l, near_r, down_block, every), between)
-    swap(blocks[2:4], blocks[4], blocks[5], down_far)
+    blocks = ring(gate_up, far, x_up, x_down, (near_l, near_r), between)
+    swap(blocks[2:4], blocks[4], blocks[5], down_far, every)
     swap(blocks[4:6])
 
     steps = jnp.array([dy + 4 * (dx % 4) for dy, dx in ORDER] + [0] * 8, jnp.int32)

time: 264 us -> 269 us (1.019)
  starting transfers between devices: 66.3 us -> 79.5 us
  waiting for transfers between devices: 127 us -> 117 us
    ppermute x45, starting transfers between devices: 66.3 us -> 79.5 us  [send(): return lax.ppermute(array, AXES, pairs)]
    ppermute x45, waiting for transfers between devices: 127 us -> 117 us  [send(): return lax.ppermute(array, AXES, pairs)]
    unnamed x62 -> x50, local copies, waits for them, and re-layouts: 5.39 us -> 3.43 us
  transfers between devices with their start and end apart: 45 -> 45, of which waited for: 22 -> 24; matrix products, arithmetic and copies ran while one was open for 8% -> 8% of each run, Pallas kernels for 14% -> 14%
where the time goes in v9:
time: 269 us; the launch traced here: 268 us
  waiting for transfers between devices  117 us (43%)
  starting transfers between devices  79.5 us (30%)
  Pallas kernels  37 us (14%)
  other arithmetic  25.6 us (10%)
  local copies, waits for them, and re-layouts  6.74 us (3%)
    ppermute x45, waiting for transfers between devices, send(): return lax.ppermute(array, AXES, pairs)  117 us
    ppermute x45, starting transfers between devices, send(): return lax.ppermute(array, AXES, pairs)  79.5 us
    pallas_call x2, Pallas kernels, token_sum(): pl.pallas_call(functools.partial(token_kernel, len(blocks), first, before...  26.7 us
    pallas_call x4, Pallas kernels, down_terms(): pl.pallas_call(down_kernel, out_shape=[jax.ShapeDtypeStruct((columns, row...  10.3 us
    another operation x3, other arithmetic, swap(): pair = jnp.stack(blocks[n:n + 2])  7.81 us
  transfers between devices with their start and end apart: 45, of which 24 were waited for; matrix products, arithmetic and copies ran while one was open for 8% of the time, Pallas kernels for 14%

profile of v9, /device:TPU:6, one launch (start us, length us, event | category | flops | bytes accessed | tf_op | source)
XLA Modules:
  0.0 267.8 jit_solution(7022064013374283874)
XLA Ops:
  2.1 4.1 %collective-permute-start.2 = (bf16[768,512]{1,0:T(8,128)(2,1)S(1)}, bf16[768,512]{1,0:T(8,128)(2,1)S(1)}, u32[]{:S(2)}, u32[]{:S(2)}) collective-permute-start(bf16[768,512]{1,0:T(8,128)(2,1)S(1)} %fusion.1.refs_0_), channel_id=1, source_target_pairs={{0,3},{1,0},{2,1},{3,2},{8,11},{9,8},{10,9},{11,10},{16,19},{17,16... | collective-permute-start | bytes 2359304 | tf_op jit(solution)/shard_map/ppermute | solution.py:44
  16.7 3.4 %collective-permute-done.8 = f32[120,128]{1,0:T(8,128)S(1)} collective-permute-done((f32[120,128]{1,0:T(8,128)S(1)}, f32[120,128]{1,0:T(8,128)S(1)}, u32[]{:S(2)}, u32[]{:S(2)}) %collective-permute-start.8) | collective-permute-done | bytes 61472 | tf_op jit(solution)/shard_map/ppermute | solution.py:44
  21.6 3.7 %multiply_convert_fusion.2 = (bf16[224,1152]{1,0:T(8,128)(2,1)S(1)}, bf16[224,1152]{1,0:T(8,128)(2,1)S(1)}) fusion(f32[224,1152]{1,0:T(8,128)} %param.6, f32[1152]{0:T(1024)S(1)} %get-tuple-element.101, f32[1152]{0:T(1024)S(1)} %get-tuple-element.102, f32[1152]{0:T(1024)S(1)} %get-tuple-element.100, pred[224]{0:T(512)(128)(4,1)S(1)} %broadcast_compare_fusion.23, ...), kind=kLoop, calls=%fused_computation.20 | loop fusion | flops 9289728 | bytes 3124896 | tf_op jit(solution)/shard_map/convert_element_type | solution.py:129
  29.7 2.8 %collective-permute-start.10 = (bf16[224,2304]{1,0:T(8,128)(2,1)}, bf16[224,2304]{1,0:T(8,128)(2,1)}, u32[]{:S(2)}, u32[]{:S(2)}) collective-permute-start(bf16[224,2304]{1,0:T(8,128)(2,1)} %pad_maximum_fusion.8), channel_id=1, source_target_pairs={{0,64},{1,65},{2,66},{3,67},{8,72},{9,73},{10,74},{11,75},{16,80},... | collective-permute-start | bytes 3096584 | tf_op jit(solution)/shard_map/ppermute | solution.py:44
  32.5 3.4 %collective-permute-start.4 = (bf16[768,512]{1,0:T(8,128)(2,1)S(1)}, bf16[768,512]{1,0:T(8,128)(2,1)S(1)}, u32[]{:S(2)}, u32[]{:S(2)}) collective-permute-start(bf16[768,512]{1,0:T(8,128)(2,1)S(1)} %collective-permute-done.refs_1_), channel_id=1, source_target_pairs={{0,3},{1,0},{2,1},{3,2},{8,11},{9,8},{10,9},{11,10},{16,19},{17,16... | collective-permute-start | bytes 2359304 | tf_op jit(solution)/shard_map/ppermute | solution.py:44
  36.1 15.3 %collective-permute-done.4.refs_5_ = bf16[768,512]{1,0:T(8,128)(2,1)S(1)} collective-permute-done((bf16[768,512]{1,0:T(8,128)(2,1)S(1)}, bf16[768,512]{1,0:T(8,128)(2,1)S(1)}, u32[]{:S(2)}, u32[]{:S(2)}) %collective-permute-start.4) | collective-permute-done | bytes 786464 | tf_op jit(solution)/shard_map/ppermute | solution.py:44
  51.4 3.5 %collective-permute-done.3.refs_4_ = bf16[768,512]{1,0:T(8,128)(2,1)} collective-permute-done((bf16[768,512]{1,0:T(8,128)(2,1)S(1)}, bf16[768,512]{1,0:T(8,128)(2,1)}, u32[]{:S(2)}, u32[]{:S(2)}) %collective-permute-start.3) | collective-permute-done | bytes 786464 | tf_op jit(solution)/shard_map/ppermute | solution.py:44
  59.1 4.9 %collective-permute-start.13 = (bf16[448,576]{1,0:T(8,128)(2,1)S(1)}, bf16[448,576]{1,0:T(8,128)(2,1)S(1)}, u32[]{:S(2)}, u32[]{:S(2)}) collective-permute-start(bf16[448,576]{1,0:T(8,128)(2,1)S(1)} %fusion.3), channel_id=1, source_target_pairs={{0,0},{1,16},{2,32},{3,48},{8,8},{9,24},{10,40},{11,56},{16,49},{1... | collective-permute-start | bytes 1548296 | tf_op jit(solution)/shard_map/ppermute | solution.py:44
  67.2 13.0 %collective-permute-done.13 = bf16[448,576]{1,0:T(8,128)(2,1)S(1)} collective-permute-done((bf16[448,576]{1,0:T(8,128)(2,1)S(1)}, bf16[448,576]{1,0:T(8,128)(2,1)S(1)}, u32[]{:S(2)}, u32[]{:S(2)}) %collective-permute-start.13) | collective-permute-done | bytes 516128 | tf_op jit(solution)/shard_map/ppermute | solution.py:44
  80.2 3.0 %collective-permute-start.19 = (f32[120,128]{1,0:T(8,128)S(1)}, f32[120,128]{1,0:T(8,128)S(1)}, u32[]{:S(2)}, u32[]{:S(2)}) collective-permute-start(f32[120,128]{1,0:T(8,128)S(1)} %max.37), channel_id=1, source_target_pairs={{0,4},{1,5},{2,6},{3,7},{8,12},{9,13},{10,14},{11,15},{16,20},{17,... | collective-permute-start | bytes 184328 | tf_op jit(solution)/shard_map/ppermute | solution.py:44
  85.4 3.5 %collective-permute-start.15 = (bf16[448,576]{1,0:T(8,128)(2,1)S(1)}, bf16[448,576]{1,0:T(8,128)(2,1)S(1)}, u32[]{:S(2)}, u32[]{:S(2)}) collective-permute-start(bf16[448,576]{1,0:T(8,128)(2,1)S(1)} %collective-permute-done.13), channel_id=1, source_target_pairs={{0,64},{1,65},{2,66},{3,67},{8,72},{9,73},{10,74},{11,75},{16,80},... | collective-permute-start | bytes 1548296 | tf_op jit(solution)/shard_map/ppermute | solution.py:44
  89.3 7.3 %collective-permute-done.5.refs_6_ = bf16[768,512]{1,0:T(8,128)(2,1)S(1)} collective-permute-done((bf16[768,512]{1,0:T(8,128)(2,1)S(1)}, bf16[768,512]{1,0:T(8,128)(2,1)S(1)}, u32[]{:S(2)}, u32[]{:S(2)}) %collective-permute-start.5) | collective-permute-done | bytes 786464 | tf_op jit(solution)/shard_map/ppermute | solution.py:44
  101.1 2.7 %pad_maximum_fusion.2.refs_12_ = bf16[2,224,2304]{2,1,0:T(8,128)(2,1)} fusion(bf16[1,224,2304]{2,1,0:T(8,128)(2,1)} %bitcast.27, bf16[1,224,2304]{2,1,0:T(8,128)(2,1)S(1)} %bitcast.51), kind=kLoop, calls=%fused_computation.2 | loop fusion | flops 1032192 | bytes 4128768 | tf_op jit(solution)/shard_map/stack | solution.py:326
  104.0 3.3 %pad_maximum_fusion.1.refs_10_ = bf16[2,224,2304]{2,1,0:T(8,128)(2,1)} fusion(bf16[1,224,2304]{2,1,0:T(8,128)(2,1)} %bitcast.25, bf16[1,224,2304]{2,1,0:T(8,128)(2,1)} %bitcast.24), kind=kLoop, calls=%fused_computation.1 | loop fusion | flops 1032192 | bytes 4128768 | tf_op jit(solution)/shard_map/stack | solution.py:326
  113.1 19.8 %shard_map.68.refs_8_ = f32[768,2304]{1,0:T(8,128)} custom-call(s32[16]{0:T(128)} %compare_select_fusion.5.info, bf16[768,512]{1,0:T(8,128)(2,1)} %copy-done.1, bf16[768,512]{1,0:T(8,128)(2,1)} %copy-done.7, bf16[768,512]{1,0:T(8,128)(2,1)} %copy-done.5, bf16[768,512]{1,0:T(8,128)(2,1)} %copy-done.3, bf16[768,512]{1,0:T(8,128)(2,1)} %collective-permute-done.3.refs_4_, ...), custom_call_target="tpu_custom_call" | custom-call | tf_op jit(solution)/shard_map/pallas_call | solution.py:213
  139.2 3.8 %collective-permute-start.24 = (f32[120,128]{1,0:T(8,128)S(1)}, f32[120,128]{1,0:T(8,128)S(1)}, u32[]{:S(2)}, u32[]{:S(2)}) collective-permute-start(f32[120,128]{1,0:T(8,128)S(1)} %max.40), channel_id=1, source_target_pairs={{0,2},{1,3},{2,0},{3,1},{8,10},{9,11},{10,8},{11,9},{16,18},{17,19... | collective-permute-start | bytes 184328 | tf_op jit(solution)/shard_map/ppermute | solution.py:44
  147.0 3.0 %copy-done = f32[768,2304]{1,0:T(8,128)S(1)} copy-done((f32[768,2304]{1,0:T(8,128)S(1)}, f32[768,2304]{1,0:T(8,128)}, u32[]{:S(2)}) %copy-start) | copy-done | bytes 7077912
  150.0 6.9 %shard_map.69.hidden = bf16[768,1152]{1,0:T(8,128)(2,1)S(1)} custom-call(s32[16]{0:T(128)S(1)} %copy-done.15, bf16[768,512]{1,0:T(8,128)(2,1)S(1)} %copy-done.2, bf16[768,512]{1,0:T(8,128)(2,1)S(1)} %copy-done.8, bf16[768,512]{1,0:T(8,128)(2,1)S(1)} %copy-done.6, bf16[768,512]{1,0:T(8,128)(2,1)S(1)} %copy-done.4, ...), custom_call_target="tpu_custom_call" | custom-call | tf_op jit(solution)/shard_map/pallas_call | solution.py:213
  159.8 4.9 %collective-permute-start.28 = (f32[120,128]{1,0:T(8,128)S(1)}, f32[120,128]{1,0:T(8,128)S(1)}, u32[]{:S(2)}, u32[]{:S(2)}) collective-permute-start(f32[120,128]{1,0:T(8,128)S(1)} %max.41), channel_id=1, source_target_pairs={{0,64},{1,65},{2,66},{3,67},{8,72},{9,73},{10,74},{11,75},{16,80},... | collective-permute-start | bytes 184328 | tf_op jit(solution)/shard_map/ppermute | solution.py:44
  167.3 5.1 %collective-permute-start.30 = (bf16[448,768]{1,0:T(8,128)(2,1)S(1)}, bf16[448,768]{1,0:T(8,128)(2,1)S(1)}, u32[]{:S(2)}, u32[]{:S(2)}) collective-permute-start(bf16[448,768]{1,0:T(8,128)(2,1)S(1)} %get-tuple-element.74), channel_id=1, source_target_pairs={{0,6},{1,7},{2,4},{3,5},{8,14},{9,15},{10,12},{11,13},{16,23},{17,... | collective-permute-start | bytes 2064392 | tf_op jit(solution)/shard_map/ppermute | solution.py:44
  172.4 4.8 %collective-permute-start.29 = (bf16[448,768]{1,0:T(8,128)(2,1)S(1)}, bf16[448,768]{1,0:T(8,128)(2,1)S(1)}, u32[]{:S(2)}, u32[]{:S(2)}) collective-permute-start(bf16[448,768]{1,0:T(8,128)(2,1)S(1)} %get-tuple-element.72), channel_id=1, source_target_pairs={{0,0},{1,1},{2,2},{3,3},{8,8},{9,9},{10,10},{11,11},{16,17},{17,18... | collective-permute-start | bytes 2064392 | tf_op jit(solution)/shard_map/ppermute | solution.py:44
  179.8 8.7 %collective-permute-done.30 = bf16[448,768]{1,0:T(8,128)(2,1)S(1)} collective-permute-done((bf16[448,768]{1,0:T(8,128)(2,1)S(1)}, bf16[448,768]{1,0:T(8,128)(2,1)S(1)}, u32[]{:S(2)}, u32[]{:S(2)}) %collective-permute-start.30) | collective-permute-done | bytes 688160 | tf_op jit(solution)/shard_map/ppermute | solution.py:44
  192.1 4.1 %collective-permute-start.34 = (bf16[448,768]{1,0:T(8,128)(2,1)S(1)}, bf16[448,768]{1,0:T(8,128)(2,1)S(1)}, u32[]{:S(2)}, u32[]{:S(2)}) collective-permute-start(bf16[448,768]{1,0:T(8,128)(2,1)S(1)} %get-tuple-element.77), channel_id=1, source_target_pairs={{0,3},{1,0},{2,1},{3,2},{8,11},{9,8},{10,9},{11,10},{16,16},{17,17... | collective-permute-start | bytes 2064392 | tf_op jit(solution)/shard_map/ppermute | solution.py:44
  196.2 2.9 %collective-permute-start.40 = (bf16[448,576]{1,0:T(8,128)(2,1)S(1)}, bf16[448,576]{1,0:T(8,128)(2,1)S(1)}, u32[]{:S(2)}, u32[]{:S(2)}) collective-permute-start(bf16[448,576]{1,0:T(8,128)(2,1)S(1)} %collective-permute-done.27), channel_id=1, source_target_pairs={{0,48},{1,49},{2,50},{3,51},{8,56},{9,57},{10,58},{11,59},{16,0},{... | collective-permute-start | bytes 1548296 | tf_op jit(solution)/shard_map/ppermute | solution.py:44
  202.1 10.5 %collective-permute-done.40 = bf16[448,576]{1,0:T(8,128)(2,1)S(1)} collective-permute-done((bf16[448,576]{1,0:T(8,128)(2,1)S(1)}, bf16[448,576]{1,0:T(8,128)(2,1)S(1)}, u32[]{:S(2)}, u32[]{:S(2)}) %collective-permute-start.40) | collective-permute-done | bytes 516128 | tf_op jit(solution)/shard_map/ppermute | solution.py:44
  213.9 2.7 %collective-permute-start.38 = (bf16[448,768]{1,0:T(8,128)(2,1)S(1)}, bf16[448,768]{1,0:T(8,128)(2,1)S(1)}, u32[]{:S(2)}, u32[]{:S(2)}) collective-permute-start(bf16[448,768]{1,0:T(8,128)(2,1)S(1)} %get-tuple-element.82), channel_id=1, source_target_pairs={{0,7},{1,4},{2,5},{3,6},{8,15},{9,12},{10,13},{11,14},{16,20},{17,... | collective-permute-start | bytes 2064392 | tf_op jit(solution)/shard_map/ppermute | solution.py:44
  216.6 4.5 %collective-permute-start.37 = (bf16[448,768]{1,0:T(8,128)(2,1)S(1)}, bf16[448,768]{1,0:T(8,128)(2,1)S(1)}, u32[]{:S(2)}, u32[]{:S(2)}) collective-permute-start(bf16[448,768]{1,0:T(8,128)(2,1)S(1)} %get-tuple-element.81), channel_id=1, source_target_pairs={{0,5},{1,6},{2,7},{3,4},{8,13},{9,14},{10,15},{11,12},{16,22},{17,... | collective-permute-start | bytes 2064392 | tf_op jit(solution)/shard_map/ppermute | solution.py:44
  223.7 3.5 %collective-permute-start.43 = (bf16[448,768]{1,0:T(8,128)(2,1)S(1)}, bf16[448,768]{1,0:T(8,128)(2,1)S(1)}, u32[]{:S(2)}, u32[]{:S(2)}) collective-permute-start(bf16[448,768]{1,0:T(8,128)(2,1)S(1)} %get-tuple-element.86), channel_id=1, source_target_pairs={{0,4},{1,5},{2,6},{3,7},{8,12},{9,13},{10,14},{11,15},{16,21},{17,... | collective-permute-start | bytes 2064392 | tf_op jit(solution)/shard_map/ppermute | solution.py:44
  227.1 2.7 %collective-permute-start.42 = (bf16[448,768]{1,0:T(8,128)(2,1)S(1)}, bf16[448,768]{1,0:T(8,128)(2,1)S(1)}, u32[]{:S(2)}, u32[]{:S(2)}) collective-permute-start(bf16[448,768]{1,0:T(8,128)(2,1)S(1)} %get-tuple-element.85), channel_id=1, source_target_pairs={{0,2},{1,3},{2,0},{3,1},{8,10},{9,11},{10,8},{11,9},{16,19},{17,16... | collective-permute-start | bytes 2064392 | tf_op jit(solution)/shard_map/ppermute | solution.py:44
  231.1 4.5 %collective-permute-done.44 = f32[120,128]{1,0:T(8,128)S(1)} collective-permute-done((f32[120,128]{1,0:T(8,128)S(1)}, f32[120,128]{1,0:T(8,128)S(1)}, u32[]{:S(2)}, u32[]{:S(2)}) %collective-permute-start.44) | collective-permute-done | bytes 61472 | tf_op jit(solution)/shard_map/ppermute | solution.py:44
  236.5 13.6 %collective-permute-done.37 = bf16[448,768]{1,0:T(8,128)(2,1)S(1)} collective-permute-done((bf16[448,768]{1,0:T(8,128)(2,1)S(1)}, bf16[448,768]{1,0:T(8,128)(2,1)S(1)}, u32[]{:S(2)}, u32[]{:S(2)}) %collective-permute-start.37) | collective-permute-done | bytes 688160 | tf_op jit(solution)/shard_map/ppermute | solution.py:44
  250.1 16.1 %collective-permute-done.43 = bf16[448,768]{1,0:T(8,128)(2,1)S(1)} collective-permute-done((bf16[448,768]{1,0:T(8,128)(2,1)S(1)}, bf16[448,768]{1,0:T(8,128)(2,1)S(1)}, u32[]{:S(2)}, u32[]{:S(2)}) %collective-permute-start.43) | collective-permute-done | bytes 688160 | tf_op jit(solution)/shard_map/ppermute | solution.py:44
  (195 shorter events, 70.2 us)
Async XLA Ops:
  2.1 27.6 %collective-permute-start.2 = (bf16[768,512]{1,0:T(8,128)(2,1)S(1)}, bf16[768,512]{1,0:T(8,128)(2,1)S(1)}, u32[]{:S(2)}, u32[]{:S(2)}) collective-permute-start(bf16[768,512]{1,0:T(8,128)(2,1)S(1)} %fusion.1.refs_0_), channel_id=1, source_target_pairs={{0,3},{1,0},{2,1},{3,2},{8,11},{9,8},{10,9},{11,10},{16,19},{17,16... | collective-permute-start | bytes 2359304 | tf_op jit(solution)/shard_map/ppermute | solution.py:44
  6.2 26.3 %collective-permute-start.1 = (bf16[768,512]{1,0:T(8,128)(2,1)S(1)}, bf16[768,512]{1,0:T(8,128)(2,1)S(1)}, u32[]{:S(2)}, u32[]{:S(2)}) collective-permute-start(bf16[768,512]{1,0:T(8,128)(2,1)S(1)} %fusion.1.refs_0_), channel_id=1, source_target_pairs={{0,1},{1,2},{2,3},{3,0},{8,9},{9,10},{10,11},{11,8},{16,17},{17,18... | collective-permute-start | bytes 2359304 | tf_op jit(solution)/shard_map/ppermute | solution.py:44
  6.2 26.3 %collective-permute-start = (bf16[768,512]{1,0:T(8,128)(2,1)S(1)}, bf16[768,512]{1,0:T(8,128)(2,1)S(1)}, u32[]{:S(2)}, u32[]{:S(2)}) collective-permute-start(bf16[768,512]{1,0:T(8,128)(2,1)S(1)} %fusion.1.refs_0_), channel_id=1, source_target_pairs={{0,4},{1,5},{2,6},{3,7},{8,12},{9,13},{10,14},{11,15},{16,20},{17,... | collective-permute-start | bytes 2359304 | tf_op jit(solution)/shard_map/ppermute | solution.py:44
  26.4 28.5 %collective-permute-start.12 = (bf16[224,2304]{1,0:T(8,128)(2,1)}, bf16[224,2304]{1,0:T(8,128)(2,1)}, u32[]{:S(2)}, u32[]{:S(2)}) collective-permute-start(bf16[224,2304]{1,0:T(8,128)(2,1)} %pad_maximum_fusion.8), channel_id=1, source_target_pairs={{0,48},{1,49},{2,50},{3,51},{8,56},{9,57},{10,58},{11,59},{16,0},{... | collective-permute-start | bytes 3096584 | tf_op jit(solution)/shard_map/ppermute | solution.py:44
  27.3 27.6 %collective-permute-start.11 = (bf16[224,2304]{1,0:T(8,128)(2,1)}, bf16[224,2304]{1,0:T(8,128)(2,1)}, u32[]{:S(2)}, u32[]{:S(2)}) collective-permute-start(bf16[224,2304]{1,0:T(8,128)(2,1)} %pad_maximum_fusion.8), channel_id=1, source_target_pairs={{0,16},{1,17},{2,18},{3,19},{8,24},{9,25},{10,26},{11,27},{16,32},... | collective-permute-start | bytes 3096584 | tf_op jit(solution)/shard_map/ppermute | solution.py:44
  29.7 25.2 %collective-permute-start.10 = (bf16[224,2304]{1,0:T(8,128)(2,1)}, bf16[224,2304]{1,0:T(8,128)(2,1)}, u32[]{:S(2)}, u32[]{:S(2)}) collective-permute-start(bf16[224,2304]{1,0:T(8,128)(2,1)} %pad_maximum_fusion.8), channel_id=1, source_target_pairs={{0,64},{1,65},{2,66},{3,67},{8,72},{9,73},{10,74},{11,75},{16,80},... | collective-permute-start | bytes 3096584 | tf_op jit(solution)/shard_map/ppermute | solution.py:44
  32.5 18.8 %collective-permute-start.4 = (bf16[768,512]{1,0:T(8,128)(2,1)S(1)}, bf16[768,512]{1,0:T(8,128)(2,1)S(1)}, u32[]{:S(2)}, u32[]{:S(2)}) collective-permute-start(bf16[768,512]{1,0:T(8,128)(2,1)S(1)} %collective-permute-done.refs_1_), channel_id=1, source_target_pairs={{0,3},{1,0},{2,1},{3,2},{8,11},{9,8},{10,9},{11,10},{16,19},{17,16... | collective-permute-start | bytes 2359304 | tf_op jit(solution)/shard_map/ppermute | solution.py:44
  35.9 18.9 %collective-permute-start.3 = (bf16[768,512]{1,0:T(8,128)(2,1)S(1)}, bf16[768,512]{1,0:T(8,128)(2,1)}, u32[]{:S(2)}, u32[]{:S(2)}) collective-permute-start(bf16[768,512]{1,0:T(8,128)(2,1)S(1)} %collective-permute-done.refs_1_), channel_id=1, source_target_pairs={{0,1},{1,2},{2,3},{3,0},{8,9},{9,10},{10,11},{11,8},{16,17},{17,18... | collective-permute-start | bytes 2359304 | tf_op jit(solution)/shard_map/ppermute | solution.py:44
  56.8 23.5 %collective-permute-start.14 = (bf16[2,224,2304]{2,1,0:T(8,128)(2,1)S(1)}, bf16[2,224,2304]{2,1,0:T(8,128)(2,1)S(1)}, u32[]{:S(2)}, u32[]{:S(2)}) collective-permute-start(bf16[2,224,2304]{2,1,0:T(8,128)(2,1)S(1)} %pad_maximum_fusion.refs_8_), channel_id=1, source_target_pairs={{0,8},{1,9},{2,10},{3,11},{8,0},{9,1},{10,2},{11,3},{16,24},{17,25... | collective-permute-start | bytes 6193160 | tf_op jit(solution)/shard_map/ppermute | solution.py:44
  59.1 21.0 %collective-permute-start.13 = (bf16[448,576]{1,0:T(8,128)(2,1)S(1)}, bf16[448,576]{1,0:T(8,128)(2,1)S(1)}, u32[]{:S(2)}, u32[]{:S(2)}) collective-permute-start(bf16[448,576]{1,0:T(8,128)(2,1)S(1)} %fusion.3), channel_id=1, source_target_pairs={{0,0},{1,16},{2,32},{3,48},{8,8},{9,24},{10,40},{11,56},{16,49},{1... | collective-permute-start | bytes 1548296 | tf_op jit(solution)/shard_map/ppermute | solution.py:44
  64.1 25.2 %collective-permute-start.17 = (bf16[224,2304]{1,0:T(8,128)(2,1)}, bf16[224,2304]{1,0:T(8,128)(2,1)S(1)}, u32[]{:S(2)}, u32[]{:S(2)}) collective-permute-start(bf16[224,2304]{1,0:T(8,128)(2,1)} %collective-permute-done.10), channel_id=1, source_target_pairs={{0,16},{1,17},{2,18},{3,19},{8,24},{9,25},{10,26},{11,27},{16,32},... | collective-permute-start | bytes 3096584 | tf_op jit(solution)/shard_map/ppermute | solution.py:44
  64.2 37.0 %collective-permute-start.18 = (bf16[224,2304]{1,0:T(8,128)(2,1)}, bf16[224,2304]{1,0:T(8,128)(2,1)}, u32[]{:S(2)}, u32[]{:S(2)}) collective-permute-start(bf16[224,2304]{1,0:T(8,128)(2,1)} %collective-permute-done.10), channel_id=1, source_target_pairs={{0,48},{1,49},{2,50},{3,51},{8,56},{9,57},{10,58},{11,59},{16,0},{... | collective-permute-start | bytes 3096584 | tf_op jit(solution)/shard_map/ppermute | solution.py:44
  66.2 30.4 %collective-permute-start.5 = (bf16[768,512]{1,0:T(8,128)(2,1)S(1)}, bf16[768,512]{1,0:T(8,128)(2,1)S(1)}, u32[]{:S(2)}, u32[]{:S(2)}) collective-permute-start(bf16[768,512]{1,0:T(8,128)(2,1)S(1)} %collective-permute-done.1.refs_2_), channel_id=1, source_target_pairs={{0,1},{1,2},{2,3},{3,0},{8,9},{9,10},{10,11},{11,8},{16,17},{17,18... | collective-permute-start | bytes 2359304 | tf_op jit(solution)/shard_map/ppermute | solution.py:44
  80.2 18.8 %collective-permute-start.6 = (bf16[768,512]{1,0:T(8,128)(2,1)S(1)}, bf16[768,512]{1,0:T(8,128)(2,1)S(1)}, u32[]{:S(2)}, u32[]{:S(2)}) collective-permute-start(bf16[768,512]{1,0:T(8,128)(2,1)S(1)} %collective-permute-done.4.refs_5_), channel_id=1, source_target_pairs={{0,3},{1,0},{2,1},{3,2},{8,11},{9,8},{10,9},{11,10},{16,19},{17,16... | collective-permute-start | bytes 2359304 | tf_op jit(solution)/shard_map/ppermute | solution.py:44
  85.4 18.5 %collective-permute-start.15 = (bf16[448,576]{1,0:T(8,128)(2,1)S(1)}, bf16[448,576]{1,0:T(8,128)(2,1)S(1)}, u32[]{:S(2)}, u32[]{:S(2)}) collective-permute-start(bf16[448,576]{1,0:T(8,128)(2,1)S(1)} %collective-permute-done.13), channel_id=1, source_target_pairs={{0,64},{1,65},{2,66},{3,67},{8,72},{9,73},{10,74},{11,75},{16,80},... | collective-permute-start | bytes 1548296 | tf_op jit(solution)/shard_map/ppermute | solution.py:44
  108.0 25.5 %collective-permute-start.22 = (bf16[224,2304]{1,0:T(8,128)(2,1)}, bf16[224,2304]{1,0:T(8,128)(2,1)}, u32[]{:S(2)}, u32[]{:S(2)}) collective-permute-start(bf16[224,2304]{1,0:T(8,128)(2,1)} %collective-permute-done.11), channel_id=1, source_target_pairs={{0,16},{1,17},{2,18},{3,19},{8,24},{9,25},{10,26},{11,27},{16,32},... | collective-permute-start | bytes 3096584 | tf_op jit(solution)/shard_map/ppermute | solution.py:44
  108.7 26.4 %collective-permute-start.23 = (bf16[224,2304]{1,0:T(8,128)(2,1)}, bf16[224,2304]{1,0:T(8,128)(2,1)}, u32[]{:S(2)}, u32[]{:S(2)}) collective-permute-start(bf16[224,2304]{1,0:T(8,128)(2,1)} %collective-permute-done.18), channel_id=1, source_target_pairs={{0,48},{1,49},{2,50},{3,51},{8,56},{9,57},{10,58},{11,59},{16,0},{... | collective-permute-start | bytes 3096584 | tf_op jit(solution)/shard_map/ppermute | solution.py:44
  137.1 22.4 %collective-permute-start.31 = (bf16[448,576]{1,0:T(8,128)(2,1)}, bf16[448,576]{1,0:T(8,128)(2,1)S(1)}, u32[]{:S(2)}, u32[]{:S(2)}) collective-permute-start(bf16[448,576]{1,0:T(8,128)(2,1)} %copy-done.19), channel_id=1, source_target_pairs={{0,16},{1,17},{2,18},{3,19},{8,24},{9,25},{10,26},{11,27},{16,32},... | collective-permute-start | bytes 1548296 | tf_op jit(solution)/shard_map/ppermute | solution.py:44
  137.9 21.6 %collective-permute-start.32 = (bf16[448,576]{1,0:T(8,128)(2,1)}, bf16[448,576]{1,0:T(8,128)(2,1)S(1)}, u32[]{:S(2)}, u32[]{:S(2)}) collective-permute-start(bf16[448,576]{1,0:T(8,128)(2,1)} %copy-done.19), channel_id=1, source_target_pairs={{0,48},{1,49},{2,50},{3,51},{8,56},{9,57},{10,58},{11,59},{16,0},{... | collective-permute-start | bytes 1548296 | tf_op jit(solution)/shard_map/ppermute | solution.py:44
  143.0 24.3 %collective-permute-start.27 = (bf16[448,576]{1,0:T(8,128)(2,1)}, bf16[448,576]{1,0:T(8,128)(2,1)S(1)}, u32[]{:S(2)}, u32[]{:S(2)}) collective-permute-start(bf16[448,576]{1,0:T(8,128)(2,1)} %copy-done.20), channel_id=1, source_target_pairs={{0,48},{1,49},{2,50},{3,51},{8,56},{9,57},{10,58},{11,59},{16,0},{... | collective-permute-start | bytes 1548296 | tf_op jit(solution)/shard_map/ppermute | solution.py:44
  145.2 22.1 %collective-permute-start.26 = (bf16[448,576]{1,0:T(8,128)(2,1)}, bf16[448,576]{1,0:T(8,128)(2,1)S(1)}, u32[]{:S(2)}, u32[]{:S(2)}) collective-permute-start(bf16[448,576]{1,0:T(8,128)(2,1)} %copy-done.20), channel_id=1, source_target_pairs={{0,16},{1,17},{2,18},{3,19},{8,24},{9,25},{10,26},{11,27},{16,32},... | collective-permute-start | bytes 1548296 | tf_op jit(solution)/shard_map/ppermute | solution.py:44
  159.7 17.5 %collective-permute-start.33 = (bf16[2,448,576]{2,1,0:T(8,128)(2,1)S(1)}, bf16[2,448,576]{2,1,0:T(8,128)(2,1)S(1)}, u32[]{:S(2)}, u32[]{:S(2)}) collective-permute-start(bf16[2,448,576]{2,1,0:T(8,128)(2,1)S(1)} %pad_maximum_fusion.5.mine), channel_id=1, source_target_pairs={{0,8},{1,9},{2,10},{3,11},{8,0},{9,1},{10,2},{11,3},{16,24},{17,25... | collective-permute-start | bytes 3096584 | tf_op jit(solution)/shard_map/ppermute | solution.py:44
  167.3 21.2 %collective-permute-start.30 = (bf16[448,768]{1,0:T(8,128)(2,1)S(1)}, bf16[448,768]{1,0:T(8,128)(2,1)S(1)}, u32[]{:S(2)}, u32[]{:S(2)}) collective-permute-start(bf16[448,768]{1,0:T(8,128)(2,1)S(1)} %get-tuple-element.74), channel_id=1, source_target_pairs={{0,6},{1,7},{2,4},{3,5},{8,14},{9,15},{10,12},{11,13},{16,23},{17,... | collective-permute-start | bytes 2064392 | tf_op jit(solution)/shard_map/ppermute | solution.py:44
  172.4 18.7 %collective-permute-start.29 = (bf16[448,768]{1,0:T(8,128)(2,1)S(1)}, bf16[448,768]{1,0:T(8,128)(2,1)S(1)}, u32[]{:S(2)}, u32[]{:S(2)}) collective-permute-start(bf16[448,768]{1,0:T(8,128)(2,1)S(1)} %get-tuple-element.72), channel_id=1, source_target_pairs={{0,0},{1,1},{2,2},{3,3},{8,8},{9,9},{10,10},{11,11},{16,17},{17,18... | collective-permute-start | bytes 2064392 | tf_op jit(solution)/shard_map/ppermute | solution.py:44
  191.4 21.2 %collective-permute-start.35 = (bf16[448,768]{1,0:T(8,128)(2,1)S(1)}, bf16[448,768]{1,0:T(8,128)(2,1)S(1)}, u32[]{:S(2)}, u32[]{:S(2)}) collective-permute-start(bf16[448,768]{1,0:T(8,128)(2,1)S(1)} %get-tuple-element.78), channel_id=1, source_target_pairs={{0,1},{1,2},{2,3},{3,0},{8,9},{9,10},{10,11},{11,8},{16,18},{17,19... | collective-permute-start | bytes 2064392 | tf_op jit(solution)/shard_map/ppermute | solution.py:44
  192.1 21.2 %collective-permute-start.34 = (bf16[448,768]{1,0:T(8,128)(2,1)S(1)}, bf16[448,768]{1,0:T(8,128)(2,1)S(1)}, u32[]{:S(2)}, u32[]{:S(2)}) collective-permute-start(bf16[448,768]{1,0:T(8,128)(2,1)S(1)} %get-tuple-element.77), channel_id=1, source_target_pairs={{0,3},{1,0},{2,1},{3,2},{8,11},{9,8},{10,9},{11,10},{16,16},{17,17... | collective-permute-start | bytes 2064392 | tf_op jit(solution)/shard_map/ppermute | solution.py:44
  196.2 16.4 %collective-permute-start.40 = (bf16[448,576]{1,0:T(8,128)(2,1)S(1)}, bf16[448,576]{1,0:T(8,128)(2,1)S(1)}, u32[]{:S(2)}, u32[]{:S(2)}) collective-permute-start(bf16[448,576]{1,0:T(8,128)(2,1)S(1)} %collective-permute-done.27), channel_id=1, source_target_pairs={{0,48},{1,49},{2,50},{3,51},{8,56},{9,57},{10,58},{11,59},{16,0},{... | collective-permute-start | bytes 1548296 | tf_op jit(solution)/shard_map/ppermute | solution.py:44
  199.1 14.5 %collective-permute-start.39 = (bf16[448,576]{1,0:T(8,128)(2,1)S(1)}, bf16[448,576]{1,0:T(8,128)(2,1)S(1)}, u32[]{:S(2)}, u32[]{:S(2)}) collective-permute-start(bf16[448,576]{1,0:T(8,128)(2,1)S(1)} %collective-permute-done.31), channel_id=1, source_target_pairs={{0,16},{1,17},{2,18},{3,19},{8,24},{9,25},{10,26},{11,27},{16,32},... | collective-permute-start | bytes 1548296 | tf_op jit(solution)/shard_map/ppermute | solution.py:44
  213.9 22.6 %collective-permute-start.38 = (bf16[448,768]{1,0:T(8,128)(2,1)S(1)}, bf16[448,768]{1,0:T(8,128)(2,1)S(1)}, u32[]{:S(2)}, u32[]{:S(2)}) collective-permute-start(bf16[448,768]{1,0:T(8,128)(2,1)S(1)} %get-tuple-element.82), channel_id=1, source_target_pairs={{0,7},{1,4},{2,5},{3,6},{8,15},{9,12},{10,13},{11,14},{16,20},{17,... | collective-permute-start | bytes 2064392 | tf_op jit(solution)/shard_map/ppermute | solution.py:44
  216.6 33.5 %collective-permute-start.37 = (bf16[448,768]{1,0:T(8,128)(2,1)S(1)}, bf16[448,768]{1,0:T(8,128)(2,1)S(1)}, u32[]{:S(2)}, u32[]{:S(2)}) collective-permute-start(bf16[448,768]{1,0:T(8,128)(2,1)S(1)} %get-tuple-element.81), channel_id=1, source_target_pairs={{0,5},{1,6},{2,7},{3,4},{8,13},{9,14},{10,15},{11,12},{16,22},{17,... | collective-permute-start | bytes 2064392 | tf_op jit(solution)/shard_map/ppermute | solution.py:44
  223.7 42.5 %collective-permute-start.43 = (bf16[448,768]{1,0:T(8,128)(2,1)S(1)}, bf16[448,768]{1,0:T(8,128)(2,1)S(1)}, u32[]{:S(2)}, u32[]{:S(2)}) collective-permute-start(bf16[448,768]{1,0:T(8,128)(2,1)S(1)} %get-tuple-element.86), channel_id=1, source_target_pairs={{0,4},{1,5},{2,6},{3,7},{8,12},{9,13},{10,14},{11,15},{16,21},{17,... | collective-permute-start | bytes 2064392 | tf_op jit(solution)/shard_map/ppermute | solution.py:44
  227.1 39.1 %collective-permute-start.42 = (bf16[448,768]{1,0:T(8,128)(2,1)S(1)}, bf16[448,768]{1,0:T(8,128)(2,1)S(1)}, u32[]{:S(2)}, u32[]{:S(2)}) collective-permute-start(bf16[448,768]{1,0:T(8,128)(2,1)S(1)} %get-tuple-element.85), channel_id=1, source_target_pairs={{0,2},{1,3},{2,0},{3,1},{8,10},{9,11},{10,8},{11,9},{16,19},{17,16... | collective-permute-start | bytes 2064392 | tf_op jit(solution)/shard_map/ppermute | solution.py:44
  (39 other events, 465.6 us)

commit v10 on v9

--- a/solution.py
+++ b/solution.py
@@ -326,7 +326,7 @@
             pair = jnp.stack(blocks[n : n + 2])
             pairs.extend((pair, send(pair, other_core)))
 
-    down_block = send(after(down_weight.T, near_l, near_r), to_ff_group)
+    down_block = send(after(down_weight.T, tokens_ll, near_rr), to_ff_group)
     every = step(after(every, near_l, near_r), y_near)
 
     down_far = None

time: 269 us -> 283 us (1.052)
  waiting for transfers between devices: 117 us -> 134 us
  starting transfers between devices: 79.5 us -> 73.4 us
  local copies, waits for them, and re-layouts: 6.74 us -> 9.64 us
    ppermute x45, waiting for transfers between devices: 117 us -> 134 us  [send(): return lax.ppermute(array, AXES, pairs)]
    ppermute x45, starting transfers between devices: 79.5 us -> 73.4 us  [send(): return lax.ppermute(array, AXES, pairs)]
    unnamed x50 -> x62, local copies, waits for them, and re-layouts: 3.43 us -> 6.34 us
  transfers between devices with their start and end apart: 45 -> 45, of which waited for: 24 -> 19; matrix products, arithmetic and copies ran while one was open for 8% -> 8% of each run, Pallas kernels for 14% -> 13%
where the time goes in v10:
time: 283 us; the launch traced here: 281 us
  waiting for transfers between devices  134 us (47%)
  starting transfers between devices  73.4 us (26%)
  Pallas kernels  36.9 us (13%)
  other arithmetic  25.8 us (9%)
  local copies, waits for them, and re-layouts  9.64 us (3%)
    ppermute x45, waiting for transfers between devices, send(): return lax.ppermute(array, AXES, pairs)  134 us
    ppermute x45, starting transfers between devices, send(): return lax.ppermute(array, AXES, pairs)  73.4 us
    pallas_call x2, Pallas kernels, token_sum(): pl.pallas_call(functools.partial(token_kernel, len(blocks), first, before...  26.7 us
    pallas_call x4, Pallas kernels, down_terms(): pl.pallas_call(down_kernel, out_shape=[jax.ShapeDtypeStruct((columns, row...  10.2 us
    another operation x3, other arithmetic, swap(): pair = jnp.stack(blocks[n:n + 2])  7.44 us
    unnamed x62, local copies, waits for them, and re-layouts  6.34 us
  transfers between devices with their start and end apart: 45, of which 19 were waited for; matrix products, arithmetic and copies ran while one was open for 8% of the time, Pallas kernels for 13%

profile of v10, /device:TPU:6, one launch (start us, length us, event | category | flops | bytes accessed | tf_op | source)
XLA Modules:
  0.0 281.0 jit_solution(13284035822280012544)
XLA Ops:
  2.1 4.1 %collective-permute-start.2 = (bf16[768,512]{1,0:T(8,128)(2,1)S(1)}, bf16[768,512]{1,0:T(8,128)(2,1)S(1)}, u32[]{:S(2)}, u32[]{:S(2)}) collective-permute-start(bf16[768,512]{1,0:T(8,128)(2,1)S(1)} %fusion.1.refs_0_), channel_id=1, source_target_pairs={{0,3},{1,0},{2,1},{3,2},{8,11},{9,8},{10,9},{11,10},{16,19},{17,16... | collective-permute-start | bytes 2359304 | tf_op jit(solution)/shard_map/ppermute | solution.py:44
  16.7 3.4 %collective-permute-done.8 = f32[120,128]{1,0:T(8,128)S(1)} collective-permute-done((f32[120,128]{1,0:T(8,128)S(1)}, f32[120,128]{1,0:T(8,128)S(1)}, u32[]{:S(2)}, u32[]{:S(2)}) %collective-permute-start.8) | collective-permute-done | bytes 61472 | tf_op jit(solution)/shard_map/ppermute | solution.py:44
  21.6 3.7 %multiply_convert_fusion.2 = (bf16[224,1152]{1,0:T(8,128)(2,1)S(1)}, bf16[224,1152]{1,0:T(8,128)(2,1)S(1)}) fusion(f32[224,1152]{1,0:T(8,128)} %param.6, f32[1152]{0:T(1024)S(1)} %get-tuple-element.101, f32[1152]{0:T(1024)S(1)} %get-tuple-element.102, f32[1152]{0:T(1024)S(1)} %get-tuple-element.100, pred[224]{0:T(512)(128)(4,1)S(1)} %broadcast_compare_fusion.23, ...), kind=kLoop, calls=%fused_computation.20 | loop fusion | flops 9289728 | bytes 3124896 | tf_op jit(solution)/shard_map/convert_element_type | solution.py:129
  28.7 2.8 %collective-permute-start.10 = (bf16[224,2304]{1,0:T(8,128)(2,1)S(1)}, bf16[224,2304]{1,0:T(8,128)(2,1)S(1)}, u32[]{:S(2)}, u32[]{:S(2)}) collective-permute-start(bf16[224,2304]{1,0:T(8,128)(2,1)S(1)} %pad_maximum_fusion.8), channel_id=1, source_target_pairs={{0,64},{1,65},{2,66},{3,67},{8,72},{9,73},{10,74},{11,75},{16,80},... | collective-permute-start | bytes 3096584 | tf_op jit(solution)/shard_map/ppermute | solution.py:44
  31.5 3.4 %collective-permute-start.4 = (bf16[768,512]{1,0:T(8,128)(2,1)S(1)}, bf16[768,512]{1,0:T(8,128)(2,1)S(1)}, u32[]{:S(2)}, u32[]{:S(2)}) collective-permute-start(bf16[768,512]{1,0:T(8,128)(2,1)S(1)} %collective-permute-done.refs_1_), channel_id=1, source_target_pairs={{0,3},{1,0},{2,1},{3,2},{8,11},{9,8},{10,9},{11,10},{16,19},{17,16... | collective-permute-start | bytes 2359304 | tf_op jit(solution)/shard_map/ppermute | solution.py:44
  35.0 15.4 %collective-permute-done.4.refs_5_ = bf16[768,512]{1,0:T(8,128)(2,1)S(1)} collective-permute-done((bf16[768,512]{1,0:T(8,128)(2,1)S(1)}, bf16[768,512]{1,0:T(8,128)(2,1)S(1)}, u32[]{:S(2)}, u32[]{:S(2)}) %collective-permute-start.4) | collective-permute-done | bytes 786464 | tf_op jit(solution)/shard_map/ppermute | solution.py:44
  50.4 3.4 %collective-permute-done.3.refs_4_ = bf16[768,512]{1,0:T(8,128)(2,1)S(1)} collective-permute-done((bf16[768,512]{1,0:T(8,128)(2,1)S(1)}, bf16[768,512]{1,0:T(8,128)(2,1)S(1)}, u32[]{:S(2)}, u32[]{:S(2)}) %collective-permute-start.3) | collective-permute-done | bytes 786464 | tf_op jit(solution)/shard_map/ppermute | solution.py:44
  59.8 3.2 %collective-permute-start.17 = (bf16[224,2304]{1,0:T(8,128)(2,1)}, bf16[224,2304]{1,0:T(8,128)(2,1)S(1)}, u32[]{:S(2)}, u32[]{:S(2)}) collective-permute-start(bf16[224,2304]{1,0:T(8,128)(2,1)} %copy-done.22), channel_id=1, source_target_pairs={{0,16},{1,17},{2,18},{3,19},{8,24},{9,25},{10,26},{11,27},{16,32},... | collective-permute-start | bytes 3096584 | tf_op jit(solution)/shard_map/ppermute | solution.py:44
  63.0 3.1 %fusion.3 = bf16[448,576]{1,0:T(8,128)(2,1)S(1)} fusion(f32[576,448]{0,1:T(8,128)} %param.8, f32[448]{0:T(512)S(1)} %bitcast.72, f32[448]{0:T(512)S(1)} %bitcast.73, f32[448]{0:T(512)S(1)} %bitcast.74, f32[448]{0:T(512)S(1)} %bitcast.75, f32[448]{0:T(512)S(1)} %bitcast.76, f32[448]{0:T(512)S(1)} %bitcast.71, pred[576]{0:T(1024)(128)(4,1)S(1)} %get-tuple-element.149, ...), kind=kLoop, calls=%fused_computation.29 | loop fusion | flops 5419008 | bytes 1562496 | tf_op jit(solution)/shard_map/transpose | solution.py:329
  66.2 13.7 %collective-permute-done.5.refs_6_ = bf16[768,512]{1,0:T(8,128)(2,1)S(1)} collective-permute-done((bf16[768,512]{1,0:T(8,128)(2,1)S(1)}, bf16[768,512]{1,0:T(8,128)(2,1)S(1)}, u32[]{:S(2)}, u32[]{:S(2)}) %collective-permute-start.5) | collective-permute-done | bytes 786464 | tf_op jit(solution)/shard_map/ppermute | solution.py:44
  81.9 18.2 %collective-permute-done.13 = bf16[448,576]{1,0:T(8,128)(2,1)S(1)} collective-permute-done((bf16[448,576]{1,0:T(8,128)(2,1)S(1)}, bf16[448,576]{1,0:T(8,128)(2,1)S(1)}, u32[]{:S(2)}, u32[]{:S(2)}) %collective-permute-start.13) | collective-permute-done | bytes 516128 | tf_op jit(solution)/shard_map/ppermute | solution.py:44
  102.7 13.1 %collective-permute-done.19 = f32[120,128]{1,0:T(8,128)S(1)} collective-permute-done((f32[120,128]{1,0:T(8,128)S(1)}, f32[120,128]{1,0:T(8,128)S(1)}, u32[]{:S(2)}, u32[]{:S(2)}) %collective-permute-start.19) | collective-permute-done | bytes 61472 | tf_op jit(solution)/shard_map/ppermute | solution.py:44
  116.5 2.9 %pad_maximum_fusion.2.refs_12_ = bf16[2,224,2304]{2,1,0:T(8,128)(2,1)} fusion(bf16[1,224,2304]{2,1,0:T(8,128)(2,1)} %bitcast.27, bf16[1,224,2304]{2,1,0:T(8,128)(2,1)S(1)} %bitcast.54), kind=kLoop, calls=%fused_computation.2 | loop fusion | flops 1032192 | bytes 4128768 | tf_op jit(solution)/shard_map/stack | solution.py:326
  119.4 2.9 %pad_maximum_fusion.1.refs_10_ = bf16[2,224,2304]{2,1,0:T(8,128)(2,1)} fusion(bf16[1,224,2304]{2,1,0:T(8,128)(2,1)S(1)} %bitcast.52, bf16[1,224,2304]{2,1,0:T(8,128)(2,1)} %bitcast.24), kind=kLoop, calls=%fused_computation.1 | loop fusion | flops 1032192 | bytes 4128768 | tf_op jit(solution)/shard_map/stack | solution.py:326
  129.2 19.8 %shard_map.68.refs_8_ = f32[768,2304]{1,0:T(8,128)} custom-call(s32[16]{0:T(128)} %compare_select_fusion.5.info, bf16[768,512]{1,0:T(8,128)(2,1)} %copy-done.1, bf16[768,512]{1,0:T(8,128)(2,1)} %copy-done.7, bf16[768,512]{1,0:T(8,128)(2,1)} %copy-done.5, bf16[768,512]{1,0:T(8,128)(2,1)} %copy-done.3, bf16[768,512]{1,0:T(8,128)(2,1)} %copy-done.11, ...), custom_call_target="tpu_custom_call" | custom-call | tf_op jit(solution)/shard_map/pallas_call | solution.py:213
  154.0 3.6 %collective-permute-start.24 = (f32[120,128]{1,0:T(8,128)S(1)}, f32[120,128]{1,0:T(8,128)S(1)}, u32[]{:S(2)}, u32[]{:S(2)}) collective-permute-start(f32[120,128]{1,0:T(8,128)S(1)} %copy-done.26), channel_id=1, source_target_pairs={{0,2},{1,3},{2,0},{3,1},{8,10},{9,11},{10,8},{11,9},{16,18},{17,19... | collective-permute-start | bytes 184328 | tf_op jit(solution)/shard_map/ppermute | solution.py:44
  159.7 2.9 %collective-permute-start.26 = (bf16[448,576]{1,0:T(8,128)(2,1)S(1)}, bf16[448,576]{1,0:T(8,128)(2,1)S(1)}, u32[]{:S(2)}, u32[]{:S(2)}) collective-permute-start(bf16[448,576]{1,0:T(8,128)(2,1)S(1)} %copy-done.24), channel_id=1, source_target_pairs={{0,16},{1,17},{2,18},{3,19},{8,24},{9,25},{10,26},{11,27},{16,32},... | collective-permute-start | bytes 1548296 | tf_op jit(solution)/shard_map/ppermute | solution.py:44
  162.8 3.0 %copy-done = f32[768,2304]{1,0:T(8,128)S(1)} copy-done((f32[768,2304]{1,0:T(8,128)S(1)}, f32[768,2304]{1,0:T(8,128)}, u32[]{:S(2)}) %copy-start) | copy-done | bytes 7077912
  165.8 6.9 %shard_map.69.hidden = bf16[768,1152]{1,0:T(8,128)(2,1)S(1)} custom-call(s32[16]{0:T(128)S(1)} %copy-done.17, bf16[768,512]{1,0:T(8,128)(2,1)S(1)} %copy-done.2, bf16[768,512]{1,0:T(8,128)(2,1)S(1)} %copy-done.8, bf16[768,512]{1,0:T(8,128)(2,1)S(1)} %copy-done.6, bf16[768,512]{1,0:T(8,128)(2,1)S(1)} %copy-done.4, bf16[768,512]{1,0:T(8,128)(2,1)S(1)} %copy-done.12, ...), custom_call_target="tpu_custom_call" | custom-call | tf_op jit(solution)/shard_map/pallas_call | solution.py:213
  172.7 2.6 shard_map.70
  175.5 2.7 collective-permute-start.28
  178.3 3.2 %collective-permute-done.28 = f32[120,128]{1,0:T(8,128)S(1)} collective-permute-done((f32[120,128]{1,0:T(8,128)S(1)}, f32[120,128]{1,0:T(8,128)S(1)}, u32[]{:S(2)}, u32[]{:S(2)}) %collective-permute-start.28) | collective-permute-done | bytes 61472 | tf_op jit(solution)/shard_map/ppermute | solution.py:44
  184.4 5.2 %collective-permute-start.29 = (bf16[448,768]{1,0:T(8,128)(2,1)S(1)}, bf16[448,768]{1,0:T(8,128)(2,1)S(1)}, u32[]{:S(2)}, u32[]{:S(2)}) collective-permute-start(bf16[448,768]{1,0:T(8,128)(2,1)S(1)} %get-tuple-element.72), channel_id=1, source_target_pairs={{0,0},{1,1},{2,2},{3,3},{8,8},{9,9},{10,10},{11,11},{16,17},{17,18... | collective-permute-start | bytes 2064392 | tf_op jit(solution)/shard_map/ppermute | solution.py:44
  192.2 11.0 %collective-permute-done.30 = bf16[448,768]{1,0:T(8,128)(2,1)S(1)} collective-permute-done((bf16[448,768]{1,0:T(8,128)(2,1)S(1)}, bf16[448,768]{1,0:T(8,128)(2,1)S(1)}, u32[]{:S(2)}, u32[]{:S(2)}) %collective-permute-start.30) | collective-permute-done | bytes 688160 | tf_op jit(solution)/shard_map/ppermute | solution.py:44
  204.8 5.3 %collective-permute-start.34 = (bf16[448,768]{1,0:T(8,128)(2,1)S(1)}, bf16[448,768]{1,0:T(8,128)(2,1)S(1)}, u32[]{:S(2)}, u32[]{:S(2)}) collective-permute-start(bf16[448,768]{1,0:T(8,128)(2,1)S(1)} %get-tuple-element.77), channel_id=1, source_target_pairs={{0,3},{1,0},{2,1},{3,2},{8,11},{9,8},{10,9},{11,10},{16,16},{17,17... | collective-permute-start | bytes 2064392 | tf_op jit(solution)/shard_map/ppermute | solution.py:44
  215.9 10.5 %collective-permute-done.40 = bf16[448,576]{1,0:T(8,128)(2,1)S(1)} collective-permute-done((bf16[448,576]{1,0:T(8,128)(2,1)S(1)}, bf16[448,576]{1,0:T(8,128)(2,1)S(1)}, u32[]{:S(2)}, u32[]{:S(2)}) %collective-permute-start.40) | collective-permute-done | bytes 516128 | tf_op jit(solution)/shard_map/ppermute | solution.py:44
  227.6 5.2 %collective-permute-start.38 = (bf16[448,768]{1,0:T(8,128)(2,1)S(1)}, bf16[448,768]{1,0:T(8,128)(2,1)S(1)}, u32[]{:S(2)}, u32[]{:S(2)}) collective-permute-start(bf16[448,768]{1,0:T(8,128)(2,1)S(1)} %get-tuple-element.82), channel_id=1, source_target_pairs={{0,7},{1,4},{2,5},{3,6},{8,15},{9,12},{10,13},{11,14},{16,20},{17,... | collective-permute-start | bytes 2064392 | tf_op jit(solution)/shard_map/ppermute | solution.py:44
  237.5 4.0 %collective-permute-start.43 = (bf16[448,768]{1,0:T(8,128)(2,1)S(1)}, bf16[448,768]{1,0:T(8,128)(2,1)S(1)}, u32[]{:S(2)}, u32[]{:S(2)}) collective-permute-start(bf16[448,768]{1,0:T(8,128)(2,1)S(1)} %get-tuple-element.86), channel_id=1, source_target_pairs={{0,4},{1,5},{2,6},{3,7},{8,12},{9,13},{10,14},{11,15},{16,21},{17,... | collective-permute-start | bytes 2064392 | tf_op jit(solution)/shard_map/ppermute | solution.py:44
  241.5 3.0 %collective-permute-start.42 = (bf16[448,768]{1,0:T(8,128)(2,1)S(1)}, bf16[448,768]{1,0:T(8,128)(2,1)S(1)}, u32[]{:S(2)}, u32[]{:S(2)}) collective-permute-start(bf16[448,768]{1,0:T(8,128)(2,1)S(1)} %get-tuple-element.85), channel_id=1, source_target_pairs={{0,2},{1,3},{2,0},{3,1},{8,10},{9,11},{10,8},{11,9},{16,19},{17,16... | collective-permute-start | bytes 2064392 | tf_op jit(solution)/shard_map/ppermute | solution.py:44
  246.3 4.0 %collective-permute-done.44 = f32[120,128]{1,0:T(8,128)S(1)} collective-permute-done((f32[120,128]{1,0:T(8,128)S(1)}, f32[120,128]{1,0:T(8,128)S(1)}, u32[]{:S(2)}, u32[]{:S(2)}) %collective-permute-start.44) | collective-permute-done | bytes 61472 | tf_op jit(solution)/shard_map/ppermute | solution.py:44
  251.0 13.0 %collective-permute-done.37 = bf16[448,768]{1,0:T(8,128)(2,1)S(1)} collective-permute-done((bf16[448,768]{1,0:T(8,128)(2,1)S(1)}, bf16[448,768]{1,0:T(8,128)(2,1)S(1)}, u32[]{:S(2)}, u32[]{:S(2)}) %collective-permute-start.37) | collective-permute-done | bytes 688160 | tf_op jit(solution)/shard_map/ppermute | solution.py:44
  264.0 15.4 %collective-permute-done.43 = bf16[448,768]{1,0:T(8,128)(2,1)S(1)} collective-permute-done((bf16[448,768]{1,0:T(8,128)(2,1)S(1)}, bf16[448,768]{1,0:T(8,128)(2,1)S(1)}, u32[]{:S(2)}, u32[]{:S(2)}) %collective-permute-start.43) | collective-permute-done | bytes 688160 | tf_op jit(solution)/shard_map/ppermute | solution.py:44
  (207 shorter events, 64.7 us)
Async XLA Ops:
  2.1 26.6 %collective-permute-start.2 = (bf16[768,512]{1,0:T(8,128)(2,1)S(1)}, bf16[768,512]{1,0:T(8,128)(2,1)S(1)}, u32[]{:S(2)}, u32[]{:S(2)}) collective-permute-start(bf16[768,512]{1,0:T(8,128)(2,1)S(1)} %fusion.1.refs_0_), channel_id=1, source_target_pairs={{0,3},{1,0},{2,1},{3,2},{8,11},{9,8},{10,9},{11,10},{16,19},{17,16... | collective-permute-start | bytes 2359304 | tf_op jit(solution)/shard_map/ppermute | solution.py:44
  6.2 25.3 %collective-permute-start.1 = (bf16[768,512]{1,0:T(8,128)(2,1)S(1)}, bf16[768,512]{1,0:T(8,128)(2,1)S(1)}, u32[]{:S(2)}, u32[]{:S(2)}) collective-permute-start(bf16[768,512]{1,0:T(8,128)(2,1)S(1)} %fusion.1.refs_0_), channel_id=1, source_target_pairs={{0,1},{1,2},{2,3},{3,0},{8,9},{9,10},{10,11},{11,8},{16,17},{17,18... | collective-permute-start | bytes 2359304 | tf_op jit(solution)/shard_map/ppermute | solution.py:44
  6.2 25.3 %collective-permute-start = (bf16[768,512]{1,0:T(8,128)(2,1)S(1)}, bf16[768,512]{1,0:T(8,128)(2,1)S(1)}, u32[]{:S(2)}, u32[]{:S(2)}) collective-permute-start(bf16[768,512]{1,0:T(8,128)(2,1)S(1)} %fusion.1.refs_0_), channel_id=1, source_target_pairs={{0,4},{1,5},{2,6},{3,7},{8,12},{9,13},{10,14},{11,15},{16,20},{17,... | collective-permute-start | bytes 2359304 | tf_op jit(solution)/shard_map/ppermute | solution.py:44
  25.4 29.3 %collective-permute-start.12 = (bf16[224,2304]{1,0:T(8,128)(2,1)S(1)}, bf16[224,2304]{1,0:T(8,128)(2,1)S(1)}, u32[]{:S(2)}, u32[]{:S(2)}) collective-permute-start(bf16[224,2304]{1,0:T(8,128)(2,1)S(1)} %pad_maximum_fusion.8), channel_id=1, source_target_pairs={{0,48},{1,49},{2,50},{3,51},{8,56},{9,57},{10,58},{11,59},{16,0},{... | collective-permute-start | bytes 3096584 | tf_op jit(solution)/shard_map/ppermute | solution.py:44
  26.3 28.4 %collective-permute-start.11 = (bf16[224,2304]{1,0:T(8,128)(2,1)S(1)}, bf16[224,2304]{1,0:T(8,128)(2,1)}, u32[]{:S(2)}, u32[]{:S(2)}) collective-permute-start(bf16[224,2304]{1,0:T(8,128)(2,1)S(1)} %pad_maximum_fusion.8), channel_id=1, source_target_pairs={{0,16},{1,17},{2,18},{3,19},{8,24},{9,25},{10,26},{11,27},{16,32},... | collective-permute-start | bytes 3096584 | tf_op jit(solution)/shard_map/ppermute | solution.py:44
  28.7 26.0 %collective-permute-start.10 = (bf16[224,2304]{1,0:T(8,128)(2,1)S(1)}, bf16[224,2304]{1,0:T(8,128)(2,1)S(1)}, u32[]{:S(2)}, u32[]{:S(2)}) collective-permute-start(bf16[224,2304]{1,0:T(8,128)(2,1)S(1)} %pad_maximum_fusion.8), channel_id=1, source_target_pairs={{0,64},{1,65},{2,66},{3,67},{8,72},{9,73},{10,74},{11,75},{16,80},... | collective-permute-start | bytes 3096584 | tf_op jit(solution)/shard_map/ppermute | solution.py:44
  31.5 18.8 %collective-permute-start.4 = (bf16[768,512]{1,0:T(8,128)(2,1)S(1)}, bf16[768,512]{1,0:T(8,128)(2,1)S(1)}, u32[]{:S(2)}, u32[]{:S(2)}) collective-permute-start(bf16[768,512]{1,0:T(8,128)(2,1)S(1)} %collective-permute-done.refs_1_), channel_id=1, source_target_pairs={{0,3},{1,0},{2,1},{3,2},{8,11},{9,8},{10,9},{11,10},{16,19},{17,16... | collective-permute-start | bytes 2359304 | tf_op jit(solution)/shard_map/ppermute | solution.py:44
  35.0 18.8 %collective-permute-start.3 = (bf16[768,512]{1,0:T(8,128)(2,1)S(1)}, bf16[768,512]{1,0:T(8,128)(2,1)S(1)}, u32[]{:S(2)}, u32[]{:S(2)}) collective-permute-start(bf16[768,512]{1,0:T(8,128)(2,1)S(1)} %collective-permute-done.refs_1_), channel_id=1, source_target_pairs={{0,1},{1,2},{2,3},{3,0},{8,9},{9,10},{10,11},{11,8},{16,17},{17,18... | collective-permute-start | bytes 2359304 | tf_op jit(solution)/shard_map/ppermute | solution.py:44
  57.4 42.8 %collective-permute-start.14 = (bf16[2,224,2304]{2,1,0:T(8,128)(2,1)}, bf16[2,224,2304]{2,1,0:T(8,128)(2,1)}, u32[]{:S(2)}, u32[]{:S(2)}) collective-permute-start(bf16[2,224,2304]{2,1,0:T(8,128)(2,1)} %pad_maximum_fusion.refs_8_), channel_id=1, source_target_pairs={{0,8},{1,9},{2,10},{3,11},{8,0},{9,1},{10,2},{11,3},{16,24},{17,25... | collective-permute-start | bytes 6193160 | tf_op jit(solution)/shard_map/ppermute | solution.py:44
  57.6 22.3 %collective-permute-start.6 = (bf16[768,512]{1,0:T(8,128)(2,1)S(1)}, bf16[768,512]{1,0:T(8,128)(2,1)S(1)}, u32[]{:S(2)}, u32[]{:S(2)}) collective-permute-start(bf16[768,512]{1,0:T(8,128)(2,1)S(1)} %collective-permute-done.4.refs_5_), channel_id=1, source_target_pairs={{0,3},{1,0},{2,1},{3,2},{8,11},{9,8},{10,9},{11,10},{16,19},{17,16... | collective-permute-start | bytes 2359304 | tf_op jit(solution)/shard_map/ppermute | solution.py:44
  59.0 20.9 %collective-permute-start.5 = (bf16[768,512]{1,0:T(8,128)(2,1)S(1)}, bf16[768,512]{1,0:T(8,128)(2,1)S(1)}, u32[]{:S(2)}, u32[]{:S(2)}) collective-permute-start(bf16[768,512]{1,0:T(8,128)(2,1)S(1)} %collective-permute-done.1.refs_2_), channel_id=1, source_target_pairs={{0,1},{1,2},{2,3},{3,0},{8,9},{9,10},{10,11},{11,8},{16,17},{17,18... | collective-permute-start | bytes 2359304 | tf_op jit(solution)/shard_map/ppermute | solution.py:44
  59.7 56.7 %collective-permute-start.18 = (bf16[224,2304]{1,0:T(8,128)(2,1)}, bf16[224,2304]{1,0:T(8,128)(2,1)}, u32[]{:S(2)}, u32[]{:S(2)}) collective-permute-start(bf16[224,2304]{1,0:T(8,128)(2,1)} %copy-done.22), channel_id=1, source_target_pairs={{0,48},{1,49},{2,50},{3,51},{8,56},{9,57},{10,58},{11,59},{16,0},{... | collective-permute-start | bytes 3096584 | tf_op jit(solution)/shard_map/ppermute | solution.py:44
  59.8 56.6 %collective-permute-start.17 = (bf16[224,2304]{1,0:T(8,128)(2,1)}, bf16[224,2304]{1,0:T(8,128)(2,1)S(1)}, u32[]{:S(2)}, u32[]{:S(2)}) collective-permute-start(bf16[224,2304]{1,0:T(8,128)(2,1)} %copy-done.22), channel_id=1, source_target_pairs={{0,16},{1,17},{2,18},{3,19},{8,24},{9,25},{10,26},{11,27},{16,32},... | collective-permute-start | bytes 3096584 | tf_op jit(solution)/shard_map/ppermute | solution.py:44
  79.8 20.3 %collective-permute-start.13 = (bf16[448,576]{1,0:T(8,128)(2,1)S(1)}, bf16[448,576]{1,0:T(8,128)(2,1)S(1)}, u32[]{:S(2)}, u32[]{:S(2)}) collective-permute-start(bf16[448,576]{1,0:T(8,128)(2,1)S(1)} %fusion.3), channel_id=1, source_target_pairs={{0,0},{1,16},{2,32},{3,48},{8,8},{9,24},{10,40},{11,56},{16,49},{1... | collective-permute-start | bytes 1548296 | tf_op jit(solution)/shard_map/ppermute | solution.py:44
  100.1 19.2 %collective-permute-start.15 = (bf16[448,576]{1,0:T(8,128)(2,1)S(1)}, bf16[448,576]{1,0:T(8,128)(2,1)S(1)}, u32[]{:S(2)}, u32[]{:S(2)}) collective-permute-start(bf16[448,576]{1,0:T(8,128)(2,1)S(1)} %collective-permute-done.13), channel_id=1, source_target_pairs={{0,64},{1,65},{2,66},{3,67},{8,72},{9,73},{10,74},{11,75},{16,80},... | collective-permute-start | bytes 1548296 | tf_op jit(solution)/shard_map/ppermute | solution.py:44
  123.1 26.0 %collective-permute-start.22 = (bf16[224,2304]{1,0:T(8,128)(2,1)}, bf16[224,2304]{1,0:T(8,128)(2,1)}, u32[]{:S(2)}, u32[]{:S(2)}) collective-permute-start(bf16[224,2304]{1,0:T(8,128)(2,1)} %collective-permute-done.11), channel_id=1, source_target_pairs={{0,16},{1,17},{2,18},{3,19},{8,24},{9,25},{10,26},{11,27},{16,32},... | collective-permute-start | bytes 3096584 | tf_op jit(solution)/shard_map/ppermute | solution.py:44
  123.1 26.7 %collective-permute-start.23 = (bf16[224,2304]{1,0:T(8,128)(2,1)}, bf16[224,2304]{1,0:T(8,128)(2,1)}, u32[]{:S(2)}, u32[]{:S(2)}) collective-permute-start(bf16[224,2304]{1,0:T(8,128)(2,1)} %collective-permute-done.18), channel_id=1, source_target_pairs={{0,48},{1,49},{2,50},{3,51},{8,56},{9,57},{10,58},{11,59},{16,0},{... | collective-permute-start | bytes 3096584 | tf_op jit(solution)/shard_map/ppermute | solution.py:44
  151.9 23.4 %collective-permute-start.31 = (bf16[448,576]{1,0:T(8,128)(2,1)}, bf16[448,576]{1,0:T(8,128)(2,1)S(1)}, u32[]{:S(2)}, u32[]{:S(2)}) collective-permute-start(bf16[448,576]{1,0:T(8,128)(2,1)} %copy-done.25), channel_id=1, source_target_pairs={{0,16},{1,17},{2,18},{3,19},{8,24},{9,25},{10,26},{11,27},{16,32},... | collective-permute-start | bytes 1548296 | tf_op jit(solution)/shard_map/ppermute | solution.py:44
  153.7 21.6 %collective-permute-start.32 = (bf16[448,576]{1,0:T(8,128)(2,1)}, bf16[448,576]{1,0:T(8,128)(2,1)S(1)}, u32[]{:S(2)}, u32[]{:S(2)}) collective-permute-start(bf16[448,576]{1,0:T(8,128)(2,1)} %copy-done.25), channel_id=1, source_target_pairs={{0,48},{1,49},{2,50},{3,51},{8,56},{9,57},{10,58},{11,59},{16,0},{... | collective-permute-start | bytes 1548296 | tf_op jit(solution)/shard_map/ppermute | solution.py:44
  157.5 24.9 %collective-permute-start.27 = (bf16[448,576]{1,0:T(8,128)(2,1)S(1)}, bf16[448,576]{1,0:T(8,128)(2,1)S(1)}, u32[]{:S(2)}, u32[]{:S(2)}) collective-permute-start(bf16[448,576]{1,0:T(8,128)(2,1)S(1)} %copy-done.24), channel_id=1, source_target_pairs={{0,48},{1,49},{2,50},{3,51},{8,56},{9,57},{10,58},{11,59},{16,0},{... | collective-permute-start | bytes 1548296 | tf_op jit(solution)/shard_map/ppermute | solution.py:44
  159.7 22.7 %collective-permute-start.26 = (bf16[448,576]{1,0:T(8,128)(2,1)S(1)}, bf16[448,576]{1,0:T(8,128)(2,1)S(1)}, u32[]{:S(2)}, u32[]{:S(2)}) collective-permute-start(bf16[448,576]{1,0:T(8,128)(2,1)S(1)} %copy-done.24), channel_id=1, source_target_pairs={{0,16},{1,17},{2,18},{3,19},{8,24},{9,25},{10,26},{11,27},{16,32},... | collective-permute-start | bytes 1548296 | tf_op jit(solution)/shard_map/ppermute | solution.py:44
  175.4 14.2 %collective-permute-start.33 = (bf16[2,448,576]{2,1,0:T(8,128)(2,1)S(1)}, bf16[2,448,576]{2,1,0:T(8,128)(2,1)S(1)}, u32[]{:S(2)}, u32[]{:S(2)}) collective-permute-start(bf16[2,448,576]{2,1,0:T(8,128)(2,1)S(1)} %pad_maximum_fusion.5.mine), channel_id=1, source_target_pairs={{0,8},{1,9},{2,10},{3,11},{8,0},{9,1},{10,2},{11,3},{16,24},{17,25... | collective-permute-start | bytes 3096584 | tf_op jit(solution)/shard_map/ppermute | solution.py:44
  182.4 20.7 %collective-permute-start.30 = (bf16[448,768]{1,0:T(8,128)(2,1)S(1)}, bf16[448,768]{1,0:T(8,128)(2,1)S(1)}, u32[]{:S(2)}, u32[]{:S(2)}) collective-permute-start(bf16[448,768]{1,0:T(8,128)(2,1)S(1)} %get-tuple-element.74), channel_id=1, source_target_pairs={{0,6},{1,7},{2,4},{3,5},{8,14},{9,15},{10,12},{11,13},{16,23},{17,... | collective-permute-start | bytes 2064392 | tf_op jit(solution)/shard_map/ppermute | solution.py:44
  184.4 19.4 %collective-permute-start.29 = (bf16[448,768]{1,0:T(8,128)(2,1)S(1)}, bf16[448,768]{1,0:T(8,128)(2,1)S(1)}, u32[]{:S(2)}, u32[]{:S(2)}) collective-permute-start(bf16[448,768]{1,0:T(8,128)(2,1)S(1)} %get-tuple-element.72), channel_id=1, source_target_pairs={{0,0},{1,1},{2,2},{3,3},{8,8},{9,9},{10,10},{11,11},{16,17},{17,18... | collective-permute-start | bytes 2064392 | tf_op jit(solution)/shard_map/ppermute | solution.py:44
  204.0 22.4 %collective-permute-start.35 = (bf16[448,768]{1,0:T(8,128)(2,1)S(1)}, bf16[448,768]{1,0:T(8,128)(2,1)S(1)}, u32[]{:S(2)}, u32[]{:S(2)}) collective-permute-start(bf16[448,768]{1,0:T(8,128)(2,1)S(1)} %get-tuple-element.78), channel_id=1, source_target_pairs={{0,1},{1,2},{2,3},{3,0},{8,9},{9,10},{10,11},{11,8},{16,18},{17,19... | collective-permute-start | bytes 2064392 | tf_op jit(solution)/shard_map/ppermute | solution.py:44
  204.8 21.7 %collective-permute-start.34 = (bf16[448,768]{1,0:T(8,128)(2,1)S(1)}, bf16[448,768]{1,0:T(8,128)(2,1)S(1)}, u32[]{:S(2)}, u32[]{:S(2)}) collective-permute-start(bf16[448,768]{1,0:T(8,128)(2,1)S(1)} %get-tuple-element.77), channel_id=1, source_target_pairs={{0,3},{1,0},{2,1},{3,2},{8,11},{9,8},{10,9},{11,10},{16,16},{17,17... | collective-permute-start | bytes 2064392 | tf_op jit(solution)/shard_map/ppermute | solution.py:44
  210.1 16.4 %collective-permute-start.40 = (bf16[448,576]{1,0:T(8,128)(2,1)S(1)}, bf16[448,576]{1,0:T(8,128)(2,1)S(1)}, u32[]{:S(2)}, u32[]{:S(2)}) collective-permute-start(bf16[448,576]{1,0:T(8,128)(2,1)S(1)} %collective-permute-done.27), channel_id=1, source_target_pairs={{0,48},{1,49},{2,50},{3,51},{8,56},{9,57},{10,58},{11,59},{16,0},{... | collective-permute-start | bytes 1548296 | tf_op jit(solution)/shard_map/ppermute | solution.py:44
  212.5 14.8 %collective-permute-start.39 = (bf16[448,576]{1,0:T(8,128)(2,1)S(1)}, bf16[448,576]{1,0:T(8,128)(2,1)S(1)}, u32[]{:S(2)}, u32[]{:S(2)}) collective-permute-start(bf16[448,576]{1,0:T(8,128)(2,1)S(1)} %collective-permute-done.31), channel_id=1, source_target_pairs={{0,16},{1,17},{2,18},{3,19},{8,24},{9,25},{10,26},{11,27},{16,32},... | collective-permute-start | bytes 1548296 | tf_op jit(solution)/shard_map/ppermute | solution.py:44
  227.6 23.4 %collective-permute-start.38 = (bf16[448,768]{1,0:T(8,128)(2,1)S(1)}, bf16[448,768]{1,0:T(8,128)(2,1)S(1)}, u32[]{:S(2)}, u32[]{:S(2)}) collective-permute-start(bf16[448,768]{1,0:T(8,128)(2,1)S(1)} %get-tuple-element.82), channel_id=1, source_target_pairs={{0,7},{1,4},{2,5},{3,6},{8,15},{9,12},{10,13},{11,14},{16,20},{17,... | collective-permute-start | bytes 2064392 | tf_op jit(solution)/shard_map/ppermute | solution.py:44
  232.7 31.3 %collective-permute-start.37 = (bf16[448,768]{1,0:T(8,128)(2,1)S(1)}, bf16[448,768]{1,0:T(8,128)(2,1)S(1)}, u32[]{:S(2)}, u32[]{:S(2)}) collective-permute-start(bf16[448,768]{1,0:T(8,128)(2,1)S(1)} %get-tuple-element.81), channel_id=1, source_target_pairs={{0,5},{1,6},{2,7},{3,4},{8,13},{9,14},{10,15},{11,12},{16,22},{17,... | collective-permute-start | bytes 2064392 | tf_op jit(solution)/shard_map/ppermute | solution.py:44
  237.5 41.9 %collective-permute-start.43 = (bf16[448,768]{1,0:T(8,128)(2,1)S(1)}, bf16[448,768]{1,0:T(8,128)(2,1)S(1)}, u32[]{:S(2)}, u32[]{:S(2)}) collective-permute-start(bf16[448,768]{1,0:T(8,128)(2,1)S(1)} %get-tuple-element.86), channel_id=1, source_target_pairs={{0,4},{1,5},{2,6},{3,7},{8,12},{9,13},{10,14},{11,15},{16,21},{17,... | collective-permute-start | bytes 2064392 | tf_op jit(solution)/shard_map/ppermute | solution.py:44
  241.5 38.0 %collective-permute-start.42 = (bf16[448,768]{1,0:T(8,128)(2,1)S(1)}, bf16[448,768]{1,0:T(8,128)(2,1)S(1)}, u32[]{:S(2)}, u32[]{:S(2)}) collective-permute-start(bf16[448,768]{1,0:T(8,128)(2,1)S(1)} %get-tuple-element.85), channel_id=1, source_target_pairs={{0,2},{1,3},{2,0},{3,1},{8,10},{9,11},{10,8},{11,9},{16,19},{17,16... | collective-permute-start | bytes 2064392 | tf_op jit(solution)/shard_map/ppermute | solution.py:44
  (45 other events, 530.1 us)

commit v11 on v7

--- a/solution.py
+++ b/solution.py
@@ -380,7 +380,7 @@
     own_l, far_r, *_ = lax.optimization_barrier((own_l, far_r, far_l, *parts[:2], *terms))
     own_ll, far_rr = send(own_l, x_up), send(far_r, x_down)
     terms = sums([far_l, after(far_r, *terms)])
-    terms = sums([own_ll, after(far_rr, *terms, *parts[2:4])])
+    terms = sums([own_ll, after(far_rr, *terms)], *parts[2:4])
     every = step(after(every, *terms), lambda y, x, core, z: (y, x ^ 2, core, z))
     log_amax = jnp.log(
         jnp.stack([every[k * rows : k * rows + D // BLOCK, : FF // BLOCK] for k in range(3)]) + EPS

time: 264 us -> 269 us (1.019)
  waiting for transfers between devices: 127 us -> 131 us
    ppermute x45, waiting for transfers between devices: 127 us -> 131 us  [send(): return lax.ppermute(array, AXES, pairs)]
  transfers between devices with their start and end apart: 45 -> 45, of which waited for: 22 -> 21; matrix products, arithmetic and copies ran while one was open for 8% -> 8% of each run, Pallas kernels for 14% -> 14%
where the time goes in v11:
time: 269 us; the launch traced here: 266 us
  waiting for transfers between devices  131 us (49%)
  starting transfers between devices  64.5 us (24%)
  Pallas kernels  36.9 us (14%)
  other arithmetic  23.3 us (9%)
  local copies, waits for them, and re-layouts  8.69 us (3%)
    ppermute x45, waiting for transfers between devices, send(): return lax.ppermute(array, AXES, pairs)  131 us
    ppermute x45, starting transfers between devices, send(): return lax.ppermute(array, AXES, pairs)  64.5 us
    pallas_call x2, Pallas kernels, token_sum(): pl.pallas_call(functools.partial(token_kernel, len(blocks), first, before...  26.7 us
    pallas_call x4, Pallas kernels, down_terms(): pl.pallas_call(down_kernel, out_shape=[jax.ShapeDtypeStruct((columns, row...  10.2 us
    another operation x3, other arithmetic, swap(): pair = jnp.stack(blocks[n:n + 2])  5.87 us
    unnamed x62, local copies, waits for them, and re-layouts  5.39 us
  transfers between devices with their start and end apart: 45, of which 21 were waited for; matrix products, arithmetic and copies ran while one was open for 8% of the time, Pallas kernels for 14%

profile of v11, /device:TPU:6, one launch (start us, length us, event | category | flops | bytes accessed | tf_op | source)
XLA Modules:
  0.0 266.5 jit_solution(2289954643082792858)
XLA Ops:
  2.1 4.1 %collective-permute-start.2 = (bf16[768,512]{1,0:T(8,128)(2,1)S(1)}, bf16[768,512]{1,0:T(8,128)(2,1)S(1)}, u32[]{:S(2)}, u32[]{:S(2)}) collective-permute-start(bf16[768,512]{1,0:T(8,128)(2,1)S(1)} %fusion.1.refs_0_), channel_id=1, source_target_pairs={{0,3},{1,0},{2,1},{3,2},{8,11},{9,8},{10,9},{11,10},{16,19},{17,16... | collective-permute-start | bytes 2359304 | tf_op jit(solution)/shard_map/ppermute | solution.py:44
  16.7 3.4 %collective-permute-done.8 = f32[120,128]{1,0:T(8,128)S(1)} collective-permute-done((f32[120,128]{1,0:T(8,128)S(1)}, f32[120,128]{1,0:T(8,128)S(1)}, u32[]{:S(2)}, u32[]{:S(2)}) %collective-permute-start.8) | collective-permute-done | bytes 61472 | tf_op jit(solution)/shard_map/ppermute | solution.py:44
  21.6 3.7 %multiply_convert_fusion.2 = (bf16[224,1152]{1,0:T(8,128)(2,1)S(1)}, bf16[224,1152]{1,0:T(8,128)(2,1)S(1)}) fusion(f32[224,1152]{1,0:T(8,128)} %param.6, f32[1152]{0:T(1024)S(1)} %get-tuple-element.105, f32[1152]{0:T(1024)S(1)} %get-tuple-element.106, f32[1152]{0:T(1024)S(1)} %get-tuple-element.104, pred[224]{0:T(512)(128)(4,1)S(1)} %broadcast_compare_fusion.23, ...), kind=kLoop, calls=%fused_computation.20 | loop fusion | flops 9289728 | bytes 3124896 | tf_op jit(solution)/shard_map/convert_element_type | solution.py:129
  28.8 2.9 %collective-permute-start.10 = (bf16[224,2304]{1,0:T(8,128)(2,1)S(1)}, bf16[224,2304]{1,0:T(8,128)(2,1)S(1)}, u32[]{:S(2)}, u32[]{:S(2)}) collective-permute-start(bf16[224,2304]{1,0:T(8,128)(2,1)S(1)} %pad_maximum_fusion.8), channel_id=1, source_target_pairs={{0,64},{1,65},{2,66},{3,67},{8,72},{9,73},{10,74},{11,75},{16,80},... | collective-permute-start | bytes 3096584 | tf_op jit(solution)/shard_map/ppermute | solution.py:44
  31.7 3.4 %collective-permute-start.4 = (bf16[768,512]{1,0:T(8,128)(2,1)S(1)}, bf16[768,512]{1,0:T(8,128)(2,1)S(1)}, u32[]{:S(2)}, u32[]{:S(2)}) collective-permute-start(bf16[768,512]{1,0:T(8,128)(2,1)S(1)} %collective-permute-done.refs_1_), channel_id=1, source_target_pairs={{0,3},{1,0},{2,1},{3,2},{8,11},{9,8},{10,9},{11,10},{16,19},{17,16... | collective-permute-start | bytes 2359304 | tf_op jit(solution)/shard_map/ppermute | solution.py:44
  37.4 13.1 %collective-permute-done.4.refs_5_ = bf16[768,512]{1,0:T(8,128)(2,1)S(1)} collective-permute-done((bf16[768,512]{1,0:T(8,128)(2,1)S(1)}, bf16[768,512]{1,0:T(8,128)(2,1)S(1)}, u32[]{:S(2)}, u32[]{:S(2)}) %collective-permute-start.4) | collective-permute-done | bytes 786464 | tf_op jit(solution)/shard_map/ppermute | solution.py:44
  50.6 3.4 %collective-permute-done.3.refs_4_ = bf16[768,512]{1,0:T(8,128)(2,1)S(1)} collective-permute-done((bf16[768,512]{1,0:T(8,128)(2,1)S(1)}, bf16[768,512]{1,0:T(8,128)(2,1)S(1)}, u32[]{:S(2)}, u32[]{:S(2)}) %collective-permute-start.3) | collective-permute-done | bytes 786464 | tf_op jit(solution)/shard_map/ppermute | solution.py:44
  57.5 3.8 %collective-permute-done.14 = f32[120,128]{1,0:T(8,128)S(1)} collective-permute-done((f32[120,128]{1,0:T(8,128)S(1)}, f32[120,128]{1,0:T(8,128)S(1)}, u32[]{:S(2)}, u32[]{:S(2)}) %collective-permute-start.14) | collective-permute-done | bytes 61472 | tf_op jit(solution)/shard_map/ppermute | solution.py:44
  62.0 10.2 %collective-permute-done.13 = bf16[448,576]{1,0:T(8,128)(2,1)S(1)} collective-permute-done((bf16[448,576]{1,0:T(8,128)(2,1)S(1)}, bf16[448,576]{1,0:T(8,128)(2,1)S(1)}, u32[]{:S(2)}, u32[]{:S(2)}) %collective-permute-start.13) | collective-permute-done | bytes 516128 | tf_op jit(solution)/shard_map/ppermute | solution.py:44
  74.7 3.2 %collective-permute-start.6 = (bf16[768,512]{1,0:T(8,128)(2,1)S(1)}, bf16[768,512]{1,0:T(8,128)(2,1)S(1)}, u32[]{:S(2)}, u32[]{:S(2)}) collective-permute-start(bf16[768,512]{1,0:T(8,128)(2,1)S(1)} %collective-permute-done.4.refs_5_), channel_id=1, source_target_pairs={{0,3},{1,0},{2,1},{3,2},{8,11},{9,8},{10,9},{11,10},{16,19},{17,16... | collective-permute-start | bytes 2359304 | tf_op jit(solution)/shard_map/ppermute | solution.py:44
  79.4 18.3 %collective-permute-done.18 = bf16[224,2304]{1,0:T(8,128)(2,1)S(1)} collective-permute-done((bf16[224,2304]{1,0:T(8,128)(2,1)S(1)}, bf16[224,2304]{1,0:T(8,128)(2,1)S(1)}, u32[]{:S(2)}, u32[]{:S(2)}) %collective-permute-start.18) | collective-permute-done | bytes 1032224 | tf_op jit(solution)/shard_map/ppermute | solution.py:44
  99.1 2.7 %pad_maximum_fusion.2.refs_12_ = bf16[2,224,2304]{2,1,0:T(8,128)(2,1)} fusion(bf16[1,224,2304]{2,1,0:T(8,128)(2,1)} %bitcast.27, bf16[1,224,2304]{2,1,0:T(8,128)(2,1)S(1)} %bitcast.54), kind=kLoop, calls=%fused_computation.2 | loop fusion | flops 1032192 | bytes 4128768 | tf_op jit(solution)/shard_map/stack | solution.py:326
  101.9 3.0 %pad_maximum_fusion.1.refs_10_ = bf16[2,224,2304]{2,1,0:T(8,128)(2,1)} fusion(bf16[1,224,2304]{2,1,0:T(8,128)(2,1)S(1)} %bitcast.52, bf16[1,224,2304]{2,1,0:T(8,128)(2,1)} %bitcast.24), kind=kLoop, calls=%fused_computation.1 | loop fusion | flops 1032192 | bytes 4128768 | tf_op jit(solution)/shard_map/stack | solution.py:326
  111.8 19.8 %shard_map.68.refs_8_ = f32[768,2304]{1,0:T(8,128)} custom-call(s32[16]{0:T(128)} %compare_select_fusion.5.info, bf16[768,512]{1,0:T(8,128)(2,1)} %copy-done.1, bf16[768,512]{1,0:T(8,128)(2,1)} %copy-done.7, bf16[768,512]{1,0:T(8,128)(2,1)} %copy-done.5, bf16[768,512]{1,0:T(8,128)(2,1)} %copy-done.3, bf16[768,512]{1,0:T(8,128)(2,1)} %copy-done.11, ...), custom_call_target="tpu_custom_call" | custom-call | tf_op jit(solution)/shard_map/pallas_call | solution.py:213
  137.1 5.6 %collective-permute-done.24 = f32[120,128]{1,0:T(8,128)S(1)} collective-permute-done((f32[120,128]{1,0:T(8,128)S(1)}, f32[120,128]{1,0:T(8,128)S(1)}, u32[]{:S(2)}, u32[]{:S(2)}) %collective-permute-start.24) | collective-permute-done | bytes 61472 | tf_op jit(solution)/shard_map/ppermute | solution.py:44
  144.4 3.0 %copy-done = f32[768,2304]{1,0:T(8,128)S(1)} copy-done((f32[768,2304]{1,0:T(8,128)S(1)}, f32[768,2304]{1,0:T(8,128)}, u32[]{:S(2)}) %copy-start) | copy-done | bytes 7077912
  147.4 6.9 %shard_map.69.hidden = bf16[768,1152]{1,0:T(8,128)(2,1)S(1)} custom-call(s32[16]{0:T(128)S(1)} %copy-done.17, bf16[768,512]{1,0:T(8,128)(2,1)S(1)} %copy-done.2, bf16[768,512]{1,0:T(8,128)(2,1)S(1)} %copy-done.8, bf16[768,512]{1,0:T(8,128)(2,1)S(1)} %copy-done.6, bf16[768,512]{1,0:T(8,128)(2,1)S(1)} %copy-done.4, bf16[768,512]{1,0:T(8,128)(2,1)S(1)} %copy-done.12, ...), custom_call_target="tpu_custom_call" | custom-call | tf_op jit(solution)/shard_map/pallas_call | solution.py:213
  154.3 2.6 shard_map.70
  158.7 4.3 %collective-permute-done.28 = f32[120,128]{1,0:T(8,128)S(1)} collective-permute-done((f32[120,128]{1,0:T(8,128)S(1)}, f32[120,128]{1,0:T(8,128)S(1)}, u32[]{:S(2)}, u32[]{:S(2)}) %collective-permute-start.28) | collective-permute-done | bytes 61472 | tf_op jit(solution)/shard_map/ppermute | solution.py:44
  166.3 6.5 %collective-permute-start.29 = (bf16[448,768]{1,0:T(8,128)(2,1)S(1)}, bf16[448,768]{1,0:T(8,128)(2,1)S(1)}, u32[]{:S(2)}, u32[]{:S(2)}) collective-permute-start(bf16[448,768]{1,0:T(8,128)(2,1)S(1)} %get-tuple-element.74), channel_id=1, source_target_pairs={{0,0},{1,1},{2,2},{3,3},{8,8},{9,9},{10,10},{11,11},{16,17},{17,18... | collective-permute-start | bytes 2064392 | tf_op jit(solution)/shard_map/ppermute | solution.py:44
  172.9 2.5 shard_map.71
  175.4 9.1 %collective-permute-done.30 = bf16[448,768]{1,0:T(8,128)(2,1)S(1)} collective-permute-done((bf16[448,768]{1,0:T(8,128)(2,1)S(1)}, bf16[448,768]{1,0:T(8,128)(2,1)S(1)}, u32[]{:S(2)}, u32[]{:S(2)}) %collective-permute-start.30) | collective-permute-done | bytes 688160 | tf_op jit(solution)/shard_map/ppermute | solution.py:44
  192.8 10.8 %collective-permute-done.40 = bf16[448,576]{1,0:T(8,128)(2,1)S(1)} collective-permute-done((bf16[448,576]{1,0:T(8,128)(2,1)S(1)}, bf16[448,576]{1,0:T(8,128)(2,1)S(1)}, u32[]{:S(2)}, u32[]{:S(2)}) %collective-permute-start.40) | collective-permute-done | bytes 516128 | tf_op jit(solution)/shard_map/ppermute | solution.py:44
  204.9 3.8 %collective-permute-start.34 = (bf16[448,768]{1,0:T(8,128)(2,1)S(1)}, bf16[448,768]{1,0:T(8,128)(2,1)S(1)}, u32[]{:S(2)}, u32[]{:S(2)}) collective-permute-start(bf16[448,768]{1,0:T(8,128)(2,1)S(1)} %get-tuple-element.79), channel_id=1, source_target_pairs={{0,3},{1,0},{2,1},{3,2},{8,11},{9,8},{10,9},{11,10},{16,16},{17,17... | collective-permute-start | bytes 2064392 | tf_op jit(solution)/shard_map/ppermute | solution.py:44
  208.7 3.3 %collective-permute-start.38 = (bf16[448,768]{1,0:T(8,128)(2,1)S(1)}, bf16[448,768]{1,0:T(8,128)(2,1)S(1)}, u32[]{:S(2)}, u32[]{:S(2)}) collective-permute-start(bf16[448,768]{1,0:T(8,128)(2,1)S(1)} %get-tuple-element.84), channel_id=1, source_target_pairs={{0,7},{1,4},{2,5},{3,6},{8,15},{9,12},{10,13},{11,14},{16,20},{17,... | collective-permute-start | bytes 2064392 | tf_op jit(solution)/shard_map/ppermute | solution.py:44
  212.0 3.6 %collective-permute-start.37 = (bf16[448,768]{1,0:T(8,128)(2,1)S(1)}, bf16[448,768]{1,0:T(8,128)(2,1)S(1)}, u32[]{:S(2)}, u32[]{:S(2)}) collective-permute-start(bf16[448,768]{1,0:T(8,128)(2,1)S(1)} %get-tuple-element.83), channel_id=1, source_target_pairs={{0,5},{1,6},{2,7},{3,4},{8,13},{9,14},{10,15},{11,12},{16,22},{17,... | collective-permute-start | bytes 2064392 | tf_op jit(solution)/shard_map/ppermute | solution.py:44
  215.7 2.5 shard_map.73
  218.2 22.7 %collective-permute-done.34 = bf16[448,768]{1,0:T(8,128)(2,1)S(1)} collective-permute-done((bf16[448,768]{1,0:T(8,128)(2,1)S(1)}, bf16[448,768]{1,0:T(8,128)(2,1)S(1)}, u32[]{:S(2)}, u32[]{:S(2)}) %collective-permute-start.34) | collective-permute-done | bytes 688160 | tf_op jit(solution)/shard_map/ppermute | solution.py:44
  240.9 4.2 %collective-permute-start.43 = (bf16[448,768]{1,0:T(8,128)(2,1)S(1)}, bf16[448,768]{1,0:T(8,128)(2,1)S(1)}, u32[]{:S(2)}, u32[]{:S(2)}) collective-permute-start(bf16[448,768]{1,0:T(8,128)(2,1)S(1)} %get-tuple-element.90), channel_id=1, source_target_pairs={{0,4},{1,5},{2,6},{3,7},{8,12},{9,13},{10,14},{11,15},{16,21},{17,... | collective-permute-start | bytes 2064392 | tf_op jit(solution)/shard_map/ppermute | solution.py:44
  247.1 5.7 %collective-permute-done.44 = f32[120,128]{1,0:T(8,128)S(1)} collective-permute-done((f32[120,128]{1,0:T(8,128)S(1)}, f32[120,128]{1,0:T(8,128)S(1)}, u32[]{:S(2)}, u32[]{:S(2)}) %collective-permute-start.44) | collective-permute-done | bytes 61472 | tf_op jit(solution)/shard_map/ppermute | solution.py:44
  253.5 7.2 %collective-permute-done.43 = bf16[448,768]{1,0:T(8,128)(2,1)S(1)} collective-permute-done((bf16[448,768]{1,0:T(8,128)(2,1)S(1)}, bf16[448,768]{1,0:T(8,128)(2,1)S(1)}, u32[]{:S(2)}, u32[]{:S(2)}) %collective-permute-start.43) | collective-permute-done | bytes 688160 | tf_op jit(solution)/shard_map/ppermute | solution.py:44
  260.7 4.2 %collective-permute-done.42 = bf16[448,768]{1,0:T(8,128)(2,1)S(1)} collective-permute-done((bf16[448,768]{1,0:T(8,128)(2,1)S(1)}, bf16[448,768]{1,0:T(8,128)(2,1)S(1)}, u32[]{:S(2)}, u32[]{:S(2)}) %collective-permute-start.42) | collective-permute-done | bytes 688160 | tf_op jit(solution)/shard_map/ppermute | solution.py:44
  (207 shorter events, 61.1 us)
Async XLA Ops:
  2.1 26.7 %collective-permute-start.2 = (bf16[768,512]{1,0:T(8,128)(2,1)S(1)}, bf16[768,512]{1,0:T(8,128)(2,1)S(1)}, u32[]{:S(2)}, u32[]{:S(2)}) collective-permute-start(bf16[768,512]{1,0:T(8,128)(2,1)S(1)} %fusion.1.refs_0_), channel_id=1, source_target_pairs={{0,3},{1,0},{2,1},{3,2},{8,11},{9,8},{10,9},{11,10},{16,19},{17,16... | collective-permute-start | bytes 2359304 | tf_op jit(solution)/shard_map/ppermute | solution.py:44
  6.2 25.5 %collective-permute-start.1 = (bf16[768,512]{1,0:T(8,128)(2,1)S(1)}, bf16[768,512]{1,0:T(8,128)(2,1)S(1)}, u32[]{:S(2)}, u32[]{:S(2)}) collective-permute-start(bf16[768,512]{1,0:T(8,128)(2,1)S(1)} %fusion.1.refs_0_), channel_id=1, source_target_pairs={{0,1},{1,2},{2,3},{3,0},{8,9},{9,10},{10,11},{11,8},{16,17},{17,18... | collective-permute-start | bytes 2359304 | tf_op jit(solution)/shard_map/ppermute | solution.py:44
  6.2 25.5 %collective-permute-start = (bf16[768,512]{1,0:T(8,128)(2,1)S(1)}, bf16[768,512]{1,0:T(8,128)(2,1)S(1)}, u32[]{:S(2)}, u32[]{:S(2)}) collective-permute-start(bf16[768,512]{1,0:T(8,128)(2,1)S(1)} %fusion.1.refs_0_), channel_id=1, source_target_pairs={{0,4},{1,5},{2,6},{3,7},{8,12},{9,13},{10,14},{11,15},{16,20},{17,... | collective-permute-start | bytes 2359304 | tf_op jit(solution)/shard_map/ppermute | solution.py:44
  25.4 36.6 %collective-permute-start.12 = (bf16[224,2304]{1,0:T(8,128)(2,1)S(1)}, bf16[224,2304]{1,0:T(8,128)(2,1)S(1)}, u32[]{:S(2)}, u32[]{:S(2)}) collective-permute-start(bf16[224,2304]{1,0:T(8,128)(2,1)S(1)} %pad_maximum_fusion.8), channel_id=1, source_target_pairs={{0,48},{1,49},{2,50},{3,51},{8,56},{9,57},{10,58},{11,59},{16,0},{... | collective-permute-start | bytes 3096584 | tf_op jit(solution)/shard_map/ppermute | solution.py:44
  26.3 35.7 %collective-permute-start.11 = (bf16[224,2304]{1,0:T(8,128)(2,1)S(1)}, bf16[224,2304]{1,0:T(8,128)(2,1)}, u32[]{:S(2)}, u32[]{:S(2)}) collective-permute-start(bf16[224,2304]{1,0:T(8,128)(2,1)S(1)} %pad_maximum_fusion.8), channel_id=1, source_target_pairs={{0,16},{1,17},{2,18},{3,19},{8,24},{9,25},{10,26},{11,27},{16,32},... | collective-permute-start | bytes 3096584 | tf_op jit(solution)/shard_map/ppermute | solution.py:44
  28.8 33.2 %collective-permute-start.10 = (bf16[224,2304]{1,0:T(8,128)(2,1)S(1)}, bf16[224,2304]{1,0:T(8,128)(2,1)S(1)}, u32[]{:S(2)}, u32[]{:S(2)}) collective-permute-start(bf16[224,2304]{1,0:T(8,128)(2,1)S(1)} %pad_maximum_fusion.8), channel_id=1, source_target_pairs={{0,64},{1,65},{2,66},{3,67},{8,72},{9,73},{10,74},{11,75},{16,80},... | collective-permute-start | bytes 3096584 | tf_op jit(solution)/shard_map/ppermute | solution.py:44
  31.7 18.8 %collective-permute-start.4 = (bf16[768,512]{1,0:T(8,128)(2,1)S(1)}, bf16[768,512]{1,0:T(8,128)(2,1)S(1)}, u32[]{:S(2)}, u32[]{:S(2)}) collective-permute-start(bf16[768,512]{1,0:T(8,128)(2,1)S(1)} %collective-permute-done.refs_1_), channel_id=1, source_target_pairs={{0,3},{1,0},{2,1},{3,2},{8,11},{9,8},{10,9},{11,10},{16,19},{17,16... | collective-permute-start | bytes 2359304 | tf_op jit(solution)/shard_map/ppermute | solution.py:44
  35.1 18.8 %collective-permute-start.3 = (bf16[768,512]{1,0:T(8,128)(2,1)S(1)}, bf16[768,512]{1,0:T(8,128)(2,1)S(1)}, u32[]{:S(2)}, u32[]{:S(2)}) collective-permute-start(bf16[768,512]{1,0:T(8,128)(2,1)S(1)} %collective-permute-done.refs_1_), channel_id=1, source_target_pairs={{0,1},{1,2},{2,3},{3,0},{8,9},{9,10},{10,11},{11,8},{16,17},{17,18... | collective-permute-start | bytes 2359304 | tf_op jit(solution)/shard_map/ppermute | solution.py:44
  54.9 17.3 %collective-permute-start.13 = (bf16[448,576]{1,0:T(8,128)(2,1)S(1)}, bf16[448,576]{1,0:T(8,128)(2,1)S(1)}, u32[]{:S(2)}, u32[]{:S(2)}) collective-permute-start(bf16[448,576]{1,0:T(8,128)(2,1)S(1)} %fusion.3), channel_id=1, source_target_pairs={{0,0},{1,16},{2,32},{3,48},{8,8},{9,24},{10,40},{11,56},{16,49},{1... | collective-permute-start | bytes 1548296 | tf_op jit(solution)/shard_map/ppermute | solution.py:44
  72.6 25.2 %collective-permute-start.18 = (bf16[224,2304]{1,0:T(8,128)(2,1)S(1)}, bf16[224,2304]{1,0:T(8,128)(2,1)S(1)}, u32[]{:S(2)}, u32[]{:S(2)}) collective-permute-start(bf16[224,2304]{1,0:T(8,128)(2,1)S(1)} %collective-permute-done.10), channel_id=1, source_target_pairs={{0,16},{1,17},{2,18},{3,19},{8,24},{9,25},{10,26},{11,27},{16,32},... | collective-permute-start | bytes 3096584 | tf_op jit(solution)/shard_map/ppermute | solution.py:44
  72.6 26.4 %collective-permute-start.19 = (bf16[224,2304]{1,0:T(8,128)(2,1)S(1)}, bf16[224,2304]{1,0:T(8,128)(2,1)}, u32[]{:S(2)}, u32[]{:S(2)}) collective-permute-start(bf16[224,2304]{1,0:T(8,128)(2,1)S(1)} %collective-permute-done.10), channel_id=1, source_target_pairs={{0,48},{1,49},{2,50},{3,51},{8,56},{9,57},{10,58},{11,59},{16,0},{... | collective-permute-start | bytes 3096584 | tf_op jit(solution)/shard_map/ppermute | solution.py:44
  74.7 23.1 %collective-permute-start.5 = (bf16[768,512]{1,0:T(8,128)(2,1)S(1)}, bf16[768,512]{1,0:T(8,128)(2,1)S(1)}, u32[]{:S(2)}, u32[]{:S(2)}) collective-permute-start(bf16[768,512]{1,0:T(8,128)(2,1)S(1)} %collective-permute-done.1.refs_2_), channel_id=1, source_target_pairs={{0,1},{1,2},{2,3},{3,0},{8,9},{9,10},{10,11},{11,8},{16,17},{17,18... | collective-permute-start | bytes 2359304 | tf_op jit(solution)/shard_map/ppermute | solution.py:44
  74.7 23.1 %collective-permute-start.6 = (bf16[768,512]{1,0:T(8,128)(2,1)S(1)}, bf16[768,512]{1,0:T(8,128)(2,1)S(1)}, u32[]{:S(2)}, u32[]{:S(2)}) collective-permute-start(bf16[768,512]{1,0:T(8,128)(2,1)S(1)} %collective-permute-done.4.refs_5_), channel_id=1, source_target_pairs={{0,3},{1,0},{2,1},{3,2},{8,11},{9,8},{10,9},{11,10},{16,19},{17,16... | collective-permute-start | bytes 2359304 | tf_op jit(solution)/shard_map/ppermute | solution.py:44
  77.9 24.0 %collective-permute-start.16 = (bf16[448,576]{1,0:T(8,128)(2,1)S(1)}, bf16[448,576]{1,0:T(8,128)(2,1)S(1)}, u32[]{:S(2)}, u32[]{:S(2)}) collective-permute-start(bf16[448,576]{1,0:T(8,128)(2,1)S(1)} %collective-permute-done.13), channel_id=1, source_target_pairs={{0,64},{1,65},{2,66},{3,67},{8,72},{9,73},{10,74},{11,75},{16,80},... | collective-permute-start | bytes 1548296 | tf_op jit(solution)/shard_map/ppermute | solution.py:44
  105.7 26.0 %collective-permute-start.22 = (bf16[224,2304]{1,0:T(8,128)(2,1)}, bf16[224,2304]{1,0:T(8,128)(2,1)}, u32[]{:S(2)}, u32[]{:S(2)}) collective-permute-start(bf16[224,2304]{1,0:T(8,128)(2,1)} %collective-permute-done.11), channel_id=1, source_target_pairs={{0,16},{1,17},{2,18},{3,19},{8,24},{9,25},{10,26},{11,27},{16,32},... | collective-permute-start | bytes 3096584 | tf_op jit(solution)/shard_map/ppermute | solution.py:44
  106.5 26.4 %collective-permute-start.23 = (bf16[224,2304]{1,0:T(8,128)(2,1)}, bf16[224,2304]{1,0:T(8,128)(2,1)}, u32[]{:S(2)}, u32[]{:S(2)}) collective-permute-start(bf16[224,2304]{1,0:T(8,128)(2,1)} %collective-permute-done.19), channel_id=1, source_target_pairs={{0,48},{1,49},{2,50},{3,51},{8,56},{9,57},{10,58},{11,59},{16,0},{... | collective-permute-start | bytes 3096584 | tf_op jit(solution)/shard_map/ppermute | solution.py:44
  134.9 21.9 %collective-permute-start.31 = (bf16[448,576]{1,0:T(8,128)(2,1)S(1)}, bf16[448,576]{1,0:T(8,128)(2,1)S(1)}, u32[]{:S(2)}, u32[]{:S(2)}) collective-permute-start(bf16[448,576]{1,0:T(8,128)(2,1)S(1)} %copy-done.24), channel_id=1, source_target_pairs={{0,16},{1,17},{2,18},{3,19},{8,24},{9,25},{10,26},{11,27},{16,32},... | collective-permute-start | bytes 1548296 | tf_op jit(solution)/shard_map/ppermute | solution.py:44
  135.3 21.6 %collective-permute-start.32 = (bf16[448,576]{1,0:T(8,128)(2,1)S(1)}, bf16[448,576]{1,0:T(8,128)(2,1)S(1)}, u32[]{:S(2)}, u32[]{:S(2)}) collective-permute-start(bf16[448,576]{1,0:T(8,128)(2,1)S(1)} %copy-done.24), channel_id=1, source_target_pairs={{0,48},{1,49},{2,50},{3,51},{8,56},{9,57},{10,58},{11,59},{16,0},{... | collective-permute-start | bytes 1548296 | tf_op jit(solution)/shard_map/ppermute | solution.py:44
  137.0 26.8 %collective-permute-start.27 = (bf16[448,576]{1,0:T(8,128)(2,1)}, bf16[448,576]{1,0:T(8,128)(2,1)S(1)}, u32[]{:S(2)}, u32[]{:S(2)}) collective-permute-start(bf16[448,576]{1,0:T(8,128)(2,1)} %copy-done.25), channel_id=1, source_target_pairs={{0,48},{1,49},{2,50},{3,51},{8,56},{9,57},{10,58},{11,59},{16,0},{... | collective-permute-start | bytes 1548296 | tf_op jit(solution)/shard_map/ppermute | solution.py:44
  142.7 21.1 %collective-permute-start.26 = (bf16[448,576]{1,0:T(8,128)(2,1)}, bf16[448,576]{1,0:T(8,128)(2,1)S(1)}, u32[]{:S(2)}, u32[]{:S(2)}) collective-permute-start(bf16[448,576]{1,0:T(8,128)(2,1)} %copy-done.25), channel_id=1, source_target_pairs={{0,16},{1,17},{2,18},{3,19},{8,24},{9,25},{10,26},{11,27},{16,32},... | collective-permute-start | bytes 1548296 | tf_op jit(solution)/shard_map/ppermute | solution.py:44
  157.0 15.8 %collective-permute-start.33 = (bf16[2,448,576]{2,1,0:T(8,128)(2,1)S(1)}, bf16[2,448,576]{2,1,0:T(8,128)(2,1)S(1)}, u32[]{:S(2)}, u32[]{:S(2)}) collective-permute-start(bf16[2,448,576]{2,1,0:T(8,128)(2,1)S(1)} %pad_maximum_fusion.5.mine), channel_id=1, source_target_pairs={{0,8},{1,9},{2,10},{3,11},{8,0},{9,1},{10,2},{11,3},{16,24},{17,25... | collective-permute-start | bytes 3096584 | tf_op jit(solution)/shard_map/ppermute | solution.py:44
  163.8 20.7 %collective-permute-start.30 = (bf16[448,768]{1,0:T(8,128)(2,1)S(1)}, bf16[448,768]{1,0:T(8,128)(2,1)S(1)}, u32[]{:S(2)}, u32[]{:S(2)}) collective-permute-start(bf16[448,768]{1,0:T(8,128)(2,1)S(1)} %get-tuple-element.76), channel_id=1, source_target_pairs={{0,6},{1,7},{2,4},{3,5},{8,14},{9,15},{10,12},{11,13},{16,23},{17,... | collective-permute-start | bytes 2064392 | tf_op jit(solution)/shard_map/ppermute | solution.py:44
  166.3 20.4 %collective-permute-start.29 = (bf16[448,768]{1,0:T(8,128)(2,1)S(1)}, bf16[448,768]{1,0:T(8,128)(2,1)S(1)}, u32[]{:S(2)}, u32[]{:S(2)}) collective-permute-start(bf16[448,768]{1,0:T(8,128)(2,1)S(1)} %get-tuple-element.74), channel_id=1, source_target_pairs={{0,0},{1,1},{2,2},{3,3},{8,8},{9,9},{10,10},{11,11},{16,17},{17,18... | collective-permute-start | bytes 2064392 | tf_op jit(solution)/shard_map/ppermute | solution.py:44
  187.0 16.6 %collective-permute-start.40 = (bf16[448,576]{1,0:T(8,128)(2,1)S(1)}, bf16[448,576]{1,0:T(8,128)(2,1)S(1)}, u32[]{:S(2)}, u32[]{:S(2)}) collective-permute-start(bf16[448,576]{1,0:T(8,128)(2,1)S(1)} %collective-permute-done.27), channel_id=1, source_target_pairs={{0,48},{1,49},{2,50},{3,51},{8,56},{9,57},{10,58},{11,59},{16,0},{... | collective-permute-start | bytes 1548296 | tf_op jit(solution)/shard_map/ppermute | solution.py:44
  188.9 15.0 %collective-permute-start.39 = (bf16[448,576]{1,0:T(8,128)(2,1)S(1)}, bf16[448,576]{1,0:T(8,128)(2,1)S(1)}, u32[]{:S(2)}, u32[]{:S(2)}) collective-permute-start(bf16[448,576]{1,0:T(8,128)(2,1)S(1)} %collective-permute-done.31), channel_id=1, source_target_pairs={{0,16},{1,17},{2,18},{3,19},{8,24},{9,25},{10,26},{11,27},{16,32},... | collective-permute-start | bytes 1548296 | tf_op jit(solution)/shard_map/ppermute | solution.py:44
  204.1 11.6 %collective-permute-start.41 = (bf16[2,448,576]{2,1,0:T(8,128)(2,1)S(1)}, bf16[2,448,576]{2,1,0:T(8,128)(2,1)S(1)}, u32[]{:S(2)}, u32[]{:S(2)}) collective-permute-start(bf16[2,448,576]{2,1,0:T(8,128)(2,1)S(1)} %pad_maximum_fusion.7.mine), channel_id=1, source_target_pairs={{0,8},{1,9},{2,10},{3,11},{8,0},{9,1},{10,2},{11,3},{16,24},{17,25... | collective-permute-start | bytes 3096584 | tf_op jit(solution)/shard_map/ppermute | solution.py:44
  204.2 14.0 %collective-permute-start.35 = (bf16[448,768]{1,0:T(8,128)(2,1)S(1)}, bf16[448,768]{1,0:T(8,128)(2,1)S(1)}, u32[]{:S(2)}, u32[]{:S(2)}) collective-permute-start(bf16[448,768]{1,0:T(8,128)(2,1)S(1)} %get-tuple-element.80), channel_id=1, source_target_pairs={{0,1},{1,2},{2,3},{3,0},{8,9},{9,10},{10,11},{11,8},{16,18},{17,19... | collective-permute-start | bytes 2064392 | tf_op jit(solution)/shard_map/ppermute | solution.py:44
  204.9 36.0 %collective-permute-start.34 = (bf16[448,768]{1,0:T(8,128)(2,1)S(1)}, bf16[448,768]{1,0:T(8,128)(2,1)S(1)}, u32[]{:S(2)}, u32[]{:S(2)}) collective-permute-start(bf16[448,768]{1,0:T(8,128)(2,1)S(1)} %get-tuple-element.79), channel_id=1, source_target_pairs={{0,3},{1,0},{2,1},{3,2},{8,11},{9,8},{10,9},{11,10},{16,16},{17,17... | collective-permute-start | bytes 2064392 | tf_op jit(solution)/shard_map/ppermute | solution.py:44
  208.7 44.8 %collective-permute-start.38 = (bf16[448,768]{1,0:T(8,128)(2,1)S(1)}, bf16[448,768]{1,0:T(8,128)(2,1)S(1)}, u32[]{:S(2)}, u32[]{:S(2)}) collective-permute-start(bf16[448,768]{1,0:T(8,128)(2,1)S(1)} %get-tuple-element.84), channel_id=1, source_target_pairs={{0,7},{1,4},{2,5},{3,6},{8,15},{9,12},{10,13},{11,14},{16,20},{17,... | collective-permute-start | bytes 2064392 | tf_op jit(solution)/shard_map/ppermute | solution.py:44
  212.0 41.5 %collective-permute-start.37 = (bf16[448,768]{1,0:T(8,128)(2,1)S(1)}, bf16[448,768]{1,0:T(8,128)(2,1)S(1)}, u32[]{:S(2)}, u32[]{:S(2)}) collective-permute-start(bf16[448,768]{1,0:T(8,128)(2,1)S(1)} %get-tuple-element.83), channel_id=1, source_target_pairs={{0,5},{1,6},{2,7},{3,4},{8,13},{9,14},{10,15},{11,12},{16,22},{17,... | collective-permute-start | bytes 2064392 | tf_op jit(solution)/shard_map/ppermute | solution.py:44
  240.9 19.8 %collective-permute-start.43 = (bf16[448,768]{1,0:T(8,128)(2,1)S(1)}, bf16[448,768]{1,0:T(8,128)(2,1)S(1)}, u32[]{:S(2)}, u32[]{:S(2)}) collective-permute-start(bf16[448,768]{1,0:T(8,128)(2,1)S(1)} %get-tuple-element.90), channel_id=1, source_target_pairs={{0,4},{1,5},{2,6},{3,7},{8,12},{9,13},{10,14},{11,15},{16,21},{17,... | collective-permute-start | bytes 2064392 | tf_op jit(solution)/shard_map/ppermute | solution.py:44
  245.1 19.9 %collective-permute-start.42 = (bf16[448,768]{1,0:T(8,128)(2,1)S(1)}, bf16[448,768]{1,0:T(8,128)(2,1)S(1)}, u32[]{:S(2)}, u32[]{:S(2)}) collective-permute-start(bf16[448,768]{1,0:T(8,128)(2,1)S(1)} %get-tuple-element.88), channel_id=1, source_target_pairs={{0,2},{1,3},{2,0},{3,1},{8,10},{9,11},{10,8},{11,9},{16,19},{17,16... | collective-permute-start | bytes 2064392 | tf_op jit(solution)/shard_map/ppermute | solution.py:44
  (45 other events, 549.6 us)
